TPU v7x, 32 devices: a whole 2x2x4 slice. The times are simulated.
32 devices in a mesh: seq: 8 (over y, x, core), chan: 4 (over z).
Axes of the slice: x: 2, y: 2, z: 4, core: 2. Of those that a mesh axis runs over, the one named last changes fastest.
Arguments:
- inner_input: bfloat16 [8192, 8192], P('seq', 'chan'), may hold values from -6 to 6
- state_maps: bfloat16 [8192, 2, 8, 128], P('seq', None, 'chan'), may hold values from -6 to 6
- gate_input: bfloat16 [8192, 8192], P('seq', 'chan'), may hold values from -6 to 6
- step_input: float32 [8192, 128], P('seq', 'chan'), may hold values from -3 to 12
- log_decay_rate: float32 [128], P('chan'), may hold values from 0 to 2.78
- step_bias: float32 [128], P('chan'), may hold values from -17 to 0
- skip_gain: float32 [128], P('chan'), may hold values from 0.5 to 1.5
- conv_kernel: float32 [4, 8192], P(None, 'chan'), may hold values from -3 to 3
- map_kernel: float32 [4, 2, 8, 128], P(None, None, 'chan'), may hold values from -3 to 3
- norm_gain: float32 [8192], P('chan'), may hold values from 0.1 to 1.9
- out_weight: bfloat16 [8192, 2048], P('chan'), may hold values from -0.09375 to 0.09375
Outputs:
- mixed_out: bfloat16 [8192, 2048], P('seq', 'chan')
All inputs are finite; a program needn't handle non-finite values.
Results may differ from a plain program's by a relative error of at most 0.011.
Values may be sent and summed in bfloat16 or wider, within the bound.
No kernel may reach another device: no remote copies, remote signals or barrier semaphores. Data moves between devices by JAX's collectives and lax.ppermute only.
A program may use at most 128 MiB of HBM per device.

v0:
```python
import jax
import jax.numpy as jnp
from jax import lax
from jax.sharding import PartitionSpec as P

HEADS = 128
HEAD_DIM = 64
STATE = 128
NGROUPS = 8
BLOCK = 256


step_limit = 0.5
epsilon = 1e-05


def passed_along(x, axis, by):
    count = lax.axis_size(axis)
    pairs = [(i, i + by) for i in range(count) if 0 <= i + by < count]
    return lax.ppermute(x, axis, pairs)


def conv_silu(padded, kernel, length):
    acc = jnp.zeros((length,) + padded.shape[1:], jnp.float32)
    for offset in range(kernel.shape[0]):
        acc = acc + kernel[offset] * padded[offset : offset + length].astype(jnp.float32)
    return jax.nn.silu(acc).astype(jnp.bfloat16)


def local(
    inner_input,
    state_maps,
    gate_input,
    step_input,
    log_decay_rate,
    step_bias,
    skip_gain,
    conv_kernel,
    map_kernel,
    norm_gain,
    out_weight,
):
    row_count = inner_input.shape[0]
    kernel_remainder = conv_kernel.shape[0] - 1
    groups = state_maps.shape[2]
    per_group = HEADS // NGROUPS
    head_count = groups * per_group
    block_count = row_count // BLOCK
    tail_inner, tail_maps = passed_along(
        (inner_input[row_count - kernel_remainder :], state_maps[row_count - kernel_remainder :]),
        "seq",
        1,
    )
    inner_conv = conv_silu(
        jnp.concatenate((tail_inner, inner_input), axis=0), conv_kernel, row_count
    )
    maps_conv = conv_silu(jnp.concatenate((tail_maps, state_maps), axis=0), map_kernel, row_count)
    step = jnp.minimum(jax.nn.softplus(step_input + step_bias), step_limit)
    log_step = step * -jnp.exp(log_decay_rate)
    step_blocks = step.reshape(block_count, BLOCK, groups, per_group)
    cumul = jnp.cumsum(log_step.reshape(block_count, BLOCK, groups, per_group), axis=1)
    x_blocks = inner_conv.reshape(block_count, BLOCK, groups, per_group, HEAD_DIM)
    b_blocks = maps_conv[:, 0].reshape(block_count, BLOCK, groups, STATE)
    c_blocks = maps_conv[:, 1].reshape(block_count, BLOCK, groups, STATE)
    scores = jnp.einsum("ctgn,csgn->cgts", c_blocks, b_blocks, preferred_element_type=jnp.float32)
    cumul_t = cumul.transpose(0, 2, 3, 1)
    gap = cumul_t[..., :, None] - cumul_t[..., None, :]
    row_ids = lax.broadcasted_iota(jnp.int32, (BLOCK, BLOCK), 0)
    col_ids = lax.broadcasted_iota(jnp.int32, (BLOCK, BLOCK), 1)
    decay = jnp.exp(jnp.where(row_ids >= col_ids, gap, -jnp.inf))
    mixing = (scores[:, :, None] * decay * step_blocks.transpose(0, 2, 3, 1)[..., None, :]).astype(
        jnp.bfloat16
    )
    y_local = jnp.einsum("cgjts,csgjp->ctgjp", mixing, x_blocks, preferred_element_type=jnp.float32)
    weighted = (
        (jnp.exp(cumul[:, -1:] - cumul) * step_blocks)[..., None] * b_blocks[:, :, :, None, :]
    ).astype(jnp.bfloat16)
    block_states = jnp.einsum(
        "csgjp,csgjn->cgjpn", x_blocks, weighted, preferred_element_type=jnp.float32
    )
    block_decay = cumul[:, -1]
    running = jnp.zeros((groups, per_group, HEAD_DIM, STATE), jnp.float32)
    local_in = []
    for block_index in range(block_count):
        local_in.append(running)
        running = (
            jnp.exp(block_decay[block_index])[..., None, None] * running + block_states[block_index]
        )
    slab_decay = jnp.sum(block_decay, axis=0)
    device_index = lax.axis_index("seq")
    decays = lax.all_gather(slab_decay[None], "seq", axis=0, tiled=True)
    before = jnp.cumsum(decays, axis=0) - decays
    through = before + decays
    mine = lax.dynamic_index_in_dim(before, device_index, 0, keepdims=False)
    shard_piece = lax.all_gather(
        running[None].astype(jnp.bfloat16), "seq", axis=0, tiled=True
    ).astype(jnp.float32)
    piece_rows = shard_piece.shape[0]
    owners = lax.broadcasted_iota(jnp.int32, (piece_rows, 1, 1), 0)
    factors = jnp.exp(jnp.where(owners < device_index, mine[None] - through, -jnp.inf))
    entering = jnp.zeros_like(running) + jnp.einsum(
        "rgj,rgjpn->gjpn", factors, shard_piece, precision=lax.Precision.HIGHEST
    )
    leading = jnp.cumsum(block_decay, axis=0) - block_decay
    state_in = (
        jnp.exp(leading)[..., None, None] * entering[None] + jnp.stack(local_in, axis=0)
    ).astype(jnp.bfloat16)
    y_carry = jnp.exp(cumul)[..., None] * jnp.einsum(
        "ctgn,cgjpn->ctgjp", c_blocks, state_in, preferred_element_type=jnp.float32
    )
    y_all = y_local + y_carry + skip_gain.reshape(groups, per_group)[:, :, None] * x_blocks
    width = per_group * HEAD_DIM
    gated = y_all.reshape(row_count, groups, width) * jax.nn.silu(
        gate_input.reshape(row_count, groups, width).astype(jnp.float32)
    )
    square_mean = jnp.mean(gated * gated, axis=-1, keepdims=True)
    normed = (
        (gated * lax.rsqrt(square_mean + epsilon) * norm_gain.reshape(groups, width))
        .astype(jnp.bfloat16)
        .reshape(row_count, head_count * HEAD_DIM)
    )
    shares = lax.psum_scatter(
        lax.dot_general(
            out_weight, normed, (((0,), (1,)), ((), ())), preferred_element_type=jnp.float32
        ),
        "chan",
        scatter_dimension=0,
        tiled=True,
    )
    return shares.T.astype(jnp.bfloat16)


def solution(mesh):
    return jax.shard_map(
        local,
        mesh=mesh,
        in_specs=(
            P("seq", "chan"),
            P("seq", None, "chan", None),
            P("seq", "chan"),
            P("seq", "chan"),
            P("chan"),
            P("chan"),
            P("chan"),
            P(None, "chan"),
            P(None, None, "chan", None),
            P("chan"),
            P("chan", None),
        ),
        out_specs=P("seq", "chan"),
        check_vma=False,
    )
```

profile of v0, /device:TPU:2, one launch (start us, length us, event | category | flops | bytes accessed | tf_op | source)
XLA Modules:
  0.0 320.6 jit_solution(11899223213507309769)
XLA Ops:
  6.5 0.0 all-gather.4.cloned.1.call-start
  6.5 0.8 slice.97
  7.3 0.3 copy.85
  7.6 1.9 collective-permute-start
  9.6 1.4 copy.88
  10.9 3.5 %collective-permute-start.1 = (bf16[3,2,2,128]{3,0,2,1:T(4,128)(2,1)S(1)}, bf16[3,2,2,128]{3,0,2,1:T(4,128)(2,1)S(1)}, u32[]{:S(2)}, u32[]{:S(2)}) collective-permute-start(bf16[3,2,2,128]{3,0,2,1:T(4,128)(2,1)S(1)} %slice.129), channel_id=1, source_target_pairs={{0,4},{4,8},{8,12},{12,16},{16,20},{20,24},{24,28},{1,5},{5,9},{9,... | collective-permute-start | bytes 9224 | tf_op jit(solution)/shard_map/ppermute | solution.py:20
  14.4 0.7 exponential_negate_fusion
  15.1 0.7 slice_bitcast_fusion.3
  15.8 0.9 fusion.47
  16.8 1.1 broadcast_multiply_fusion
  17.9 0.1 reshape.120
  18.0 0.1 reshape.123
  18.0 4.6 %reduce-window.6 = f32[4,16,2,2,128]{4,1,2,3,0:T(8,128)S(1)} reduce-window(f32[4,16,2,2,128]{4,1,2,3,0:T(8,128)S(1)} %copy_bitcast_fusion, f32[]{:T(128)} %constant.23.clone.1), window={size=1x1x1x1x128 pad=0_0x0_0x0_0x0_0x127_0}, to_apply=%region_0.1 | reduce-window | flops 4161536 | bytes 262148 | tf_op jit(solution)/shard_map/reduce-window
  22.6 0.1 slice.136
  22.7 0.2 copy.95
  22.9 0.1 bitcast_bitcast_fusion.1
  23.0 0.2 slice_reduce_fusion
  23.2 0.8 fusion.44
  23.9 0.2 fusion.39
  24.1 6.4 %copy.86 = bf16[1024,2048]{0,1:T(8,128)(2,1)} copy(bf16[1024,2048]{1,0:T(8,128)(2,1)} %param.11) | data formatting | bytes 8388608 | tf_op args[0]
  30.5 0.0 collective-permute-done.1
  30.6 1.5 multiply_convert_fusion.7
  32.0 0.1 fusion.46
  32.1 0.0 collective-permute-done
  32.1 15.8 %multiply_convert_fusion.4 = bf16[1024,2048]{0,1:T(8,128)(2,1)} fusion(bf16[1024,2048]{0,1:T(8,128)(2,1)} %copy.86, bf16[3,2048]{0,1:T(8,128)(2,1)S(1)} %collective-permute-done, f32[2048]{0:T(1024)S(1)} %bitcast.103, f32[2048]{0:T(1024)S(1)} %bitcast.104, f32[2048]{0:T(1024)S(1)} %bitcast.102, f32[2048]{0:T(1024)S(1)} %bitcast.101), kind=kLoop, calls=%fused_computation.19 | loop fusion | flops 52428800 | bytes 8433664 | tf_op jit(solution)/shard_map/convert_element_type | solution.py:27
  48.0 7.9 %reshape.119 = bf16[4,256,2,16,64]{1,0,4,3,2:T(4,128)(2,1)} reshape(bf16[1024,2048]{0,1:T(8,128)(2,1)} %multiply_convert_fusion.4) | data formatting | bytes 8388608 | tf_op jit(solution)/shard_map/reshape | solution.py:62
  55.9 0.0 copy-start.5
  55.9 8.5 %fusion.7 = f32[4,2,16,64,128]{4,3,2,1,0:T(8,128)S(1)} fusion(f32[4,256,2,16]{1,3,2,0:T(8,128)S(1)} %get-tuple-element.22, bf16[4,256,2,16,64]{1,0,4,3,2:T(4,128)(2,1)} %reshape.119, bf16[4,256,2,128]{3,1,0,2:T(8,128)(2,1)S(1)} %bitcast.97), kind=kOutput, calls=%fused_computation.9 | convolution fusion | flops 545259520 | bytes 9043968 | tf_op jit(solution)/shard_map/csgjp,csgjn->cgjpn/dot_general | solution.py:78
  64.4 1.5 fusion.29
  65.9 0.0 all-gather.4.cloned.1.call-update
  65.9 0.0 reduce-scatter.2.cloned.1.call-start
  66.0 0.0 copy-done.5
  66.0 0.1 mul.290
  66.1 8.1 %all-gather.1 = f32[8,2,16]{2,1,0:T(2,128)S(1)} all-gather(f32[1,2,16]{2,1,0:T(2,128)S(1)} %bitcast.105), channel_id=2, replica_groups=mesh['seq'=8,'chan'=4] {'seq'}, dimensions={0}, use_global_device_ids=true | all-gather | bytes 1152 | tf_op jit(solution)/shard_map/all_gather | solution.py:91
  74.2 0.1 exponential_bitcast_fusion
  74.3 0.1 copy.109
  74.4 6.5 %copy.106 = bf16[1024,2048]{0,1:T(8,128)(2,1)} copy(bf16[1024,2048]{1,0:T(8,128)(2,1)} %param.13) | data formatting | bytes 8388608 | tf_op args[2]
  80.8 8.8 %reshape.125 = f32[4,256,2,16,64]{1,0,4,3,2:T(4,128)} reshape(bf16[1024,2048]{0,1:T(8,128)(2,1)} %copy.106) | data formatting | bytes 12582912 | tf_op jit(solution)/shard_map/convert_element_type | solution.py:114
  89.7 1.8 fusion.31
  91.5 11.6 %all-gather.4.cloned.1.call-done = bf16[8,2,16,64,128]{4,3,2,1,0:T(8,128)(2,1)} async-done(((bf16[1,2,16,64,128]{4,3,2,1,0:T(8,128)(2,1)}), bf16[8,2,16,64,128]{4,3,2,1,0:T(8,128)(2,1)}) %all-gather.4.cloned.1.call-update) | async-done | bytes 4194320 | tf_op jit(solution)/shard_map/all_gather | solution.py:95
  103.1 7.1 %fusion.17 = f32[2,16,1,64,128]{4,2,3,1,0:T(1,128)S(1)} fusion(f32[8,2,16,1,1]{0,3,4,2,1:T(1,128)S(1)} %copy.109, bf16[8,2,16,64,128]{4,3,2,1,0:T(8,128)(2,1)} %all-gather.4.cloned.1.call-done), kind=kOutput, calls=%fused_computation.30 | convolution fusion | flops 25165824 | bytes 5243904 | tf_op jit(solution)/shard_map/rgj,rgjpn->gjpn/dot_general | solution.py:101
  110.2 0.0 slice-start
  110.2 0.0 copy-start.1
  110.3 0.0 copy-start.2
  110.3 0.0 copy-start.3
  110.3 0.0 slice-start.1
  110.3 2.8 fusion.21
  113.1 0.0 slice-done
  113.1 0.9 copy-done.1
  114.0 0.6 copy-done.2
  114.6 0.0 copy-done.3
  114.6 1.2 slice-done.1
  115.9 14.4 %multiply_reduce_fusion = (f32[4,256,2]{1,2,0:T(2,128)S(1)}, f32[4,256,2,16,64]{1,4,3,2,0:T(8,128)}) fusion(f32[4,256,2,16,64]{1,0,4,3,2:T(4,128)S(1)} %bitcast.94, bf16[4,256,2,16,64]{1,0,4,3,2:T(4,128)(2,1)S(1)} %copy-done.1, f32[2,16]{1,0:T(2,128)S(1)} %mul.290, f32[4,2,16,64,256]{4,3,2,1,0:T(8,128)S(1)} %fusion.21, f32[4,256,2,16]{1,3,2,0:T(8,128)S(1)} %copy-done.3, ...), kind=kOutput, calls=%fused_computation.16 | convolution fusion | flops 1140848640 | bytes 31924352 | tf_op jit(solution)/shard_map/cgjts,csgjp->ctgjp/dot_general | solution.py:74
  130.3 13.8 %copy.105 = f32[4,256,2,16,64]{1,0,4,3,2:T(4,128)} copy(f32[4,256,2,16,64]{1,4,3,2,0:T(8,128)} %get-tuple-element.32) | data formatting | bytes 16777216 | tf_op jit(solution)/shard_map/add | solution.py:111
  144.0 0.0 copy-start
  144.0 0.0 copy-start.4
  144.0 5.6 %copy.117 = f32[256,8,4,256]{3,1,2,0:T(8,128)S(1)} copy(f32[256,8,4,256]{3,2,1,0:T(4,128)} %bitcast.91) | data formatting | bytes 16777216
  149.7 0.0 copy-done
  149.7 0.0 copy-done.4
  149.7 2.9 fusion.9
  152.6 13.8 %convolution_bitcast_fusion = f32[2048,1024]{0,1:T(8,128)} fusion(bf16[1024,2048]{0,1:T(8,128)(2,1)S(1)} %fusion.9, bf16[2048,2048]{1,0:T(8,128)(2,1)} %param.21), kind=kOutput, calls=%fused_computation.24 | convolution fusion | flops 8589934592 | bytes 20971520 | tf_op jit(solution)/shard_map/dot_general | solution.py:123
  166.4 0.0 reduce-scatter.2.cloned.1.call-update
  166.5 144.6 %reduce-scatter.2.cloned.1.call-done = f32[512,1024]{0,1:T(8,128)} async-done(((f32[2048,1024]{0,1:T(8,128)}), f32[512,1024]{0,1:T(8,128)}) %reduce-scatter.2.cloned.1.call-update) | async-done | bytes 2097168 | tf_op jit(solution)/shard_map/reduce_scatter | solution.py:122
  311.1 2.7 convert_bitcast_fusion
  (14 shorter events, 0.2 us)
Async XLA Ops:
  6.5 96.6 %all-gather.4.cloned.1.call-start = ((), (), s32[]{:S(2)}) async-start(), calls=%async_computation.1 | async-start | bytes 4718592 | tf_op jit(solution)/shard_map/all_gather | solution.py:95
  7.6 24.5 %collective-permute-start = (bf16[3,2048]{0,1:T(8,128)(2,1)S(1)}, bf16[3,2048]{0,1:T(8,128)(2,1)S(1)}, u32[]{:S(2)}, u32[]{:S(2)}) collective-permute-start(bf16[3,2048]{0,1:T(8,128)(2,1)S(1)} %copy.85), channel_id=1, source_target_pairs={{0,4},{4,8},{8,12},{12,16},{16,20},{20,24},{24,28},{1,5},{5,9},{9,... | collective-permute-start | bytes 36872 | tf_op jit(solution)/shard_map/ppermute | solution.py:20
  10.9 19.6 %collective-permute-start.1 = (bf16[3,2,2,128]{3,0,2,1:T(4,128)(2,1)S(1)}, bf16[3,2,2,128]{3,0,2,1:T(4,128)(2,1)S(1)}, u32[]{:S(2)}, u32[]{:S(2)}) collective-permute-start(bf16[3,2,2,128]{3,0,2,1:T(4,128)(2,1)S(1)} %slice.129), channel_id=1, source_target_pairs={{0,4},{4,8},{8,12},{12,16},{16,20},{20,24},{24,28},{1,5},{5,9},{9,... | collective-permute-start | bytes 9224 | tf_op jit(solution)/shard_map/ppermute | solution.py:20
  55.9 10.1 %copy-start.5 = (f32[32]{0:T(128)S(1)}, f32[32]{0:T(128)}, u32[]{:S(2)}) copy-start(f32[32]{0:T(128)} %param.17) | copy-start | bytes 388
  65.9 245.2 %reduce-scatter.2.cloned.1.call-start = ((), (), s32[]{:S(2)}) async-start(), calls=%async_computation.2 | async-start | bytes 10485760 | tf_op jit(solution)/shard_map/reduce_scatter | solution.py:122
  110.2 2.9 slice-start
  110.2 3.8 %copy-start.1 = (bf16[4,256,2,16,64]{1,0,4,3,2:T(4,128)(2,1)S(1)}, bf16[4,256,2,16,64]{1,0,4,3,2:T(4,128)(2,1)}, u32[]{:S(2)}) copy-start(bf16[4,256,2,16,64]{1,0,4,3,2:T(4,128)(2,1)} %reshape.119) | copy-start | bytes 12582916
  110.3 4.4 %copy-start.2 = (f32[4,2,256,256]{3,2,1,0:T(8,128)S(1)}, f32[4,2,256,256]{3,2,1,0:T(8,128)}, u32[]{:S(2)}) copy-start(f32[4,2,256,256]{3,2,1,0:T(8,128)} %fusion.31) | copy-start | bytes 6291460
  110.3 4.4 %copy-start.3 = (f32[4,256,2,16]{1,3,2,0:T(8,128)S(1)}, f32[4,256,2,16]{1,3,2,0:T(8,128)}, u32[]{:S(2)}) copy-start(f32[4,256,2,16]{1,3,2,0:T(8,128)} %get-tuple-element.21) | copy-start | bytes 393220
  110.3 5.6 %slice-start.1 = ((s8[8388608]{0:T(1024)(128)(4,1)}), s8[4194304]{0:T(1024)(128)(4,1)S(1)}, s32[]{:S(2)}) async-start(s8[8388608]{0:T(1024)(128)(4,1)} %bitcast.93), calls=%async_computation.4 | async-start | bytes 8388608
  144.0 5.7 %copy-start = (bf16[1024,2048]{0,1:T(8,128)(2,1)S(1)}, bf16[1024,2048]{0,1:T(8,128)(2,1)}, u32[]{:S(2)}) copy-start(bf16[1024,2048]{0,1:T(8,128)(2,1)} %copy.106) | copy-start | bytes 12582916
  144.0 5.7 %copy-start.4 = (f32[2048]{0:T(1024)S(1)}, f32[2048]{0:T(1024)}, u32[]{:S(2)}) copy-start(f32[2048]{0:T(1024)} %param.20) | copy-start | bytes 24580
Sparse Core Ops, SparseCore 0:
  66.0 37.0 all-gather.3
  166.6 144.4 reduce-scatter.1
where the time goes:
time: 323 us; the launch traced here: 321 us
  waiting for transfers between devices  156 us (48%)
  local copies, waits for them, and re-layouts  56.6 us (18%)
  matrix products  48.4 us (15%)
  other arithmetic  32.1 us (10%)
  between operations  13.7 us (4%)
  blocking collectives  8.09 us (3%)
  starting transfers between devices  5.47 us (2%)
    reduce_scatter x1, waiting for transfers between devices, local(): lax.psum_scatter(lax.dot_general(out_weight, normed, (((0,), (1,)), ((),...  145 us
    unnamed x20, local copies, waits for them, and re-layouts  22.6 us
    convert_element_type x2, other arithmetic, conv_silu(): return jax.nn.silu(acc).astype(jnp.bfloat16)  17.3 us
    dot_general x1, matrix products, local(): jnp.einsum('cgjts,csgjp->ctgjp', mixing, x_blocks, preferred_element_type...  14.4 us
    dot_general x1, matrix products, local(): lax.dot_general(out_weight, normed, (((0,), (1,)), ((), ())), preferred_e...  13.8 us
    add x1, local copies, waits for them, and re-layouts, local(): y_local + y_carry  13.8 us
    all_gather x1, waiting for transfers between devices, local(): lax.all_gather(running[None].astype(jnp.bfloat16), 'seq', axis=0, tiled=T...  11.6 us
    convert_element_type x1, local copies, waits for them, and re-layouts, local(): gate_input.reshape(row_count, groups, width).astype(jnp.float32)  8.83 us
  transfers between devices with their start and end apart: 4, of which 2 were waited for; matrix products, arithmetic and copies ran while one was open for 11% of the time, Pallas kernels for 0%

commit v1 on v0

v1 whole, which is shorter than its diff:
```python
import functools

import jax
import jax.numpy as jnp
from jax import lax
from jax.experimental import pallas as pl
from jax.experimental.pallas import tpu as pltpu
from jax.sharding import PartitionSpec as P

HEAD_DIM = 64
STATE = 128
BLK = 128
LANES = 128
HALO = 8
CHUNKS = 4

step_limit = 0.5
epsilon = 1e-05
LOG2E = 1.4426950408889634
F32 = jnp.float32
BF16 = jnp.bfloat16
VMEM_LIMIT = 56 * 1024 * 1024


def silu(v):
    half = 0.5 * v
    return half + half * jnp.tanh(half)


def high_low(v):
    high = v.astype(BF16).astype(F32)
    return high, v - high


def spread(first_row, heads, width):
    row = lax.broadcasted_iota(jnp.int32, (LANES, width), 0) - first_row
    col = lax.broadcasted_iota(jnp.int32, (LANES, width), 1)
    low = jnp.logical_and(col >= row * HEAD_DIM, col < (row + 1) * HEAD_DIM)
    again = row - heads
    high = jnp.logical_and(col >= again * HEAD_DIM, col < (again + 1) * HEAD_DIM)
    return jnp.where(jnp.logical_or(low, high), 1.0, 0.0).astype(BF16)


def dot(a, b):
    return jnp.dot(a, b, preferred_element_type=F32)


def dot_t(a, b):
    return lax.dot_general(a, b, (((1,), (1,)), ((), ())), preferred_element_type=F32)


def padded(rows):
    return jnp.concatenate([rows, jnp.zeros((LANES - rows.shape[0], rows.shape[1]), rows.dtype)], 0)


def states_kernel(
    x_ref, maps_ref, step_ref, tail_ref, par_ref, ck_ref, mk_ref,
    xc_ref, bc_ref, crow_ref, ec_ref, cols_ref, sloc_ref, pay_ref,
    lead, state, prev_x, prev_m, e_w, pick, tri,
):
    b = pl.program_id(0)
    heads = step_ref.shape[0]
    width = x_ref.shape[1]
    parts = mk_ref.shape[0] // 4
    groups = parts // 2
    gw = width // groups

    @pl.when(b == 0)
    def _():
        lead[...] = jnp.zeros_like(lead)
        state[...] = jnp.zeros_like(state)
        prev_x[...] = tail_ref[:, :width].astype(F32)
        for q in range(parts):
            prev_m[q] = tail_ref[:, width + q * STATE : width + (q + 1) * STATE].astype(F32)
        e_w[...] = spread(0, heads, width)
        row = lax.broadcasted_iota(jnp.int32, pick.shape, 0)
        col = lax.broadcasted_iota(jnp.int32, pick.shape, 1)
        source = (row & (BLK - 1)) * parts + row // BLK
        pick[...] = jnp.where(col == source, 1.0, 0.0).astype(BF16)
        row = lax.broadcasted_iota(jnp.int32, tri.shape, 0)
        col = lax.broadcasted_iota(jnp.int32, tri.shape, 1)
        tri[...] = jnp.where(row <= col, 1.0, 0.0).astype(BF16)

    bias, rate, = par_ref[:, 0:1], -jnp.exp(par_ref[:, 1:2])
    v = step_ref[...] + bias
    step = jnp.minimum(jnp.maximum(v, 0.0) + jnp.log1p(jnp.exp(-jnp.abs(v))), step_limit)
    log_step = rate * step
    first, rest = high_low(log_step)
    second, third = high_low(rest)
    sums = dot(jnp.concatenate([first, second, third], 0).astype(BF16), tri[...])
    cum = sums[:heads] + sums[heads : 2 * heads] + sums[2 * heads :]
    total = cum[:, BLK - 1 : BLK]
    weight = jnp.exp(total - cum) * step
    leading = lead[:, 0:1]
    lead[...] = jnp.broadcast_to(leading + total, lead.shape)
    grown = jnp.exp(cum)
    entered = jnp.exp(cum + leading)
    crow_ref[...] = (cum - jnp.log(step)) * LOG2E
    one = padded(jnp.concatenate(high_low(weight), 0)).T
    two = padded(jnp.concatenate(high_low(grown), 0)).T
    three = padded(jnp.concatenate((cum * LOG2E,) + high_low(entered), 0)).T
    ec_ref[...] = two.astype(BF16)
    cols_ref[...] = three
    expanded = dot(
        jnp.concatenate([one, two[BLK - HALO :]], 0).astype(BF16), e_w[...]
    )

    sorted_maps = dot(pick[...], maps_ref[...])
    b_t = []
    for q in range(parts):
        cur = sorted_maps[q * BLK : (q + 1) * BLK]
        full = jnp.concatenate([prev_m[q], cur], 0)
        acc = cur * mk_ref[3 * parts + q : 3 * parts + q + 1]
        for back in range(1, 4):
            k = (3 - back) * parts + q
            acc = acc + pltpu.roll(full, back, 0)[HALO:] * mk_ref[k : k + 1]
        prev_m[q] = cur[BLK - HALO :]
        conv = silu(acc)
        bc_ref[:, q * STATE : (q + 1) * STATE] = conv.astype(BF16)
        if q < groups:
            b_t.append(conv.astype(BF16).astype(F32).T.astype(BF16))

    cw = 256
    for c in range(0, width, cw):
        at = slice(c, c + cw)
        cur = x_ref[:, at].astype(F32)
        full = jnp.concatenate([prev_x[:, at], cur], 0)
        acc = cur * ck_ref[3:4, at]
        for back in range(1, 4):
            acc = acc + pltpu.roll(full, back, 0)[HALO:] * ck_ref[3 - back : 4 - back, at]
        prev_x[:, at] = cur[BLK - HALO :]
        conv = silu(acc).astype(BF16)
        xc_ref[:, at] = conv
        weighted = (conv.astype(F32) * expanded[:BLK, at]).astype(BF16)
        before = state[:, at]
        sloc_ref[0, :, at] = before.astype(BF16)
        after = expanded[BLK + HALO - 1 : BLK + HALO, at] * before + dot(b_t[c // gw], weighted)
        state[:, at] = after
        pay_ref[:, at] = after.astype(BF16)
    pay_ref[:, width:] = jnp.broadcast_to(three[BLK - 1 :], (STATE, LANES)).astype(BF16)


def local_kernel(xc_ref, bc_ref, crow_ref, ec_ref, cols_ref, sloc_ref, gain_ref, y_ref, e_c):
    heads = crow_ref.shape[0]
    width = xc_ref.shape[1]
    groups = bc_ref.shape[1] // (2 * STATE)
    gw = width // groups

    @pl.when(pl.program_id(0) == 0)
    def _():
        e_c[...] = spread(0, heads, width)

    lane = lax.broadcasted_iota(jnp.int32, (BLK, LANES), 1)
    row = lax.broadcasted_iota(jnp.int32, (BLK, BLK), 0)
    left = lane < HEAD_DIM
    causal = row >= lax.broadcasted_iota(jnp.int32, (BLK, BLK), 1)
    for g in range(groups):
        b_g = bc_ref[:, g * STATE : (g + 1) * STATE]
        c_g = bc_ref[:, (groups + g) * STATE : (groups + g + 1) * STATE]
        scores = jnp.where(causal, dot_t(c_g, b_g), 0.0)
        for c in range(g * gw, (g + 1) * gw, LANES):
            at = slice(c, c + LANES)
            mixing = []
            for h in (c // HEAD_DIM, c // HEAD_DIM + 1):
                gap = jnp.minimum(cols_ref[:, h : h + 1] - crow_ref[h : h + 1], 0.0)
                mixing.append((jnp.exp2(gap) * scores).astype(BF16))
            x = xc_ref[:, at]
            nil = jnp.zeros_like(x)
            stacked = jnp.concatenate([jnp.where(left, x, nil), jnp.where(left, nil, x)], 0)
            y = dot(jnp.concatenate(mixing, 1), stacked)
            carry = dot(c_g, sloc_ref[0, :, at])
            y = y + dot(ec_ref[...], e_c[:, at]) * carry + gain_ref[:, at] * x.astype(F32)
            y_ref[:, at] = y.astype(BF16)


def prefix_kernel(pay_ref, out_ref, *, heads):
    width = out_ref.shape[2]
    decays = dot(pay_ref[:, 0, width:], spread(heads, heads, width))
    running = jnp.zeros(out_ref.shape[1:], F32)
    for slab in range(out_ref.shape[0]):
        out_ref[slab] = running.astype(BF16)
        running = decays[slab : slab + 1] * running + pay_ref[slab, :, :width].astype(F32)


def project_kernel(y_ref, bc_ref, cols_ref, enter_ref, gate_ref, gain_ref, w_ref, out_ref, e_c, *, heads):
    width = y_ref.shape[1]
    groups = bc_ref.shape[1] // (2 * STATE)
    gw = width // groups
    count, _, part = out_ref.shape

    @pl.when(pl.program_id(0) == 0)
    def _():
        e_c[...] = spread(heads, heads, width)

    grown = cols_ref[...].astype(BF16)
    normed = []
    for g in range(groups):
        at = slice(g * gw, (g + 1) * gw)
        c_g = bc_ref[:, (groups + g) * STATE : (groups + g + 1) * STATE]
        carry = dot(c_g, enter_ref[:, at])
        y = y_ref[:, at].astype(F32) + dot(grown, e_c[:, at]) * carry
        gated = y * silu(gate_ref[:, at].astype(F32))
        square_mean = jnp.mean(gated * gated, axis=-1, keepdims=True)
        normed.append((gated * lax.rsqrt(square_mean + epsilon) * gain_ref[:, at]).astype(BF16))
    normed = jnp.concatenate(normed, 1)
    for k in range(count):
        out_ref[k] = dot(normed, w_ref[:, k * part : (k + 1) * part]).astype(BF16)


def params():
    return pltpu.CompilerParams(
        dimension_semantics=("arbitrary",), vmem_limit_bytes=VMEM_LIMIT
    )


def whole(shape):
    return pl.BlockSpec(shape, lambda b: (0,) * len(shape))


def rows(count, width, start=0):
    return pl.BlockSpec((count, width), lambda b: (start + b, 0))


def local(
    inner_input, state_maps, gate_input, step_input, log_decay_rate, step_bias,
    skip_gain, conv_kernel, map_kernel, norm_gain, out_weight,
):
    tokens, width = inner_input.shape
    groups = state_maps.shape[2]
    parts = 2 * groups
    heads = step_input.shape[1]
    blocks = tokens // BLK
    slabs = lax.axis_size("seq")
    chans = lax.axis_size("chan")
    features = out_weight.shape[1]
    map_width = parts * STATE

    tail = jnp.concatenate(
        [inner_input[tokens - HALO :], state_maps[tokens - HALO :].reshape(HALO, map_width)], 1
    )
    tail = lax.ppermute(tail, "seq", [(i, i + 1) for i in range(slabs - 1)])
    per_head = jnp.stack([step_bias, log_decay_rate], 1)
    xc, bc, crow, ec, cols, sloc, pay = pl.pallas_call(
        states_kernel,
        grid=(blocks,),
        in_specs=[
            rows(BLK, width),
            rows(BLK * parts, STATE),
            pl.BlockSpec((heads, BLK), lambda b: (0, b)),
            whole((HALO, width + map_width)),
            whole((heads, 2)),
            whole((4, width)),
            whole((4 * parts, STATE)),
        ],
        out_specs=[
            rows(BLK, width),
            rows(BLK, map_width),
            pl.BlockSpec((heads, BLK), lambda b: (0, b)),
            rows(BLK, LANES),
            rows(BLK, LANES),
            pl.BlockSpec((1, STATE, width), lambda b: (b, 0, 0)),
            whole((STATE, width + LANES)),
        ],
        out_shape=[
            jax.ShapeDtypeStruct((tokens, width), BF16),
            jax.ShapeDtypeStruct((tokens, map_width), BF16),
            jax.ShapeDtypeStruct((heads, tokens), F32),
            jax.ShapeDtypeStruct((tokens, LANES), BF16),
            jax.ShapeDtypeStruct((tokens, LANES), F32),
            jax.ShapeDtypeStruct((blocks, STATE, width), BF16),
            jax.ShapeDtypeStruct((STATE, width + LANES), BF16),
        ],
        scratch_shapes=[
            pltpu.VMEM((heads, LANES), F32),
            pltpu.VMEM((STATE, width), F32),
            pltpu.VMEM((HALO, width), F32),
            pltpu.VMEM((parts, HALO, STATE), F32),
            pltpu.VMEM((LANES, width), BF16),
            pltpu.VMEM((BLK * parts, BLK * parts), BF16),
            pltpu.VMEM((BLK, BLK), BF16),
        ],
        compiler_params=params(),
        name="states",
    )(
        inner_input, state_maps.reshape(tokens * parts, STATE), step_input.T, tail, per_head,
        conv_kernel, map_kernel.reshape(4 * parts, STATE),
    )

    part = STATE // slabs
    arrived = lax.all_to_all(
        pay.reshape(slabs, part, width + LANES), "seq", split_axis=0, concat_axis=0, tiled=True
    )

    gain = jnp.repeat(skip_gain, HEAD_DIM).reshape(1, width)

    def local_part(start, count):
        return pl.pallas_call(
            local_kernel,
            grid=(count,),
            in_specs=[
                rows(BLK, width, start),
                rows(BLK, map_width, start),
                pl.BlockSpec((heads, BLK), lambda b: (0, b + start)),
                rows(BLK, LANES, start),
                rows(BLK, LANES, start),
                pl.BlockSpec((1, STATE, width), lambda b: (b + start, 0, 0)),
                whole((1, width)),
            ],
            out_specs=rows(BLK, width),
            out_shape=jax.ShapeDtypeStruct((count * BLK, width), BF16),
            scratch_shapes=[pltpu.VMEM((LANES, width), BF16)],
            compiler_params=params(),
            name="local_part",
        )(xc, bc, crow, ec, cols, sloc, gain)

    half = blocks // 2
    y_halves = [local_part(0, half), local_part(half, blocks - half)]

    entering = pl.pallas_call(
        functools.partial(prefix_kernel, heads=heads),
        out_shape=jax.ShapeDtypeStruct((slabs, part, width), BF16),
        compiler_params=pltpu.CompilerParams(vmem_limit_bytes=VMEM_LIMIT),
        name="prefix",
    )(arrived)
    entering = lax.all_to_all(entering, "seq", split_axis=0, concat_axis=0, tiled=True)
    entering = entering.reshape(STATE, width)

    pieces = []
    per_chunk = blocks // CHUNKS
    norm_row = norm_gain.reshape(1, width)
    for chunk in range(CHUNKS):
        start = chunk * per_chunk
        y_half, y_start = (y_halves[0], start) if start < half else (y_halves[1], start - half)
        shares = pl.pallas_call(
            functools.partial(project_kernel, heads=heads),
            grid=(per_chunk,),
            in_specs=[
                rows(BLK, width, y_start),
                rows(BLK, map_width, start),
                rows(BLK, LANES, start),
                whole((STATE, width)),
                rows(BLK, width, start),
                whole((1, width)),
                whole((width, features)),
            ],
            out_specs=pl.BlockSpec((chans, BLK, features // chans), lambda b: (0, b, 0)),
            out_shape=jax.ShapeDtypeStruct((chans, per_chunk * BLK, features // chans), BF16),
            scratch_shapes=[pltpu.VMEM((LANES, width), BF16)],
            compiler_params=params(),
            name="project",
        )(y_half, bc, cols, entering, gate_input, norm_row, out_weight)
        piece = lax.psum_scatter(shares, "chan", scatter_dimension=0, tiled=True)
        pieces.append(piece.reshape(per_chunk * BLK, features // chans))
    return jnp.concatenate(pieces, 0)


def solution(mesh):
    return jax.shard_map(
        local,
        mesh=mesh,
        in_specs=(
            P("seq", "chan"),
            P("seq", None, "chan", None),
            P("seq", "chan"),
            P("seq", "chan"),
            P("chan"),
            P("chan"),
            P("chan"),
            P(None, "chan"),
            P(None, None, "chan", None),
            P("chan"),
            P("chan", None),
        ),
        out_specs=P("seq", "chan"),
        check_vma=False,
    )
```

time: 323 us -> 194 us (0.60)
  waiting for transfers between devices: 156 us -> 80.4 us
  Pallas kernels: 0 us -> 70.7 us
  local copies, waits for them, and re-layouts: 56.6 us -> 4.33 us
  matrix products: 48.4 us -> 0 us
  other arithmetic: 32.1 us -> 2.91 us
  blocking collectives: 8.09 us -> 13 us
    pallas_call x0 -> x8, Pallas kernels: none -> 70.7 us  [the longest x4 35.7 us: local(): pl.pallas_call(functools.partial(project_kernel, heads=heads), grid=(per_...]
    reduce_scatter x1 -> x4, waiting for transfers between devices: 145 us -> 78.2 us  [local(): piece = lax.psum_scatter(shares, 'chan', scatter_dimension=0, tiled=True)]
    dot_general x6 -> x0, matrix products: 48.4 us -> none  [the longest x1 14.4 us: local(): jnp.einsum('cgjts,csgjp->ctgjp', mixing, x_blocks, preferred_element_type...]
    convert_element_type x5 -> x0, other arithmetic: 24.4 us -> none  [the longest x2 17.3 us: conv_silu(): return jax.nn.silu(acc).astype(jnp.bfloat16)]
    unnamed x20 -> x6, local copies, waits for them, and re-layouts: 22.6 us -> 1.43 us
    add x1 -> x0, local copies, waits for them, and re-layouts: 13.8 us -> none  [local(): y_local + y_carry]
    all_to_all x0 -> x1, blocking collectives: none -> 13 us  [local(): lax.all_to_all(pay.reshape(slabs, part, width + LANES), 'seq', split_axis...]
    all_gather x1 -> x0, waiting for transfers between devices: 11.6 us -> none  [local(): lax.all_gather(running[None].astype(jnp.bfloat16), 'seq', axis=0, tiled=T...]
  transfers between devices with their start and end apart: 4 -> 6, of which waited for: 2 -> 5; matrix products, arithmetic and copies ran while one was open for 11% -> 1% of each run, Pallas kernels for 0% -> 22%
where the time goes in v1:
time: 194 us; the launch traced here: 192 us
  waiting for transfers between devices  80.4 us (41%)
  Pallas kernels  70.7 us (36%)
  between operations  13.2 us (7%)
  blocking collectives  13 us (7%)
  starting transfers between devices  7.09 us (4%)
  local copies, waits for them, and re-layouts  4.33 us (2%)
  other arithmetic  2.91 us (2%)
    reduce_scatter x4, waiting for transfers between devices, local(): piece = lax.psum_scatter(shares, 'chan', scatter_dimension=0, tiled=True)  78.2 us
    pallas_call x4, Pallas kernels, local(): pl.pallas_call(functools.partial(project_kernel, heads=heads), grid=(per_...  35.7 us
    pallas_call x1, Pallas kernels, local(): pl.pallas_call(states_kernel, grid=(blocks,), in_specs=[rows(BLK, width),...  17.8 us
    pallas_call x2, Pallas kernels, local_part(): pl.pallas_call(local_kernel, grid=(count,), in_specs=[rows(BLK, width, st...  14.7 us
    all_to_all x1, blocking collectives, local(): lax.all_to_all(pay.reshape(slabs, part, width + LANES), 'seq', split_axis...  13 us
    all_to_all x1, starting transfers between devices, local(): lax.all_to_all(entering, 'seq', split_axis=0, concat_axis=0, tiled=True)  4.86 us
  transfers between devices with their start and end apart: 6, of which 5 were waited for; matrix products, arithmetic and copies ran while one was open for 1% of the time, Pallas kernels for 22%

profile of v1, /device:TPU:2, one launch (start us, length us, event | category | flops | bytes accessed | tf_op | source)
XLA Modules:
  0.0 191.7 jit_solution(13996085145385111212)
XLA Ops:
  6.5 0.8 slice.6
  7.3 0.7 slice.7
  8.0 1.9 %collective-permute-start = (bf16[8,2560]{1,0:T(8,128)(2,1)S(1)}, bf16[8,2560]{1,0:T(8,128)(2,1)S(1)}, u32[]{:S(2)}, u32[]{:S(2)}) collective-permute-start(bf16[8,2560]{1,0:T(8,128)(2,1)S(1)} %pad_maximum_fusion.1), channel_id=1, source_target_pairs={{0,4},{4,8},{8,12},{12,16},{16,20},{20,24},{24,28},{1,5},{5,9},{9,... | collective-permute-start | bytes 122888 | tf_op jit(solution)/shard_map/ppermute | solution.py:241
  10.0 0.7 pad_maximum_fusion.2
  10.6 0.7 copy.14.par_ref
  11.3 2.0 %collective-permute-done.tail_ref = bf16[8,2560]{1,0:T(8,128)(2,1)S(1)} collective-permute-done((bf16[8,2560]{1,0:T(8,128)(2,1)S(1)}, bf16[8,2560]{1,0:T(8,128)(2,1)S(1)}, u32[]{:S(2)}, u32[]{:S(2)}) %collective-permute-start) | collective-permute-done | bytes 40992 | tf_op jit(solution)/shard_map/ppermute | solution.py:241
  13.3 0.0 copy-start.1
  13.3 0.6 copy-done.1
  13.9 17.8 %states.1 = (bf16[1024,2048]{1,0:T(8,128)(2,1)}, bf16[1024,512]{1,0:T(8,128)(2,1)}, f32[32,1024]{1,0:T(8,128)}, bf16[1024,128]{1,0:T(8,128)(2,1)}, f32[1024,128]...) custom-call(bf16[1024,2048]{1,0:T(8,128)(2,1)} %x_ref.1, bf16[4096,128]{1,0:T(8,128)(2,1)} %bitcast.16, ...), custom_call_target="tpu_custom_call" | custom-call | tf_op jit(solution)/shard_map/states/pallas_call | solution.py:243
  31.7 0.0 copy-start.2
  31.7 13.0 %all_to_all.10.pay_ref = bf16[8,16,2176]{2,1,0:T(8,128)(2,1)} all-to-all(bf16[8,16,2176]{2,1,0:T(8,128)(2,1)} %bitcast.17), channel_id=1, replica_groups=mesh['seq'=8,'chan'=4] {'seq'}, dimensions={0} | all-to-all | bytes 1114112 | tf_op jit(solution)/shard_map/all_to_all | solution.py:290
  44.8 2.6 %prefix.1 = bf16[8,16,2048]{2,1,0:T(8,128)(2,1)} custom-call(bf16[8,16,2176]{2,1,0:T(8,128)(2,1)} %all_to_all.10.pay_ref), custom_call_target="tpu_custom_call" | custom-call | tf_op jit(solution)/shard_map/prefix/pallas_call | solution.py:319
  47.3 4.9 %all-to-all-start.1 = ((bf16[8,16,2048]{2,1,0:T(8,128)(2,1)}), bf16[8,16,2048]{2,1,0:T(8,128)(2,1)S(1)}, u32[]{:S(2)}, u32[]{:S(2)}) async-start(bf16[8,16,2048]{2,1,0:T(8,128)(2,1)} %prefix.1), calls=%async_computation.1 | async-start | bytes 1048576 | tf_op jit(solution)/shard_map/all_to_all | solution.py:325
  52.2 0.0 reduce-scatter.5.cloned.1.call-start
  52.2 0.0 copy-done.2
  52.2 0.1 broadcast_in_dim.3
  52.3 0.7 reshape_reshape.3.gain_ref
  52.9 7.3 %local_part.2.y_ref = bf16[512,2048]{1,0:T(8,128)(2,1)} custom-call(bf16[1024,2048]{1,0:T(8,128)(2,1)} %get-tuple-element.12.xc_ref, bf16[1024,512]{1,0:T(8,128)(2,1)} %get-tuple-element.13.bc_ref, f32[32,1024]{1,0:T(8,128)} %get-tuple-element.14.crow_ref, bf16[1024,128]{1,0:T(8,128)(2,1)} %get-tuple-element.15.ec_ref, ...), custom_call_target="tpu_custom_call" | custom-call | tf_op jit(solution)/shard_map/local_part/pallas_call | solution.py:297
  60.3 0.2 all-to-all-done.1
  60.5 0.0 copy-start
  60.5 0.8 copy-done
  61.3 8.9 %project.4 = bf16[4,256,512]{2,1,0:T(8,128)(2,1)} custom-call(bf16[512,2048]{1,0:T(8,128)(2,1)} %local_part.2.y_ref, bf16[1024,512]{1,0:T(8,128)(2,1)} %get-tuple-element.13.bc_ref, f32[1024,128]{1,0:T(8,128)} %get-tuple-element.16.cols_ref, bf16[128,2048]{1,0:T(8,128)(2,1)} %bitcast.12, bf16[1024,2048]{1,0:T(8,128)(2,1)} %gate_ref.7, f32[1,2048]{1,0:T(1,128)} %bitcast.22, ...), custom_call_target="tpu_custom_call" | custom-call | tf_op jit(solution)/shard_map/project/pallas_call | solution.py:334
  70.2 0.0 reduce-scatter.5.cloned.1.call-update
  70.2 0.0 reduce-scatter.7.cloned.1.call-start
  70.2 8.9 %project.5 = bf16[4,256,512]{2,1,0:T(8,128)(2,1)} custom-call(bf16[512,2048]{1,0:T(8,128)(2,1)} %local_part.2.y_ref, bf16[1024,512]{1,0:T(8,128)(2,1)} %get-tuple-element.13.bc_ref, f32[1024,128]{1,0:T(8,128)} %get-tuple-element.16.cols_ref, bf16[128,2048]{1,0:T(8,128)(2,1)} %bitcast.13, bf16[1024,2048]{1,0:T(8,128)(2,1)} %gate_ref.7, f32[1,2048]{1,0:T(1,128)} %bitcast.23, ...), custom_call_target="tpu_custom_call" | custom-call | tf_op jit(solution)/shard_map/project/pallas_call | solution.py:334
  79.1 0.0 reduce-scatter.7.cloned.1.call-update
  79.2 0.2 reduce-scatter.9.cloned.1.call-start
  79.4 7.4 %local_part.3.y_ref = bf16[512,2048]{1,0:T(8,128)(2,1)} custom-call(bf16[1024,2048]{1,0:T(8,128)(2,1)} %get-tuple-element.12.xc_ref, bf16[1024,512]{1,0:T(8,128)(2,1)} %get-tuple-element.13.bc_ref, f32[32,1024]{1,0:T(8,128)} %get-tuple-element.14.crow_ref, bf16[1024,128]{1,0:T(8,128)(2,1)} %get-tuple-element.15.ec_ref, ...), custom_call_target="tpu_custom_call" | custom-call | tf_op jit(solution)/shard_map/local_part/pallas_call | solution.py:297
  86.8 9.0 %project.6 = bf16[4,256,512]{2,1,0:T(8,128)(2,1)} custom-call(bf16[512,2048]{1,0:T(8,128)(2,1)} %local_part.3.y_ref, bf16[1024,512]{1,0:T(8,128)(2,1)} %get-tuple-element.13.bc_ref, f32[1024,128]{1,0:T(8,128)} %get-tuple-element.16.cols_ref, bf16[128,2048]{1,0:T(8,128)(2,1)} %bitcast.14, bf16[1024,2048]{1,0:T(8,128)(2,1)} %gate_ref.7, f32[1,2048]{1,0:T(1,128)} %bitcast.24, ...), custom_call_target="tpu_custom_call" | custom-call | tf_op jit(solution)/shard_map/project/pallas_call | solution.py:334
  95.7 0.0 reduce-scatter.9.cloned.1.call-update
  95.7 0.0 reduce-scatter.11.cloned.1.call-start
  95.8 8.9 %project.7 = bf16[4,256,512]{2,1,0:T(8,128)(2,1)} custom-call(bf16[512,2048]{1,0:T(8,128)(2,1)} %local_part.3.y_ref, bf16[1024,512]{1,0:T(8,128)(2,1)} %get-tuple-element.13.bc_ref, f32[1024,128]{1,0:T(8,128)} %get-tuple-element.16.cols_ref, bf16[128,2048]{1,0:T(8,128)(2,1)} %bitcast.15, bf16[1024,2048]{1,0:T(8,128)(2,1)} %gate_ref.7, f32[1,2048]{1,0:T(1,128)} %bitcast.25, ...), custom_call_target="tpu_custom_call" | custom-call | tf_op jit(solution)/shard_map/project/pallas_call | solution.py:334
  104.7 0.0 reduce-scatter.11.cloned.1.call-update
  104.8 0.0 reduce-scatter.5.cloned.1.call-done
  104.8 21.9 %reduce-scatter.7.cloned.1.call-done = bf16[1,256,512]{2,1,0:T(8,128)(2,1)} async-done(((bf16[4,256,512]{2,1,0:T(8,128)(2,1)}), bf16[1,256,512]{2,1,0:T(8,128)(2,1)}) %reduce-scatter.7.cloned.1.call-update) | async-done | bytes 262160 | tf_op jit(solution)/shard_map/reduce_scatter | solution.py:352
  126.7 28.1 %reduce-scatter.9.cloned.1.call-done = bf16[1,256,512]{2,1,0:T(8,128)(2,1)} async-done(((bf16[4,256,512]{2,1,0:T(8,128)(2,1)}), bf16[1,256,512]{2,1,0:T(8,128)(2,1)}) %reduce-scatter.9.cloned.1.call-update) | async-done | bytes 262160 | tf_op jit(solution)/shard_map/reduce_scatter | solution.py:352
  154.8 28.1 %reduce-scatter.11.cloned.1.call-done = bf16[1,256,512]{2,1,0:T(8,128)(2,1)} async-done(((bf16[4,256,512]{2,1,0:T(8,128)(2,1)}), bf16[1,256,512]{2,1,0:T(8,128)(2,1)}) %reduce-scatter.11.cloned.1.call-update) | async-done | bytes 262160 | tf_op jit(solution)/shard_map/reduce_scatter | solution.py:352
  182.9 2.2 %pad_maximum_fusion = bf16[1024,512]{1,0:T(8,128)(2,1)} fusion(bf16[256,512]{1,0:T(8,128)(2,1)} %bitcast.21, bf16[256,512]{1,0:T(8,128)(2,1)} %bitcast.20, bf16[256,512]{1,0:T(8,128)(2,1)} %bitcast.19, bf16[256,512]{1,0:T(8,128)(2,1)} %bitcast.18), kind=kLoop, calls=%fused_computation | loop fusion | flops 4194304 | bytes 2097152 | tf_op jit(solution)/shard_map/concatenate | solution.py:354
  (2 shorter events, 0.0 us)
Async XLA Ops:
  8.0 5.3 %collective-permute-start = (bf16[8,2560]{1,0:T(8,128)(2,1)S(1)}, bf16[8,2560]{1,0:T(8,128)(2,1)S(1)}, u32[]{:S(2)}, u32[]{:S(2)}) collective-permute-start(bf16[8,2560]{1,0:T(8,128)(2,1)S(1)} %pad_maximum_fusion.1), channel_id=1, source_target_pairs={{0,4},{4,8},{8,12},{12,16},{16,20},{20,24},{24,28},{1,5},{5,9},{9,... | collective-permute-start | bytes 122888 | tf_op jit(solution)/shard_map/ppermute | solution.py:241
  13.3 0.6 copy-start.1
  31.7 20.4 %copy-start.2 = (f32[32]{0:T(128)S(1)}, f32[32]{0:T(128)}, u32[]{:S(2)}) copy-start(f32[32]{0:T(128)} %param.17) | copy-start | bytes 388
  47.3 13.2 %all-to-all-start.1 = ((bf16[8,16,2048]{2,1,0:T(8,128)(2,1)}), bf16[8,16,2048]{2,1,0:T(8,128)(2,1)S(1)}, u32[]{:S(2)}, u32[]{:S(2)}) async-start(bf16[8,16,2048]{2,1,0:T(8,128)(2,1)} %prefix.1), calls=%async_computation.1 | async-start | bytes 1048576 | tf_op jit(solution)/shard_map/all_to_all | solution.py:325
  52.2 52.6 %reduce-scatter.5.cloned.1.call-start = ((), (), s32[]{:S(2)}) async-start(), calls=%async_computation.6 | async-start | bytes 1310720 | tf_op jit(solution)/shard_map/reduce_scatter | solution.py:352
  60.5 0.8 copy-start
  70.2 56.5 %reduce-scatter.7.cloned.1.call-start = ((), (), s32[]{:S(2)}) async-start(), calls=%async_computation.7 | async-start | bytes 1310720 | tf_op jit(solution)/shard_map/reduce_scatter | solution.py:352
  79.2 75.7 %reduce-scatter.9.cloned.1.call-start = ((), (), s32[]{:S(2)}) async-start(), calls=%async_computation.8 | async-start | bytes 1310720 | tf_op jit(solution)/shard_map/reduce_scatter | solution.py:352
  95.7 87.2 %reduce-scatter.11.cloned.1.call-start = ((), (), s32[]{:S(2)}) async-start(), calls=%async_computation.9 | async-start | bytes 1310720 | tf_op jit(solution)/shard_map/reduce_scatter | solution.py:352
Sparse Core Ops, SparseCore 0:
  70.3 28.1 reduce-scatter.4
  100.9 25.7 reduce-scatter.6
  129.0 25.7 reduce-scatter.8
  157.1 25.8 reduce-scatter.10

commit v2 on v1

--- a/solution.py
+++ b/solution.py
@@ -12,7 +12,7 @@
 BLK = 128
 LANES = 128
 HALO = 8
-CHUNKS = 4
+CHUNKS = 2
 
 step_limit = 0.5
 epsilon = 1e-05
@@ -49,12 +49,20 @@
     return lax.dot_general(a, b, (((1,), (1,)), ((), ())), preferred_element_type=F32)
 
 
+def column(row):
+    count = row.shape[1]
+    eye = lax.broadcasted_iota(jnp.int32, (count, count), 0) == lax.broadcasted_iota(
+        jnp.int32, (count, count), 1
+    )
+    return jnp.sum(jnp.where(eye, row, 0.0), axis=1, keepdims=True)
+
+
 def padded(rows):
     return jnp.concatenate([rows, jnp.zeros((LANES - rows.shape[0], rows.shape[1]), rows.dtype)], 0)
 
 
 def states_kernel(
-    x_ref, maps_ref, step_ref, tail_ref, par_ref, ck_ref, mk_ref,
+    x_ref, maps_ref, step_ref, tail_ref, bias_ref, rate_ref, ck_ref, mk_ref,
     xc_ref, bc_ref, crow_ref, ec_ref, cols_ref, sloc_ref, pay_ref,
     lead, state, prev_x, prev_m, e_w, pick, tri,
 ):
@@ -81,7 +89,7 @@
         col = lax.broadcasted_iota(jnp.int32, tri.shape, 1)
         tri[...] = jnp.where(row <= col, 1.0, 0.0).astype(BF16)
 
-    bias, rate, = par_ref[:, 0:1], -jnp.exp(par_ref[:, 1:2])
+    bias, rate = column(bias_ref[...]), -jnp.exp(column(rate_ref[...]))
     v = step_ref[...] + bias
     step = jnp.minimum(jnp.maximum(v, 0.0) + jnp.log1p(jnp.exp(-jnp.abs(v))), step_limit)
     log_step = rate * step
@@ -140,7 +148,7 @@
     pay_ref[:, width:] = jnp.broadcast_to(three[BLK - 1 :], (STATE, LANES)).astype(BF16)
 
 
-def local_kernel(xc_ref, bc_ref, crow_ref, ec_ref, cols_ref, sloc_ref, gain_ref, y_ref, e_c):
+def local_kernel(xc_ref, bc_ref, crow_ref, ec_ref, cols_ref, sloc_ref, skip_ref, y_ref, e_c, gain_ref):
     heads = crow_ref.shape[0]
     width = xc_ref.shape[1]
     groups = bc_ref.shape[1] // (2 * STATE)
@@ -149,6 +157,9 @@
     @pl.when(pl.program_id(0) == 0)
     def _():
         e_c[...] = spread(0, heads, width)
+        skip = jnp.concatenate(high_low(skip_ref[...]), 1)
+        skip = jnp.concatenate([skip, jnp.zeros((1, LANES - 2 * heads), F32)], 1)
+        gain_ref[...] = dot(jnp.broadcast_to(skip, (HALO, LANES)).astype(BF16), e_c[...])
 
     lane = lax.broadcasted_iota(jnp.int32, (BLK, LANES), 1)
     row = lax.broadcasted_iota(jnp.int32, (BLK, BLK), 0)
@@ -169,11 +180,11 @@
             stacked = jnp.concatenate([jnp.where(left, x, nil), jnp.where(left, nil, x)], 0)
             y = dot(jnp.concatenate(mixing, 1), stacked)
             carry = dot(c_g, sloc_ref[0, :, at])
-            y = y + dot(ec_ref[...], e_c[:, at]) * carry + gain_ref[:, at] * x.astype(F32)
+            y = y + dot(ec_ref[...], e_c[:, at]) * carry + gain_ref[0:1, at] * x.astype(F32)
             y_ref[:, at] = y.astype(BF16)
 
 
-def prefix_kernel(pay_ref, out_ref, *, heads):
+def prefix_kernel(pay_ref, after_ref, out_ref, *, heads):
     width = out_ref.shape[2]
     decays = dot(pay_ref[:, 0, width:], spread(heads, heads, width))
     running = jnp.zeros(out_ref.shape[1:], F32)
@@ -182,29 +193,57 @@
         running = decays[slab : slab + 1] * running + pay_ref[slab, :, :width].astype(F32)
 
 
-def project_kernel(y_ref, bc_ref, cols_ref, enter_ref, gate_ref, gain_ref, w_ref, out_ref, e_c, *, heads):
+def project_kernel(
+    y_ref, bc_ref, cols_ref, enter_ref, gate_ref, gain_ref, w_ref, after_ref, out_ref, e_c, normed,
+    *, heads, tiles,
+):
+    i = pl.program_id(0)
     width = y_ref.shape[1]
     groups = bc_ref.shape[1] // (2 * STATE)
     gw = width // groups
-    count, _, part = out_ref.shape
-
-    @pl.when(pl.program_id(0) == 0)
+
+    @pl.when(i == 0)
     def _():
         e_c[...] = spread(heads, heads, width)
 
-    grown = cols_ref[...].astype(BF16)
-    normed = []
-    for g in range(groups):
-        at = slice(g * gw, (g + 1) * gw)
-        c_g = bc_ref[:, (groups + g) * STATE : (groups + g + 1) * STATE]
-        carry = dot(c_g, enter_ref[:, at])
-        y = y_ref[:, at].astype(F32) + dot(grown, e_c[:, at]) * carry
-        gated = y * silu(gate_ref[:, at].astype(F32))
-        square_mean = jnp.mean(gated * gated, axis=-1, keepdims=True)
-        normed.append((gated * lax.rsqrt(square_mean + epsilon) * gain_ref[:, at]).astype(BF16))
-    normed = jnp.concatenate(normed, 1)
-    for k in range(count):
-        out_ref[k] = dot(normed, w_ref[:, k * part : (k + 1) * part]).astype(BF16)
+    @pl.when(i < tiles)
+    def _():
+        grown = cols_ref[...].astype(BF16)
+        at_rows = pl.ds(pl.multiple_of(i * BLK, BLK), BLK)
+        for g in range(groups):
+            at = slice(g * gw, (g + 1) * gw)
+            c_g = bc_ref[:, (groups + g) * STATE : (groups + g + 1) * STATE]
+            carry = dot(c_g, enter_ref[:, at])
+            y = y_ref[:, at].astype(F32) + dot(grown, e_c[:, at]) * carry
+            gated = y * silu(gate_ref[:, at].astype(F32))
+            square_mean = jnp.mean(gated * gated, axis=-1, keepdims=True)
+            scaled = gated * lax.rsqrt(square_mean + epsilon) * gain_ref[:, at]
+            normed[at_rows, at] = scaled.astype(BF16)
+
+    @pl.when(i >= tiles)
+    def _():
+        out_ref[0] = dot(normed[...], w_ref[...]).astype(BF16)
+
+
+def final_kernel(where_ref, own_ref, right_ref, left_ref, *rest):
+    out_ref = rest[-1]
+    total = own_ref[0].astype(F32) + right_ref[...].astype(F32) + left_ref[...].astype(F32)
+    out_ref[...] = total.astype(BF16)
+
+
+def along_line(shares, count, mine):
+    up = down = None
+    for s in range(count - 1):
+        up_for = jnp.minimum(count - 1 - s + mine, count - 1)
+        down_for = jnp.maximum(mine - (count - 1) + s, 0)
+        up_part = lax.dynamic_index_in_dim(shares, up_for, 0, keepdims=False)
+        down_part = lax.dynamic_index_in_dim(shares, down_for, 0, keepdims=False)
+        if s:
+            up_part = (up_part.astype(F32) + up.astype(F32)).astype(BF16)
+            down_part = (down_part.astype(F32) + down.astype(F32)).astype(BF16)
+        up = lax.ppermute(up_part, "chan", [(a, a + 1) for a in range(s + 1)])
+        down = lax.ppermute(down_part, "chan", [(a, a - 1) for a in range(count - 1 - s, count)])
+    return up, down
 
 
 def params():
@@ -239,7 +278,6 @@
         [inner_input[tokens - HALO :], state_maps[tokens - HALO :].reshape(HALO, map_width)], 1
     )
     tail = lax.ppermute(tail, "seq", [(i, i + 1) for i in range(slabs - 1)])
-    per_head = jnp.stack([step_bias, log_decay_rate], 1)
     xc, bc, crow, ec, cols, sloc, pay = pl.pallas_call(
         states_kernel,
         grid=(blocks,),
@@ -248,7 +286,8 @@
             rows(BLK * parts, STATE),
             pl.BlockSpec((heads, BLK), lambda b: (0, b)),
             whole((HALO, width + map_width)),
-            whole((heads, 2)),
+            whole((1, heads)),
+            whole((1, heads)),
             whole((4, width)),
             whole((4 * parts, STATE)),
         ],
@@ -282,8 +321,8 @@
         compiler_params=params(),
         name="states",
     )(
-        inner_input, state_maps.reshape(tokens * parts, STATE), step_input.T, tail, per_head,
-        conv_kernel, map_kernel.reshape(4 * parts, STATE),
+        inner_input, state_maps.reshape(tokens * parts, STATE), step_input.T, tail,
+        step_bias.reshape(1, heads), log_decay_rate.reshape(1, heads), conv_kernel, map_kernel.reshape(4 * parts, STATE),
     )
 
     part = STATE // slabs
@@ -291,7 +330,7 @@
         pay.reshape(slabs, part, width + LANES), "seq", split_axis=0, concat_axis=0, tiled=True
     )
 
-    gain = jnp.repeat(skip_gain, HEAD_DIM).reshape(1, width)
+    skip_row = skip_gain.reshape(1, heads)
 
     def local_part(start, count):
         return pl.pallas_call(
@@ -304,14 +343,14 @@
                 rows(BLK, LANES, start),
                 rows(BLK, LANES, start),
                 pl.BlockSpec((1, STATE, width), lambda b: (b + start, 0, 0)),
-                whole((1, width)),
+                whole((1, heads)),
             ],
             out_specs=rows(BLK, width),
             out_shape=jax.ShapeDtypeStruct((count * BLK, width), BF16),
-            scratch_shapes=[pltpu.VMEM((LANES, width), BF16)],
+            scratch_shapes=[pltpu.VMEM((LANES, width), BF16), pltpu.VMEM((HALO, width), F32)],
             compiler_params=params(),
             name="local_part",
-        )(xc, bc, crow, ec, cols, sloc, gain)
+        )(xc, bc, crow, ec, cols, sloc, skip_row)
 
     half = blocks // 2
     y_halves = [local_part(0, half), local_part(half, blocks - half)]
@@ -319,39 +358,90 @@
     entering = pl.pallas_call(
         functools.partial(prefix_kernel, heads=heads),
         out_shape=jax.ShapeDtypeStruct((slabs, part, width), BF16),
+        in_specs=[pl.BlockSpec(memory_space=pltpu.VMEM), pl.BlockSpec(memory_space=pl.ANY)],
+        out_specs=pl.BlockSpec(memory_space=pltpu.VMEM),
         compiler_params=pltpu.CompilerParams(vmem_limit_bytes=VMEM_LIMIT),
         name="prefix",
-    )(arrived)
+    )(arrived, y_halves[0])
     entering = lax.all_to_all(entering, "seq", split_axis=0, concat_axis=0, tiled=True)
     entering = entering.reshape(STATE, width)
 
-    pieces = []
     per_chunk = blocks // CHUNKS
+    part_out = features // chans
     norm_row = norm_gain.reshape(1, width)
+    mine = lax.axis_index("chan")
+    where = mine.reshape(1).astype(jnp.int32)
+    out = None
+    sums = []
     for chunk in range(CHUNKS):
         start = chunk * per_chunk
         y_half, y_start = (y_halves[0], start) if start < half else (y_halves[1], start - half)
+
+        def tile(width, start):
+            return pl.BlockSpec(
+                (BLK, width), lambda i: (start + jnp.minimum(i, per_chunk - 1), 0)
+            )
+
         shares = pl.pallas_call(
-            functools.partial(project_kernel, heads=heads),
-            grid=(per_chunk,),
+            functools.partial(project_kernel, heads=heads, tiles=per_chunk),
+            grid=(per_chunk + chans,),
             in_specs=[
-                rows(BLK, width, y_start),
-                rows(BLK, map_width, start),
-                rows(BLK, LANES, start),
+                tile(width, y_start),
+                tile(map_width, start),
+                tile(LANES, start),
                 whole((STATE, width)),
-                rows(BLK, width, start),
+                tile(width, start),
                 whole((1, width)),
-                whole((width, features)),
+                pl.BlockSpec((width, part_out), lambda i: (0, jnp.maximum(i - per_chunk, 0))),
+                pl.BlockSpec(memory_space=pl.ANY),
             ],
-            out_specs=pl.BlockSpec((chans, BLK, features // chans), lambda b: (0, b, 0)),
-            out_shape=jax.ShapeDtypeStruct((chans, per_chunk * BLK, features // chans), BF16),
-            scratch_shapes=[pltpu.VMEM((LANES, width), BF16)],
+            out_specs=pl.BlockSpec(
+                (1, per_chunk * BLK, part_out), lambda i: (jnp.maximum(i - per_chunk, 0), 0, 0)
+            ),
+            out_shape=jax.ShapeDtypeStruct((chans, per_chunk * BLK, part_out), BF16),
+            scratch_shapes=[
+                pltpu.VMEM((LANES, width), BF16),
+                pltpu.VMEM((per_chunk * BLK, width), BF16),
+            ],
             compiler_params=params(),
             name="project",
-        )(y_half, bc, cols, entering, gate_input, norm_row, out_weight)
-        piece = lax.psum_scatter(shares, "chan", scatter_dimension=0, tiled=True)
-        pieces.append(piece.reshape(per_chunk * BLK, features // chans))
-    return jnp.concatenate(pieces, 0)
+        )(y_half, bc, cols, entering, gate_input, norm_row, out_weight, y_halves[1])
+        sums.append((start, shares) + along_line(shares, chans, mine))
+
+    for start, shares, up, down in sums:
+        count = shares.shape[1] // BLK
+
+        def plain(i, where):
+            return (i, 0)
+
+        def placed(i, where, start=start):
+            return (start + i, 0)
+
+        operands = [where, shares, up, down]
+        in_specs = [
+            pl.BlockSpec((1, BLK, part_out), lambda i, where: (where[0], i, 0)),
+            pl.BlockSpec((BLK, part_out), plain),
+            pl.BlockSpec((BLK, part_out), plain),
+        ]
+        aliases = {}
+        if out is not None:
+            aliases = {len(operands): 0}
+            operands.append(out)
+            in_specs.append(pl.BlockSpec(memory_space=pl.ANY))
+        out = pl.pallas_call(
+            final_kernel,
+            grid_spec=pltpu.PrefetchScalarGridSpec(
+                num_scalar_prefetch=1,
+                grid=(count,),
+                in_specs=in_specs,
+                out_specs=pl.BlockSpec((BLK, part_out), placed),
+            ),
+            out_shape=jax.ShapeDtypeStruct((tokens, part_out), BF16),
+            input_output_aliases=aliases,
+            compiler_params=params(),
+            name="final",
+        )(*operands)
+    return out
 
 
 def solution(mesh):

time: 194 us -> 172 us (0.89)
  the two profiles are of different devices: /device:TPU:2 before, /device:TPU:18 now
where the time goes in v2:
time: 172 us; the launch traced here: 171 us
  Pallas kernels  69 us (40%)
  waiting for transfers between devices  47.6 us (28%)
  starting transfers between devices  35.3 us (21%)
  local copies, waits for them, and re-layouts  9.82 us (6%)
  other arithmetic  8.91 us (5%)
    pallas_call x2, Pallas kernels, local(): pl.pallas_call(functools.partial(project_kernel, heads=heads, tiles=per_c...  26.2 us
    ppermute x6, waiting for transfers between devices, along_line(): lax.ppermute(down_part, 'chan', [(a, a - 1) for a in range(count - 1 - s,...  24 us
    ppermute x6, waiting for transfers between devices, along_line(): up = lax.ppermute(up_part, 'chan', [(a, a + 1) for a in range(s + 1)])  18.6 us
    pallas_call x1, Pallas kernels, local(): pl.pallas_call(states_kernel, grid=(blocks,), in_specs=[rows(BLK, width),...  18 us
    pallas_call x2, Pallas kernels, local_part(): pl.pallas_call(local_kernel, grid=(count,), in_specs=[rows(BLK, width, st...  15.4 us
    ppermute x6, starting transfers between devices, along_line(): lax.ppermute(down_part, 'chan', [(a, a - 1) for a in range(count - 1 - s,...  12.9 us
    ppermute x6, starting transfers between devices, along_line(): up = lax.ppermute(up_part, 'chan', [(a, a + 1) for a in range(s + 1)])  11.4 us
    convert_element_type x4, other arithmetic, along_line(): down_part = (down_part.astype(F32) + down.astype(F32)).astype(BF16)  7.59 us
  transfers between devices with their start and end apart: 15, of which 9 were waited for; matrix products, arithmetic and copies ran while one was open for 7% of the time, Pallas kernels for 19%

profile of v2, /device:TPU:18, one launch (start us, length us, event | category | flops | bytes accessed | tf_op | source)
XLA Modules:
  0.0 170.9 jit_solution(13622478128825783564)
XLA Ops:
  0.0 0.8 slice.6
  0.8 0.7 slice.7
  1.5 1.9 %collective-permute-start = (bf16[8,2560]{1,0:T(8,128)(2,1)S(1)}, bf16[8,2560]{1,0:T(8,128)(2,1)S(1)}, u32[]{:S(2)}, u32[]{:S(2)}) collective-permute-start(bf16[8,2560]{1,0:T(8,128)(2,1)S(1)} %pad_maximum_fusion), channel_id=1, source_target_pairs={{0,4},{4,8},{8,12},{12,16},{16,20},{20,24},{24,28},{1,5},{5,9},{9,... | collective-permute-start | bytes 122888 | tf_op jit(solution)/shard_map/ppermute | solution.py:280
  3.4 3.4 %collective-permute-done.tail_ref = bf16[8,2560]{1,0:T(8,128)(2,1)S(1)} collective-permute-done((bf16[8,2560]{1,0:T(8,128)(2,1)S(1)}, bf16[8,2560]{1,0:T(8,128)(2,1)S(1)}, u32[]{:S(2)}, u32[]{:S(2)}) %collective-permute-start) | collective-permute-done | bytes 40992 | tf_op jit(solution)/shard_map/ppermute | solution.py:280
  6.8 0.0 copy-start.7
  6.8 0.6 copy-done.7
  7.4 18.0 %states.1 = (bf16[1024,2048]{1,0:T(8,128)(2,1)}, bf16[1024,512]{1,0:T(8,128)(2,1)}, f32[32,1024]{1,0:T(8,128)}, bf16[1024,128]{1,0:T(8,128)(2,1)}, f32[1024,128]...) custom-call(bf16[1024,2048]{1,0:T(8,128)(2,1)} %x_ref.1, bf16[4096,128]{1,0:T(8,128)(2,1)} %bitcast.44, ...), custom_call_target="tpu_custom_call" | custom-call | tf_op jit(solution)/shard_map/states/pallas_call | solution.py:281
  25.4 4.3 %all-to-all-start = ((bf16[8,16,2176]{2,1,0:T(8,128)(2,1)}), bf16[8,16,2176]{2,1,0:T(8,128)(2,1)S(1)}, u32[]{:S(2)}, u32[]{:S(2)}) async-start(bf16[8,16,2176]{2,1,0:T(8,128)(2,1)} %bitcast.45), calls=%async_computation | async-start | bytes 1114112 | tf_op jit(solution)/shard_map/all_to_all | solution.py:329
  29.7 7.7 %local_part.3.after_ref.y_ref = bf16[512,2048]{1,0:T(8,128)(2,1)} custom-call(bf16[1024,2048]{1,0:T(8,128)(2,1)} %get-tuple-element.12.xc_ref, bf16[1024,512]{1,0:T(8,128)(2,1)} %get-tuple-element.13.bc_ref, f32[32,1024]{1,0:T(8,128)} %get-tuple-element.14.crow_ref, bf16[1024,128]{1,0:T(8,128)(2,1)} %get-tuple-element.15.ec_ref, ...), custom_call_target="tpu_custom_call" | custom-call | tf_op jit(solution)/shard_map/local_part/pallas_call | solution.py:336
  37.4 1.0 all-to-all-done.pay_ref
  38.3 0.0 copy-start.2
  38.3 0.8 copy-done.2
  39.1 2.5 %prefix.1 = bf16[8,16,2048]{2,1,0:T(8,128)(2,1)} custom-call(bf16[8,16,2176]{2,1,0:T(8,128)(2,1)} %copy-done.2, bf16[512,2048]{1,0:T(8,128)(2,1)} %local_part.3.after_ref.y_ref), custom_call_target="tpu_custom_call" | custom-call | tf_op jit(solution)/shard_map/prefix/pallas_call | solution.py:358
  41.7 4.9 %all-to-all-start.1 = ((bf16[8,16,2048]{2,1,0:T(8,128)(2,1)}), bf16[8,16,2048]{2,1,0:T(8,128)(2,1)S(1)}, u32[]{:S(2)}, u32[]{:S(2)}) async-start(bf16[8,16,2048]{2,1,0:T(8,128)(2,1)} %prefix.1), calls=%async_computation.1 | async-start | bytes 1048576 | tf_op jit(solution)/shard_map/all_to_all | solution.py:366
  46.5 7.7 %local_part.2.y_ref.after_ref = bf16[512,2048]{1,0:T(8,128)(2,1)} custom-call(bf16[1024,2048]{1,0:T(8,128)(2,1)} %get-tuple-element.12.xc_ref, bf16[1024,512]{1,0:T(8,128)(2,1)} %get-tuple-element.13.bc_ref, f32[32,1024]{1,0:T(8,128)} %get-tuple-element.14.crow_ref, bf16[1024,128]{1,0:T(8,128)(2,1)} %get-tuple-element.15.ec_ref, ...), custom_call_target="tpu_custom_call" | custom-call | tf_op jit(solution)/shard_map/local_part/pallas_call | solution.py:336
  54.2 0.6 all-to-all-done.1
  54.8 0.0 copy-start.1
  54.8 0.8 copy-done.1
  55.6 13.1 %project.3.own_ref = bf16[4,512,512]{2,1,0:T(8,128)(2,1)} custom-call(bf16[512,2048]{1,0:T(8,128)(2,1)} %local_part.3.after_ref.y_ref, bf16[1024,512]{1,0:T(8,128)(2,1)} %get-tuple-element.13.bc_ref, f32[1024,128]{1,0:T(8,128)} %get-tuple-element.16.cols_ref, bf16[128,2048]{1,0:T(8,128)(2,1)} %bitcast.42, bf16[1024,2048]{1,0:T(8,128)(2,1)} %gate_ref.3, ...), custom_call_target="tpu_custom_call" | custom-call | tf_op jit(solution)/shard_map/project/pallas_call | solution.py:385
  68.7 2.1 %dynamic-slice_bitcast_fusion = (bf16[512,512]{1,0:T(8,128)(2,1)S(1)}, bf16[512,512]{1,0:T(8,128)(2,1)}) fusion(bf16[4,512,512]{2,1,0:T(8,128)(2,1)} %project.3.own_ref, s32[]{:T(128)S(6)} %max.14, s32[]{:T(128)S(6)} %select_n.21), kind=kLoop, calls=%fused_computation.16 | loop fusion | bytes 2097160 | tf_op jit(solution)/shard_map/jit(dynamic_index_in_dim)/squeeze | solution.py:240
  70.8 1.3 collective-permute-start.10
  72.1 13.1 %project.2.own_ref = bf16[4,512,512]{2,1,0:T(8,128)(2,1)} custom-call(bf16[512,2048]{1,0:T(8,128)(2,1)} %local_part.2.y_ref.after_ref, bf16[1024,512]{1,0:T(8,128)(2,1)} %get-tuple-element.13.bc_ref, f32[1024,128]{1,0:T(8,128)} %get-tuple-element.16.cols_ref, bf16[128,2048]{1,0:T(8,128)(2,1)} %bitcast.43, bf16[1024,2048]{1,0:T(8,128)(2,1)} %gate_ref.3, ...), custom_call_target="tpu_custom_call" | custom-call | tf_op jit(solution)/shard_map/project/pallas_call | solution.py:385
  85.2 0.0 copy-start
  85.2 2.4 %dynamic-slice_bitcast_fusion.2 = (bf16[512,512]{1,0:T(8,128)(2,1)}, bf16[512,512]{1,0:T(8,128)(2,1)}) fusion(bf16[4,512,512]{2,1,0:T(8,128)(2,1)} %project.2.own_ref, s32[]{:T(128)S(6)} %max.14, s32[]{:T(128)S(6)} %select_n.21), kind=kLoop, calls=%fused_computation.18 | loop fusion | bytes 2097160 | tf_op jit(solution)/shard_map/jit(dynamic_index_in_dim)/squeeze | solution.py:240
  87.6 1.3 collective-permute-start.4
  88.9 1.5 collective-permute-start.7
  90.4 0.0 collective-permute-done.10
  90.4 1.2 fusion
  91.5 1.9 %collective-permute-start.11 = (bf16[512,512]{1,0:T(8,128)(2,1)S(1)}, bf16[512,512]{1,0:T(8,128)(2,1)}, u32[]{:S(2)}, u32[]{:S(2)}) collective-permute-start(bf16[512,512]{1,0:T(8,128)(2,1)S(1)} %fusion), channel_id=1, source_target_pairs={{2,1},{3,2},{6,5},{7,6},{10,9},{11,10},{14,13},{15,14},{18,17},{19... | collective-permute-start | bytes 1572872 | tf_op jit(solution)/shard_map/ppermute | solution.py:245
  93.5 1.5 collective-permute-start.1
  94.9 9.7 %collective-permute-done.4 = bf16[512,512]{1,0:T(8,128)(2,1)} collective-permute-done((bf16[512,512]{1,0:T(8,128)(2,1)}, bf16[512,512]{1,0:T(8,128)(2,1)}, u32[]{:S(2)}, u32[]{:S(2)}) %collective-permute-start.4) | collective-permute-done | bytes 524320 | tf_op jit(solution)/shard_map/ppermute | solution.py:245
  104.6 0.0 copy-done
  104.6 1.2 fusion.4
  105.8 1.9 %collective-permute-start.5 = (bf16[512,512]{1,0:T(8,128)(2,1)S(1)}, bf16[512,512]{1,0:T(8,128)(2,1)}, u32[]{:S(2)}, u32[]{:S(2)}) collective-permute-start(bf16[512,512]{1,0:T(8,128)(2,1)S(1)} %fusion.4), channel_id=1, source_target_pairs={{2,1},{3,2},{6,5},{7,6},{10,9},{11,10},{14,13},{15,14},{18,17},{19... | collective-permute-start | bytes 1572872 | tf_op jit(solution)/shard_map/ppermute | solution.py:245
  107.7 0.0 collective-permute-done.7
  107.7 8.1 %collective-permute-done.11 = bf16[512,512]{1,0:T(8,128)(2,1)} collective-permute-done((bf16[512,512]{1,0:T(8,128)(2,1)S(1)}, bf16[512,512]{1,0:T(8,128)(2,1)}, u32[]{:S(2)}, u32[]{:S(2)}) %collective-permute-start.11) | collective-permute-done | bytes 524320 | tf_op jit(solution)/shard_map/ppermute | solution.py:245
  115.8 2.8 %fusion.1 = (bf16[512,512]{1,0:T(8,128)(2,1)}, bf16[512,512]{1,0:T(8,128)(2,1)}) fusion(bf16[512,512]{1,0:T(8,128)(2,1)} %collective-permute-done.11, bf16[4,512,512]{2,1,0:T(8,128)(2,1)} %project.3.own_ref, s32[]{:T(128)S(6)} %max.12, bf16[512,512]{1,0:T(8,128)(2,1)} %collective-permute-done.7, s32[]{:T(128)S(6)} %select_n.20), kind=kLoop, calls=%fused_computation.3 | loop fusion | flops 2097152 | bytes 3145736 | tf_op jit(solution)/shard_map/convert_element_type | solution.py:243
  118.6 1.3 collective-permute-start.8
  119.9 0.0 collective-permute-done.1
  119.9 6.2 %collective-permute-done.5 = bf16[512,512]{1,0:T(8,128)(2,1)} collective-permute-done((bf16[512,512]{1,0:T(8,128)(2,1)S(1)}, bf16[512,512]{1,0:T(8,128)(2,1)}, u32[]{:S(2)}, u32[]{:S(2)}) %collective-permute-start.5) | collective-permute-done | bytes 524320 | tf_op jit(solution)/shard_map/ppermute | solution.py:245
  126.2 2.4 %fusion.5 = (bf16[512,512]{1,0:T(8,128)(2,1)}, bf16[512,512]{1,0:T(8,128)(2,1)}) fusion(bf16[512,512]{1,0:T(8,128)(2,1)} %collective-permute-done.5, bf16[4,512,512]{2,1,0:T(8,128)(2,1)S(1)} %copy-done, s32[]{:T(128)S(6)} %max.12, bf16[512,512]{1,0:T(8,128)(2,1)} %collective-permute-done.1, s32[]{:T(128)S(6)} %select_n.20), kind=kLoop, calls=%fused_computation.11 | loop fusion | flops 2097152 | bytes 3145736 | tf_op jit(solution)/shard_map/convert_element_type | solution.py:243
  128.6 1.3 collective-permute-start.2
  129.9 4.5 %collective-permute-start.12 = (bf16[512,512]{1,0:T(8,128)(2,1)}, bf16[512,512]{1,0:T(8,128)(2,1)S(1)}, u32[]{:S(2)}, u32[]{:S(2)}) collective-permute-start(bf16[512,512]{1,0:T(8,128)(2,1)} %get-tuple-element.19), channel_id=1, source_target_pairs={{1,0},{2,1},{3,2},{5,4},{6,5},{7,6},{9,8},{10,9},{11,10},{13,12},{... | collective-permute-start | bytes 1572872 | tf_op jit(solution)/shard_map/ppermute | solution.py:245
  134.5 1.9 %collective-permute-start.6 = (bf16[512,512]{1,0:T(8,128)(2,1)}, bf16[512,512]{1,0:T(8,128)(2,1)S(1)}, u32[]{:S(2)}, u32[]{:S(2)}) collective-permute-start(bf16[512,512]{1,0:T(8,128)(2,1)} %get-tuple-element.23), channel_id=1, source_target_pairs={{1,0},{2,1},{3,2},{5,4},{6,5},{7,6},{9,8},{10,9},{11,10},{13,12},{... | collective-permute-start | bytes 1572872 | tf_op jit(solution)/shard_map/ppermute | solution.py:245
  136.4 0.0 collective-permute-done.8
  136.4 1.2 fusion.3
  137.6 4.0 %collective-permute-start.9 = (bf16[512,512]{1,0:T(8,128)(2,1)S(1)}, bf16[512,512]{1,0:T(8,128)(2,1)S(1)}, u32[]{:S(2)}, u32[]{:S(2)}) collective-permute-start(bf16[512,512]{1,0:T(8,128)(2,1)S(1)} %fusion.3), channel_id=1, source_target_pairs={{0,1},{1,2},{2,3},{4,5},{5,6},{6,7},{8,9},{9,10},{10,11},{12,13},{... | collective-permute-start | bytes 1572872 | tf_op jit(solution)/shard_map/ppermute | solution.py:244
  141.6 4.0 %collective-permute-done.2 = bf16[512,512]{1,0:T(8,128)(2,1)S(1)} collective-permute-done((bf16[512,512]{1,0:T(8,128)(2,1)}, bf16[512,512]{1,0:T(8,128)(2,1)S(1)}, u32[]{:S(2)}, u32[]{:S(2)}) %collective-permute-start.2) | collective-permute-done | bytes 524320 | tf_op jit(solution)/shard_map/ppermute | solution.py:244
  145.6 0.1 fusion.7
  145.7 1.9 %collective-permute-start.3 = (bf16[512,512]{1,0:T(8,128)(2,1)S(1)}, bf16[512,512]{1,0:T(8,128)(2,1)S(1)}, u32[]{:S(2)}, u32[]{:S(2)}) collective-permute-start(bf16[512,512]{1,0:T(8,128)(2,1)S(1)} %fusion.7), channel_id=1, source_target_pairs={{0,1},{1,2},{2,3},{4,5},{5,6},{6,7},{8,9},{9,10},{10,11},{12,13},{... | collective-permute-start | bytes 1572872 | tf_op jit(solution)/shard_map/ppermute | solution.py:244
  147.7 0.0 collective-permute-done.12.left_ref
  147.7 0.0 copy-start.3
  147.7 9.1 %collective-permute-done.9.right_ref = bf16[512,512]{1,0:T(8,128)(2,1)S(1)} collective-permute-done((bf16[512,512]{1,0:T(8,128)(2,1)S(1)}, bf16[512,512]{1,0:T(8,128)(2,1)S(1)}, u32[]{:S(2)}, u32[]{:S(2)}) %collective-permute-start.9) | collective-permute-done | bytes 524320 | tf_op jit(solution)/shard_map/ppermute | solution.py:244
  156.8 0.0 copy-start.4
  156.8 0.0 copy-done.3
  156.8 0.8 copy-done.4
  157.6 3.5 %final.2.rest_0_ = bf16[1024,512]{1,0:T(8,128)(2,1)} custom-call(s32[1]{0:T(128)} %bitcast.where_ref, bf16[4,512,512]{2,1,0:T(8,128)(2,1)} %project.3.own_ref, bf16[512,512]{1,0:T(8,128)(2,1)} %copy-done.4, bf16[512,512]{1,0:T(8,128)(2,1)} %copy-done.3), custom_call_target="tpu_custom_call" | custom-call | tf_op jit(solution)/shard_map/final/pallas_call | solution.py:431
  161.1 0.0 collective-permute-done.6.left_ref
  161.1 0.0 copy-start.5
  161.1 5.5 %collective-permute-done.3.right_ref = bf16[512,512]{1,0:T(8,128)(2,1)S(1)} collective-permute-done((bf16[512,512]{1,0:T(8,128)(2,1)S(1)}, bf16[512,512]{1,0:T(8,128)(2,1)S(1)}, u32[]{:S(2)}, u32[]{:S(2)}) %collective-permute-start.3) | collective-permute-done | bytes 524320 | tf_op jit(solution)/shard_map/ppermute | solution.py:244
  166.6 0.0 copy-done.5
  166.6 0.0 copy-start.6
  166.6 0.8 copy-done.6
  167.4 3.5 %final.3 = bf16[1024,512]{1,0:T(8,128)(2,1)} custom-call(s32[1]{0:T(128)} %bitcast.where_ref, bf16[4,512,512]{2,1,0:T(8,128)(2,1)} %project.2.own_ref, bf16[512,512]{1,0:T(8,128)(2,1)} %copy-done.6, bf16[512,512]{1,0:T(8,128)(2,1)} %copy-done.5, bf16[1024,512]{1,0:T(8,128)(2,1)} %final.2.rest_0_), custom_call_target="tpu_custom_call", output_to_operand_aliasing={{}: (4, {})} | custom-call | tf_op jit(solution)/shard_map/final/pallas_call | solution.py:431
  (2 shorter events, 0.0 us)
Async XLA Ops:
  1.5 5.3 %collective-permute-start = (bf16[8,2560]{1,0:T(8,128)(2,1)S(1)}, bf16[8,2560]{1,0:T(8,128)(2,1)S(1)}, u32[]{:S(2)}, u32[]{:S(2)}) collective-permute-start(bf16[8,2560]{1,0:T(8,128)(2,1)S(1)} %pad_maximum_fusion), channel_id=1, source_target_pairs={{0,4},{4,8},{8,12},{12,16},{16,20},{20,24},{24,28},{1,5},{5,9},{9,... | collective-permute-start | bytes 122888 | tf_op jit(solution)/shard_map/ppermute | solution.py:280
  6.8 0.6 copy-start.7
  25.4 12.9 %all-to-all-start = ((bf16[8,16,2176]{2,1,0:T(8,128)(2,1)}), bf16[8,16,2176]{2,1,0:T(8,128)(2,1)S(1)}, u32[]{:S(2)}, u32[]{:S(2)}) async-start(bf16[8,16,2176]{2,1,0:T(8,128)(2,1)} %bitcast.45), calls=%async_computation | async-start | bytes 1114112 | tf_op jit(solution)/shard_map/all_to_all | solution.py:329
  38.3 0.8 copy-start.2
  41.7 13.2 %all-to-all-start.1 = ((bf16[8,16,2048]{2,1,0:T(8,128)(2,1)}), bf16[8,16,2048]{2,1,0:T(8,128)(2,1)S(1)}, u32[]{:S(2)}, u32[]{:S(2)}) async-start(bf16[8,16,2048]{2,1,0:T(8,128)(2,1)} %prefix.1), calls=%async_computation.1 | async-start | bytes 1048576 | tf_op jit(solution)/shard_map/all_to_all | solution.py:366
  54.8 0.8 copy-start.1
  70.8 19.6 %collective-permute-start.10 = (bf16[512,512]{1,0:T(8,128)(2,1)S(1)}, bf16[512,512]{1,0:T(8,128)(2,1)S(1)}, u32[]{:S(2)}, u32[]{:S(2)}) collective-permute-start(bf16[512,512]{1,0:T(8,128)(2,1)S(1)} %get-tuple-element.21), channel_id=1, source_target_pairs={{3,2},{7,6},{11,10},{15,14},{19,18},{23,22},{27,26},{31,30}} | collective-permute-start | bytes 1572872 | tf_op jit(solution)/shard_map/ppermute | solution.py:245
  85.2 19.4 %copy-start = (bf16[4,512,512]{2,1,0:T(8,128)(2,1)S(1)}, bf16[4,512,512]{2,1,0:T(8,128)(2,1)}, u32[]{:S(2)}) copy-start(bf16[4,512,512]{2,1,0:T(8,128)(2,1)} %project.2.own_ref) | copy-start | bytes 6291460
  87.6 17.0 %collective-permute-start.4 = (bf16[512,512]{1,0:T(8,128)(2,1)}, bf16[512,512]{1,0:T(8,128)(2,1)}, u32[]{:S(2)}, u32[]{:S(2)}) collective-permute-start(bf16[512,512]{1,0:T(8,128)(2,1)} %get-tuple-element.25), channel_id=1, source_target_pairs={{3,2},{7,6},{11,10},{15,14},{19,18},{23,22},{27,26},{31,30}} | collective-permute-start | bytes 1572872 | tf_op jit(solution)/shard_map/ppermute | solution.py:245
  88.9 18.8 %collective-permute-start.7 = (bf16[512,512]{1,0:T(8,128)(2,1)}, bf16[512,512]{1,0:T(8,128)(2,1)}, u32[]{:S(2)}, u32[]{:S(2)}) collective-permute-start(bf16[512,512]{1,0:T(8,128)(2,1)} %get-tuple-element.22), channel_id=1, source_target_pairs={{0,1},{4,5},{8,9},{12,13},{16,17},{20,21},{24,25},{28,29}} | collective-permute-start | bytes 1572872 | tf_op jit(solution)/shard_map/ppermute | solution.py:244
  91.5 24.3 %collective-permute-start.11 = (bf16[512,512]{1,0:T(8,128)(2,1)S(1)}, bf16[512,512]{1,0:T(8,128)(2,1)}, u32[]{:S(2)}, u32[]{:S(2)}) collective-permute-start(bf16[512,512]{1,0:T(8,128)(2,1)S(1)} %fusion), channel_id=1, source_target_pairs={{2,1},{3,2},{6,5},{7,6},{10,9},{11,10},{14,13},{15,14},{18,17},{19... | collective-permute-start | bytes 1572872 | tf_op jit(solution)/shard_map/ppermute | solution.py:245
  93.5 26.5 %collective-permute-start.1 = (bf16[512,512]{1,0:T(8,128)(2,1)}, bf16[512,512]{1,0:T(8,128)(2,1)}, u32[]{:S(2)}, u32[]{:S(2)}) collective-permute-start(bf16[512,512]{1,0:T(8,128)(2,1)} %get-tuple-element.26), channel_id=1, source_target_pairs={{0,1},{4,5},{8,9},{12,13},{16,17},{20,21},{24,25},{28,29}} | collective-permute-start | bytes 1572872 | tf_op jit(solution)/shard_map/ppermute | solution.py:244
  105.8 20.4 %collective-permute-start.5 = (bf16[512,512]{1,0:T(8,128)(2,1)S(1)}, bf16[512,512]{1,0:T(8,128)(2,1)}, u32[]{:S(2)}, u32[]{:S(2)}) collective-permute-start(bf16[512,512]{1,0:T(8,128)(2,1)S(1)} %fusion.4), channel_id=1, source_target_pairs={{2,1},{3,2},{6,5},{7,6},{10,9},{11,10},{14,13},{15,14},{18,17},{19... | collective-permute-start | bytes 1572872 | tf_op jit(solution)/shard_map/ppermute | solution.py:245
  118.6 17.8 %collective-permute-start.8 = (bf16[512,512]{1,0:T(8,128)(2,1)}, bf16[512,512]{1,0:T(8,128)(2,1)S(1)}, u32[]{:S(2)}, u32[]{:S(2)}) collective-permute-start(bf16[512,512]{1,0:T(8,128)(2,1)} %get-tuple-element.20), channel_id=1, source_target_pairs={{0,1},{1,2},{4,5},{5,6},{8,9},{9,10},{12,13},{13,14},{16,17},{17,1... | collective-permute-start | bytes 1572872 | tf_op jit(solution)/shard_map/ppermute | solution.py:244
  128.6 17.0 %collective-permute-start.2 = (bf16[512,512]{1,0:T(8,128)(2,1)}, bf16[512,512]{1,0:T(8,128)(2,1)S(1)}, u32[]{:S(2)}, u32[]{:S(2)}) collective-permute-start(bf16[512,512]{1,0:T(8,128)(2,1)} %get-tuple-element.24), channel_id=1, source_target_pairs={{0,1},{1,2},{4,5},{5,6},{8,9},{9,10},{12,13},{13,14},{16,17},{17,1... | collective-permute-start | bytes 1572872 | tf_op jit(solution)/shard_map/ppermute | solution.py:244
  129.9 17.7 %collective-permute-start.12 = (bf16[512,512]{1,0:T(8,128)(2,1)}, bf16[512,512]{1,0:T(8,128)(2,1)S(1)}, u32[]{:S(2)}, u32[]{:S(2)}) collective-permute-start(bf16[512,512]{1,0:T(8,128)(2,1)} %get-tuple-element.19), channel_id=1, source_target_pairs={{1,0},{2,1},{3,2},{5,4},{6,5},{7,6},{9,8},{10,9},{11,10},{13,12},{... | collective-permute-start | bytes 1572872 | tf_op jit(solution)/shard_map/ppermute | solution.py:245
  134.5 26.6 %collective-permute-start.6 = (bf16[512,512]{1,0:T(8,128)(2,1)}, bf16[512,512]{1,0:T(8,128)(2,1)S(1)}, u32[]{:S(2)}, u32[]{:S(2)}) collective-permute-start(bf16[512,512]{1,0:T(8,128)(2,1)} %get-tuple-element.23), channel_id=1, source_target_pairs={{1,0},{2,1},{3,2},{5,4},{6,5},{7,6},{9,8},{10,9},{11,10},{13,12},{... | collective-permute-start | bytes 1572872 | tf_op jit(solution)/shard_map/ppermute | solution.py:245
  137.6 19.2 %collective-permute-start.9 = (bf16[512,512]{1,0:T(8,128)(2,1)S(1)}, bf16[512,512]{1,0:T(8,128)(2,1)S(1)}, u32[]{:S(2)}, u32[]{:S(2)}) collective-permute-start(bf16[512,512]{1,0:T(8,128)(2,1)S(1)} %fusion.3), channel_id=1, source_target_pairs={{0,1},{1,2},{2,3},{4,5},{5,6},{6,7},{8,9},{9,10},{10,11},{12,13},{... | collective-permute-start | bytes 1572872 | tf_op jit(solution)/shard_map/ppermute | solution.py:244
  145.7 20.9 %collective-permute-start.3 = (bf16[512,512]{1,0:T(8,128)(2,1)S(1)}, bf16[512,512]{1,0:T(8,128)(2,1)S(1)}, u32[]{:S(2)}, u32[]{:S(2)}) collective-permute-start(bf16[512,512]{1,0:T(8,128)(2,1)S(1)} %fusion.7), channel_id=1, source_target_pairs={{0,1},{1,2},{2,3},{4,5},{5,6},{6,7},{8,9},{9,10},{10,11},{12,13},{... | collective-permute-start | bytes 1572872 | tf_op jit(solution)/shard_map/ppermute | solution.py:244
  147.7 9.2 %copy-start.3 = (bf16[512,512]{1,0:T(8,128)(2,1)}, bf16[512,512]{1,0:T(8,128)(2,1)S(1)}, u32[]{:S(2)}) copy-start(bf16[512,512]{1,0:T(8,128)(2,1)S(1)} %collective-permute-done.12.left_ref) | copy-start | bytes 1572868
  156.8 0.8 copy-start.4
  161.1 5.5 %copy-start.5 = (bf16[512,512]{1,0:T(8,128)(2,1)}, bf16[512,512]{1,0:T(8,128)(2,1)S(1)}, u32[]{:S(2)}) copy-start(bf16[512,512]{1,0:T(8,128)(2,1)S(1)} %collective-permute-done.6.left_ref) | copy-start | bytes 1572868
  166.6 0.8 copy-start.6

commit v3 on v2

v3 whole, which is shorter than its diff:
```python
import functools

import jax
import jax.numpy as jnp
import numpy as np
from jax import lax
from jax.experimental import pallas as pl
from jax.experimental.pallas import tpu as pltpu
from jax.sharding import PartitionSpec as P

HEAD_DIM = 64
STATE = 128
BLK = 128
LANES = 128
HALO = 8
WIDE = 256

step_limit = 0.5
epsilon = 1e-05
LOG2E = 1.4426950408889634
F32 = jnp.float32
BF16 = jnp.bfloat16
VMEM_LIMIT = 40 * 1024 * 1024


def silu(v):
    half = 0.5 * v
    return half + half * jnp.tanh(half)


def high_low(v):
    high = v.astype(BF16).astype(F32)
    return high, v - high


def spread(first_row, heads, width):
    result = np.zeros((LANES, width), np.float32)
    for k in range(2 * heads):
        h = k % heads
        result[first_row + k, h * HEAD_DIM : (h + 1) * HEAD_DIM] = 1.0
    return jnp.asarray(result, BF16)


def dot(a, b):
    return jnp.dot(a, b, preferred_element_type=F32)


def dot_t(a, b):
    return lax.dot_general(a, b, (((1,), (1,)), ((), ())), preferred_element_type=F32)


def column(row):
    count = row.shape[1]
    eye = lax.broadcasted_iota(jnp.int32, (count, count), 0) == lax.broadcasted_iota(
        jnp.int32, (count, count), 1
    )
    return jnp.sum(jnp.where(eye, row, 0.0), axis=1, keepdims=True)


def padded(pieces):
    rows = jnp.concatenate(pieces, 0)
    if rows.shape[0] == LANES:
        return rows
    return jnp.concatenate([rows, jnp.zeros((LANES - rows.shape[0], rows.shape[1]), rows.dtype)], 0)


def conv(before, cur, taps):
    full = jnp.concatenate([before, cur], 0)
    acc = cur * taps[3]
    for back in range(1, 4):
        acc = acc + pltpu.roll(full, back, 0)[HALO:] * taps[3 - back]
    return silu(acc).astype(BF16)


def states_kernel(
    x_ref, maps_ref, step_ref, tail_ref, mtail_ref, bias_ref, rate_ref, ck_ref, mk_ref, e_ref,
    xc_ref, bc_ref, bt_ref, crow_ref, cols_ref, w_ref, g_ref, pay_ref,
    weighted,
):
    c = pl.program_id(0)
    heads, tokens = step_ref.shape
    parts = mk_ref.shape[0] // 4
    groups = parts // 2
    blocks = tokens // BLK

    @pl.when(c == 0)
    def _():
        bias, rate = column(bias_ref[...]), -jnp.exp(column(rate_ref[...]))
        v = step_ref[...] + bias
        step = jnp.minimum(jnp.maximum(v, 0.0) + jnp.log1p(jnp.exp(-jnp.abs(v))), step_limit)
        log_step = rate * step
        first, rest = high_low(log_step)
        second, third = high_low(rest)
        pieces = []
        for b in range(blocks):
            at = slice(b * BLK, (b + 1) * BLK)
            pieces += [first[:, at], second[:, at], third[:, at]]
        row = lax.broadcasted_iota(jnp.int32, (BLK, BLK), 0)
        col = lax.broadcasted_iota(jnp.int32, (BLK, BLK), 1)
        tri = jnp.where(row <= col, 1.0, 0.0).astype(BF16)
        sums = dot(jnp.concatenate(pieces, 0).astype(BF16), tri)
        cums, leads = [], [jnp.zeros((heads, 1), F32)]
        for b in range(blocks):
            at = 3 * b * heads
            cum = (
                sums[at : at + heads]
                + sums[at + heads : at + 2 * heads]
                + sums[at + 2 * heads : at + 3 * heads]
            )
            cums.append(cum)
            leads.append(leads[-1] + cum[:, BLK - 1 : BLK])
        last = None
        for b in range(blocks):
            at = slice(b * BLK, (b + 1) * BLK)
            cum, step_b = cums[b], step[:, at]
            total = cum[:, BLK - 1 : BLK]
            block_weight = jnp.exp(total - cum) * step_b
            slab_weight = jnp.exp(leads[blocks] - (leads[b] + cum)) * step_b
            grown = jnp.exp(cum)
            entered = jnp.exp(cum + leads[b])
            crow_ref[:, at] = (cum - jnp.log(step_b)) * LOG2E
            w_ref[at, :] = padded(high_low(slab_weight) + high_low(block_weight)).T.astype(BF16)
            last = padded(high_low(grown) + high_low(entered)).T
            g_ref[at, :] = last.astype(BF16)
            cols_ref[at, :] = padded((cum * LOG2E,)).T
        pay_ref[:, heads * HEAD_DIM :] = jnp.broadcast_to(last[BLK - 1 :], (STATE, LANES)).astype(BF16)

        row = lax.broadcasted_iota(jnp.int32, (BLK * parts, BLK * parts), 0)
        col = lax.broadcasted_iota(jnp.int32, (BLK * parts, BLK * parts), 1)
        source = (row & (BLK - 1)) * parts + row // BLK
        pick = jnp.where(col == source, 1.0, 0.0).astype(BF16)
        before = [mtail_ref[:, q * STATE : (q + 1) * STATE].astype(F32) for q in range(parts)]
        for b in range(blocks):
            ordered = dot(pick, maps_ref[b * BLK * parts : (b + 1) * BLK * parts, :])
            for q in range(parts):
                cur = ordered[q * BLK : (q + 1) * BLK]
                taps = [mk_ref[k * parts + q : k * parts + q + 1] for k in range(4)]
                result = conv(before[q], cur, taps)
                before[q] = cur[BLK - HALO :]
                bc_ref[b * BLK : (b + 1) * BLK, q * STATE : (q + 1) * STATE] = result
                if q < groups:
                    bt_ref[q, :, b * BLK : (b + 1) * BLK] = result.astype(F32).T.astype(BF16)

    taps = [ck_ref[k : k + 1] for k in range(4)]
    before = tail_ref[...].astype(F32)
    for b in range(blocks):
        at = slice(b * BLK, (b + 1) * BLK)
        cur = x_ref[at, :].astype(F32)
        result = conv(before, cur, taps)
        before = cur[BLK - HALO :]
        xc_ref[at, :] = result
        weighted[at, :] = (result.astype(F32) * dot(w_ref[at, :], e_ref[...])).astype(BF16)
    step_width = x_ref.shape[1]
    group = c * step_width * groups // (heads * HEAD_DIM)
    at = pl.ds(pl.multiple_of(c * step_width, step_width), step_width)
    pay_ref[:, at] = dot(bt_ref[group], weighted[...]).astype(BF16)


def local_kernel(
    xc_ref, bc_ref, bt_ref, crow_ref, cols_ref, w_ref, g_ref, skip_ref, low_ref, high_ref, *rest
):
    y_ref, state, gain_ref = rest[-3:]
    heads = crow_ref.shape[0]
    width = xc_ref.shape[1]
    groups = bt_ref.shape[0]
    gw = width // groups

    @pl.when(pl.program_id(0) == 0)
    def _():
        state[...] = rest[0][...] if len(rest) > 4 else jnp.zeros_like(state)
        skip = jnp.concatenate(high_low(skip_ref[...]), 1)
        skip = jnp.concatenate([skip, jnp.zeros((1, LANES - 2 * heads), F32)], 1)
        gain_ref[...] = dot(jnp.broadcast_to(skip, (HALO, LANES)).astype(BF16), low_ref[...])

    left = lax.broadcasted_iota(jnp.int32, (BLK, LANES), 1) < HEAD_DIM
    row = lax.broadcasted_iota(jnp.int32, (BLK, BLK), 0)
    causal = row >= lax.broadcasted_iota(jnp.int32, (BLK, BLK), 1)
    for g in range(groups):
        b_g = bc_ref[:, g * STATE : (g + 1) * STATE]
        c_g = bc_ref[:, (groups + g) * STATE : (groups + g + 1) * STATE]
        scores = jnp.where(causal, dot_t(c_g, b_g), 0.0)
        for wide in range(g * gw, (g + 1) * gw, 2 * LANES):
            at_wide = slice(wide, wide + 2 * LANES)
            grown = dot(g_ref[...], low_ref[:, at_wide])
            before = state[:, at_wide]
            carry = grown * dot(c_g, before.astype(BF16))
            x_wide = xc_ref[:, at_wide].astype(F32)
            weighted = (x_wide * dot(w_ref[...], high_ref[:, at_wide])).astype(BF16)
            state[:, at_wide] = grown[BLK - 1 :] * before + dot(bt_ref[g], weighted)
            carry = carry + gain_ref[0:1, at_wide] * x_wide
            for k in range(2):
                at = slice(wide + k * LANES, wide + (k + 1) * LANES)
                mixing = []
                for h in (at.start // HEAD_DIM, at.start // HEAD_DIM + 1):
                    gap = jnp.minimum(cols_ref[:, h : h + 1] - crow_ref[h : h + 1], 0.0)
                    mixing.append((jnp.exp2(gap) * scores).astype(BF16))
                x = xc_ref[:, at]
                nil = jnp.zeros_like(x)
                stacked = jnp.concatenate([jnp.where(left, x, nil), jnp.where(left, nil, x)], 0)
                y = dot(jnp.concatenate(mixing, 1), stacked) + carry[:, k * LANES : (k + 1) * LANES]
                y_ref[:, at] = y.astype(BF16)


def prefix_kernel(pay_ref, e_ref, after_ref, out_ref):
    width = out_ref.shape[2]
    decays = dot(pay_ref[:, 0, width:], e_ref[...])
    running = jnp.zeros(out_ref.shape[1:], F32)
    for slab in range(out_ref.shape[0]):
        out_ref[slab] = running.astype(BF16)
        running = decays[slab : slab + 1] * running + pay_ref[slab, :, :width].astype(F32)


def ends_kernel(
    y_ref, bc_ref, g_ref, enter_ref, gate_ref, gain_ref, w_ref, e_ref, after_ref,
    shares_ref, up_ref, down_ref, normed_ref, *, tiles,
):
    i = pl.program_id(0)
    width = y_ref.shape[1]
    groups = bc_ref.shape[1] // (2 * STATE)
    gw = width // groups

    @pl.when(i < tiles)
    def _():
        at_rows = pl.ds(pl.multiple_of(i * BLK, BLK), BLK)
        for g in range(groups):
            at = slice(g * gw, (g + 1) * gw)
            c_g = bc_ref[:, (groups + g) * STATE : (groups + g + 1) * STATE]
            carry = dot(c_g, enter_ref[:, at])
            y = y_ref[:, at].astype(F32) + dot(g_ref[...], e_ref[:, at]) * carry
            gated = y * silu(gate_ref[:, at].astype(F32))
            square_mean = jnp.mean(gated * gated, axis=-1, keepdims=True)
            scaled = gated * lax.rsqrt(square_mean + epsilon) * gain_ref[:, at]
            normed_ref[at_rows, at] = scaled.astype(BF16)

    @pl.when(i >= tiles)
    def _():
        shares_ref[0] = dot(normed_ref[...], w_ref[...]).astype(BF16)

    @pl.when(i == tiles)
    def _():
        down_ref[...] = shares_ref[0]

    @pl.when(i == tiles + 1)
    def _():
        up_ref[...] = shares_ref[0]


def middle_kernel(normed_ref, w_ref, ends_ref, after_ref, shares_ref):
    shares_ref[0] = dot(normed_ref[...], w_ref[...]).astype(BF16)


def onward_kernel(where_ref, up_own_ref, down_own_ref, up_ref, down_ref, up_out, down_out):
    up_out[...] = (up_own_ref[0].astype(F32) + up_ref[...].astype(F32)).astype(BF16)
    down_out[...] = (down_own_ref[0].astype(F32) + down_ref[...].astype(F32)).astype(BF16)


def final_kernel(where_ref, own_ref, up_ref, down_ref, *rest):
    out_ref = rest[-1]
    total = own_ref[0].astype(F32) + up_ref[...].astype(F32) + down_ref[...].astype(F32)
    out_ref[...] = total.astype(BF16)


def params():
    return pltpu.CompilerParams(
        dimension_semantics=("arbitrary",), vmem_limit_bytes=VMEM_LIMIT
    )


def whole(shape):
    return pl.BlockSpec(shape, lambda *b: (0,) * len(shape))


def unread():
    return pl.BlockSpec(memory_space=pl.ANY)


def shaped(shape, dtype=BF16):
    return jax.ShapeDtypeStruct(shape, dtype)


def local(
    inner_input, state_maps, gate_input, step_input, log_decay_rate, step_bias,
    skip_gain, conv_kernel, map_kernel, norm_gain, out_weight,
):
    tokens, width = inner_input.shape
    groups = state_maps.shape[2]
    parts = 2 * groups
    heads = step_input.shape[1]
    blocks = tokens // BLK
    slabs = lax.axis_size("seq")
    chans = lax.axis_size("chan")
    features = out_weight.shape[1]
    map_width = parts * STATE
    low, high = spread(0, heads, width), spread(2 * heads, heads, width)

    tail = jnp.concatenate(
        [inner_input[tokens - HALO :], state_maps[tokens - HALO :].reshape(HALO, map_width)], 1
    )
    tail = lax.ppermute(tail, "seq", [(i, i + 1) for i in range(slabs - 1)])

    def lanes_at(count):
        return pl.BlockSpec((count, WIDE), lambda c: (0, c))

    xc, bc, bt, crow, cols, w_hl, g_hl, pay = pl.pallas_call(
        states_kernel,
        grid=(width // WIDE,),
        in_specs=[
            lanes_at(tokens),
            whole((tokens * parts, STATE)),
            whole((heads, tokens)),
            lanes_at(HALO),
            pl.BlockSpec((HALO, map_width), lambda c: (0, width // map_width)),
            whole((1, heads)),
            whole((1, heads)),
            lanes_at(4),
            whole((4 * parts, STATE)),
            lanes_at(LANES),
        ],
        out_specs=[
            lanes_at(tokens),
            whole((tokens, map_width)),
            whole((groups, STATE, tokens)),
            whole((heads, tokens)),
            whole((tokens, LANES)),
            whole((tokens, LANES)),
            whole((tokens, LANES)),
            whole((STATE, width + LANES)),
        ],
        out_shape=[
            shaped((tokens, width)),
            shaped((tokens, map_width)),
            shaped((groups, STATE, tokens)),
            shaped((heads, tokens), F32),
            shaped((tokens, LANES), F32),
            shaped((tokens, LANES)),
            shaped((tokens, LANES)),
            shaped((STATE, width + LANES)),
        ],
        scratch_shapes=[pltpu.VMEM((tokens, WIDE), BF16)],
        compiler_params=params(),
        name="states",
    )(
        inner_input, state_maps.reshape(tokens * parts, STATE), step_input.T, tail, tail,
        step_bias.reshape(1, heads), log_decay_rate.reshape(1, heads),
        conv_kernel, map_kernel.reshape(4 * parts, STATE), low,
    )

    part = STATE // slabs
    arrived = lax.all_to_all(
        pay.reshape(slabs, part, width + LANES), "seq", split_axis=0, concat_axis=0, tiled=True
    )

    def local_part(start, count, state, after):
        def tile(width):
            return pl.BlockSpec((BLK, width), lambda b: (start + b, 0))

        operands = [xc, bc, bt, crow, cols, w_hl, g_hl, skip_gain.reshape(1, heads), low, high]
        specs = [
            tile(width),
            tile(map_width),
            pl.BlockSpec((groups, STATE, BLK), lambda b: (0, 0, start + b)),
            pl.BlockSpec((heads, BLK), lambda b: (0, start + b)),
            tile(LANES),
            tile(LANES),
            tile(LANES),
            whole((1, heads)),
            whole((LANES, width)),
            whole((LANES, width)),
        ]
        if state is not None:
            operands.append(state)
            specs.append(whole((STATE, width)))
        operands.append(after)
        specs.append(unread())
        return pl.pallas_call(
            local_kernel,
            grid=(count,),
            in_specs=specs,
            out_specs=[
                pl.BlockSpec((BLK, width), lambda b: (b, 0)),
                whole((STATE, width)),
            ],
            out_shape=[shaped((count * BLK, width)), shaped((STATE, width), F32)],
            scratch_shapes=[pltpu.VMEM((HALO, width), F32)],
            compiler_params=params(),
            name="local_part",
        )(*operands)

    third = (blocks - blocks // 4) // 2
    spans = [(0, blocks // 4), (blocks // 4, third), (blocks // 4 + third, third)]
    y_first, state = local_part(*spans[0], None, pay)
    y_second, state = local_part(*spans[1], state, y_first)

    entering = pl.pallas_call(
        prefix_kernel,
        out_shape=shaped((slabs, part, width)),
        in_specs=[
            pl.BlockSpec(memory_space=pltpu.VMEM),
            pl.BlockSpec(memory_space=pltpu.VMEM),
            unread(),
        ],
        out_specs=pl.BlockSpec(memory_space=pltpu.VMEM),
        compiler_params=pltpu.CompilerParams(vmem_limit_bytes=VMEM_LIMIT),
        name="prefix",
    )(arrived, high, y_first)
    entering = lax.all_to_all(entering, "seq", split_axis=0, concat_axis=0, tiled=True)
    entering = entering.reshape(STATE, width)

    part_out = features // chans
    norm_row = norm_gain.reshape(1, width)
    mine = lax.axis_index("chan").astype(jnp.int32)
    where = mine.reshape(1)

    def project(start, count, y, after):
        def tile(width, start=start):
            return pl.BlockSpec((BLK, width), lambda i: (start + jnp.minimum(i, count - 1), 0))

        def end(i):
            return jnp.where(i <= count, 0, chans - 1)

        size = count * BLK
        shares, up, down, normed = pl.pallas_call(
            functools.partial(ends_kernel, tiles=count),
            grid=(count + 2,),
            in_specs=[
                tile(width, 0),
                tile(map_width),
                tile(LANES),
                whole((STATE, width)),
                tile(width),
                whole((1, width)),
                pl.BlockSpec((width, part_out), lambda i: (0, end(i))),
                whole((LANES, width)),
                unread(),
            ],
            out_specs=[
                pl.BlockSpec((1, size, part_out), lambda i: (end(i), 0, 0)),
                whole((size, part_out)),
                whole((size, part_out)),
                whole((size, width)),
            ],
            out_shape=[
                shaped((chans, size, part_out)),
                shaped((size, part_out)),
                shaped((size, part_out)),
                shaped((size, width)),
            ],
            compiler_params=params(),
            name="project_ends",
        )(y, bc, g_hl, entering, gate_input, norm_row, out_weight, high, after)
        return shares, up, down, normed

    def project_middle(shares, normed, after):
        size = normed.shape[0]
        return pl.pallas_call(
            middle_kernel,
            grid=(chans - 2,),
            in_specs=[
                whole((size, width)),
                pl.BlockSpec((width, part_out), lambda i: (0, i + 1)),
                unread(),
                unread(),
            ],
            out_specs=pl.BlockSpec((1, size, part_out), lambda i: (i + 1, 0, 0)),
            out_shape=shaped((chans, size, part_out)),
            input_output_aliases={2: 0},
            compiler_params=params(),
            name="project_middle",
        )(normed, out_weight, shares, after)

    def permuted(up, down, s):
        up = lax.ppermute(up, "chan", [(a, a + 1) for a in range(s + 1)])
        down = lax.ppermute(down, "chan", [(a, a - 1) for a in range(chans - 1 - s, chans)])
        return up, down

    def onward(shares, up, down, s):
        def plain(i, where):
            return (i, 0)

        return pl.pallas_call(
            onward_kernel,
            grid_spec=pltpu.PrefetchScalarGridSpec(
                num_scalar_prefetch=1,
                grid=(shares.shape[1] // BLK,),
                in_specs=[
                    pl.BlockSpec(
                        (1, BLK, part_out),
                        lambda i, where: (jnp.minimum(chans - 1 - s + where[0], chans - 1), i, 0),
                    ),
                    pl.BlockSpec(
                        (1, BLK, part_out),
                        lambda i, where: (jnp.maximum(where[0] - (chans - 1) + s, 0), i, 0),
                    ),
                    pl.BlockSpec((BLK, part_out), plain),
                    pl.BlockSpec((BLK, part_out), plain),
                ],
                out_specs=[pl.BlockSpec((BLK, part_out), plain)] * 2,
            ),
            out_shape=[shaped(up.shape)] * 2,
            compiler_params=params(),
            name="onward",
        )(where, shares, shares, up, down)

    def final(start, shares, up, down, out):
        def plain(i, where):
            return (i, 0)

        operands = [where, shares, up, down]
        in_specs = [
            pl.BlockSpec((1, BLK, part_out), lambda i, where: (where[0], i, 0)),
            pl.BlockSpec((BLK, part_out), plain),
            pl.BlockSpec((BLK, part_out), plain),
        ]
        aliases = {}
        if out is not None:
            aliases = {len(operands): 0}
            operands.append(out)
            in_specs.append(unread())
        return pl.pallas_call(
            final_kernel,
            grid_spec=pltpu.PrefetchScalarGridSpec(
                num_scalar_prefetch=1,
                grid=(shares.shape[1] // BLK,),
                in_specs=in_specs,
                out_specs=pl.BlockSpec((BLK, part_out), lambda i, where: (start + i, 0)),
            ),
            out_shape=shaped((tokens, part_out)),
            input_output_aliases=aliases,
            compiler_params=params(),
            name="final",
        )(*operands)

    after, y = y_second, y_first
    sums = []
    for k, (start, count) in enumerate(spans):
        shares, up, down, normed = project(start, count, y, after)
        up, down = permuted(up, down, 0)
        shares = project_middle(shares, normed, normed)
        if k == 0:
            y_third, _ = local_part(*spans[2], state, shares)
        for s in range(1, chans - 1):
            up, down = onward(shares, up, down, s)
            up, down = permuted(up, down, s)
        sums.append((start, shares, up, down))
        y = (y_second, y_third, None)[k]
        after = shares
    out = None
    for start, shares, up, down in sums:
        out = final(start, shares, up, down, out)
    return out


def solution(mesh):
    return jax.shard_map(
        local,
        mesh=mesh,
        in_specs=(
            P("seq", "chan"),
            P("seq", None, "chan", None),
            P("seq", "chan"),
            P("seq", "chan"),
            P("chan"),
            P("chan"),
            P("chan"),
            P(None, "chan"),
            P(None, None, "chan", None),
            P("chan"),
            P("chan", None),
        ),
        out_specs=P("seq", "chan"),
        check_vma=False,
    )
```

time: 172 us -> 186 us (1.081)
  the two profiles are of different devices: /device:TPU:18 before, /device:TPU:2 now
where the time goes in v3:
time: 186 us; the launch traced here: 182 us
  Pallas kernels  63 us (34%)
  starting transfers between devices  55.2 us (30%)
  local copies, waits for them, and re-layouts  47.2 us (25%)
  waiting for transfers between devices  16.1 us (9%)
    unnamed x108, local copies, waits for them, and re-layouts  45.7 us
    ppermute x9, starting transfers between devices, permuted(): up = lax.ppermute(up, 'chan', [(a, a + 1) for a in range(s + 1)])  35.1 us
    pallas_call x3, Pallas kernels, project(): pl.pallas_call(functools.partial(ends_kernel, tiles=count), grid=(count +...  21.8 us
    pallas_call x3, Pallas kernels, local_part(): pl.pallas_call(local_kernel, grid=(count,), in_specs=specs, out_specs=[pl...  12.8 us
    ppermute x9, waiting for transfers between devices, permuted(): lax.ppermute(down, 'chan', [(a, a - 1) for a in range(chans - 1 - s, chan...  12.7 us
    pallas_call x1, Pallas kernels, local(): pl.pallas_call(states_kernel, grid=(width // WIDE,), in_specs=[lanes_at(t...  12.3 us
    ppermute x9, starting transfers between devices, permuted(): lax.ppermute(down, 'chan', [(a, a - 1) for a in range(chans - 1 - s, chan...  9.38 us
    pallas_call x3, Pallas kernels, project_middle(): pl.pallas_call(middle_kernel, grid=(chans - 2,), in_specs=[whole((size, w...  6.43 us
  transfers between devices with their start and end apart: 21, of which 2 were waited for; matrix products, arithmetic and copies ran while one was open for 0% of the time, Pallas kernels for 23%

profile of v3, /device:TPU:2, one launch (start us, length us, event | category | flops | bytes accessed | tf_op | source)
XLA Modules:
  0.0 182.1 jit_solution(17744484748004427886)
XLA Ops:
  1.5 1.9 %collective-permute-start = (bf16[8,2560]{1,0:T(8,128)(2,1)S(1)}, bf16[8,2560]{1,0:T(8,128)(2,1)S(1)}, u32[]{:S(2)}, u32[]{:S(2)}) collective-permute-start(bf16[8,2560]{1,0:T(8,128)(2,1)S(1)} %pad_maximum_fusion), channel_id=1, source_target_pairs={{0,4},{4,8},{8,12},{12,16},{16,20},{20,24},{24,28},{1,5},{5,9},{9,... | collective-permute-start | bytes 122888 | tf_op jit(solution)/shard_map/ppermute | solution.py:299
  3.4 3.4 %collective-permute-done.tail_ref.mtail_ref = bf16[8,2560]{1,0:T(8,128)(2,1)S(1)} collective-permute-done((bf16[8,2560]{1,0:T(8,128)(2,1)S(1)}, bf16[8,2560]{1,0:T(8,128)(2,1)S(1)}, u32[]{:S(2)}, u32[]{:S(2)}) %collective-permute-start) | collective-permute-done | bytes 40992 | tf_op jit(solution)/shard_map/ppermute | solution.py:299
  6.8 1.0 copy-done.17
  7.8 2.2 %copy-done.34 = bf16[1024,2048]{1,0:T(8,128)(2,1)S(1)} copy-done((bf16[1024,2048]{1,0:T(8,128)(2,1)S(1)}, bf16[1024,2048]{1,0:T(8,128)(2,1)}, u32[]{:S(2)}) %copy-start.34) | copy-done | bytes 4194328
  10.0 1.2 copy-done.40
  11.3 0.9 copy-done.45
  14.9 12.3 %states.1 = (bf16[1024,2048]{1,0:T(8,128)(2,1)S(1)}, bf16[1024,512]{1,0:T(8,128)(2,1)S(1)}, bf16[2,128,1024]{2,1,0:T(8,128)(2,1)S(1)}, f32[32,1024]{1,0:T(8,128)...) custom-call(bf16[1024,2048]{1,0:T(8,128)(2,1)S(1)} %copy-done.34, ...), custom_call_target="tpu_custom_call" | custom-call | tf_op jit(solution)/shard_map/states/pallas_call | solution.py:304
  27.2 2.0 %copy-done.4 = bf16[1024,2048]{1,0:T(8,128)(2,1)} copy-done((bf16[1024,2048]{1,0:T(8,128)(2,1)}, bf16[1024,2048]{1,0:T(8,128)(2,1)S(1)}, u32[]{:S(2)}) %copy-start.4) | copy-done | bytes 4194328
  29.3 0.8 copy-done.26
  30.1 0.8 copy-done.30
  30.9 4.3 %all-to-all-start = ((bf16[8,16,2176]{2,1,0:T(8,128)(2,1)}), bf16[8,16,2176]{2,1,0:T(8,128)(2,1)}, u32[]{:S(2)}, u32[]{:S(2)}) async-start(bf16[8,16,2176]{2,1,0:T(8,128)(2,1)} %bitcast.7), calls=%async_computation | async-start | bytes 1114112 | tf_op jit(solution)/shard_map/all_to_all | solution.py:349
  35.2 2.2 %copy-done.5 = bf16[1024,2048]{1,0:T(8,128)(2,1)S(1)} copy-done((bf16[1024,2048]{1,0:T(8,128)(2,1)S(1)}, bf16[1024,2048]{1,0:T(8,128)(2,1)}, u32[]{:S(2)}) %copy-start.5) | copy-done | bytes 4194328
  37.3 1.0 copy-done.18
  38.4 1.0 copy-done.27
  39.4 1.0 copy-done.31
  40.5 2.9 %local_part.3 = (bf16[256,2048]{1,0:T(8,128)(2,1)S(1)}, f32[128,2048]{1,0:T(8,128)S(1)}) custom-call(bf16[1024,2048]{1,0:T(8,128)(2,1)S(1)} %copy-done.5, bf16[1024,512]{1,0:T(8,128)(2,1)S(1)} %get-tuple-element.43.bc_ref, bf16[2,128,1024]{2,1,0:T(8,128)(2,1)S(1)} %copy-done.27, f32[32,1024]{1,0:T(8,128)S(1)} %get-tuple-element.45.crow_ref, ...), custom_call_target="tpu_custom_call" | custom-call | tf_op jit(solution)/shard_map/local_part/pallas_call | solution.py:375
  43.4 1.0 copy-done.43
  44.4 1.7 prefix.1
  46.1 0.8 copy-done.37
  46.9 4.6 %all-to-all-start.1 = ((bf16[8,16,2048]{2,1,0:T(8,128)(2,1)}), bf16[8,16,2048]{2,1,0:T(8,128)(2,1)}, u32[]{:S(2)}, u32[]{:S(2)}) async-start(bf16[8,16,2048]{2,1,0:T(8,128)(2,1)} %copy-done.37), calls=%async_computation.1 | async-start | bytes 1048576 | tf_op jit(solution)/shard_map/all_to_all | solution.py:406
  51.5 2.2 %copy-done.6 = bf16[1024,2048]{1,0:T(8,128)(2,1)S(1)} copy-done((bf16[1024,2048]{1,0:T(8,128)(2,1)S(1)}, bf16[1024,2048]{1,0:T(8,128)(2,1)}, u32[]{:S(2)}) %copy-start.6) | copy-done | bytes 4194328
  53.7 1.0 copy-done.19
  54.7 1.0 copy-done.28
  55.8 1.0 copy-done.32
  56.8 1.2 copy-done.44
  58.0 4.3 %local_part.4 = (bf16[384,2048]{1,0:T(8,128)(2,1)S(1)}, f32[128,2048]{1,0:T(8,128)S(1)}) custom-call(bf16[1024,2048]{1,0:T(8,128)(2,1)S(1)} %copy-done.6, bf16[1024,512]{1,0:T(8,128)(2,1)S(1)} %get-tuple-element.43.bc_ref, bf16[2,128,1024]{2,1,0:T(8,128)(2,1)S(1)} %copy-done.28, f32[32,1024]{1,0:T(8,128)S(1)} %get-tuple-element.45.crow_ref, ...), custom_call_target="tpu_custom_call" | custom-call | tf_op jit(solution)/shard_map/local_part/pallas_call | solution.py:375
  62.4 1.2 copy-done.23
  63.5 1.0 copy-done.41
  64.5 2.3 %copy-done.8 = bf16[1024,2048]{1,0:T(8,128)(2,1)S(1)} copy-done((bf16[1024,2048]{1,0:T(8,128)(2,1)S(1)}, bf16[1024,2048]{1,0:T(8,128)(2,1)}, u32[]{:S(2)}) %copy-start.8) | copy-done | bytes 4194328
  66.9 1.4 copy-done.16
  68.3 1.4 copy-done.24
  69.7 6.5 %project_ends.3 = (bf16[4,256,512]{2,1,0:T(8,128)(2,1)S(1)}, bf16[256,512]{1,0:T(8,128)(2,1)}, bf16[256,512]{1,0:T(8,128)(2,1)}, bf16[256,2048]{1,0:T(8,128)(2,1)S(1)}) custom-call(bf16[256,2048]{1,0:T(8,128)(2,1)S(1)} %copy-done.16, bf16[1024,512]{1,0:T(8,128)(2,1)S(1)} %get-tuple-element.43.bc_ref, bf16[1024,128]{1,0:T(8,128)(2,1)S(1)} %get-tuple-element.48.g_ref, ...), custom_call_target="tpu_custom_call" | custom-call | tf_op jit(solution)/shard_map/project_ends/pallas_call | solution.py:422
  76.2 4.2 %collective-permute-start.13 = (bf16[256,512]{1,0:T(8,128)(2,1)}, bf16[256,512]{1,0:T(8,128)(2,1)}, u32[]{:S(2)}, u32[]{:S(2)}) collective-permute-start(bf16[256,512]{1,0:T(8,128)(2,1)} %get-tuple-element.73), channel_id=1, source_target_pairs={{0,1},{4,5},{8,9},{12,13},{16,17},{20,21},{24,25},{28,29}} | collective-permute-start | bytes 786440 | tf_op jit(solution)/shard_map/ppermute | solution.py:472
  80.4 1.4 collective-permute-start.14
  81.8 1.8 project_middle.3.rest_1_.after_ref.up_own_ref.down_own_ref.own_ref
  84.8 7.7 %project_ends.4 = (bf16[4,384,512]{2,1,0:T(8,128)(2,1)S(1)}, bf16[384,512]{1,0:T(8,128)(2,1)}, bf16[384,512]{1,0:T(8,128)(2,1)}, bf16[384,2048]{1,0:T(8,128)(2,1)S(1)}) custom-call(bf16[384,2048]{1,0:T(8,128)(2,1)S(1)} %copy-done.25, bf16[1024,512]{1,0:T(8,128)(2,1)S(1)} %copy-done.12, bf16[1024,128]{1,0:T(8,128)(2,1)S(1)} %get-tuple-element.48.g_ref, ...), custom_call_target="tpu_custom_call" | custom-call | tf_op jit(solution)/shard_map/project_ends/pallas_call | solution.py:422
  92.6 5.5 %local_part.5 = (bf16[384,2048]{1,0:T(8,128)(2,1)S(1)}, f32[128,2048]{1,0:T(8,128)}) custom-call(bf16[1024,2048]{1,0:T(8,128)(2,1)S(1)} %copy-done.7, bf16[1024,512]{1,0:T(8,128)(2,1)S(1)} %copy-done.13, bf16[2,128,1024]{2,1,0:T(8,128)(2,1)S(1)} %copy-done.29, f32[32,1024]{1,0:T(8,128)S(1)} %get-tuple-element.45.crow_ref, f32[1024,128]{1,0:T(8,128)S(1)} %copy-done.33, ...), custom_call_target="tpu_custom_call" | custom-call | tf_op jit(solution)/shard_map/local_part/pallas_call | solution.py:375
  98.1 2.0 %collective-permute-start.7 = (bf16[384,512]{1,0:T(8,128)(2,1)}, bf16[384,512]{1,0:T(8,128)(2,1)}, u32[]{:S(2)}, u32[]{:S(2)}) collective-permute-start(bf16[384,512]{1,0:T(8,128)(2,1)} %get-tuple-element.67), channel_id=1, source_target_pairs={{0,1},{4,5},{8,9},{12,13},{16,17},{20,21},{24,25},{28,29}} | collective-permute-start | bytes 1179656 | tf_op jit(solution)/shard_map/ppermute | solution.py:472
  100.1 1.4 collective-permute-start.8
  101.5 3.4 %copy-done = bf16[2048,2048]{1,0:T(8,128)(2,1)S(1)} copy-done((bf16[2048,2048]{1,0:T(8,128)(2,1)S(1)}, bf16[2048,2048]{1,0:T(8,128)(2,1)}, u32[]{:S(2)}) %copy-start) | copy-done | bytes 8388632
  104.9 2.3 %project_middle.4.after_ref.up_own_ref.down_own_ref.own_ref = bf16[4,384,512]{2,1,0:T(8,128)(2,1)S(1)} custom-call(bf16[384,2048]{1,0:T(8,128)(2,1)S(1)} %get-tuple-element.57.normed_ref.after_ref, bf16[2048,2048]{1,0:T(8,128)(2,1)S(1)} %copy-done, bf16[4,384,512]{2,1,0:T(8,128)(2,1)S(1)} %get-tuple-element.58.ends_ref, ...), custom_call_target="tpu_custom_call", output_to_operand_aliasing={{}: (2, {})} | custom-call | tf_op jit(solution)/shard_map/project_middle/pallas_call | solution.py:455
  107.3 1.4 copy-done.39
  108.7 7.5 %project_ends.5 = (bf16[4,384,512]{2,1,0:T(8,128)(2,1)S(1)}, bf16[384,512]{1,0:T(8,128)(2,1)}, bf16[384,512]{1,0:T(8,128)(2,1)}, bf16[384,2048]{1,0:T(8,128)(2,1)S(1)}) custom-call(bf16[384,2048]{1,0:T(8,128)(2,1)S(1)} %copy-done.39, bf16[1024,512]{1,0:T(8,128)(2,1)S(1)} %copy-done.13, bf16[1024,128]{1,0:T(8,128)(2,1)S(1)} %get-tuple-element.48.g_ref, ...), custom_call_target="tpu_custom_call" | custom-call | tf_op jit(solution)/shard_map/project_ends/pallas_call | solution.py:422
  116.2 1.1 copy-done.2
  117.3 1.1 copy-done.21
  118.5 1.3 collective-permute-start.1
  120.5 1.3 onward.10
  121.8 1.3 collective-permute-start.15
  123.1 3.4 %copy-done.1 = bf16[2048,2048]{1,0:T(8,128)(2,1)S(1)} copy-done((bf16[2048,2048]{1,0:T(8,128)(2,1)S(1)}, bf16[2048,2048]{1,0:T(8,128)(2,1)}, u32[]{:S(2)}) %copy-start.1) | copy-done | bytes 8388632
  126.5 1.4 copy-done.22
  127.9 2.3 %project_middle.5.up_own_ref.down_own_ref.own_ref = bf16[4,384,512]{2,1,0:T(8,128)(2,1)S(1)} custom-call(bf16[384,2048]{1,0:T(8,128)(2,1)S(1)} %copy-done.22, bf16[2048,2048]{1,0:T(8,128)(2,1)S(1)} %copy-done.1, bf16[4,384,512]{2,1,0:T(8,128)(2,1)S(1)} %copy-done.3, bf16[384,2048]{1,0:T(8,128)(2,1)S(1)} %copy-done.22), custom_call_target="tpu_custom_call", output_to_operand_aliasing={{}: (2, {})} | custom-call | tf_op jit(solution)/shard_map/project_middle/pallas_call | solution.py:455
  131.0 2.1 %onward.8 = (bf16[384,512]{1,0:T(8,128)(2,1)S(1)}, bf16[384,512]{1,0:T(8,128)(2,1)S(1)}) custom-call(s32[1]{0:T(128)} %bitcast.where_ref, bf16[4,384,512]{2,1,0:T(8,128)(2,1)S(1)} %project_middle.4.after_ref.up_own_ref.down_own_ref.own_ref, bf16[4,384,512]{2,1,0:T(8,128)(2,1)S(1)} %project_middle.4.after_ref.up_own_ref.down_own_ref.own_ref, ...), custom_call_target="tpu_custom_call" | custom-call | tf_op jit(solution)/shard_map/onward/pallas_call | solution.py:480
  133.1 2.9 %collective-permute-start.9 = (bf16[384,512]{1,0:T(8,128)(2,1)S(1)}, bf16[384,512]{1,0:T(8,128)(2,1)S(1)}, u32[]{:S(2)}, u32[]{:S(2)}) collective-permute-start(bf16[384,512]{1,0:T(8,128)(2,1)S(1)} %get-tuple-element.69), channel_id=1, source_target_pairs={{0,1},{1,2},{4,5},{5,6},{8,9},{9,10},{12,13},{13,14},{16,17},{17,1... | collective-permute-start | bytes 1179656 | tf_op jit(solution)/shard_map/ppermute | solution.py:472
  136.9 5.2 %collective-permute-start.3 = (bf16[384,512]{1,0:T(8,128)(2,1)S(1)}, bf16[384,512]{1,0:T(8,128)(2,1)S(1)}, u32[]{:S(2)}, u32[]{:S(2)}) collective-permute-start(bf16[384,512]{1,0:T(8,128)(2,1)S(1)} %get-tuple-element.63), channel_id=1, source_target_pairs={{0,1},{1,2},{4,5},{5,6},{8,9},{9,10},{12,13},{13,14},{16,17},{17,1... | collective-permute-start | bytes 1179656 | tf_op jit(solution)/shard_map/ppermute | solution.py:472
  143.0 5.1 %collective-permute-start.17 = (bf16[256,512]{1,0:T(8,128)(2,1)S(1)}, bf16[256,512]{1,0:T(8,128)(2,1)S(1)}, u32[]{:S(2)}, u32[]{:S(2)}) collective-permute-start(bf16[256,512]{1,0:T(8,128)(2,1)S(1)} %get-tuple-element.77), channel_id=1, source_target_pairs={{0,1},{1,2},{2,3},{4,5},{5,6},{6,7},{8,9},{9,10},{10,11},{12,13},{... | collective-permute-start | bytes 786440 | tf_op jit(solution)/shard_map/ppermute | solution.py:472
  148.4 6.3 %collective-permute-start.11 = (bf16[384,512]{1,0:T(8,128)(2,1)S(1)}, bf16[384,512]{1,0:T(8,128)(2,1)S(1)}, u32[]{:S(2)}, u32[]{:S(2)}) collective-permute-start(bf16[384,512]{1,0:T(8,128)(2,1)S(1)} %get-tuple-element.71), channel_id=1, source_target_pairs={{0,1},{1,2},{2,3},{4,5},{5,6},{6,7},{8,9},{9,10},{10,11},{12,13},{... | collective-permute-start | bytes 1179656 | tf_op jit(solution)/shard_map/ppermute | solution.py:472
  154.7 1.3 collective-permute-start.12
  156.3 6.8 %collective-permute-start.5 = (bf16[384,512]{1,0:T(8,128)(2,1)S(1)}, bf16[384,512]{1,0:T(8,128)(2,1)S(1)}, u32[]{:S(2)}, u32[]{:S(2)}) collective-permute-start(bf16[384,512]{1,0:T(8,128)(2,1)S(1)} %get-tuple-element.65), channel_id=1, source_target_pairs={{0,1},{1,2},{2,3},{4,5},{5,6},{6,7},{8,9},{9,10},{10,11},{12,13},{... | collective-permute-start | bytes 1179656 | tf_op jit(solution)/shard_map/ppermute | solution.py:472
  163.1 1.3 collective-permute-start.6
  164.4 1.3 collective-permute-start.18
  165.7 12.7 %collective-permute-done.18.down_ref = bf16[256,512]{1,0:T(8,128)(2,1)S(1)} collective-permute-done((bf16[256,512]{1,0:T(8,128)(2,1)S(1)}, bf16[256,512]{1,0:T(8,128)(2,1)S(1)}, u32[]{:S(2)}, u32[]{:S(2)}) %collective-permute-start.18) | collective-permute-done | bytes 262176 | tf_op jit(solution)/shard_map/ppermute | solution.py:473
  178.4 0.8 final.3.rest_0_
  179.2 1.4 final.4.rest_0_
  180.7 1.4 final.5
  (111 shorter events, 9.3 us)
Async XLA Ops:
  1.5 5.3 %collective-permute-start = (bf16[8,2560]{1,0:T(8,128)(2,1)S(1)}, bf16[8,2560]{1,0:T(8,128)(2,1)S(1)}, u32[]{:S(2)}, u32[]{:S(2)}) collective-permute-start(bf16[8,2560]{1,0:T(8,128)(2,1)S(1)} %pad_maximum_fusion), channel_id=1, source_target_pairs={{0,4},{4,8},{8,12},{12,16},{16,20},{20,24},{24,28},{1,5},{5,9},{9,... | collective-permute-start | bytes 122888 | tf_op jit(solution)/shard_map/ppermute | solution.py:299
  6.8 1.0 copy-start.17
  7.8 2.2 %copy-start.34 = (bf16[1024,2048]{1,0:T(8,128)(2,1)S(1)}, bf16[1024,2048]{1,0:T(8,128)(2,1)}, u32[]{:S(2)}) copy-start(bf16[1024,2048]{1,0:T(8,128)(2,1)} %x_ref.1) | copy-start | bytes 12582916
  10.0 1.2 copy-start.40
  14.9 20.2 %copy-start.14 = (bf16[128,2048]{1,0:T(8,128)(2,1)S(1)}, bf16[128,2048]{1,0:T(8,128)(2,1)}, u32[]{:S(2)}) copy-start(bf16[128,2048]{1,0:T(8,128)(2,1)} %constant.9.clone.high_ref.e_ref) | copy-start | bytes 1572868
  14.9 20.2 %copy-start.49 = (f32[32]{0:T(128)S(1)}, f32[32]{0:T(128)}, u32[]{:S(2)}) copy-start(f32[32]{0:T(128)} %param.19) | copy-start | bytes 388
  27.2 2.0 %copy-start.4 = (bf16[1024,2048]{1,0:T(8,128)(2,1)}, bf16[1024,2048]{1,0:T(8,128)(2,1)S(1)}, u32[]{:S(2)}) copy-start(bf16[1024,2048]{1,0:T(8,128)(2,1)S(1)} %get-tuple-element.42.xc_ref) | copy-start | bytes 12582916
  30.9 20.6 %copy-start.35 = (bf16[1024,128]{1,0:T(8,128)(2,1)}, bf16[1024,128]{1,0:T(8,128)(2,1)S(1)}, u32[]{:S(2)}) copy-start(bf16[1024,128]{1,0:T(8,128)(2,1)S(1)} %get-tuple-element.47.w_ref) | copy-start | bytes 786436
  30.9 33.6 %copy-start.11 = (bf16[1024,512]{1,0:T(8,128)(2,1)}, bf16[1024,512]{1,0:T(8,128)(2,1)S(1)}, u32[]{:S(2)}) copy-start(bf16[1024,512]{1,0:T(8,128)(2,1)S(1)} %get-tuple-element.43.bc_ref) | copy-start | bytes 3145732
  30.9 13.5 %all-to-all-start = ((bf16[8,16,2176]{2,1,0:T(8,128)(2,1)}), bf16[8,16,2176]{2,1,0:T(8,128)(2,1)}, u32[]{:S(2)}, u32[]{:S(2)}) async-start(bf16[8,16,2176]{2,1,0:T(8,128)(2,1)} %bitcast.7), calls=%async_computation | async-start | bytes 1114112 | tf_op jit(solution)/shard_map/all_to_all | solution.py:349
  35.2 2.2 %copy-start.5 = (bf16[1024,2048]{1,0:T(8,128)(2,1)S(1)}, bf16[1024,2048]{1,0:T(8,128)(2,1)}, u32[]{:S(2)}) copy-start(bf16[1024,2048]{1,0:T(8,128)(2,1)} %copy-done.4) | copy-start | bytes 12582916
  37.3 1.0 copy-start.18
  38.4 1.0 copy-start.27
  39.4 1.0 copy-start.31
  44.4 7.1 %copy-start.15 = (bf16[256,2048]{1,0:T(8,128)(2,1)}, bf16[256,2048]{1,0:T(8,128)(2,1)S(1)}, u32[]{:S(2)}) copy-start(bf16[256,2048]{1,0:T(8,128)(2,1)S(1)} %get-tuple-element.51.rest_1_.after_ref.y_ref) | copy-start | bytes 3145732
  46.9 17.6 %all-to-all-start.1 = ((bf16[8,16,2048]{2,1,0:T(8,128)(2,1)}), bf16[8,16,2048]{2,1,0:T(8,128)(2,1)}, u32[]{:S(2)}, u32[]{:S(2)}) async-start(bf16[8,16,2048]{2,1,0:T(8,128)(2,1)} %copy-done.37), calls=%async_computation.1 | async-start | bytes 1048576 | tf_op jit(solution)/shard_map/all_to_all | solution.py:406
  51.5 2.2 %copy-start.6 = (bf16[1024,2048]{1,0:T(8,128)(2,1)S(1)}, bf16[1024,2048]{1,0:T(8,128)(2,1)}, u32[]{:S(2)}) copy-start(bf16[1024,2048]{1,0:T(8,128)(2,1)} %copy-done.4) | copy-start | bytes 12582916
  53.7 1.0 copy-start.19
  54.7 1.0 copy-start.28
  56.8 1.2 copy-start.44
  58.0 6.5 %copy-start.46 = (f32[2048]{0:T(1024)S(1)}, f32[2048]{0:T(1024)}, u32[]{:S(2)}) copy-start(f32[2048]{0:T(1024)} %param.22) | copy-start | bytes 24580
  62.4 1.2 copy-start.23
  64.5 17.2 %slice-start = ((s8[8388608]{0:T(1024)(128)(4,1)}), s8[4194304]{0:T(1024)(128)(4,1)S(1)}, s32[]{:S(2)}) async-start(s8[8388608]{0:T(1024)(128)(4,1)} %bitcast.10), calls=%async_computation.2 | async-start | bytes 8388608
  64.5 2.3 %copy-start.8 = (bf16[1024,2048]{1,0:T(8,128)(2,1)S(1)}, bf16[1024,2048]{1,0:T(8,128)(2,1)}, u32[]{:S(2)}) copy-start(bf16[1024,2048]{1,0:T(8,128)(2,1)} %gate_ref.5) | copy-start | bytes 12582916
  66.9 1.4 copy-start.16
  68.3 1.4 copy-start.24
  69.7 12.1 %slice-start.1 = ((s8[8388608]{0:T(1024)(128)(4,1)}), s8[4194304]{0:T(1024)(128)(4,1)S(1)}, s32[]{:S(2)}) async-start(s8[8388608]{0:T(1024)(128)(4,1)} %bitcast.10), calls=%async_computation.3 | async-start | bytes 8388608
  76.2 43.6 %collective-permute-start.13 = (bf16[256,512]{1,0:T(8,128)(2,1)}, bf16[256,512]{1,0:T(8,128)(2,1)}, u32[]{:S(2)}, u32[]{:S(2)}) collective-permute-start(bf16[256,512]{1,0:T(8,128)(2,1)} %get-tuple-element.73), channel_id=1, source_target_pairs={{0,1},{4,5},{8,9},{12,13},{16,17},{20,21},{24,25},{28,29}} | collective-permute-start | bytes 786440 | tf_op jit(solution)/shard_map/ppermute | solution.py:472
  80.4 40.1 %collective-permute-start.14 = (bf16[256,512]{1,0:T(8,128)(2,1)}, bf16[256,512]{1,0:T(8,128)(2,1)}, u32[]{:S(2)}, u32[]{:S(2)}) collective-permute-start(bf16[256,512]{1,0:T(8,128)(2,1)} %get-tuple-element.74), channel_id=1, source_target_pairs={{3,2},{7,6},{11,10},{15,14},{19,18},{23,22},{27,26},{31,30}} | collective-permute-start | bytes 786440 | tf_op jit(solution)/shard_map/ppermute | solution.py:473
  81.8 2.2 %copy-start.9 = (bf16[1024,2048]{1,0:T(8,128)(2,1)S(1)}, bf16[1024,2048]{1,0:T(8,128)(2,1)}, u32[]{:S(2)}) copy-start(bf16[1024,2048]{1,0:T(8,128)(2,1)} %gate_ref.5) | copy-start | bytes 12582916
  81.8 2.5 %copy-start.12 = (bf16[1024,512]{1,0:T(8,128)(2,1)S(1)}, bf16[1024,512]{1,0:T(8,128)(2,1)}, u32[]{:S(2)}) copy-start(bf16[1024,512]{1,0:T(8,128)(2,1)} %copy-done.11) | copy-start | bytes 3145732
  81.8 3.0 %copy-start.25 = (bf16[384,2048]{1,0:T(8,128)(2,1)S(1)}, bf16[384,2048]{1,0:T(8,128)(2,1)}, u32[]{:S(2)}) copy-start(bf16[384,2048]{1,0:T(8,128)(2,1)} %copy-done.23) | copy-start | bytes 4718596
  84.8 7.8 %copy-start.7 = (bf16[1024,2048]{1,0:T(8,128)(2,1)S(1)}, bf16[1024,2048]{1,0:T(8,128)(2,1)}, u32[]{:S(2)}) copy-start(bf16[1024,2048]{1,0:T(8,128)(2,1)} %copy-done.4) | copy-start | bytes 12582916
  84.8 7.8 %copy-start.13 = (bf16[1024,512]{1,0:T(8,128)(2,1)S(1)}, bf16[1024,512]{1,0:T(8,128)(2,1)}, u32[]{:S(2)}) copy-start(bf16[1024,512]{1,0:T(8,128)(2,1)} %copy-done.11) | copy-start | bytes 3145732
  84.8 7.8 %copy-start.20 = (bf16[128,2048]{1,0:T(8,128)(2,1)S(1)}, bf16[128,2048]{1,0:T(8,128)(2,1)}, u32[]{:S(2)}) copy-start(bf16[128,2048]{1,0:T(8,128)(2,1)} %constant.8.clone.e_ref.low_ref) | copy-start | bytes 1572868
  84.8 7.8 %copy-start.29 = (bf16[2,128,1024]{2,1,0:T(8,128)(2,1)S(1)}, bf16[2,128,1024]{2,1,0:T(8,128)(2,1)}, u32[]{:S(2)}) copy-start(bf16[2,128,1024]{2,1,0:T(8,128)(2,1)} %copy-done.26) | copy-start | bytes 1572868
  84.8 7.8 %copy-start.33 = (f32[1024,128]{1,0:T(8,128)S(1)}, f32[1024,128]{1,0:T(8,128)}, u32[]{:S(2)}) copy-start(f32[1024,128]{1,0:T(8,128)} %copy-done.30) | copy-start | bytes 1572868
  84.8 7.8 %copy-start.36 = (bf16[1024,128]{1,0:T(8,128)(2,1)S(1)}, bf16[1024,128]{1,0:T(8,128)(2,1)}, u32[]{:S(2)}) copy-start(bf16[1024,128]{1,0:T(8,128)(2,1)} %copy-done.35) | copy-start | bytes 786436
  84.8 7.8 %copy-start.42 = (f32[128,2048]{1,0:T(8,128)S(1)}, f32[128,2048]{1,0:T(8,128)}, u32[]{:S(2)}) copy-start(f32[128,2048]{1,0:T(8,128)} %copy-done.41) | copy-start | bytes 3145732
  98.1 9.2 %copy-start.38 = (bf16[384,2048]{1,0:T(8,128)(2,1)}, bf16[384,2048]{1,0:T(8,128)(2,1)S(1)}, u32[]{:S(2)}) copy-start(bf16[384,2048]{1,0:T(8,128)(2,1)S(1)} %get-tuple-element.56.y_ref) | copy-start | bytes 4718596
  98.1 32.2 %collective-permute-start.7 = (bf16[384,512]{1,0:T(8,128)(2,1)}, bf16[384,512]{1,0:T(8,128)(2,1)}, u32[]{:S(2)}, u32[]{:S(2)}) collective-permute-start(bf16[384,512]{1,0:T(8,128)(2,1)} %get-tuple-element.67), channel_id=1, source_target_pairs={{0,1},{4,5},{8,9},{12,13},{16,17},{20,21},{24,25},{28,29}} | collective-permute-start | bytes 1179656 | tf_op jit(solution)/shard_map/ppermute | solution.py:472
  100.1 30.8 %collective-permute-start.8 = (bf16[384,512]{1,0:T(8,128)(2,1)}, bf16[384,512]{1,0:T(8,128)(2,1)}, u32[]{:S(2)}, u32[]{:S(2)}) collective-permute-start(bf16[384,512]{1,0:T(8,128)(2,1)} %get-tuple-element.68), channel_id=1, source_target_pairs={{3,2},{7,6},{11,10},{15,14},{19,18},{23,22},{27,26},{31,30}} | collective-permute-start | bytes 1179656 | tf_op jit(solution)/shard_map/ppermute | solution.py:473
  101.5 3.4 %copy-start = (bf16[2048,2048]{1,0:T(8,128)(2,1)S(1)}, bf16[2048,2048]{1,0:T(8,128)(2,1)}, u32[]{:S(2)}) copy-start(bf16[2048,2048]{1,0:T(8,128)(2,1)} %w_ref.11) | copy-start | bytes 25165828
  104.9 2.3 %copy-start.10 = (bf16[1024,2048]{1,0:T(8,128)(2,1)S(1)}, bf16[1024,2048]{1,0:T(8,128)(2,1)}, u32[]{:S(2)}) copy-start(bf16[1024,2048]{1,0:T(8,128)(2,1)} %gate_ref.5) | copy-start | bytes 12582916
  107.3 1.4 copy-start.39
  116.2 1.1 copy-start.2
  117.3 1.1 copy-start.21
  118.5 17.5 %collective-permute-start.1 = (bf16[384,512]{1,0:T(8,128)(2,1)}, bf16[384,512]{1,0:T(8,128)(2,1)S(1)}, u32[]{:S(2)}, u32[]{:S(2)}) collective-permute-start(bf16[384,512]{1,0:T(8,128)(2,1)} %get-tuple-element.61), channel_id=1, source_target_pairs={{0,1},{4,5},{8,9},{12,13},{16,17},{20,21},{24,25},{28,29}} | collective-permute-start | bytes 1179656 | tf_op jit(solution)/shard_map/ppermute | solution.py:472
  119.8 16.9 %collective-permute-start.2 = (bf16[384,512]{1,0:T(8,128)(2,1)}, bf16[384,512]{1,0:T(8,128)(2,1)S(1)}, u32[]{:S(2)}, u32[]{:S(2)}) collective-permute-start(bf16[384,512]{1,0:T(8,128)(2,1)} %get-tuple-element.62), channel_id=1, source_target_pairs={{3,2},{7,6},{11,10},{15,14},{19,18},{23,22},{27,26},{31,30}} | collective-permute-start | bytes 1179656 | tf_op jit(solution)/shard_map/ppermute | solution.py:473
  120.5 2.6 %copy-start.3 = (bf16[4,384,512]{2,1,0:T(8,128)(2,1)S(1)}, bf16[4,384,512]{2,1,0:T(8,128)(2,1)}, u32[]{:S(2)}) copy-start(bf16[4,384,512]{2,1,0:T(8,128)(2,1)} %copy-done.2) | copy-start | bytes 4718596
  121.8 20.3 %collective-permute-start.15 = (bf16[256,512]{1,0:T(8,128)(2,1)S(1)}, bf16[256,512]{1,0:T(8,128)(2,1)S(1)}, u32[]{:S(2)}, u32[]{:S(2)}) collective-permute-start(bf16[256,512]{1,0:T(8,128)(2,1)S(1)} %get-tuple-element.75), channel_id=1, source_target_pairs={{0,1},{1,2},{4,5},{5,6},{8,9},{9,10},{12,13},{13,14},{16,17},{17,1... | collective-permute-start | bytes 786440 | tf_op jit(solution)/shard_map/ppermute | solution.py:472
  123.1 3.4 %copy-start.1 = (bf16[2048,2048]{1,0:T(8,128)(2,1)S(1)}, bf16[2048,2048]{1,0:T(8,128)(2,1)}, u32[]{:S(2)}) copy-start(bf16[2048,2048]{1,0:T(8,128)(2,1)} %w_ref.11) | copy-start | bytes 25165828
  126.5 1.4 copy-start.22
  130.3 12.5 %collective-permute-start.16 = (bf16[256,512]{1,0:T(8,128)(2,1)S(1)}, bf16[256,512]{1,0:T(8,128)(2,1)S(1)}, u32[]{:S(2)}, u32[]{:S(2)}) collective-permute-start(bf16[256,512]{1,0:T(8,128)(2,1)S(1)} %get-tuple-element.76), channel_id=1, source_target_pairs={{2,1},{3,2},{6,5},{7,6},{10,9},{11,10},{14,13},{15,14},{18,17},{19... | collective-permute-start | bytes 786440 | tf_op jit(solution)/shard_map/ppermute | solution.py:473
  133.1 15.1 %collective-permute-start.9 = (bf16[384,512]{1,0:T(8,128)(2,1)S(1)}, bf16[384,512]{1,0:T(8,128)(2,1)S(1)}, u32[]{:S(2)}, u32[]{:S(2)}) collective-permute-start(bf16[384,512]{1,0:T(8,128)(2,1)S(1)} %get-tuple-element.69), channel_id=1, source_target_pairs={{0,1},{1,2},{4,5},{5,6},{8,9},{9,10},{12,13},{13,14},{16,17},{17,1... | collective-permute-start | bytes 1179656 | tf_op jit(solution)/shard_map/ppermute | solution.py:472
  136.0 12.2 %collective-permute-start.10 = (bf16[384,512]{1,0:T(8,128)(2,1)S(1)}, bf16[384,512]{1,0:T(8,128)(2,1)S(1)}, u32[]{:S(2)}, u32[]{:S(2)}) collective-permute-start(bf16[384,512]{1,0:T(8,128)(2,1)S(1)} %get-tuple-element.70), channel_id=1, source_target_pairs={{2,1},{3,2},{6,5},{7,6},{10,9},{11,10},{14,13},{15,14},{18,17},{19... | collective-permute-start | bytes 1179656 | tf_op jit(solution)/shard_map/ppermute | solution.py:473
  136.9 19.1 %collective-permute-start.3 = (bf16[384,512]{1,0:T(8,128)(2,1)S(1)}, bf16[384,512]{1,0:T(8,128)(2,1)S(1)}, u32[]{:S(2)}, u32[]{:S(2)}) collective-permute-start(bf16[384,512]{1,0:T(8,128)(2,1)S(1)} %get-tuple-element.63), channel_id=1, source_target_pairs={{0,1},{1,2},{4,5},{5,6},{8,9},{9,10},{12,13},{13,14},{16,17},{17,1... | collective-permute-start | bytes 1179656 | tf_op jit(solution)/shard_map/ppermute | solution.py:472
  142.1 13.9 %collective-permute-start.4 = (bf16[384,512]{1,0:T(8,128)(2,1)S(1)}, bf16[384,512]{1,0:T(8,128)(2,1)S(1)}, u32[]{:S(2)}, u32[]{:S(2)}) collective-permute-start(bf16[384,512]{1,0:T(8,128)(2,1)S(1)} %get-tuple-element.64), channel_id=1, source_target_pairs={{2,1},{3,2},{6,5},{7,6},{10,9},{11,10},{14,13},{15,14},{18,17},{19... | collective-permute-start | bytes 1179656 | tf_op jit(solution)/shard_map/ppermute | solution.py:473
  143.0 21.4 %collective-permute-start.17 = (bf16[256,512]{1,0:T(8,128)(2,1)S(1)}, bf16[256,512]{1,0:T(8,128)(2,1)S(1)}, u32[]{:S(2)}, u32[]{:S(2)}) collective-permute-start(bf16[256,512]{1,0:T(8,128)(2,1)S(1)} %get-tuple-element.77), channel_id=1, source_target_pairs={{0,1},{1,2},{2,3},{4,5},{5,6},{6,7},{8,9},{9,10},{10,11},{12,13},{... | collective-permute-start | bytes 786440 | tf_op jit(solution)/shard_map/ppermute | solution.py:472
  148.4 30.8 %collective-permute-start.11 = (bf16[384,512]{1,0:T(8,128)(2,1)S(1)}, bf16[384,512]{1,0:T(8,128)(2,1)S(1)}, u32[]{:S(2)}, u32[]{:S(2)}) collective-permute-start(bf16[384,512]{1,0:T(8,128)(2,1)S(1)} %get-tuple-element.71), channel_id=1, source_target_pairs={{0,1},{1,2},{2,3},{4,5},{5,6},{6,7},{8,9},{9,10},{10,11},{12,13},{... | collective-permute-start | bytes 1179656 | tf_op jit(solution)/shard_map/ppermute | solution.py:472
  154.7 24.5 %collective-permute-start.12 = (bf16[384,512]{1,0:T(8,128)(2,1)S(1)}, bf16[384,512]{1,0:T(8,128)(2,1)S(1)}, u32[]{:S(2)}, u32[]{:S(2)}) collective-permute-start(bf16[384,512]{1,0:T(8,128)(2,1)S(1)} %get-tuple-element.72), channel_id=1, source_target_pairs={{1,0},{2,1},{3,2},{5,4},{6,5},{7,6},{9,8},{10,9},{11,10},{13,12},{... | collective-permute-start | bytes 1179656 | tf_op jit(solution)/shard_map/ppermute | solution.py:473
  156.3 24.3 %collective-permute-start.5 = (bf16[384,512]{1,0:T(8,128)(2,1)S(1)}, bf16[384,512]{1,0:T(8,128)(2,1)S(1)}, u32[]{:S(2)}, u32[]{:S(2)}) collective-permute-start(bf16[384,512]{1,0:T(8,128)(2,1)S(1)} %get-tuple-element.65), channel_id=1, source_target_pairs={{0,1},{1,2},{2,3},{4,5},{5,6},{6,7},{8,9},{9,10},{10,11},{12,13},{... | collective-permute-start | bytes 1179656 | tf_op jit(solution)/shard_map/ppermute | solution.py:472
  163.1 17.5 %collective-permute-start.6 = (bf16[384,512]{1,0:T(8,128)(2,1)S(1)}, bf16[384,512]{1,0:T(8,128)(2,1)S(1)}, u32[]{:S(2)}, u32[]{:S(2)}) collective-permute-start(bf16[384,512]{1,0:T(8,128)(2,1)S(1)} %get-tuple-element.66), channel_id=1, source_target_pairs={{1,0},{2,1},{3,2},{5,4},{6,5},{7,6},{9,8},{10,9},{11,10},{13,12},{... | collective-permute-start | bytes 1179656 | tf_op jit(solution)/shard_map/ppermute | solution.py:473
  164.4 14.0 %collective-permute-start.18 = (bf16[256,512]{1,0:T(8,128)(2,1)S(1)}, bf16[256,512]{1,0:T(8,128)(2,1)S(1)}, u32[]{:S(2)}, u32[]{:S(2)}) collective-permute-start(bf16[256,512]{1,0:T(8,128)(2,1)S(1)} %get-tuple-element.78), channel_id=1, source_target_pairs={{1,0},{2,1},{3,2},{5,4},{6,5},{7,6},{9,8},{10,9},{11,10},{13,12},{... | collective-permute-start | bytes 786440 | tf_op jit(solution)/shard_map/ppermute | solution.py:473
  (11 other events, 9.1 us)

commit v4 on v3

--- a/solution.py
+++ b/solution.py
@@ -20,7 +20,8 @@
 LOG2E = 1.4426950408889634
 F32 = jnp.float32
 BF16 = jnp.bfloat16
-VMEM_LIMIT = 40 * 1024 * 1024
+VMEM_LIMIT = 58 * 1024 * 1024
+SMALL_LIMIT = 10 * 1024 * 1024
 
 
 def silu(v):
@@ -210,27 +211,56 @@
         running = decays[slab : slab + 1] * running + pay_ref[slab, :, :width].astype(F32)
 
 
-def ends_kernel(
-    y_ref, bc_ref, g_ref, enter_ref, gate_ref, gain_ref, w_ref, e_ref, after_ref,
+def norm_tile(y_ref, bc_ref, g_ref, enter_ref, gate_ref, gain_ref, e_ref, normed_ref, i):
+    width = y_ref.shape[1]
+    groups = bc_ref.shape[1] // (2 * STATE)
+    gw = width // groups
+    at_rows = pl.ds(pl.multiple_of(i * BLK, BLK), BLK)
+    for g in range(groups):
+        at = slice(g * gw, (g + 1) * gw)
+        c_g = bc_ref[:, (groups + g) * STATE : (groups + g + 1) * STATE]
+        carry = dot(c_g, enter_ref[:, at])
+        y = y_ref[:, at].astype(F32) + dot(g_ref[...], e_ref[:, at]) * carry
+        gated = y * silu(gate_ref[:, at].astype(F32))
+        square_mean = jnp.mean(gated * gated, axis=-1, keepdims=True)
+        scaled = gated * lax.rsqrt(square_mean + epsilon) * gain_ref[:, at]
+        normed_ref[at_rows, at] = scaled.astype(BF16)
+
+
+def direct_kernel(
+    where_ref, y_ref, bc_ref, g_ref, enter_ref, gate_ref, gain_ref, e_ref, w_ref, after_ref,
+    *rest, tiles,
+):
+    *out_refs, normed_ref = rest
+    i = pl.program_id(0)
+
+    @pl.when(i < tiles)
+    def _():
+        norm_tile(y_ref, bc_ref, g_ref, enter_ref, gate_ref, gain_ref, e_ref, normed_ref, i)
+
+    for k, out_ref in enumerate(out_refs):
+        @pl.when(i == tiles + k)
+        def _(out_ref=out_ref):
+            out_ref[...] = dot(normed_ref[...], w_ref[...]).astype(BF16)
+
+
+def more_kernel(where_ref, normed_ref, w_ref, *out_refs):
+    i = pl.program_id(0)
+    for k, out_ref in enumerate(out_refs):
+        @pl.when(i == k)
+        def _(out_ref=out_ref):
+            out_ref[...] = dot(normed_ref[...], w_ref[...]).astype(BF16)
+
+
+def line_kernel(
+    y_ref, bc_ref, g_ref, enter_ref, gate_ref, gain_ref, e_ref, w_ref, after_ref,
     shares_ref, up_ref, down_ref, normed_ref, *, tiles,
 ):
     i = pl.program_id(0)
-    width = y_ref.shape[1]
-    groups = bc_ref.shape[1] // (2 * STATE)
-    gw = width // groups
 
     @pl.when(i < tiles)
     def _():
-        at_rows = pl.ds(pl.multiple_of(i * BLK, BLK), BLK)
-        for g in range(groups):
-            at = slice(g * gw, (g + 1) * gw)
-            c_g = bc_ref[:, (groups + g) * STATE : (groups + g + 1) * STATE]
-            carry = dot(c_g, enter_ref[:, at])
-            y = y_ref[:, at].astype(F32) + dot(g_ref[...], e_ref[:, at]) * carry
-            gated = y * silu(gate_ref[:, at].astype(F32))
-            square_mean = jnp.mean(gated * gated, axis=-1, keepdims=True)
-            scaled = gated * lax.rsqrt(square_mean + epsilon) * gain_ref[:, at]
-            normed_ref[at_rows, at] = scaled.astype(BF16)
+        norm_tile(y_ref, bc_ref, g_ref, enter_ref, gate_ref, gain_ref, e_ref, normed_ref, i)
 
     @pl.when(i >= tiles)
     def _():
@@ -240,16 +270,12 @@
     def _():
         down_ref[...] = shares_ref[0]
 
-    @pl.when(i == tiles + 1)
+    @pl.when(i == pl.num_programs(0) - 1)
     def _():
         up_ref[...] = shares_ref[0]
 
 
-def middle_kernel(normed_ref, w_ref, ends_ref, after_ref, shares_ref):
-    shares_ref[0] = dot(normed_ref[...], w_ref[...]).astype(BF16)
-
-
-def onward_kernel(where_ref, up_own_ref, down_own_ref, up_ref, down_ref, up_out, down_out):
+def onward_kernel(where_ref, up_own_ref, down_own_ref, up_ref, down_ref, after_ref, up_out, down_out):
     up_out[...] = (up_own_ref[0].astype(F32) + up_ref[...].astype(F32)).astype(BF16)
     down_out[...] = (down_own_ref[0].astype(F32) + down_ref[...].astype(F32)).astype(BF16)
 
@@ -260,10 +286,16 @@
     out_ref[...] = total.astype(BF16)
 
 
-def params():
-    return pltpu.CompilerParams(
-        dimension_semantics=("arbitrary",), vmem_limit_bytes=VMEM_LIMIT
-    )
+def direct_final_kernel(*refs):
+    *in_refs, after_ref, out_ref = refs
+    total = in_refs[0][...].astype(F32)
+    for ref in in_refs[1:]:
+        total = total + ref[...].astype(F32)
+    out_ref[...] = total.astype(BF16)
+
+
+def params(limit=VMEM_LIMIT):
+    return pltpu.CompilerParams(dimension_semantics=("arbitrary",), vmem_limit_bytes=limit)
 
 
 def whole(shape):
@@ -386,8 +418,9 @@
             name="local_part",
         )(*operands)
 
-    third = (blocks - blocks // 4) // 2
-    spans = [(0, blocks // 4), (blocks // 4, third), (blocks // 4 + third, third)]
+    third = blocks - blocks * 3 // 8
+    spans = [(0, blocks - third), (blocks - third, (third + 1) // 2)]
+    spans.append((spans[1][0] + spans[1][1], third // 2))
     y_first, state = local_part(*spans[0], None, pay)
     y_second, state = local_part(*spans[1], state, y_first)
 
@@ -400,7 +433,7 @@
             unread(),
         ],
         out_specs=pl.BlockSpec(memory_space=pltpu.VMEM),
-        compiler_params=pltpu.CompilerParams(vmem_limit_bytes=VMEM_LIMIT),
+        compiler_params=pltpu.CompilerParams(vmem_limit_bytes=SMALL_LIMIT),
         name="prefix",
     )(arrived, high, y_first)
     entering = lax.all_to_all(entering, "seq", split_axis=0, concat_axis=0, tiled=True)
@@ -411,69 +444,95 @@
     mine = lax.axis_index("chan").astype(jnp.int32)
     where = mine.reshape(1)
 
-    def project(start, count, y, after):
+    def norm_operands(start, count, y):
         def tile(width, start=start):
-            return pl.BlockSpec((BLK, width), lambda i: (start + jnp.minimum(i, count - 1), 0))
-
-        def end(i):
-            return jnp.where(i <= count, 0, chans - 1)
-
+            return pl.BlockSpec((BLK, width), lambda i, *_: (start + jnp.minimum(i, count - 1), 0))
+
+        operands = [y, bc, g_hl, entering, gate_input, norm_row, high]
+        specs = [
+            tile(width, 0),
+            tile(map_width),
+            tile(LANES),
+            whole((STATE, width)),
+            tile(width),
+            whole((1, width)),
+            whole((LANES, width)),
+        ]
+        return operands, specs
+
+    def project_direct(start, count, y, after, slots, more_slots):
+        operands, specs = norm_operands(start, count, y)
         size = count * BLK
-        shares, up, down, normed = pl.pallas_call(
-            functools.partial(ends_kernel, tiles=count),
-            grid=(count + 2,),
-            in_specs=[
-                tile(width, 0),
-                tile(map_width),
-                tile(LANES),
-                whole((STATE, width)),
-                tile(width),
-                whole((1, width)),
-                pl.BlockSpec((width, part_out), lambda i: (0, end(i))),
-                whole((LANES, width)),
-                unread(),
-            ],
+
+        def weights(slots, first):
+            def index(i, where):
+                step = i - first
+                slot = slots[-1]
+                for k in range(len(slots) - 1, -1, -1):
+                    slot = jnp.where(step <= k, slots[k], slot)
+                return (0, lax.rem(where[0] + slot, chans))
+
+            return pl.BlockSpec((width, part_out), index)
+
+        *shares, normed = pl.pallas_call(
+            functools.partial(direct_kernel, tiles=count),
+            grid_spec=pltpu.PrefetchScalarGridSpec(
+                num_scalar_prefetch=1,
+                grid=(count + len(slots),),
+                in_specs=specs + [weights(slots, count), unread()],
+                out_specs=[whole((size, part_out))] * len(slots) + [whole((size, width))],
+            ),
+            out_shape=[shaped((size, part_out))] * len(slots) + [shaped((size, width))],
+            compiler_params=params(),
+            name="project_direct",
+        )(where, *operands, out_weight, after)
+        more = pl.pallas_call(
+            more_kernel,
+            grid_spec=pltpu.PrefetchScalarGridSpec(
+                num_scalar_prefetch=1,
+                grid=(len(more_slots),),
+                in_specs=[whole((size, width)), weights(more_slots, 0)],
+                out_specs=[whole((size, part_out))] * len(more_slots),
+            ),
+            out_shape=[shaped((size, part_out))] * len(more_slots),
+            compiler_params=params(),
+            name="project_more",
+        )(where, normed, out_weight)
+        return dict(zip(slots + more_slots, shares + list(more)))
+
+    def project_line(start, count, y, after):
+        operands, specs = norm_operands(start, count, y)
+        size = count * BLK
+
+        def dest(i):
+            return jnp.maximum(i - count, 0)
+
+        return pl.pallas_call(
+            functools.partial(line_kernel, tiles=count),
+            grid=(count + chans,),
+            in_specs=specs
+            + [pl.BlockSpec((width, part_out), lambda i: (0, dest(i))), unread()],
             out_specs=[
-                pl.BlockSpec((1, size, part_out), lambda i: (end(i), 0, 0)),
+                pl.BlockSpec((1, size, part_out), lambda i: (dest(i), 0, 0)),
                 whole((size, part_out)),
                 whole((size, part_out)),
-                whole((size, width)),
             ],
             out_shape=[
                 shaped((chans, size, part_out)),
                 shaped((size, part_out)),
                 shaped((size, part_out)),
-                shaped((size, width)),
             ],
+            scratch_shapes=[pltpu.VMEM((size, width), BF16)],
             compiler_params=params(),
-            name="project_ends",
-        )(y, bc, g_hl, entering, gate_input, norm_row, out_weight, high, after)
-        return shares, up, down, normed
-
-    def project_middle(shares, normed, after):
-        size = normed.shape[0]
-        return pl.pallas_call(
-            middle_kernel,
-            grid=(chans - 2,),
-            in_specs=[
-                whole((size, width)),
-                pl.BlockSpec((width, part_out), lambda i: (0, i + 1)),
-                unread(),
-                unread(),
-            ],
-            out_specs=pl.BlockSpec((1, size, part_out), lambda i: (i + 1, 0, 0)),
-            out_shape=shaped((chans, size, part_out)),
-            input_output_aliases={2: 0},
-            compiler_params=params(),
-            name="project_middle",
-        )(normed, out_weight, shares, after)
+            name="project_line",
+        )(*operands, out_weight, after)
 
     def permuted(up, down, s):
         up = lax.ppermute(up, "chan", [(a, a + 1) for a in range(s + 1)])
         down = lax.ppermute(down, "chan", [(a, a - 1) for a in range(chans - 1 - s, chans)])
         return up, down
 
-    def onward(shares, up, down, s):
+    def onward(shares, up, down, s, after):
         def plain(i, where):
             return (i, 0)
 
@@ -493,13 +552,14 @@
                     ),
                     pl.BlockSpec((BLK, part_out), plain),
                     pl.BlockSpec((BLK, part_out), plain),
+                    unread(),
                 ],
                 out_specs=[pl.BlockSpec((BLK, part_out), plain)] * 2,
             ),
             out_shape=[shaped(up.shape)] * 2,
-            compiler_params=params(),
+            compiler_params=params(SMALL_LIMIT),
             name="onward",
-        )(where, shares, shares, up, down)
+        )(where, shares, shares, up, down, after)
 
     def final(start, shares, up, down, out):
         def plain(i, where):
@@ -526,27 +586,41 @@
             ),
             out_shape=shaped((tokens, part_out)),
             input_output_aliases=aliases,
-            compiler_params=params(),
+            compiler_params=params(SMALL_LIMIT),
             name="final",
         )(*operands)
 
-    after, y = y_second, y_first
-    sums = []
-    for k, (start, count) in enumerate(spans):
-        shares, up, down, normed = project(start, count, y, after)
-        up, down = permuted(up, down, 0)
-        shares = project_middle(shares, normed, normed)
-        if k == 0:
-            y_third, _ = local_part(*spans[2], state, shares)
-        for s in range(1, chans - 1):
-            up, down = onward(shares, up, down, s)
-            up, down = permuted(up, down, s)
-        sums.append((start, shares, up, down))
-        y = (y_second, y_third, None)[k]
-        after = shares
-    out = None
-    for start, shares, up, down in sums:
-        out = final(start, shares, up, down, out)
+    order = sorted(range(chans), key=lambda k: (k == 0, -min(k, chans - k), k))
+    slots = project_direct(
+        *spans[0], y_first, y_second, order[: chans // 2], order[chans // 2 :]
+    )
+    pieces = [slots[0]]
+    for k in order[:-1]:
+        turn = [(a, (a + k) % chans) for a in range(chans)]
+        pieces.append(lax.ppermute(slots[k], "chan", turn))
+
+    chunks = [project_line(*spans[1], y_second, slots[0])]
+    y_third, _ = local_part(*spans[2], state, chunks[0][0])
+    chunks.append(project_line(*spans[2], y_third, chunks[0][0]))
+    moving = [permuted(up, down, 0) for _, up, down in chunks]
+    out = pl.pallas_call(
+        direct_final_kernel,
+        grid=(spans[0][1],),
+        in_specs=[pl.BlockSpec((BLK, part_out), lambda i: (i, 0))] * chans + [unread()],
+        out_specs=pl.BlockSpec((BLK, part_out), lambda i: (i, 0)),
+        out_shape=shaped((tokens, part_out)),
+        compiler_params=params(SMALL_LIMIT),
+        name="direct_final",
+    )(*pieces, chunks[1][0])
+    after = out
+    for s in range(1, chans - 1):
+        for k in range(2):
+            up, down = onward(chunks[k][0], *moving[k], s, after)
+            after = up
+            moving[k] = permuted(up, down, s)
+
+    for k in range(2):
+        out = final(spans[k + 1][0], chunks[k][0], *moving[k], out)
     return out
 
 

time: 186 us -> 144 us (0.77)
  local copies, waits for them, and re-layouts: 47.2 us -> 6.75 us
  Pallas kernels: 63 us -> 75.5 us
  starting transfers between devices: 55.2 us -> 43.6 us
    unnamed x108 -> x22, local copies, waits for them, and re-layouts: 45.7 us -> 5.28 us
    ppermute x9 -> x6, starting transfers between devices: 35.1 us -> 22.4 us  [permuted(): up = lax.ppermute(up, 'chan', [(a, a + 1) for a in range(s + 1)])]
    ppermute x9 -> x6, waiting for transfers between devices: 12.7 us -> 1.75 us  [permuted(): lax.ppermute(down, 'chan', [(a, a - 1) for a in range(chans - 1 - s, chan...]
    pallas_call x6 -> x5, Pallas kernels: 28.2 us -> 37.4 us  [the longest x2 21.6 us: project_line(): pl.pallas_call(functools.partial(line_kernel, tiles=count), grid=(count +...]
    pallas_call x3, Pallas kernels: 12.8 us -> 20.6 us  [local_part(): pl.pallas_call(local_kernel, grid=(count,), in_specs=specs, out_specs=[pl...]
    ppermute x9 -> x6, waiting for transfers between devices: 0.02 us -> 7.28 us  [permuted(): up = lax.ppermute(up, 'chan', [(a, a + 1) for a in range(s + 1)])]
    ppermute x0 -> x3, starting transfers between devices: none -> 4.64 us  [local(): pieces.append(lax.ppermute(slots[k], 'chan', turn))]
    ppermute x9 -> x6, starting transfers between devices: 9.38 us -> 5.49 us  [permuted(): lax.ppermute(down, 'chan', [(a, a - 1) for a in range(chans - 1 - s, chan...]
  transfers between devices with their start and end apart: 21 -> 18, of which waited for: 2 -> 7; matrix products, arithmetic and copies ran while one was open for 0% -> 0% of each run, Pallas kernels for 23% -> 32%
where the time goes in v4:
time: 144 us; the launch traced here: 141 us
  Pallas kernels  75.5 us (52%)
  starting transfers between devices  43.6 us (30%)
  waiting for transfers between devices  15 us (10%)
  local copies, waits for them, and re-layouts  6.75 us (5%)
    ppermute x6, starting transfers between devices, permuted(): up = lax.ppermute(up, 'chan', [(a, a + 1) for a in range(s + 1)])  22.4 us
    pallas_call x2, Pallas kernels, project_line(): pl.pallas_call(functools.partial(line_kernel, tiles=count), grid=(count +...  21.6 us
    pallas_call x3, Pallas kernels, local_part(): pl.pallas_call(local_kernel, grid=(count,), in_specs=specs, out_specs=[pl...  20.6 us
    pallas_call x1, Pallas kernels, local(): pl.pallas_call(states_kernel, grid=(width // WIDE,), in_specs=[lanes_at(t...  13.6 us
    pallas_call x1, Pallas kernels, project_direct(): pl.pallas_call(functools.partial(direct_kernel, tiles=count), grid_spec=p...  9.28 us
    ppermute x6, waiting for transfers between devices, permuted(): up = lax.ppermute(up, 'chan', [(a, a + 1) for a in range(s + 1)])  7.28 us
    ppermute x6, starting transfers between devices, permuted(): lax.ppermute(down, 'chan', [(a, a - 1) for a in range(chans - 1 - s, chan...  5.49 us
    unnamed x22, local copies, waits for them, and re-layouts  5.28 us
  transfers between devices with their start and end apart: 18, of which 7 were waited for; matrix products, arithmetic and copies ran while one was open for 0% of the time, Pallas kernels for 32%

profile of v4, /device:TPU:2, one launch (start us, length us, event | category | flops | bytes accessed | tf_op | source)
XLA Modules:
  0.0 141.1 jit_solution(3386008558266351836)
XLA Ops:
  0.0 0.7 slice.7
  0.7 0.8 slice.6
  1.5 1.9 %collective-permute-start = (bf16[8,2560]{1,0:T(8,128)(2,1)S(1)}, bf16[8,2560]{1,0:T(8,128)(2,1)S(1)}, u32[]{:S(2)}, u32[]{:S(2)}) collective-permute-start(bf16[8,2560]{1,0:T(8,128)(2,1)S(1)} %pad_maximum_fusion), channel_id=1, source_target_pairs={{0,4},{4,8},{8,12},{12,16},{16,20},{20,24},{24,28},{1,5},{5,9},{9,... | collective-permute-start | bytes 122888 | tf_op jit(solution)/shard_map/ppermute | solution.py:331
  3.4 3.4 %collective-permute-done.tail_ref.mtail_ref = bf16[8,2560]{1,0:T(8,128)(2,1)S(1)} collective-permute-done((bf16[8,2560]{1,0:T(8,128)(2,1)S(1)}, bf16[8,2560]{1,0:T(8,128)(2,1)S(1)}, u32[]{:S(2)}, u32[]{:S(2)}) %collective-permute-start) | collective-permute-done | bytes 40992 | tf_op jit(solution)/shard_map/ppermute | solution.py:331
  6.8 0.6 copy-done.8
  7.4 13.6 %states.1 = (bf16[1024,2048]{1,0:T(8,128)(2,1)}, bf16[1024,512]{1,0:T(8,128)(2,1)}, bf16[2,128,1024]{2,1,0:T(8,128)(2,1)}, f32[32,1024]{1,0:T(8,128)}, f32[1024,...) custom-call(bf16[1024,2048]{1,0:T(8,128)(2,1)} %x_ref.1, ...), custom_call_target="tpu_custom_call" | custom-call | tf_op jit(solution)/shard_map/states/pallas_call | solution.py:336
  21.0 4.3 %all-to-all-start = ((bf16[8,16,2176]{2,1,0:T(8,128)(2,1)}), bf16[8,16,2176]{2,1,0:T(8,128)(2,1)S(1)}, u32[]{:S(2)}, u32[]{:S(2)}) async-start(bf16[8,16,2176]{2,1,0:T(8,128)(2,1)} %bitcast.13), calls=%async_computation | async-start | bytes 1114112 | tf_op jit(solution)/shard_map/all_to_all | solution.py:381
  25.2 7.0 %local_part.3 = (bf16[384,2048]{1,0:T(8,128)(2,1)}, f32[128,2048]{1,0:T(8,128)}) custom-call(bf16[1024,2048]{1,0:T(8,128)(2,1)} %get-tuple-element.37.xc_ref, bf16[1024,512]{1,0:T(8,128)(2,1)} %get-tuple-element.38.bc_ref, bf16[2,128,1024]{2,1,0:T(8,128)(2,1)} %get-tuple-element.39.bt_ref, f32[32,1024]{1,0:T(8,128)} %get-tuple-element.40.crow_ref, ...), custom_call_target="tpu_custom_call" | custom-call | tf_op jit(solution)/shard_map/local_part/pallas_call | solution.py:407
  32.3 1.6 %all-to-all-done.pay_ref = bf16[8,16,2176]{2,1,0:T(8,128)(2,1)S(1)} async-done(((bf16[8,16,2176]{2,1,0:T(8,128)(2,1)}), bf16[8,16,2176]{2,1,0:T(8,128)(2,1)S(1)}, u32[]{:S(2)}, u32[]{:S(2)}) %all-to-all-start) | async-done | bytes 557088 | tf_op jit(solution)/shard_map/all_to_all | solution.py:381
  33.9 0.0 copy-done.3
  33.9 1.4 copy-done.5
  35.3 1.1 prefix.1
  36.3 4.9 %all-to-all-start.1 = ((bf16[8,16,2048]{2,1,0:T(8,128)(2,1)}), bf16[8,16,2048]{2,1,0:T(8,128)(2,1)S(1)}, u32[]{:S(2)}, u32[]{:S(2)}) async-start(bf16[8,16,2048]{2,1,0:T(8,128)(2,1)} %prefix.1), calls=%async_computation.1 | async-start | bytes 1048576 | tf_op jit(solution)/shard_map/all_to_all | solution.py:439
  41.2 7.4 %local_part.4 = (bf16[384,2048]{1,0:T(8,128)(2,1)}, f32[128,2048]{1,0:T(8,128)}) custom-call(bf16[1024,2048]{1,0:T(8,128)(2,1)} %get-tuple-element.37.xc_ref, bf16[1024,512]{1,0:T(8,128)(2,1)} %get-tuple-element.38.bc_ref, bf16[2,128,1024]{2,1,0:T(8,128)(2,1)} %get-tuple-element.39.bt_ref, f32[32,1024]{1,0:T(8,128)} %get-tuple-element.40.crow_ref, ...), custom_call_target="tpu_custom_call" | custom-call | tf_op jit(solution)/shard_map/local_part/pallas_call | solution.py:407
  48.6 0.9 all-to-all-done.1
  49.5 0.8 copy-done.7
  50.3 9.3 %project_direct.1 = (bf16[384,512]{1,0:T(8,128)(2,1)}, bf16[384,512]{1,0:T(8,128)(2,1)}, bf16[384,2048]{1,0:T(8,128)(2,1)}) custom-call(s32[1]{0:T(128)} %bitcast.where_ref, bf16[384,2048]{1,0:T(8,128)(2,1)} %get-tuple-element.46.rest_1_.after_ref.y_ref, bf16[1024,512]{1,0:T(8,128)(2,1)} %get-tuple-element.38.bc_ref, ...), custom_call_target="tpu_custom_call" | custom-call | tf_op jit(solution)/shard_map/project_direct/pallas_call | solution.py:477
  59.6 5.1 %project_more.1 = (bf16[384,512]{1,0:T(8,128)(2,1)}, bf16[384,512]{1,0:T(8,128)(2,1)}) custom-call(s32[1]{0:T(128)} %bitcast.where_ref, bf16[384,2048]{1,0:T(8,128)(2,1)} %get-tuple-element.49.normed_ref, bf16[2048,2048]{1,0:T(8,128)(2,1)} %w_ref.7), custom_call_target="tpu_custom_call" | custom-call | tf_op jit(solution)/shard_map/project_more/pallas_call | solution.py:489
  64.7 3.6 %collective-permute-start.7 = (bf16[384,512]{1,0:T(8,128)(2,1)}, bf16[384,512]{1,0:T(8,128)(2,1)S(1)}, u32[]{:S(2)}, u32[]{:S(2)}) collective-permute-start(bf16[384,512]{1,0:T(8,128)(2,1)} %get-tuple-element.60), channel_id=1, source_target_pairs={{0,3},{1,0},{2,1},{3,2},{4,7},{5,4},{6,5},{7,6},{8,11},{9,8},{10,9... | collective-permute-start | bytes 1179656 | tf_op jit(solution)/shard_map/ppermute | solution.py:600
  68.3 0.0 copy-done.10
  68.3 0.0 collective-permute-start.5
  68.3 1.0 collective-permute-start.6
  69.3 11.7 %project_line.2 = (bf16[4,384,512]{2,1,0:T(8,128)(2,1)}, bf16[384,512]{1,0:T(8,128)(2,1)}, bf16[384,512]{1,0:T(8,128)(2,1)}) custom-call(bf16[384,2048]{1,0:T(8,128)(2,1)} %get-tuple-element.48.after_ref.y_ref, bf16[1024,512]{1,0:T(8,128)(2,1)} %get-tuple-element.38.bc_ref, bf16[1024,128]{1,0:T(8,128)(2,1)} %get-tuple-element.43.g_ref, ...), custom_call_target="tpu_custom_call" | custom-call | tf_op jit(solution)/shard_map/project_line/pallas_call | solution.py:510
  81.0 4.4 %collective-permute-start.3 = (bf16[384,512]{1,0:T(8,128)(2,1)}, bf16[384,512]{1,0:T(8,128)(2,1)S(1)}, u32[]{:S(2)}, u32[]{:S(2)}) collective-permute-start(bf16[384,512]{1,0:T(8,128)(2,1)} %get-tuple-element.56), channel_id=1, source_target_pairs={{0,1},{4,5},{8,9},{12,13},{16,17},{20,21},{24,25},{28,29}} | collective-permute-start | bytes 1179656 | tf_op jit(solution)/shard_map/ppermute | solution.py:531
  85.4 0.9 collective-permute-start.4
  86.3 6.1 %local_part.5 = (bf16[256,2048]{1,0:T(8,128)(2,1)}, f32[128,2048]{1,0:T(8,128)}) custom-call(bf16[1024,2048]{1,0:T(8,128)(2,1)} %get-tuple-element.37.xc_ref, bf16[1024,512]{1,0:T(8,128)(2,1)} %get-tuple-element.38.bc_ref, bf16[2,128,1024]{2,1,0:T(8,128)(2,1)} %get-tuple-element.39.bt_ref, f32[32,1024]{1,0:T(8,128)} %get-tuple-element.40.crow_ref, ...), custom_call_target="tpu_custom_call" | custom-call | tf_op jit(solution)/shard_map/local_part/pallas_call | solution.py:407
  92.4 9.8 %project_line.3 = (bf16[4,256,512]{2,1,0:T(8,128)(2,1)}, bf16[256,512]{1,0:T(8,128)(2,1)}, bf16[256,512]{1,0:T(8,128)(2,1)}) custom-call(bf16[256,2048]{1,0:T(8,128)(2,1)} %get-tuple-element.52.y_ref, bf16[1024,512]{1,0:T(8,128)(2,1)} %get-tuple-element.38.bc_ref, bf16[1024,128]{1,0:T(8,128)(2,1)} %get-tuple-element.43.g_ref, bf16[128,2048]{1,0:T(8,128)(2,1)} %bitcast.12, ...), custom_call_target="tpu_custom_call" | custom-call | tf_op jit(solution)/shard_map/project_line/pallas_call | solution.py:510
  102.3 0.0 collective-permute-done.7.refs_3_
  102.3 1.4 %collective-permute-start.1 = (bf16[256,512]{1,0:T(8,128)(2,1)}, bf16[256,512]{1,0:T(8,128)(2,1)S(1)}, u32[]{:S(2)}, u32[]{:S(2)}) collective-permute-start(bf16[256,512]{1,0:T(8,128)(2,1)} %get-tuple-element.54), channel_id=1, source_target_pairs={{0,1},{4,5},{8,9},{12,13},{16,17},{20,21},{24,25},{28,29}} | collective-permute-start | bytes 786440 | tf_op jit(solution)/shard_map/ppermute | solution.py:531
  103.7 0.0 collective-permute-done.5.refs_1_
  103.8 0.7 collective-permute-start.2
  104.4 0.0 collective-permute-done.6.refs_2_
  104.5 0.0 copy-done.6
  104.5 0.0 copy-start.1
  104.5 1.2 copy-done.1
  105.7 1.4 %direct_final.1.after_ref.rest_0_ = bf16[1024,512]{1,0:T(8,128)(2,1)} custom-call(bf16[384,512]{1,0:T(8,128)(2,1)S(1)} %copy-done.6, bf16[384,512]{1,0:T(8,128)(2,1)S(1)} %collective-permute-done.5.refs_1_, bf16[384,512]{1,0:T(8,128)(2,1)S(1)} %collective-permute-done.6.refs_2_, bf16[384,512]{1,0:T(8,128)(2,1)S(1)} %collective-permute-done.7.refs_3_, ...), custom_call_target="tpu_custom_call" | custom-call | tf_op jit(solution)/shard_map/direct_final/pallas_call | solution.py:606
  107.1 0.0 collective-permute-done.3.up_ref
  107.1 0.0 collective-permute-done.4.down_ref
  107.1 0.0 copy-start.4
  107.2 1.2 copy-done.4
  108.4 0.2 onward.4
  108.6 0.7 collective-permute-start.11
  109.3 1.9 %collective-permute-start.10 = (bf16[384,512]{1,0:T(8,128)(2,1)S(1)}, bf16[384,512]{1,0:T(8,128)(2,1)S(1)}, u32[]{:S(2)}, u32[]{:S(2)}) collective-permute-start(bf16[384,512]{1,0:T(8,128)(2,1)S(1)} %get-tuple-element.61.after_ref), channel_id=1, source_target_pairs={{0,1},{1,2},{4,5},{5,6},{8,9},{9,10},{12,13},{13,14},{16,17},{17,1... | collective-permute-start | bytes 1179656 | tf_op jit(solution)/shard_map/ppermute | solution.py:531
  111.2 0.0 collective-permute-done.1.up_ref
  111.2 0.0 collective-permute-done.2.down_ref
  111.2 0.2 onward.5
  111.4 0.7 collective-permute-start.9
  112.1 5.2 %collective-permute-start.8 = (bf16[256,512]{1,0:T(8,128)(2,1)S(1)}, bf16[256,512]{1,0:T(8,128)(2,1)S(1)}, u32[]{:S(2)}, u32[]{:S(2)}) collective-permute-start(bf16[256,512]{1,0:T(8,128)(2,1)S(1)} %get-tuple-element.62.after_ref), channel_id=1, source_target_pairs={{0,1},{1,2},{4,5},{5,6},{8,9},{9,10},{12,13},{13,14},{16,17},{17,1... | collective-permute-start | bytes 786440 | tf_op jit(solution)/shard_map/ppermute | solution.py:531
  117.3 0.0 collective-permute-done.11.down_ref
  117.3 3.5 %collective-permute-done.10.up_ref = bf16[384,512]{1,0:T(8,128)(2,1)S(1)} collective-permute-done((bf16[384,512]{1,0:T(8,128)(2,1)S(1)}, bf16[384,512]{1,0:T(8,128)(2,1)S(1)}, u32[]{:S(2)}, u32[]{:S(2)}) %collective-permute-start.10) | collective-permute-done | bytes 393248 | tf_op jit(solution)/shard_map/ppermute | solution.py:531
  120.7 0.2 onward.6
  121.0 1.3 collective-permute-start.15
  122.3 5.2 %collective-permute-start.14 = (bf16[384,512]{1,0:T(8,128)(2,1)S(1)}, bf16[384,512]{1,0:T(8,128)(2,1)S(1)}, u32[]{:S(2)}, u32[]{:S(2)}) collective-permute-start(bf16[384,512]{1,0:T(8,128)(2,1)S(1)} %get-tuple-element.65.after_ref), channel_id=1, source_target_pairs={{0,1},{1,2},{2,3},{4,5},{5,6},{6,7},{8,9},{9,10},{10,11},{12,13},{... | collective-permute-start | bytes 1179656 | tf_op jit(solution)/shard_map/ppermute | solution.py:531
  127.5 0.0 collective-permute-done.9.down_ref
  127.5 0.0 collective-permute-done.8.up_ref
  127.5 0.2 onward.7
  127.7 4.4 %collective-permute-start.12 = (bf16[256,512]{1,0:T(8,128)(2,1)S(1)}, bf16[256,512]{1,0:T(8,128)(2,1)S(1)}, u32[]{:S(2)}, u32[]{:S(2)}) collective-permute-start(bf16[256,512]{1,0:T(8,128)(2,1)S(1)} %get-tuple-element.66), channel_id=1, source_target_pairs={{0,1},{1,2},{2,3},{4,5},{5,6},{6,7},{8,9},{9,10},{10,11},{12,13},{... | collective-permute-start | bytes 786440 | tf_op jit(solution)/shard_map/ppermute | solution.py:531
  132.1 1.3 collective-permute-start.13
  133.4 0.0 collective-permute-done.15.down_ref
  133.4 2.4 %collective-permute-done.14.up_ref = bf16[384,512]{1,0:T(8,128)(2,1)S(1)} collective-permute-done((bf16[384,512]{1,0:T(8,128)(2,1)S(1)}, bf16[384,512]{1,0:T(8,128)(2,1)S(1)}, u32[]{:S(2)}, u32[]{:S(2)}) %collective-permute-start.14) | collective-permute-done | bytes 393248 | tf_op jit(solution)/shard_map/ppermute | solution.py:531
  135.8 1.4 final.2.rest_0_
  137.2 1.4 collective-permute-done.12.up_ref
  138.6 1.7 %collective-permute-done.13.down_ref = bf16[256,512]{1,0:T(8,128)(2,1)S(1)} collective-permute-done((bf16[256,512]{1,0:T(8,128)(2,1)S(1)}, bf16[256,512]{1,0:T(8,128)(2,1)S(1)}, u32[]{:S(2)}, u32[]{:S(2)}) %collective-permute-start.13) | collective-permute-done | bytes 262176 | tf_op jit(solution)/shard_map/ppermute | solution.py:532
  140.3 0.8 final.3
  (14 shorter events, 0.0 us)
Async XLA Ops:
  1.5 5.3 %collective-permute-start = (bf16[8,2560]{1,0:T(8,128)(2,1)S(1)}, bf16[8,2560]{1,0:T(8,128)(2,1)S(1)}, u32[]{:S(2)}, u32[]{:S(2)}) collective-permute-start(bf16[8,2560]{1,0:T(8,128)(2,1)S(1)} %pad_maximum_fusion), channel_id=1, source_target_pairs={{0,4},{4,8},{8,12},{12,16},{16,20},{20,24},{24,28},{1,5},{5,9},{9,... | collective-permute-start | bytes 122888 | tf_op jit(solution)/shard_map/ppermute | solution.py:331
  6.8 0.6 copy-start.8
  21.0 12.9 %all-to-all-start = ((bf16[8,16,2176]{2,1,0:T(8,128)(2,1)}), bf16[8,16,2176]{2,1,0:T(8,128)(2,1)S(1)}, u32[]{:S(2)}, u32[]{:S(2)}) async-start(bf16[8,16,2176]{2,1,0:T(8,128)(2,1)} %bitcast.13), calls=%async_computation | async-start | bytes 1114112 | tf_op jit(solution)/shard_map/all_to_all | solution.py:381
  25.2 8.6 %copy-start.3 = (bf16[128,2048]{1,0:T(8,128)(2,1)S(1)}, bf16[128,2048]{1,0:T(8,128)(2,1)}, u32[]{:S(2)}) copy-start(bf16[128,2048]{1,0:T(8,128)(2,1)} %constant.9.clone.high_ref.e_ref) | copy-start | bytes 1572868
  33.9 1.4 copy-start.5
  36.3 13.2 %all-to-all-start.1 = ((bf16[8,16,2048]{2,1,0:T(8,128)(2,1)}), bf16[8,16,2048]{2,1,0:T(8,128)(2,1)S(1)}, u32[]{:S(2)}, u32[]{:S(2)}) async-start(bf16[8,16,2048]{2,1,0:T(8,128)(2,1)} %prefix.1), calls=%async_computation.1 | async-start | bytes 1048576 | tf_op jit(solution)/shard_map/all_to_all | solution.py:439
  49.5 0.8 copy-start.7
  59.6 8.7 %copy-start.10 = (bf16[384,512]{1,0:T(8,128)(2,1)S(1)}, bf16[384,512]{1,0:T(8,128)(2,1)}, u32[]{:S(2)}) copy-start(bf16[384,512]{1,0:T(8,128)(2,1)} %get-tuple-element.58) | copy-start | bytes 1179652
  59.6 8.7 %copy-start.9 = (bf16[384,512]{1,0:T(8,128)(2,1)S(1)}, bf16[384,512]{1,0:T(8,128)(2,1)}, u32[]{:S(2)}) copy-start(bf16[384,512]{1,0:T(8,128)(2,1)} %get-tuple-element.59) | copy-start | bytes 1179652
  64.7 37.6 %collective-permute-start.7 = (bf16[384,512]{1,0:T(8,128)(2,1)}, bf16[384,512]{1,0:T(8,128)(2,1)S(1)}, u32[]{:S(2)}, u32[]{:S(2)}) collective-permute-start(bf16[384,512]{1,0:T(8,128)(2,1)} %get-tuple-element.60), channel_id=1, source_target_pairs={{0,3},{1,0},{2,1},{3,2},{4,7},{5,4},{6,5},{7,6},{8,11},{9,8},{10,9... | collective-permute-start | bytes 1179656 | tf_op jit(solution)/shard_map/ppermute | solution.py:600
  68.3 35.5 %collective-permute-start.5 = (bf16[384,512]{1,0:T(8,128)(2,1)S(1)}, bf16[384,512]{1,0:T(8,128)(2,1)S(1)}, u32[]{:S(2)}, u32[]{:S(2)}) collective-permute-start(bf16[384,512]{1,0:T(8,128)(2,1)S(1)} %copy-done.10), channel_id=1, source_target_pairs={{0,2},{1,3},{2,0},{3,1},{4,6},{5,7},{6,4},{7,5},{8,10},{9,11},{10,... | collective-permute-start | bytes 1179656 | tf_op jit(solution)/shard_map/ppermute | solution.py:600
  68.3 36.2 %collective-permute-start.6 = (bf16[384,512]{1,0:T(8,128)(2,1)S(1)}, bf16[384,512]{1,0:T(8,128)(2,1)S(1)}, u32[]{:S(2)}, u32[]{:S(2)}) collective-permute-start(bf16[384,512]{1,0:T(8,128)(2,1)S(1)} %copy-done.9), channel_id=1, source_target_pairs={{0,1},{1,2},{2,3},{3,0},{4,5},{5,6},{6,7},{7,4},{8,9},{9,10},{10,1... | collective-permute-start | bytes 1179656 | tf_op jit(solution)/shard_map/ppermute | solution.py:600
  81.0 26.1 %collective-permute-start.3 = (bf16[384,512]{1,0:T(8,128)(2,1)}, bf16[384,512]{1,0:T(8,128)(2,1)S(1)}, u32[]{:S(2)}, u32[]{:S(2)}) collective-permute-start(bf16[384,512]{1,0:T(8,128)(2,1)} %get-tuple-element.56), channel_id=1, source_target_pairs={{0,1},{4,5},{8,9},{12,13},{16,17},{20,21},{24,25},{28,29}} | collective-permute-start | bytes 1179656 | tf_op jit(solution)/shard_map/ppermute | solution.py:531
  85.4 21.7 %collective-permute-start.4 = (bf16[384,512]{1,0:T(8,128)(2,1)}, bf16[384,512]{1,0:T(8,128)(2,1)S(1)}, u32[]{:S(2)}, u32[]{:S(2)}) collective-permute-start(bf16[384,512]{1,0:T(8,128)(2,1)} %get-tuple-element.57), channel_id=1, source_target_pairs={{3,2},{7,6},{11,10},{15,14},{19,18},{23,22},{27,26},{31,30}} | collective-permute-start | bytes 1179656 | tf_op jit(solution)/shard_map/ppermute | solution.py:532
  92.4 12.0 %copy-start.6 = (bf16[384,512]{1,0:T(8,128)(2,1)S(1)}, bf16[384,512]{1,0:T(8,128)(2,1)}, u32[]{:S(2)}) copy-start(bf16[384,512]{1,0:T(8,128)(2,1)} %get-tuple-element.50.after_ref.refs_0_) | copy-start | bytes 1179652
  102.3 4.9 %copy-start = (bf16[4,384,512]{2,1,0:T(8,128)(2,1)S(1)}, bf16[4,384,512]{2,1,0:T(8,128)(2,1)}, u32[]{:S(2)}) copy-start(bf16[4,384,512]{2,1,0:T(8,128)(2,1)} %get-tuple-element.51.rest_1_.after_ref.up_own_ref.down_own_ref.own_ref) | copy-start | bytes 4718596
  102.3 8.9 %collective-permute-start.1 = (bf16[256,512]{1,0:T(8,128)(2,1)}, bf16[256,512]{1,0:T(8,128)(2,1)S(1)}, u32[]{:S(2)}, u32[]{:S(2)}) collective-permute-start(bf16[256,512]{1,0:T(8,128)(2,1)} %get-tuple-element.54), channel_id=1, source_target_pairs={{0,1},{4,5},{8,9},{12,13},{16,17},{20,21},{24,25},{28,29}} | collective-permute-start | bytes 786440 | tf_op jit(solution)/shard_map/ppermute | solution.py:531
  103.8 7.5 %collective-permute-start.2 = (bf16[256,512]{1,0:T(8,128)(2,1)}, bf16[256,512]{1,0:T(8,128)(2,1)S(1)}, u32[]{:S(2)}, u32[]{:S(2)}) collective-permute-start(bf16[256,512]{1,0:T(8,128)(2,1)} %get-tuple-element.55), channel_id=1, source_target_pairs={{3,2},{7,6},{11,10},{15,14},{19,18},{23,22},{27,26},{31,30}} | collective-permute-start | bytes 786440 | tf_op jit(solution)/shard_map/ppermute | solution.py:532
  104.5 1.2 copy-start.1
  105.7 5.5 %copy-start.2 = (bf16[4,256,512]{2,1,0:T(8,128)(2,1)S(1)}, bf16[4,256,512]{2,1,0:T(8,128)(2,1)}, u32[]{:S(2)}) copy-start(bf16[4,256,512]{2,1,0:T(8,128)(2,1)} %get-tuple-element.53.refs_4_.up_own_ref.down_own_ref.own_ref) | copy-start | bytes 3145732
  107.1 1.2 copy-start.4
  108.6 8.7 %collective-permute-start.11 = (bf16[384,512]{1,0:T(8,128)(2,1)S(1)}, bf16[384,512]{1,0:T(8,128)(2,1)S(1)}, u32[]{:S(2)}, u32[]{:S(2)}) collective-permute-start(bf16[384,512]{1,0:T(8,128)(2,1)S(1)} %get-tuple-element.64), channel_id=1, source_target_pairs={{2,1},{3,2},{6,5},{7,6},{10,9},{11,10},{14,13},{15,14},{18,17},{19... | collective-permute-start | bytes 1179656 | tf_op jit(solution)/shard_map/ppermute | solution.py:532
  109.3 11.4 %collective-permute-start.10 = (bf16[384,512]{1,0:T(8,128)(2,1)S(1)}, bf16[384,512]{1,0:T(8,128)(2,1)S(1)}, u32[]{:S(2)}, u32[]{:S(2)}) collective-permute-start(bf16[384,512]{1,0:T(8,128)(2,1)S(1)} %get-tuple-element.61.after_ref), channel_id=1, source_target_pairs={{0,1},{1,2},{4,5},{5,6},{8,9},{9,10},{12,13},{13,14},{16,17},{17,1... | collective-permute-start | bytes 1179656 | tf_op jit(solution)/shard_map/ppermute | solution.py:531
  111.4 16.1 %collective-permute-start.9 = (bf16[256,512]{1,0:T(8,128)(2,1)S(1)}, bf16[256,512]{1,0:T(8,128)(2,1)S(1)}, u32[]{:S(2)}, u32[]{:S(2)}) collective-permute-start(bf16[256,512]{1,0:T(8,128)(2,1)S(1)} %get-tuple-element.63), channel_id=1, source_target_pairs={{2,1},{3,2},{6,5},{7,6},{10,9},{11,10},{14,13},{15,14},{18,17},{19... | collective-permute-start | bytes 786440 | tf_op jit(solution)/shard_map/ppermute | solution.py:532
  112.1 15.4 %collective-permute-start.8 = (bf16[256,512]{1,0:T(8,128)(2,1)S(1)}, bf16[256,512]{1,0:T(8,128)(2,1)S(1)}, u32[]{:S(2)}, u32[]{:S(2)}) collective-permute-start(bf16[256,512]{1,0:T(8,128)(2,1)S(1)} %get-tuple-element.62.after_ref), channel_id=1, source_target_pairs={{0,1},{1,2},{4,5},{5,6},{8,9},{9,10},{12,13},{13,14},{16,17},{17,1... | collective-permute-start | bytes 786440 | tf_op jit(solution)/shard_map/ppermute | solution.py:531
  121.0 12.4 %collective-permute-start.15 = (bf16[384,512]{1,0:T(8,128)(2,1)S(1)}, bf16[384,512]{1,0:T(8,128)(2,1)S(1)}, u32[]{:S(2)}, u32[]{:S(2)}) collective-permute-start(bf16[384,512]{1,0:T(8,128)(2,1)S(1)} %get-tuple-element.68), channel_id=1, source_target_pairs={{1,0},{2,1},{3,2},{5,4},{6,5},{7,6},{9,8},{10,9},{11,10},{13,12},{... | collective-permute-start | bytes 1179656 | tf_op jit(solution)/shard_map/ppermute | solution.py:532
  122.3 13.5 %collective-permute-start.14 = (bf16[384,512]{1,0:T(8,128)(2,1)S(1)}, bf16[384,512]{1,0:T(8,128)(2,1)S(1)}, u32[]{:S(2)}, u32[]{:S(2)}) collective-permute-start(bf16[384,512]{1,0:T(8,128)(2,1)S(1)} %get-tuple-element.65.after_ref), channel_id=1, source_target_pairs={{0,1},{1,2},{2,3},{4,5},{5,6},{6,7},{8,9},{9,10},{10,11},{12,13},{... | collective-permute-start | bytes 1179656 | tf_op jit(solution)/shard_map/ppermute | solution.py:531
  127.7 10.9 %collective-permute-start.12 = (bf16[256,512]{1,0:T(8,128)(2,1)S(1)}, bf16[256,512]{1,0:T(8,128)(2,1)S(1)}, u32[]{:S(2)}, u32[]{:S(2)}) collective-permute-start(bf16[256,512]{1,0:T(8,128)(2,1)S(1)} %get-tuple-element.66), channel_id=1, source_target_pairs={{0,1},{1,2},{2,3},{4,5},{5,6},{6,7},{8,9},{9,10},{10,11},{12,13},{... | collective-permute-start | bytes 786440 | tf_op jit(solution)/shard_map/ppermute | solution.py:531
  132.1 8.3 %collective-permute-start.13 = (bf16[256,512]{1,0:T(8,128)(2,1)S(1)}, bf16[256,512]{1,0:T(8,128)(2,1)S(1)}, u32[]{:S(2)}, u32[]{:S(2)}) collective-permute-start(bf16[256,512]{1,0:T(8,128)(2,1)S(1)} %get-tuple-element.67), channel_id=1, source_target_pairs={{1,0},{2,1},{3,2},{5,4},{6,5},{7,6},{9,8},{10,9},{11,10},{13,12},{... | collective-permute-start | bytes 786440 | tf_op jit(solution)/shard_map/ppermute | solution.py:532

commit v5 on v4

--- a/solution.py
+++ b/solution.py
@@ -13,6 +13,7 @@
 BLK = 128
 LANES = 128
 HALO = 8
+ROWS = 16
 WIDE = 256
 
 step_limit = 0.5
@@ -67,9 +68,9 @@
 
 def conv(before, cur, taps):
     full = jnp.concatenate([before, cur], 0)
-    acc = cur * taps[3]
-    for back in range(1, 4):
-        acc = acc + pltpu.roll(full, back, 0)[HALO:] * taps[3 - back]
+    late = pltpu.roll(full, 1, 0)
+    early = taps[1] * full + taps[0] * late
+    acc = taps[3] * cur + taps[2] * late[HALO:] + pltpu.roll(early, 2, 0)[HALO:]
     return silu(acc).astype(BF16)
 
 
@@ -142,15 +143,18 @@
                 if q < groups:
                     bt_ref[q, :, b * BLK : (b + 1) * BLK] = result.astype(F32).T.astype(BF16)
 
-    taps = [ck_ref[k : k + 1] for k in range(4)]
-    before = tail_ref[...].astype(F32)
-    for b in range(blocks):
-        at = slice(b * BLK, (b + 1) * BLK)
-        cur = x_ref[at, :].astype(F32)
-        result = conv(before, cur, taps)
-        before = cur[BLK - HALO :]
-        xc_ref[at, :] = result
-        weighted[at, :] = (result.astype(F32) * dot(w_ref[at, :], e_ref[...])).astype(BF16)
+    for lane in range(0, x_ref.shape[1], LANES):
+        at_lanes = slice(lane, lane + LANES)
+        taps = [ck_ref[k : k + 1, at_lanes] for k in range(4)]
+        before = tail_ref[:, at_lanes].astype(F32)
+        for b in range(blocks):
+            at = slice(b * BLK, (b + 1) * BLK)
+            cur = x_ref[at, at_lanes].astype(F32)
+            result = conv(before, cur, taps)
+            before = cur[BLK - HALO :]
+            xc_ref[at, at_lanes] = result
+            scale = dot(w_ref[at, :], e_ref[:, at_lanes])
+            weighted[at, at_lanes] = (result.astype(F32) * scale).astype(BF16)
     step_width = x_ref.shape[1]
     group = c * step_width * groups // (heads * HEAD_DIM)
     at = pl.ds(pl.multiple_of(c * step_width, step_width), step_width)
@@ -211,32 +215,40 @@
         running = decays[slab : slab + 1] * running + pay_ref[slab, :, :width].astype(F32)
 
 
-def norm_tile(y_ref, bc_ref, g_ref, enter_ref, gate_ref, gain_ref, e_ref, normed_ref, i):
+def norm_tile(
+    y_ref, bc_ref, g_ref, enter_ref, gate_ref, gain_ref, e_ref, normed_ref, carry, grown, i
+):
     width = y_ref.shape[1]
     groups = bc_ref.shape[1] // (2 * STATE)
     gw = width // groups
-    at_rows = pl.ds(pl.multiple_of(i * BLK, BLK), BLK)
+    grown[...] = dot(g_ref[...], e_ref[...])
     for g in range(groups):
         at = slice(g * gw, (g + 1) * gw)
-        c_g = bc_ref[:, (groups + g) * STATE : (groups + g + 1) * STATE]
-        carry = dot(c_g, enter_ref[:, at])
-        y = y_ref[:, at].astype(F32) + dot(g_ref[...], e_ref[:, at]) * carry
-        gated = y * silu(gate_ref[:, at].astype(F32))
-        square_mean = jnp.mean(gated * gated, axis=-1, keepdims=True)
-        scaled = gated * lax.rsqrt(square_mean + epsilon) * gain_ref[:, at]
-        normed_ref[at_rows, at] = scaled.astype(BF16)
+        carry[:, at] = dot(bc_ref[:, (groups + g) * STATE : (groups + g + 1) * STATE], enter_ref[:, at])
+    for r in range(0, BLK, ROWS):
+        rows = slice(r, r + ROWS)
+        out_rows = pl.ds(pl.multiple_of(i * BLK + r, ROWS), ROWS)
+        for g in range(groups):
+            at = slice(g * gw, (g + 1) * gw)
+            y = y_ref[rows, at].astype(F32) + grown[rows, at] * carry[rows, at]
+            gated = y * silu(gate_ref[rows, at].astype(F32))
+            square_mean = jnp.mean(gated * gated, axis=-1, keepdims=True)
+            scaled = gated * lax.rsqrt(square_mean + epsilon) * gain_ref[:, at]
+            normed_ref[out_rows, at] = scaled.astype(BF16)
 
 
 def direct_kernel(
     where_ref, y_ref, bc_ref, g_ref, enter_ref, gate_ref, gain_ref, e_ref, w_ref, after_ref,
     *rest, tiles,
 ):
-    *out_refs, normed_ref = rest
+    *out_refs, normed_ref, carry, grown = rest
     i = pl.program_id(0)
 
     @pl.when(i < tiles)
     def _():
-        norm_tile(y_ref, bc_ref, g_ref, enter_ref, gate_ref, gain_ref, e_ref, normed_ref, i)
+        norm_tile(
+            y_ref, bc_ref, g_ref, enter_ref, gate_ref, gain_ref, e_ref, normed_ref, carry, grown, i
+        )
 
     for k, out_ref in enumerate(out_refs):
         @pl.when(i == tiles + k)
@@ -244,23 +256,17 @@
             out_ref[...] = dot(normed_ref[...], w_ref[...]).astype(BF16)
 
 
-def more_kernel(where_ref, normed_ref, w_ref, *out_refs):
-    i = pl.program_id(0)
-    for k, out_ref in enumerate(out_refs):
-        @pl.when(i == k)
-        def _(out_ref=out_ref):
-            out_ref[...] = dot(normed_ref[...], w_ref[...]).astype(BF16)
-
-
 def line_kernel(
     y_ref, bc_ref, g_ref, enter_ref, gate_ref, gain_ref, e_ref, w_ref, after_ref,
-    shares_ref, up_ref, down_ref, normed_ref, *, tiles,
+    shares_ref, up_ref, down_ref, normed_ref, carry, grown, *, tiles,
 ):
     i = pl.program_id(0)
 
     @pl.when(i < tiles)
     def _():
-        norm_tile(y_ref, bc_ref, g_ref, enter_ref, gate_ref, gain_ref, e_ref, normed_ref, i)
+        norm_tile(
+            y_ref, bc_ref, g_ref, enter_ref, gate_ref, gain_ref, e_ref, normed_ref, carry, grown, i
+        )
 
     @pl.when(i >= tiles)
     def _():
@@ -286,10 +292,14 @@
     out_ref[...] = total.astype(BF16)
 
 
-def direct_final_kernel(*refs):
-    *in_refs, after_ref, out_ref = refs
-    total = in_refs[0][...].astype(F32)
-    for ref in in_refs[1:]:
+def place_kernel(piece_ref, out_before_ref, out_ref):
+    out_ref[...] = piece_ref[...]
+
+
+def direct_final_kernel(where_ref, normed_ref, w_ref, *refs, count):
+    out_ref = refs[-1]
+    total = dot(normed_ref[...], w_ref[...])
+    for ref in refs[:count]:
         total = total + ref[...].astype(F32)
     out_ref[...] = total.astype(BF16)
 
@@ -382,7 +392,7 @@
         pay.reshape(slabs, part, width + LANES), "seq", split_axis=0, concat_axis=0, tiled=True
     )
 
-    def local_part(start, count, state, after):
+    def local_part(start, count, before, after):
         def tile(width):
             return pl.BlockSpec((BLK, width), lambda b: (start + b, 0))
 
@@ -399,31 +409,28 @@
             whole((LANES, width)),
             whole((LANES, width)),
         ]
-        if state is not None:
-            operands.append(state)
-            specs.append(whole((STATE, width)))
+        aliases = {}
+        if before is not None:
+            y, state = before
+            aliases = {len(operands) + 1: 0}
+            operands += [state, y]
+            specs += [whole((STATE, width)), unread()]
         operands.append(after)
         specs.append(unread())
         return pl.pallas_call(
             local_kernel,
             grid=(count,),
             in_specs=specs,
-            out_specs=[
-                pl.BlockSpec((BLK, width), lambda b: (b, 0)),
-                whole((STATE, width)),
-            ],
-            out_shape=[shaped((count * BLK, width)), shaped((STATE, width), F32)],
+            out_specs=[tile(width), whole((STATE, width))],
+            out_shape=[shaped((tokens, width)), shaped((STATE, width), F32)],
+            input_output_aliases=aliases,
             scratch_shapes=[pltpu.VMEM((HALO, width), F32)],
             compiler_params=params(),
             name="local_part",
         )(*operands)
 
-    third = blocks - blocks * 3 // 8
-    spans = [(0, blocks - third), (blocks - third, (third + 1) // 2)]
-    spans.append((spans[1][0] + spans[1][1], third // 2))
-    y_first, state = local_part(*spans[0], None, pay)
-    y_second, state = local_part(*spans[1], state, y_first)
-
+    some = (blocks * 3 + 7) // 8
+    y_first = local_part(0, some, None, pay)
     entering = pl.pallas_call(
         prefix_kernel,
         out_shape=shaped((slabs, part, width)),
@@ -435,7 +442,8 @@
         out_specs=pl.BlockSpec(memory_space=pltpu.VMEM),
         compiler_params=pltpu.CompilerParams(vmem_limit_bytes=SMALL_LIMIT),
         name="prefix",
-    )(arrived, high, y_first)
+    )(arrived, high, y_first[1])
+    y_second = local_part(some, some, y_first, entering)
     entering = lax.all_to_all(entering, "seq", split_axis=0, concat_axis=0, tiled=True)
     entering = entering.reshape(STATE, width)
 
@@ -445,12 +453,12 @@
     where = mine.reshape(1)
 
     def norm_operands(start, count, y):
-        def tile(width, start=start):
+        def tile(width):
             return pl.BlockSpec((BLK, width), lambda i, *_: (start + jnp.minimum(i, count - 1), 0))
 
         operands = [y, bc, g_hl, entering, gate_input, norm_row, high]
         specs = [
-            tile(width, 0),
+            tile(width),
             tile(map_width),
             tile(LANES),
             whole((STATE, width)),
@@ -460,45 +468,59 @@
         ]
         return operands, specs
 
-    def project_direct(start, count, y, after, slots, more_slots):
+    def project_direct(start, count, y, after, slots):
         operands, specs = norm_operands(start, count, y)
         size = count * BLK
 
-        def weights(slots, first):
-            def index(i, where):
-                step = i - first
-                slot = slots[-1]
-                for k in range(len(slots) - 1, -1, -1):
-                    slot = jnp.where(step <= k, slots[k], slot)
-                return (0, lax.rem(where[0] + slot, chans))
-
-            return pl.BlockSpec((width, part_out), index)
-
-        *shares, normed = pl.pallas_call(
+        def weights(i, where):
+            step = i - count
+            slot = slots[-1]
+            for k in range(len(slots) - 1, -1, -1):
+                slot = jnp.where(step <= k, slots[k], slot)
+            return (0, lax.rem(where[0] + slot, chans))
+
+        return pl.pallas_call(
             functools.partial(direct_kernel, tiles=count),
             grid_spec=pltpu.PrefetchScalarGridSpec(
                 num_scalar_prefetch=1,
                 grid=(count + len(slots),),
-                in_specs=specs + [weights(slots, count), unread()],
+                in_specs=specs + [pl.BlockSpec((width, part_out), weights), unread()],
                 out_specs=[whole((size, part_out))] * len(slots) + [whole((size, width))],
+                scratch_shapes=[pltpu.VMEM((BLK, width), F32)] * 2,
             ),
             out_shape=[shaped((size, part_out))] * len(slots) + [shaped((size, width))],
             compiler_params=params(),
             name="project_direct",
         )(where, *operands, out_weight, after)
-        more = pl.pallas_call(
-            more_kernel,
+
+    def direct_final(start, normed, pieces, out, after):
+        def tile(width, start=0):
+            return pl.BlockSpec((BLK, width), lambda i, where: (start + i, 0))
+
+        operands = [where, normed, out_weight] + pieces + [after]
+        specs = [
+            tile(width),
+            pl.BlockSpec((width, part_out), lambda i, where: (0, where[0])),
+        ]
+        specs += [tile(part_out)] * len(pieces) + [unread()]
+        aliases = {}
+        if out is not None:
+            aliases = {len(operands): 0}
+            operands.append(out)
+            specs.append(unread())
+        return pl.pallas_call(
+            functools.partial(direct_final_kernel, count=len(pieces)),
             grid_spec=pltpu.PrefetchScalarGridSpec(
                 num_scalar_prefetch=1,
-                grid=(len(more_slots),),
-                in_specs=[whole((size, width)), weights(more_slots, 0)],
-                out_specs=[whole((size, part_out))] * len(more_slots),
+                grid=(normed.shape[0] // BLK,),
+                in_specs=specs,
+                out_specs=tile(part_out, start),
             ),
-            out_shape=[shaped((size, part_out))] * len(more_slots),
-            compiler_params=params(),
-            name="project_more",
-        )(where, normed, out_weight)
-        return dict(zip(slots + more_slots, shares + list(more)))
+            out_shape=shaped((tokens, part_out)),
+            input_output_aliases=aliases,
+            compiler_params=params(SMALL_LIMIT),
+            name="direct_final",
+        )(*operands)
 
     def project_line(start, count, y, after):
         operands, specs = norm_operands(start, count, y)
@@ -522,7 +544,7 @@
                 shaped((size, part_out)),
                 shaped((size, part_out)),
             ],
-            scratch_shapes=[pltpu.VMEM((size, width), BF16)],
+            scratch_shapes=[pltpu.VMEM((size, width), BF16)] + [pltpu.VMEM((BLK, width), F32)] * 2,
             compiler_params=params(),
             name="project_line",
         )(*operands, out_weight, after)
@@ -590,37 +612,41 @@
             name="final",
         )(*operands)
 
-    order = sorted(range(chans), key=lambda k: (k == 0, -min(k, chans - k), k))
-    slots = project_direct(
-        *spans[0], y_first, y_second, order[: chans // 2], order[chans // 2 :]
-    )
-    pieces = [slots[0]]
-    for k in order[:-1]:
+    quarter = blocks // 4
+    order = sorted(range(1, chans), key=lambda k: (-min(k, chans - k), k))
+    *slots, normed = project_direct(0, quarter, y_second[0], y_second[1], order)
+    pieces = []
+    for k, slot in zip(order, slots):
         turn = [(a, (a + k) % chans) for a in range(chans)]
-        pieces.append(lax.ppermute(slots[k], "chan", turn))
-
-    chunks = [project_line(*spans[1], y_second, slots[0])]
-    y_third, _ = local_part(*spans[2], state, chunks[0][0])
-    chunks.append(project_line(*spans[2], y_third, chunks[0][0]))
+        pieces.append(lax.ppermute(slot, "chan", turn))
+
+    shares, _, _ = project_line(quarter, quarter, y_second[0], normed)
+    scattered = lax.psum_scatter(shares, "chan", scatter_dimension=0, tiled=True)
+
+    starts = (2 * quarter, 3 * quarter)
+    chunks = [project_line(starts[0], quarter, y_second[0], shares)]
+    y_third = local_part(2 * some, blocks - 2 * some, y_second, chunks[0][0])
+    chunks.append(project_line(starts[1], quarter, y_third[0], chunks[0][0]))
     moving = [permuted(up, down, 0) for _, up, down in chunks]
-    out = pl.pallas_call(
-        direct_final_kernel,
-        grid=(spans[0][1],),
-        in_specs=[pl.BlockSpec((BLK, part_out), lambda i: (i, 0))] * chans + [unread()],
-        out_specs=pl.BlockSpec((BLK, part_out), lambda i: (i, 0)),
-        out_shape=shaped((tokens, part_out)),
-        compiler_params=params(SMALL_LIMIT),
-        name="direct_final",
-    )(*pieces, chunks[1][0])
+    out = direct_final(0, normed, pieces, None, chunks[1][0])
     after = out
     for s in range(1, chans - 1):
         for k in range(2):
             up, down = onward(chunks[k][0], *moving[k], s, after)
             after = up
             moving[k] = permuted(up, down, s)
-
+    out = pl.pallas_call(
+        place_kernel,
+        grid=(quarter,),
+        in_specs=[pl.BlockSpec((BLK, part_out), lambda i: (i, 0)), unread()],
+        out_specs=pl.BlockSpec((BLK, part_out), lambda i: (quarter + i, 0)),
+        out_shape=shaped((tokens, part_out)),
+        input_output_aliases={1: 0},
+        compiler_params=params(SMALL_LIMIT),
+        name="place",
+    )(scattered.reshape(quarter * BLK, part_out), out)
     for k in range(2):
-        out = final(spans[k + 1][0], chunks[k][0], *moving[k], out)
+        out = final(starts[k], chunks[k][0], *moving[k], out)
     return out
 
 

time: 144 us -> 168 us (1.17)
  between operations: 0.28 us -> 13.7 us
  starting transfers between devices: 43.6 us -> 48.4 us
  local copies, waits for them, and re-layouts: 6.75 us -> 11 us
  Pallas kernels: 75.5 us -> 79.6 us
    pallas_call x2 -> x3, Pallas kernels: 21.6 us -> 29.6 us  [project_line(): pl.pallas_call(functools.partial(line_kernel, tiles=count), grid=(count +...]
    ppermute x6, waiting for transfers between devices: 7.28 us -> 1.87 us  [permuted(): up = lax.ppermute(up, 'chan', [(a, a + 1) for a in range(s + 1)])]
    unnamed x22 -> x32, local copies, waits for them, and re-layouts: 5.28 us -> 9.48 us
    pallas_call x5, Pallas kernels: 27.1 us -> 23 us  [the longest x3 20.5 us: local_part(): pl.pallas_call(local_kernel, grid=(count,), in_specs=specs, out_specs=[ti...]
    ppermute x3, waiting for transfers between devices: 0.01 us -> 3.08 us  [local(): pieces.append(lax.ppermute(slot, 'chan', turn))]
    ppermute x6, starting transfers between devices: 22.4 us -> 25.4 us  [permuted(): up = lax.ppermute(up, 'chan', [(a, a + 1) for a in range(s + 1)])]
    ppermute x3, starting transfers between devices: 4.64 us -> 6.68 us  [local(): pieces.append(lax.ppermute(slot, 'chan', turn))]
  transfers between devices with their start and end apart: 18 -> 19, of which waited for: 7 -> 6; matrix products, arithmetic and copies ran while one was open for 0% -> 0% of each run, Pallas kernels for 32% -> 27%
where the time goes in v5:
time: 168 us; the launch traced here: 167 us
  Pallas kernels  79.6 us (47%)
  starting transfers between devices  48.4 us (29%)
  waiting for transfers between devices  14.2 us (8%)
  between operations  13.7 us (8%)
  local copies, waits for them, and re-layouts  11 us (7%)
    pallas_call x3, Pallas kernels, project_line(): pl.pallas_call(functools.partial(line_kernel, tiles=count), grid=(count +...  29.6 us
    ppermute x6, starting transfers between devices, permuted(): up = lax.ppermute(up, 'chan', [(a, a + 1) for a in range(s + 1)])  25.4 us
    pallas_call x3, Pallas kernels, local_part(): pl.pallas_call(local_kernel, grid=(count,), in_specs=specs, out_specs=[ti...  20.5 us
    pallas_call x1, Pallas kernels, local(): pl.pallas_call(states_kernel, grid=(width // WIDE,), in_specs=[lanes_at(t...  13.7 us
    unnamed x32, local copies, waits for them, and re-layouts  9.48 us
    pallas_call x1, Pallas kernels, project_direct(): pl.pallas_call(functools.partial(direct_kernel, tiles=count), grid_spec=p...  8.55 us
    ppermute x3, starting transfers between devices, local(): pieces.append(lax.ppermute(slot, 'chan', turn))  6.68 us
    ppermute x6, starting transfers between devices, permuted(): lax.ppermute(down, 'chan', [(a, a - 1) for a in range(chans - 1 - s, chan...  5.28 us
  transfers between devices with their start and end apart: 19, of which 6 were waited for; matrix products, arithmetic and copies ran while one was open for 0% of the time, Pallas kernels for 27%

profile of v5, /device:TPU:2, one launch (start us, length us, event | category | flops | bytes accessed | tf_op | source)
XLA Modules:
  0.0 166.7 jit_solution(1299377381321944427)
XLA Ops:
  6.5 0.7 slice.7
  7.3 0.8 slice.6
  8.0 1.9 %collective-permute-start = (bf16[8,2560]{1,0:T(8,128)(2,1)S(1)}, bf16[8,2560]{1,0:T(8,128)(2,1)S(1)}, u32[]{:S(2)}, u32[]{:S(2)}) collective-permute-start(bf16[8,2560]{1,0:T(8,128)(2,1)S(1)} %pad_maximum_fusion), channel_id=1, source_target_pairs={{0,4},{4,8},{8,12},{12,16},{16,20},{20,24},{24,28},{1,5},{5,9},{9,... | collective-permute-start | bytes 122888 | tf_op jit(solution)/shard_map/ppermute | solution.py:341
  9.9 3.4 %collective-permute-done.tail_ref.mtail_ref = bf16[8,2560]{1,0:T(8,128)(2,1)S(1)} collective-permute-done((bf16[8,2560]{1,0:T(8,128)(2,1)S(1)}, bf16[8,2560]{1,0:T(8,128)(2,1)S(1)}, u32[]{:S(2)}, u32[]{:S(2)}) %collective-permute-start) | collective-permute-done | bytes 40992 | tf_op jit(solution)/shard_map/ppermute | solution.py:341
  13.3 0.6 copy-done.10
  13.9 13.7 %states.1 = (bf16[1024,2048]{1,0:T(8,128)(2,1)}, bf16[1024,512]{1,0:T(8,128)(2,1)}, bf16[2,128,1024]{2,1,0:T(8,128)(2,1)}, f32[32,1024]{1,0:T(8,128)}, f32[1024,...) custom-call(bf16[1024,2048]{1,0:T(8,128)(2,1)} %x_ref.1, ...), custom_call_target="tpu_custom_call" | custom-call | tf_op jit(solution)/shard_map/states/pallas_call | solution.py:346
  27.7 4.3 %all-to-all-start = ((bf16[8,16,2176]{2,1,0:T(8,128)(2,1)}), bf16[8,16,2176]{2,1,0:T(8,128)(2,1)S(1)}, u32[]{:S(2)}, u32[]{:S(2)}) async-start(bf16[8,16,2176]{2,1,0:T(8,128)(2,1)} %bitcast.16), calls=%async_computation | async-start | bytes 1114112 | tf_op jit(solution)/shard_map/all_to_all | solution.py:391
  31.9 7.0 %local_part.3 = (bf16[1024,2048]{1,0:T(8,128)(2,1)}, f32[128,2048]{1,0:T(8,128)}) custom-call(bf16[1024,2048]{1,0:T(8,128)(2,1)} %get-tuple-element.37.xc_ref, bf16[1024,512]{1,0:T(8,128)(2,1)} %get-tuple-element.38.bc_ref, bf16[2,128,1024]{2,1,0:T(8,128)(2,1)} %get-tuple-element.39.bt_ref, f32[32,1024]{1,0:T(8,128)} %get-tuple-element.40.crow_ref, ...), custom_call_target="tpu_custom_call" | custom-call | tf_op jit(solution)/shard_map/local_part/pallas_call | solution.py:420
  39.0 1.6 all-to-all-done.pay_ref
  40.6 1.2 copy-done.7
  41.8 1.1 prefix.1.rest_2_
  42.9 4.9 %all-to-all-start.1 = ((bf16[8,16,2048]{2,1,0:T(8,128)(2,1)}), bf16[8,16,2048]{2,1,0:T(8,128)(2,1)S(1)}, u32[]{:S(2)}, u32[]{:S(2)}) async-start(bf16[8,16,2048]{2,1,0:T(8,128)(2,1)} %prefix.1.rest_2_), calls=%async_computation.1 | async-start | bytes 1048576 | tf_op jit(solution)/shard_map/all_to_all | solution.py:447
  47.8 7.4 %local_part.4 = (bf16[1024,2048]{1,0:T(8,128)(2,1)}, f32[128,2048]{1,0:T(8,128)}) custom-call(bf16[1024,2048]{1,0:T(8,128)(2,1)} %get-tuple-element.37.xc_ref, bf16[1024,512]{1,0:T(8,128)(2,1)} %get-tuple-element.38.bc_ref, bf16[2,128,1024]{2,1,0:T(8,128)(2,1)} %get-tuple-element.39.bt_ref, ...), custom_call_target="tpu_custom_call", output_to_operand_aliasing={{0}: (11, {})} | custom-call | tf_op jit(solution)/shard_map/local_part/pallas_call | solution.py:420
  55.1 0.9 all-to-all-done.1
  56.1 0.8 copy-done.9
  56.9 8.5 %project_direct.1 = (bf16[256,512]{1,0:T(8,128)(2,1)}, bf16[256,512]{1,0:T(8,128)(2,1)}, bf16[256,512]{1,0:T(8,128)(2,1)}, bf16[256,2048]{1,0:T(8,128)(2,1)}) custom-call(s32[1]{0:T(128)} %bitcast.where_ref, bf16[1024,2048]{1,0:T(8,128)(2,1)} %get-tuple-element.48.y_ref.rest_1_, bf16[1024,512]{1,0:T(8,128)(2,1)} %get-tuple-element.38.bc_ref, ...), custom_call_target="tpu_custom_call" | custom-call | tf_op jit(solution)/shard_map/project_direct/pallas_call | solution.py:482
  65.4 9.9 %project_line.3 = (bf16[4,256,512]{2,1,0:T(8,128)(2,1)}, bf16[256,512]{1,0:T(8,128)(2,1)}, bf16[256,512]{1,0:T(8,128)(2,1)}) custom-call(bf16[1024,2048]{1,0:T(8,128)(2,1)} %get-tuple-element.48.y_ref.rest_1_, bf16[1024,512]{1,0:T(8,128)(2,1)} %get-tuple-element.38.bc_ref, bf16[1024,128]{1,0:T(8,128)(2,1)} %get-tuple-element.43.g_ref, ...), custom_call_target="tpu_custom_call" | custom-call | tf_op jit(solution)/shard_map/project_line/pallas_call | solution.py:532
  75.3 0.0 reduce-scatter.2.cloned.1.call-update
  75.4 2.6 %collective-permute-start.5 = (bf16[256,512]{1,0:T(8,128)(2,1)S(1)}, bf16[256,512]{1,0:T(8,128)(2,1)S(1)}, u32[]{:S(2)}, u32[]{:S(2)}) collective-permute-start(bf16[256,512]{1,0:T(8,128)(2,1)S(1)} %copy-done.14), channel_id=1, source_target_pairs={{0,2},{1,3},{2,0},{3,1},{4,6},{5,7},{6,4},{7,5},{8,10},{9,11},{10,... | collective-permute-start | bytes 786440 | tf_op jit(solution)/shard_map/ppermute | solution.py:621
  78.0 1.6 collective-permute-start.6
  79.6 9.8 %project_line.4 = (bf16[4,256,512]{2,1,0:T(8,128)(2,1)}, bf16[256,512]{1,0:T(8,128)(2,1)}, bf16[256,512]{1,0:T(8,128)(2,1)}) custom-call(bf16[1024,2048]{1,0:T(8,128)(2,1)} %get-tuple-element.48.y_ref.rest_1_, bf16[1024,512]{1,0:T(8,128)(2,1)} %get-tuple-element.38.bc_ref, bf16[1024,128]{1,0:T(8,128)(2,1)} %get-tuple-element.43.g_ref, ...), custom_call_target="tpu_custom_call" | custom-call | tf_op jit(solution)/shard_map/project_line/pallas_call | solution.py:532
  89.4 2.5 %collective-permute-start.7 = (bf16[256,512]{1,0:T(8,128)(2,1)S(1)}, bf16[256,512]{1,0:T(8,128)(2,1)S(1)}, u32[]{:S(2)}, u32[]{:S(2)}) collective-permute-start(bf16[256,512]{1,0:T(8,128)(2,1)S(1)} %copy-done.11), channel_id=1, source_target_pairs={{0,3},{1,0},{2,1},{3,2},{4,7},{5,4},{6,5},{7,6},{8,11},{9,8},{10,9... | collective-permute-start | bytes 786440 | tf_op jit(solution)/shard_map/ppermute | solution.py:621
  91.9 6.1 %local_part.5 = (bf16[1024,2048]{1,0:T(8,128)(2,1)}, f32[128,2048]{1,0:T(8,128)}) custom-call(bf16[1024,2048]{1,0:T(8,128)(2,1)} %get-tuple-element.37.xc_ref, bf16[1024,512]{1,0:T(8,128)(2,1)} %get-tuple-element.38.bc_ref, bf16[2,128,1024]{2,1,0:T(8,128)(2,1)} %get-tuple-element.39.bt_ref, ...), custom_call_target="tpu_custom_call", output_to_operand_aliasing={{0}: (11, {})} | custom-call | tf_op jit(solution)/shard_map/local_part/pallas_call | solution.py:420
  98.0 1.7 %collective-permute-start.3 = (bf16[256,512]{1,0:T(8,128)(2,1)S(1)}, bf16[256,512]{1,0:T(8,128)(2,1)S(1)}, u32[]{:S(2)}, u32[]{:S(2)}) collective-permute-start(bf16[256,512]{1,0:T(8,128)(2,1)S(1)} %copy-done.15), channel_id=1, source_target_pairs={{0,1},{4,5},{8,9},{12,13},{16,17},{20,21},{24,25},{28,29}} | collective-permute-start | bytes 786440 | tf_op jit(solution)/shard_map/ppermute | solution.py:553
  99.7 0.7 collective-permute-start.4
  100.4 9.9 %project_line.5 = (bf16[4,256,512]{2,1,0:T(8,128)(2,1)}, bf16[256,512]{1,0:T(8,128)(2,1)}, bf16[256,512]{1,0:T(8,128)(2,1)}) custom-call(bf16[1024,2048]{1,0:T(8,128)(2,1)} %get-tuple-element.52.y_ref, bf16[1024,512]{1,0:T(8,128)(2,1)} %get-tuple-element.38.bc_ref, bf16[1024,128]{1,0:T(8,128)(2,1)} %get-tuple-element.43.g_ref, bf16[128,2048]{1,0:T(8,128)(2,1)} %bitcast.15, ...), custom_call_target="tpu_custom_call" | custom-call | tf_op jit(solution)/shard_map/project_line/pallas_call | solution.py:532
  110.3 0.0 collective-permute-done.5.refs_0_
  110.3 1.3 collective-permute-start.1
  111.6 0.0 collective-permute-done.6.refs_1_
  111.6 0.7 collective-permute-start.2
  112.3 3.1 %collective-permute-done.7.refs_2_ = bf16[256,512]{1,0:T(8,128)(2,1)S(1)} collective-permute-done((bf16[256,512]{1,0:T(8,128)(2,1)S(1)}, bf16[256,512]{1,0:T(8,128)(2,1)S(1)}, u32[]{:S(2)}, u32[]{:S(2)}) %collective-permute-start.7) | collective-permute-done | bytes 262176 | tf_op jit(solution)/shard_map/ppermute | solution.py:621
  115.4 3.4 %copy-done = bf16[2048,2048]{1,0:T(8,128)(2,1)S(1)} copy-done((bf16[2048,2048]{1,0:T(8,128)(2,1)S(1)}, bf16[2048,2048]{1,0:T(8,128)(2,1)}, u32[]{:S(2)}) %copy-start) | copy-done | bytes 8388632
  118.8 1.2 copy-done.2
  120.1 1.8 %direct_final.1.after_ref.out_before_ref = bf16[1024,512]{1,0:T(8,128)(2,1)} custom-call(s32[1]{0:T(128)} %bitcast.where_ref, bf16[256,2048]{1,0:T(8,128)(2,1)S(1)} %copy-done.6, bf16[2048,2048]{1,0:T(8,128)(2,1)S(1)} %copy-done, bf16[256,512]{1,0:T(8,128)(2,1)S(1)} %collective-permute-done.5.refs_0_, bf16[256,512]{1,0:T(8,128)(2,1)S(1)} %collective-permute-done.6.refs_1_, ...), custom_call_target="tpu_custom_call" | custom-call | tf_op jit(solution)/shard_map/direct_final/pallas_call | solution.py:511
  121.8 0.0 collective-permute-done.3.up_ref
  121.8 0.0 collective-permute-done.4.down_ref
  121.8 0.0 copy-start.5
  121.9 1.2 copy-done.5
  123.1 0.1 onward.4
  123.2 0.7 collective-permute-start.11
  123.9 6.7 %collective-permute-start.10 = (bf16[256,512]{1,0:T(8,128)(2,1)S(1)}, bf16[256,512]{1,0:T(8,128)(2,1)S(1)}, u32[]{:S(2)}, u32[]{:S(2)}) collective-permute-start(bf16[256,512]{1,0:T(8,128)(2,1)S(1)} %get-tuple-element.61.after_ref), channel_id=1, source_target_pairs={{0,1},{1,2},{4,5},{5,6},{8,9},{9,10},{12,13},{13,14},{16,17},{17,1... | collective-permute-start | bytes 786440 | tf_op jit(solution)/shard_map/ppermute | solution.py:553
  130.7 0.0 collective-permute-done.1.up_ref
  130.7 0.0 collective-permute-done.2.down_ref
  130.7 0.2 onward.5
  130.9 0.7 collective-permute-start.9
  131.6 6.3 %collective-permute-start.8 = (bf16[256,512]{1,0:T(8,128)(2,1)S(1)}, bf16[256,512]{1,0:T(8,128)(2,1)S(1)}, u32[]{:S(2)}, u32[]{:S(2)}) collective-permute-start(bf16[256,512]{1,0:T(8,128)(2,1)S(1)} %get-tuple-element.62.after_ref), channel_id=1, source_target_pairs={{0,1},{1,2},{4,5},{5,6},{8,9},{9,10},{12,13},{13,14},{16,17},{17,1... | collective-permute-start | bytes 786440 | tf_op jit(solution)/shard_map/ppermute | solution.py:553
  137.8 0.0 collective-permute-done.11.down_ref
  137.8 0.0 collective-permute-done.10.up_ref
  137.8 0.8 onward.6
  138.6 1.3 collective-permute-start.15
  139.9 5.3 %collective-permute-start.14 = (bf16[256,512]{1,0:T(8,128)(2,1)S(1)}, bf16[256,512]{1,0:T(8,128)(2,1)S(1)}, u32[]{:S(2)}, u32[]{:S(2)}) collective-permute-start(bf16[256,512]{1,0:T(8,128)(2,1)S(1)} %get-tuple-element.65.after_ref), channel_id=1, source_target_pairs={{0,1},{1,2},{2,3},{4,5},{5,6},{6,7},{8,9},{9,10},{10,11},{12,13},{... | collective-permute-start | bytes 786440 | tf_op jit(solution)/shard_map/ppermute | solution.py:553
  145.3 0.0 collective-permute-done.9.down_ref
  145.3 0.0 collective-permute-done.8.up_ref
  145.3 0.9 onward.7
  146.2 4.0 %collective-permute-start.12 = (bf16[256,512]{1,0:T(8,128)(2,1)}, bf16[256,512]{1,0:T(8,128)(2,1)S(1)}, u32[]{:S(2)}, u32[]{:S(2)}) collective-permute-start(bf16[256,512]{1,0:T(8,128)(2,1)} %get-tuple-element.66), channel_id=1, source_target_pairs={{0,1},{1,2},{2,3},{4,5},{5,6},{6,7},{8,9},{9,10},{10,11},{12,13},{... | collective-permute-start | bytes 786440 | tf_op jit(solution)/shard_map/ppermute | solution.py:553
  150.2 1.3 collective-permute-start.13
  151.5 0.0 reduce-scatter.2.cloned.1.call-done
  151.6 0.9 copy-done.8
  152.5 0.7 place.1.rest_0_
  153.2 0.0 collective-permute-done.15.down_ref
  153.2 0.8 final.2.rest_0_
  154.0 1.9 %collective-permute-done.12.up_ref = bf16[256,512]{1,0:T(8,128)(2,1)S(1)} collective-permute-done((bf16[256,512]{1,0:T(8,128)(2,1)}, bf16[256,512]{1,0:T(8,128)(2,1)S(1)}, u32[]{:S(2)}, u32[]{:S(2)}) %collective-permute-start.12) | collective-permute-done | bytes 262176 | tf_op jit(solution)/shard_map/ppermute | solution.py:553
  155.9 3.2 %collective-permute-done.13.down_ref = bf16[256,512]{1,0:T(8,128)(2,1)S(1)} collective-permute-done((bf16[256,512]{1,0:T(8,128)(2,1)}, bf16[256,512]{1,0:T(8,128)(2,1)S(1)}, u32[]{:S(2)}, u32[]{:S(2)}) %collective-permute-start.13) | collective-permute-done | bytes 262176 | tf_op jit(solution)/shard_map/ppermute | solution.py:554
  159.1 0.8 final.3
  (28 shorter events, 0.1 us)
Async XLA Ops:
  8.0 5.3 %collective-permute-start = (bf16[8,2560]{1,0:T(8,128)(2,1)S(1)}, bf16[8,2560]{1,0:T(8,128)(2,1)S(1)}, u32[]{:S(2)}, u32[]{:S(2)}) collective-permute-start(bf16[8,2560]{1,0:T(8,128)(2,1)S(1)} %pad_maximum_fusion), channel_id=1, source_target_pairs={{0,4},{4,8},{8,12},{12,16},{16,20},{20,24},{24,28},{1,5},{5,9},{9,... | collective-permute-start | bytes 122888 | tf_op jit(solution)/shard_map/ppermute | solution.py:341
  13.3 0.6 copy-start.10
  27.7 12.9 %all-to-all-start = ((bf16[8,16,2176]{2,1,0:T(8,128)(2,1)}), bf16[8,16,2176]{2,1,0:T(8,128)(2,1)S(1)}, u32[]{:S(2)}, u32[]{:S(2)}) async-start(bf16[8,16,2176]{2,1,0:T(8,128)(2,1)} %bitcast.16), calls=%async_computation | async-start | bytes 1114112 | tf_op jit(solution)/shard_map/all_to_all | solution.py:391
  31.9 8.6 %copy-start.4 = (bf16[128,2048]{1,0:T(8,128)(2,1)S(1)}, bf16[128,2048]{1,0:T(8,128)(2,1)}, u32[]{:S(2)}) copy-start(bf16[128,2048]{1,0:T(8,128)(2,1)} %constant.9.clone.high_ref.e_ref) | copy-start | bytes 1572868
  40.6 1.2 copy-start.7
  42.9 13.2 %all-to-all-start.1 = ((bf16[8,16,2048]{2,1,0:T(8,128)(2,1)}), bf16[8,16,2048]{2,1,0:T(8,128)(2,1)S(1)}, u32[]{:S(2)}, u32[]{:S(2)}) async-start(bf16[8,16,2048]{2,1,0:T(8,128)(2,1)} %prefix.1.rest_2_), calls=%async_computation.1 | async-start | bytes 1048576 | tf_op jit(solution)/shard_map/all_to_all | solution.py:447
  47.7 103.8 %reduce-scatter.2.cloned.1.call-start = ((), (), s32[]{:S(2)}) async-start(), calls=%async_computation.3 | async-start | bytes 1310720 | tf_op jit(solution)/shard_map/reduce_scatter | solution.py:624
  56.0 0.8 copy-start.9
  65.4 9.9 %copy-start.14 = (bf16[256,512]{1,0:T(8,128)(2,1)S(1)}, bf16[256,512]{1,0:T(8,128)(2,1)}, u32[]{:S(2)}) copy-start(bf16[256,512]{1,0:T(8,128)(2,1)} %get-tuple-element.58) | copy-start | bytes 786436
  65.4 12.6 %copy-start.12 = (bf16[256,512]{1,0:T(8,128)(2,1)S(1)}, bf16[256,512]{1,0:T(8,128)(2,1)}, u32[]{:S(2)}) copy-start(bf16[256,512]{1,0:T(8,128)(2,1)} %get-tuple-element.59) | copy-start | bytes 786436
  75.4 35.0 %collective-permute-start.5 = (bf16[256,512]{1,0:T(8,128)(2,1)S(1)}, bf16[256,512]{1,0:T(8,128)(2,1)S(1)}, u32[]{:S(2)}, u32[]{:S(2)}) collective-permute-start(bf16[256,512]{1,0:T(8,128)(2,1)S(1)} %copy-done.14), channel_id=1, source_target_pairs={{0,2},{1,3},{2,0},{3,1},{4,6},{5,7},{6,4},{7,5},{8,10},{9,11},{10,... | collective-permute-start | bytes 786440 | tf_op jit(solution)/shard_map/ppermute | solution.py:621
  78.0 11.4 %copy-start.11 = (bf16[256,512]{1,0:T(8,128)(2,1)S(1)}, bf16[256,512]{1,0:T(8,128)(2,1)}, u32[]{:S(2)}) copy-start(bf16[256,512]{1,0:T(8,128)(2,1)} %get-tuple-element.60) | copy-start | bytes 786436
  78.0 33.6 %collective-permute-start.6 = (bf16[256,512]{1,0:T(8,128)(2,1)S(1)}, bf16[256,512]{1,0:T(8,128)(2,1)S(1)}, u32[]{:S(2)}, u32[]{:S(2)}) collective-permute-start(bf16[256,512]{1,0:T(8,128)(2,1)S(1)} %copy-done.12), channel_id=1, source_target_pairs={{0,1},{1,2},{2,3},{3,0},{4,5},{5,6},{6,7},{7,4},{8,9},{9,10},{10,1... | collective-permute-start | bytes 786440 | tf_op jit(solution)/shard_map/ppermute | solution.py:621
  89.4 26.0 %collective-permute-start.7 = (bf16[256,512]{1,0:T(8,128)(2,1)S(1)}, bf16[256,512]{1,0:T(8,128)(2,1)S(1)}, u32[]{:S(2)}, u32[]{:S(2)}) collective-permute-start(bf16[256,512]{1,0:T(8,128)(2,1)S(1)} %copy-done.11), channel_id=1, source_target_pairs={{0,3},{1,0},{2,1},{3,2},{4,7},{5,4},{6,5},{7,6},{8,11},{9,8},{10,9... | collective-permute-start | bytes 786440 | tf_op jit(solution)/shard_map/ppermute | solution.py:621
  91.9 6.1 %copy-start.15 = (bf16[256,512]{1,0:T(8,128)(2,1)S(1)}, bf16[256,512]{1,0:T(8,128)(2,1)}, u32[]{:S(2)}) copy-start(bf16[256,512]{1,0:T(8,128)(2,1)} %get-tuple-element.56) | copy-start | bytes 786436
  91.9 7.8 %copy-start.13 = (bf16[256,512]{1,0:T(8,128)(2,1)S(1)}, bf16[256,512]{1,0:T(8,128)(2,1)}, u32[]{:S(2)}) copy-start(bf16[256,512]{1,0:T(8,128)(2,1)} %get-tuple-element.57) | copy-start | bytes 786436
  98.0 23.9 %collective-permute-start.3 = (bf16[256,512]{1,0:T(8,128)(2,1)S(1)}, bf16[256,512]{1,0:T(8,128)(2,1)S(1)}, u32[]{:S(2)}, u32[]{:S(2)}) collective-permute-start(bf16[256,512]{1,0:T(8,128)(2,1)S(1)} %copy-done.15), channel_id=1, source_target_pairs={{0,1},{4,5},{8,9},{12,13},{16,17},{20,21},{24,25},{28,29}} | collective-permute-start | bytes 786440 | tf_op jit(solution)/shard_map/ppermute | solution.py:553
  99.7 22.1 %collective-permute-start.4 = (bf16[256,512]{1,0:T(8,128)(2,1)S(1)}, bf16[256,512]{1,0:T(8,128)(2,1)S(1)}, u32[]{:S(2)}, u32[]{:S(2)}) collective-permute-start(bf16[256,512]{1,0:T(8,128)(2,1)S(1)} %copy-done.13), channel_id=1, source_target_pairs={{3,2},{7,6},{11,10},{15,14},{19,18},{23,22},{27,26},{31,30}} | collective-permute-start | bytes 786440 | tf_op jit(solution)/shard_map/ppermute | solution.py:554
  100.4 15.0 %copy-start.6 = (bf16[256,2048]{1,0:T(8,128)(2,1)S(1)}, bf16[256,2048]{1,0:T(8,128)(2,1)}, u32[]{:S(2)}) copy-start(bf16[256,2048]{1,0:T(8,128)(2,1)} %get-tuple-element.49.after_ref.normed_ref) | copy-start | bytes 3145732
  110.3 20.3 %collective-permute-start.1 = (bf16[256,512]{1,0:T(8,128)(2,1)}, bf16[256,512]{1,0:T(8,128)(2,1)S(1)}, u32[]{:S(2)}, u32[]{:S(2)}) collective-permute-start(bf16[256,512]{1,0:T(8,128)(2,1)} %get-tuple-element.54), channel_id=1, source_target_pairs={{0,1},{4,5},{8,9},{12,13},{16,17},{20,21},{24,25},{28,29}} | collective-permute-start | bytes 786440 | tf_op jit(solution)/shard_map/ppermute | solution.py:553
  111.6 19.0 %collective-permute-start.2 = (bf16[256,512]{1,0:T(8,128)(2,1)}, bf16[256,512]{1,0:T(8,128)(2,1)S(1)}, u32[]{:S(2)}, u32[]{:S(2)}) collective-permute-start(bf16[256,512]{1,0:T(8,128)(2,1)} %get-tuple-element.55), channel_id=1, source_target_pairs={{3,2},{7,6},{11,10},{15,14},{19,18},{23,22},{27,26},{31,30}} | collective-permute-start | bytes 786440 | tf_op jit(solution)/shard_map/ppermute | solution.py:554
  115.4 3.4 %copy-start = (bf16[2048,2048]{1,0:T(8,128)(2,1)S(1)}, bf16[2048,2048]{1,0:T(8,128)(2,1)}, u32[]{:S(2)}) copy-start(bf16[2048,2048]{1,0:T(8,128)(2,1)} %w_ref.9) | copy-start | bytes 25165828
  118.8 1.2 copy-start.2
  120.0 1.8 %copy-start.1 = (bf16[4,256,512]{2,1,0:T(8,128)(2,1)S(1)}, bf16[4,256,512]{2,1,0:T(8,128)(2,1)}, u32[]{:S(2)}) copy-start(bf16[4,256,512]{2,1,0:T(8,128)(2,1)} %get-tuple-element.51.rest_2_.after_ref.up_own_ref.down_own_ref.own_ref) | copy-start | bytes 3145732
  121.8 1.2 copy-start.5
  123.2 14.6 %collective-permute-start.11 = (bf16[256,512]{1,0:T(8,128)(2,1)S(1)}, bf16[256,512]{1,0:T(8,128)(2,1)S(1)}, u32[]{:S(2)}, u32[]{:S(2)}) collective-permute-start(bf16[256,512]{1,0:T(8,128)(2,1)S(1)} %get-tuple-element.64), channel_id=1, source_target_pairs={{2,1},{3,2},{6,5},{7,6},{10,9},{11,10},{14,13},{15,14},{18,17},{19... | collective-permute-start | bytes 786440 | tf_op jit(solution)/shard_map/ppermute | solution.py:554
  123.9 13.9 %collective-permute-start.10 = (bf16[256,512]{1,0:T(8,128)(2,1)S(1)}, bf16[256,512]{1,0:T(8,128)(2,1)S(1)}, u32[]{:S(2)}, u32[]{:S(2)}) collective-permute-start(bf16[256,512]{1,0:T(8,128)(2,1)S(1)} %get-tuple-element.61.after_ref), channel_id=1, source_target_pairs={{0,1},{1,2},{4,5},{5,6},{8,9},{9,10},{12,13},{13,14},{16,17},{17,1... | collective-permute-start | bytes 786440 | tf_op jit(solution)/shard_map/ppermute | solution.py:553
  130.9 14.4 %collective-permute-start.9 = (bf16[256,512]{1,0:T(8,128)(2,1)S(1)}, bf16[256,512]{1,0:T(8,128)(2,1)S(1)}, u32[]{:S(2)}, u32[]{:S(2)}) collective-permute-start(bf16[256,512]{1,0:T(8,128)(2,1)S(1)} %get-tuple-element.63), channel_id=1, source_target_pairs={{2,1},{3,2},{6,5},{7,6},{10,9},{11,10},{14,13},{15,14},{18,17},{19... | collective-permute-start | bytes 786440 | tf_op jit(solution)/shard_map/ppermute | solution.py:554
  131.6 13.7 %collective-permute-start.8 = (bf16[256,512]{1,0:T(8,128)(2,1)S(1)}, bf16[256,512]{1,0:T(8,128)(2,1)S(1)}, u32[]{:S(2)}, u32[]{:S(2)}) collective-permute-start(bf16[256,512]{1,0:T(8,128)(2,1)S(1)} %get-tuple-element.62.after_ref), channel_id=1, source_target_pairs={{0,1},{1,2},{4,5},{5,6},{8,9},{9,10},{12,13},{13,14},{16,17},{17,1... | collective-permute-start | bytes 786440 | tf_op jit(solution)/shard_map/ppermute | solution.py:553
  138.6 14.6 %collective-permute-start.15 = (bf16[256,512]{1,0:T(8,128)(2,1)}, bf16[256,512]{1,0:T(8,128)(2,1)S(1)}, u32[]{:S(2)}, u32[]{:S(2)}) collective-permute-start(bf16[256,512]{1,0:T(8,128)(2,1)} %get-tuple-element.68), channel_id=1, source_target_pairs={{1,0},{2,1},{3,2},{5,4},{6,5},{7,6},{9,8},{10,9},{11,10},{13,12},{... | collective-permute-start | bytes 786440 | tf_op jit(solution)/shard_map/ppermute | solution.py:554
  139.9 19.2 %copy-start.3 = (bf16[4,256,512]{2,1,0:T(8,128)(2,1)S(1)}, bf16[4,256,512]{2,1,0:T(8,128)(2,1)}, u32[]{:S(2)}) copy-start(bf16[4,256,512]{2,1,0:T(8,128)(2,1)} %get-tuple-element.53.refs_3_.up_own_ref.down_own_ref.own_ref) | copy-start | bytes 3145732
  139.9 13.3 %collective-permute-start.14 = (bf16[256,512]{1,0:T(8,128)(2,1)S(1)}, bf16[256,512]{1,0:T(8,128)(2,1)S(1)}, u32[]{:S(2)}, u32[]{:S(2)}) collective-permute-start(bf16[256,512]{1,0:T(8,128)(2,1)S(1)} %get-tuple-element.65.after_ref), channel_id=1, source_target_pairs={{0,1},{1,2},{2,3},{4,5},{5,6},{6,7},{8,9},{9,10},{10,11},{12,13},{... | collective-permute-start | bytes 786440 | tf_op jit(solution)/shard_map/ppermute | solution.py:553
  146.2 9.7 %collective-permute-start.12 = (bf16[256,512]{1,0:T(8,128)(2,1)}, bf16[256,512]{1,0:T(8,128)(2,1)S(1)}, u32[]{:S(2)}, u32[]{:S(2)}) collective-permute-start(bf16[256,512]{1,0:T(8,128)(2,1)} %get-tuple-element.66), channel_id=1, source_target_pairs={{0,1},{1,2},{2,3},{4,5},{5,6},{6,7},{8,9},{9,10},{10,11},{12,13},{... | collective-permute-start | bytes 786440 | tf_op jit(solution)/shard_map/ppermute | solution.py:553
  150.2 8.9 %collective-permute-start.13 = (bf16[256,512]{1,0:T(8,128)(2,1)}, bf16[256,512]{1,0:T(8,128)(2,1)S(1)}, u32[]{:S(2)}, u32[]{:S(2)}) collective-permute-start(bf16[256,512]{1,0:T(8,128)(2,1)} %get-tuple-element.67), channel_id=1, source_target_pairs={{1,0},{2,1},{3,2},{5,4},{6,5},{7,6},{9,8},{10,9},{11,10},{13,12},{... | collective-permute-start | bytes 786440 | tf_op jit(solution)/shard_map/ppermute | solution.py:554
  151.5 1.0 copy-start.8
Sparse Core Ops, SparseCore 0:
  75.5 43.3 reduce-scatter.1

commit v6 on v5

--- a/solution.py
+++ b/solution.py
@@ -258,7 +258,7 @@
 
 def line_kernel(
     y_ref, bc_ref, g_ref, enter_ref, gate_ref, gain_ref, e_ref, w_ref, after_ref,
-    shares_ref, up_ref, down_ref, normed_ref, carry, grown, *, tiles,
+    shares_ref, up_a_ref, up_b_ref, down_a_ref, down_b_ref, normed_ref, carry, grown, *, tiles,
 ):
     i = pl.program_id(0)
 
@@ -272,13 +272,17 @@
     def _():
         shares_ref[0] = dot(normed_ref[...], w_ref[...]).astype(BF16)
 
+    size = up_a_ref.shape[0]
+
     @pl.when(i == tiles)
     def _():
-        down_ref[...] = shares_ref[0]
+        down_a_ref[...] = shares_ref[0, :size]
+        down_b_ref[...] = shares_ref[0, size:]
 
     @pl.when(i == pl.num_programs(0) - 1)
     def _():
-        up_ref[...] = shares_ref[0]
+        up_a_ref[...] = shares_ref[0, :size]
+        up_b_ref[...] = shares_ref[0, size:]
 
 
 def onward_kernel(where_ref, up_own_ref, down_own_ref, up_ref, down_ref, after_ref, up_out, down_out):
@@ -290,10 +294,6 @@
     out_ref = rest[-1]
     total = own_ref[0].astype(F32) + up_ref[...].astype(F32) + down_ref[...].astype(F32)
     out_ref[...] = total.astype(BF16)
-
-
-def place_kernel(piece_ref, out_before_ref, out_ref):
-    out_ref[...] = piece_ref[...]
 
 
 def direct_final_kernel(where_ref, normed_ref, w_ref, *refs, count):
@@ -302,6 +302,14 @@
     for ref in refs[:count]:
         total = total + ref[...].astype(F32)
     out_ref[...] = total.astype(BF16)
+
+
+def in_hbm(x):
+    return pltpu.with_memory_space_constraint(x, pltpu.HBM)
+
+
+def brief():
+    return pl.CostEstimate(flops=1, transcendentals=0, bytes_accessed=1)
 
 
 def params(limit=VMEM_LIMIT):
@@ -426,10 +434,11 @@
             input_output_aliases=aliases,
             scratch_shapes=[pltpu.VMEM((HALO, width), F32)],
             compiler_params=params(),
+            cost_estimate=brief(),
             name="local_part",
         )(*operands)
 
-    some = (blocks * 3 + 7) // 8
+    some = blocks // 4
     y_first = local_part(0, some, None, pay)
     entering = pl.pallas_call(
         prefix_kernel,
@@ -497,7 +506,7 @@
         def tile(width, start=0):
             return pl.BlockSpec((BLK, width), lambda i, where: (start + i, 0))
 
-        operands = [where, normed, out_weight] + pieces + [after]
+        operands = [where, in_hbm(normed), in_hbm(out_weight)] + pieces + [after]
         specs = [
             tile(width),
             pl.BlockSpec((width, part_out), lambda i, where: (0, where[0])),
@@ -536,16 +545,12 @@
             + [pl.BlockSpec((width, part_out), lambda i: (0, dest(i))), unread()],
             out_specs=[
                 pl.BlockSpec((1, size, part_out), lambda i: (dest(i), 0, 0)),
-                whole((size, part_out)),
-                whole((size, part_out)),
-            ],
-            out_shape=[
-                shaped((chans, size, part_out)),
-                shaped((size, part_out)),
-                shaped((size, part_out)),
-            ],
+            ]
+            + [whole((size // 2, part_out))] * 4,
+            out_shape=[shaped((chans, size, part_out))] + [shaped((size // 2, part_out))] * 4,
             scratch_shapes=[pltpu.VMEM((size, width), BF16)] + [pltpu.VMEM((BLK, width), F32)] * 2,
             compiler_params=params(),
+            cost_estimate=brief(),
             name="project_line",
         )(*operands, out_weight, after)
 
@@ -554,7 +559,9 @@
         down = lax.ppermute(down, "chan", [(a, a - 1) for a in range(chans - 1 - s, chans)])
         return up, down
 
-    def onward(shares, up, down, s, after):
+    def onward(shares, half, up, down, s, after):
+        count = up.shape[0] // BLK
+
         def plain(i, where):
             return (i, 0)
 
@@ -562,15 +569,19 @@
             onward_kernel,
             grid_spec=pltpu.PrefetchScalarGridSpec(
                 num_scalar_prefetch=1,
-                grid=(shares.shape[1] // BLK,),
+                grid=(count,),
                 in_specs=[
                     pl.BlockSpec(
                         (1, BLK, part_out),
-                        lambda i, where: (jnp.minimum(chans - 1 - s + where[0], chans - 1), i, 0),
+                        lambda i, where: (
+                            jnp.minimum(chans - 1 - s + where[0], chans - 1), half * count + i, 0
+                        ),
                     ),
                     pl.BlockSpec(
                         (1, BLK, part_out),
-                        lambda i, where: (jnp.maximum(where[0] - (chans - 1) + s, 0), i, 0),
+                        lambda i, where: (
+                            jnp.maximum(where[0] - (chans - 1) + s, 0), half * count + i, 0
+                        ),
                     ),
                     pl.BlockSpec((BLK, part_out), plain),
                     pl.BlockSpec((BLK, part_out), plain),
@@ -581,15 +592,17 @@
             out_shape=[shaped(up.shape)] * 2,
             compiler_params=params(SMALL_LIMIT),
             name="onward",
-        )(where, shares, shares, up, down, after)
-
-    def final(start, shares, up, down, out):
+        )(where, in_hbm(shares), in_hbm(shares), up, down, after)
+
+    def final(start, shares, half, up, down, out):
+        count = up.shape[0] // BLK
+
         def plain(i, where):
             return (i, 0)
 
-        operands = [where, shares, up, down]
+        operands = [where, in_hbm(shares), up, down]
         in_specs = [
-            pl.BlockSpec((1, BLK, part_out), lambda i, where: (where[0], i, 0)),
+            pl.BlockSpec((1, BLK, part_out), lambda i, where: (where[0], half * count + i, 0)),
             pl.BlockSpec((BLK, part_out), plain),
             pl.BlockSpec((BLK, part_out), plain),
         ]
@@ -602,9 +615,9 @@
             final_kernel,
             grid_spec=pltpu.PrefetchScalarGridSpec(
                 num_scalar_prefetch=1,
-                grid=(shares.shape[1] // BLK,),
+                grid=(count,),
                 in_specs=in_specs,
-                out_specs=pl.BlockSpec((BLK, part_out), lambda i, where: (start + i, 0)),
+                out_specs=pl.BlockSpec((BLK, part_out), lambda i, where: (start + half * count + i, 0)),
             ),
             out_shape=shaped((tokens, part_out)),
             input_output_aliases=aliases,
@@ -612,41 +625,26 @@
             name="final",
         )(*operands)
 
-    quarter = blocks // 4
-    order = sorted(range(1, chans), key=lambda k: (-min(k, chans - k), k))
-    *slots, normed = project_direct(0, quarter, y_second[0], y_second[1], order)
+    half = blocks // 2
+    order = sorted(range(1, chans), key=lambda k: (min(k, chans - k), k))
+    *slots, normed = project_direct(0, half, y_second[0], y_second[1], order)
     pieces = []
     for k, slot in zip(order, slots):
         turn = [(a, (a + k) % chans) for a in range(chans)]
         pieces.append(lax.ppermute(slot, "chan", turn))
 
-    shares, _, _ = project_line(quarter, quarter, y_second[0], normed)
-    scattered = lax.psum_scatter(shares, "chan", scatter_dimension=0, tiled=True)
-
-    starts = (2 * quarter, 3 * quarter)
-    chunks = [project_line(starts[0], quarter, y_second[0], shares)]
-    y_third = local_part(2 * some, blocks - 2 * some, y_second, chunks[0][0])
-    chunks.append(project_line(starts[1], quarter, y_third[0], chunks[0][0]))
-    moving = [permuted(up, down, 0) for _, up, down in chunks]
-    out = direct_final(0, normed, pieces, None, chunks[1][0])
+    y_third = local_part(2 * some, blocks - 2 * some, y_second, normed)
+    shares, up_a, up_b, down_a, down_b = project_line(half, blocks - half, y_third[0], normed)
+    moving = [permuted(up_a, down_a, 0), permuted(up_b, down_b, 0)]
+    out = direct_final(0, normed, pieces, None, shares)
     after = out
     for s in range(1, chans - 1):
         for k in range(2):
-            up, down = onward(chunks[k][0], *moving[k], s, after)
+            up, down = onward(shares, k, *moving[k], s, after)
             after = up
             moving[k] = permuted(up, down, s)
-    out = pl.pallas_call(
-        place_kernel,
-        grid=(quarter,),
-        in_specs=[pl.BlockSpec((BLK, part_out), lambda i: (i, 0)), unread()],
-        out_specs=pl.BlockSpec((BLK, part_out), lambda i: (quarter + i, 0)),
-        out_shape=shaped((tokens, part_out)),
-        input_output_aliases={1: 0},
-        compiler_params=params(SMALL_LIMIT),
-        name="place",
-    )(scattered.reshape(quarter * BLK, part_out), out)
     for k in range(2):
-        out = final(starts[k], chunks[k][0], *moving[k], out)
+        out = final(half, shares, k, *moving[k], out)
     return out
 
 

time: 168 us -> 155 us (0.923)
  between operations: 13.7 us -> 0.25 us
  waiting for transfers between devices: 14.2 us -> 23.1 us
  Pallas kernels: 79.6 us -> 74.1 us
  local copies, waits for them, and re-layouts: 11 us -> 6.93 us
    pallas_call x3 -> x1, Pallas kernels: 29.6 us -> 13.4 us  [project_line(): pl.pallas_call(functools.partial(line_kernel, tiles=count), grid=(count +...]
    ppermute x3, waiting for transfers between devices: 3.08 us -> 9.26 us  [local(): pieces.append(lax.ppermute(slot, 'chan', turn))]
    unnamed x32 -> x12, local copies, waits for them, and re-layouts: 9.48 us -> 5.45 us
    pallas_call x1, Pallas kernels: 8.55 us -> 12.3 us  [project_direct(): pl.pallas_call(functools.partial(direct_kernel, tiles=count), grid_spec=p...]
    pallas_call x1, Pallas kernels: 1.78 us -> 5.1 us  [direct_final(): pl.pallas_call(functools.partial(direct_final_kernel, count=len(pieces)),...]
    pallas_call x4, Pallas kernels: 2.02 us -> 4.82 us  [onward(): pl.pallas_call(onward_kernel, grid_spec=pltpu.PrefetchScalarGridSpec(num_...]
    ppermute x6, starting transfers between devices: 25.4 us -> 28 us  [permuted(): up = lax.ppermute(up, 'chan', [(a, a + 1) for a in range(s + 1)])]
    ppermute x3, starting transfers between devices: 6.68 us -> 4.62 us  [local(): pieces.append(lax.ppermute(slot, 'chan', turn))]
  transfers between devices with their start and end apart: 19 -> 18, of which waited for: 6 -> 6; matrix products, arithmetic and copies ran while one was open for 0% -> 0% of each run, Pallas kernels for 27% -> 30%
where the time goes in v6:
time: 155 us; the launch traced here: 153 us
  Pallas kernels  74.1 us (48%)
  starting transfers between devices  49 us (32%)
  waiting for transfers between devices  23.1 us (15%)
  local copies, waits for them, and re-layouts  6.93 us (4%)
    ppermute x6, starting transfers between devices, permuted(): up = lax.ppermute(up, 'chan', [(a, a + 1) for a in range(s + 1)])  28 us
    pallas_call x3, Pallas kernels, local_part(): pl.pallas_call(local_kernel, grid=(count,), in_specs=specs, out_specs=[ti...  20.5 us
    pallas_call x1, Pallas kernels, local(): pl.pallas_call(states_kernel, grid=(width // WIDE,), in_specs=[lanes_at(t...  13.7 us
    pallas_call x1, Pallas kernels, project_line(): pl.pallas_call(functools.partial(line_kernel, tiles=count), grid=(count +...  13.4 us
    pallas_call x1, Pallas kernels, project_direct(): pl.pallas_call(functools.partial(direct_kernel, tiles=count), grid_spec=p...  12.3 us
    ppermute x3, waiting for transfers between devices, local(): pieces.append(lax.ppermute(slot, 'chan', turn))  9.26 us
    unnamed x12, local copies, waits for them, and re-layouts  5.45 us
    ppermute x6, starting transfers between devices, permuted(): lax.ppermute(down, 'chan', [(a, a - 1) for a in range(chans - 1 - s, chan...  5.29 us
  transfers between devices with their start and end apart: 18, of which 6 were waited for; matrix products, arithmetic and copies ran while one was open for 0% of the time, Pallas kernels for 30%

profile of v6, /device:TPU:2, one launch (start us, length us, event | category | flops | bytes accessed | tf_op | source)
XLA Modules:
  0.0 153.4 jit_solution(14947306556145089512)
XLA Ops:
  0.0 0.7 slice.7
  0.7 0.8 slice.6
  1.5 1.9 %collective-permute-start = (bf16[8,2560]{1,0:T(8,128)(2,1)S(1)}, bf16[8,2560]{1,0:T(8,128)(2,1)S(1)}, u32[]{:S(2)}, u32[]{:S(2)}) collective-permute-start(bf16[8,2560]{1,0:T(8,128)(2,1)S(1)} %pad_maximum_fusion), channel_id=1, source_target_pairs={{0,4},{4,8},{8,12},{12,16},{16,20},{20,24},{24,28},{1,5},{5,9},{9,... | collective-permute-start | bytes 122888 | tf_op jit(solution)/shard_map/ppermute | solution.py:349
  3.4 3.4 %collective-permute-done.tail_ref.mtail_ref = bf16[8,2560]{1,0:T(8,128)(2,1)S(1)} collective-permute-done((bf16[8,2560]{1,0:T(8,128)(2,1)S(1)}, bf16[8,2560]{1,0:T(8,128)(2,1)S(1)}, u32[]{:S(2)}, u32[]{:S(2)}) %collective-permute-start) | collective-permute-done | bytes 40992 | tf_op jit(solution)/shard_map/ppermute | solution.py:349
  6.8 0.0 copy-start.5
  6.8 0.6 copy-done.5
  7.4 13.7 %states.1 = (bf16[1024,2048]{1,0:T(8,128)(2,1)}, bf16[1024,512]{1,0:T(8,128)(2,1)}, bf16[2,128,1024]{2,1,0:T(8,128)(2,1)}, f32[32,1024]{1,0:T(8,128)}, f32[1024,...) custom-call(bf16[1024,2048]{1,0:T(8,128)(2,1)} %x_ref.1, ...), custom_call_target="tpu_custom_call" | custom-call | tf_op jit(solution)/shard_map/states/pallas_call | solution.py:354
  21.1 4.3 %all-to-all-start = ((bf16[8,16,2176]{2,1,0:T(8,128)(2,1)}), bf16[8,16,2176]{2,1,0:T(8,128)(2,1)S(1)}, u32[]{:S(2)}, u32[]{:S(2)}) async-start(bf16[8,16,2176]{2,1,0:T(8,128)(2,1)} %bitcast.12), calls=%async_computation | async-start | bytes 1114112 | tf_op jit(solution)/shard_map/all_to_all | solution.py:399
  25.4 0.0 copy-start.1
  25.4 5.7 %local_part.3 = (bf16[1024,2048]{1,0:T(8,128)(2,1)}, f32[128,2048]{1,0:T(8,128)}) custom-call(bf16[1024,2048]{1,0:T(8,128)(2,1)} %get-tuple-element.35.xc_ref, bf16[1024,512]{1,0:T(8,128)(2,1)} %get-tuple-element.36.bc_ref, bf16[2,128,1024]{2,1,0:T(8,128)(2,1)} %get-tuple-element.37.bt_ref, f32[32,1024]{1,0:T(8,128)} %get-tuple-element.38.crow_ref, ...), custom_call_target="tpu_custom_call" | custom-call | flops 1 | bytes 1 | tf_op jit(solution)/shard_map/local_part/pallas_call | solution.py:428
  31.1 2.9 %all-to-all-done.pay_ref = bf16[8,16,2176]{2,1,0:T(8,128)(2,1)S(1)} async-done(((bf16[8,16,2176]{2,1,0:T(8,128)(2,1)}), bf16[8,16,2176]{2,1,0:T(8,128)(2,1)S(1)}, u32[]{:S(2)}, u32[]{:S(2)}) %all-to-all-start) | async-done | bytes 557088 | tf_op jit(solution)/shard_map/all_to_all | solution.py:399
  34.0 0.0 copy-done.1
  34.0 0.0 copy-start.3
  34.0 1.2 copy-done.3
  35.2 1.0 prefix.1.rest_2_
  36.3 4.9 %all-to-all-start.1 = ((bf16[8,16,2048]{2,1,0:T(8,128)(2,1)}), bf16[8,16,2048]{2,1,0:T(8,128)(2,1)S(1)}, u32[]{:S(2)}, u32[]{:S(2)}) async-start(bf16[8,16,2048]{2,1,0:T(8,128)(2,1)} %prefix.1.rest_2_), calls=%async_computation.1 | async-start | bytes 1048576 | tf_op jit(solution)/shard_map/all_to_all | solution.py:456
  41.1 6.0 %local_part.4 = (bf16[1024,2048]{1,0:T(8,128)(2,1)}, f32[128,2048]{1,0:T(8,128)}) custom-call(bf16[1024,2048]{1,0:T(8,128)(2,1)} %get-tuple-element.35.xc_ref, bf16[1024,512]{1,0:T(8,128)(2,1)} %get-tuple-element.36.bc_ref, bf16[2,128,1024]{2,1,0:T(8,128)(2,1)} %get-tuple-element.37.bt_ref, ...), custom_call_target="tpu_custom_call", output_to_operand_aliasing={{0}: (11, {})} | custom-call | flops 1 | bytes 1 | tf_op jit(solution)/shard_map/local_part/pallas_call | solution.py:428
  47.2 2.3 %all-to-all-done.1 = bf16[8,16,2048]{2,1,0:T(8,128)(2,1)S(1)} async-done(((bf16[8,16,2048]{2,1,0:T(8,128)(2,1)}), bf16[8,16,2048]{2,1,0:T(8,128)(2,1)S(1)}, u32[]{:S(2)}, u32[]{:S(2)}) %all-to-all-start.1) | async-done | bytes 524320 | tf_op jit(solution)/shard_map/all_to_all | solution.py:456
  49.4 0.0 copy-start.4
  49.4 0.8 copy-done.4
  50.2 12.3 %project_direct.1 = (bf16[512,512]{1,0:T(8,128)(2,1)}, bf16[512,512]{1,0:T(8,128)(2,1)}, bf16[512,512]{1,0:T(8,128)(2,1)}, bf16[512,2048]{1,0:T(8,128)(2,1)}) custom-call(s32[1]{0:T(128)} %bitcast.where_ref, bf16[1024,2048]{1,0:T(8,128)(2,1)} %get-tuple-element.46.y_ref.rest_1_, bf16[1024,512]{1,0:T(8,128)(2,1)} %get-tuple-element.36.bc_ref, ...), custom_call_target="tpu_custom_call" | custom-call | tf_op jit(solution)/shard_map/project_direct/pallas_call | solution.py:491
  62.5 1.6 %collective-permute-start.5 = (bf16[512,512]{1,0:T(8,128)(2,1)}, bf16[512,512]{1,0:T(8,128)(2,1)S(1)}, u32[]{:S(2)}, u32[]{:S(2)}) collective-permute-start(bf16[512,512]{1,0:T(8,128)(2,1)} %get-tuple-element.54), channel_id=1, source_target_pairs={{0,1},{1,2},{2,3},{3,0},{4,5},{5,6},{6,7},{7,4},{8,9},{9,10},{10,1... | collective-permute-start | bytes 1572872 | tf_op jit(solution)/shard_map/ppermute | solution.py:634
  64.1 2.3 %collective-permute-start.6 = (bf16[512,512]{1,0:T(8,128)(2,1)}, bf16[512,512]{1,0:T(8,128)(2,1)S(1)}, u32[]{:S(2)}, u32[]{:S(2)}) collective-permute-start(bf16[512,512]{1,0:T(8,128)(2,1)} %get-tuple-element.55), channel_id=1, source_target_pairs={{0,3},{1,0},{2,1},{3,2},{4,7},{5,4},{6,5},{7,6},{8,11},{9,8},{10,9... | collective-permute-start | bytes 1572872 | tf_op jit(solution)/shard_map/ppermute | solution.py:634
  66.3 0.8 collective-permute-start.7
  67.1 8.7 %local_part.5 = (bf16[1024,2048]{1,0:T(8,128)(2,1)}, f32[128,2048]{1,0:T(8,128)}) custom-call(bf16[1024,2048]{1,0:T(8,128)(2,1)} %get-tuple-element.35.xc_ref, bf16[1024,512]{1,0:T(8,128)(2,1)} %get-tuple-element.36.bc_ref, bf16[2,128,1024]{2,1,0:T(8,128)(2,1)} %get-tuple-element.37.bt_ref, ...), custom_call_target="tpu_custom_call", output_to_operand_aliasing={{0}: (11, {})} | custom-call | flops 1 | bytes 1 | tf_op jit(solution)/shard_map/local_part/pallas_call | solution.py:428
  75.8 13.4 %project_line.1 = (bf16[4,512,512]{2,1,0:T(8,128)(2,1)}, bf16[256,512]{1,0:T(8,128)(2,1)}, bf16[256,512]{1,0:T(8,128)(2,1)}, bf16[256,512]{1,0:T(8,128)(2,1)}, bf16[256,512]{1,0:T(8,128)(2,1)}) custom-call(bf16[1024,2048]{1,0:T(8,128)(2,1)} %get-tuple-element.48.y_ref, bf16[1024,512]{1,0:T(8,128)(2,1)} %get-tuple-element.36.bc_ref, ...), custom_call_target="tpu_custom_call" | custom-call | flops 1 | bytes 1 | tf_op jit(solution)/shard_map/project_line/pallas_call | solution.py:541
  89.2 3.5 %collective-permute-start.3 = (bf16[256,512]{1,0:T(8,128)(2,1)}, bf16[256,512]{1,0:T(8,128)(2,1)S(1)}, u32[]{:S(2)}, u32[]{:S(2)}) collective-permute-start(bf16[256,512]{1,0:T(8,128)(2,1)} %get-tuple-element.52), channel_id=1, source_target_pairs={{0,1},{4,5},{8,9},{12,13},{16,17},{20,21},{24,25},{28,29}} | collective-permute-start | bytes 786440 | tf_op jit(solution)/shard_map/ppermute | solution.py:558
  92.7 0.7 collective-permute-start.4
  93.4 0.0 collective-permute-done.5.refs_0_
  93.4 8.8 %collective-permute-start.1 = (bf16[256,512]{1,0:T(8,128)(2,1)}, bf16[256,512]{1,0:T(8,128)(2,1)S(1)}, u32[]{:S(2)}, u32[]{:S(2)}) collective-permute-start(bf16[256,512]{1,0:T(8,128)(2,1)} %get-tuple-element.50), channel_id=1, source_target_pairs={{0,1},{4,5},{8,9},{12,13},{16,17},{20,21},{24,25},{28,29}} | collective-permute-start | bytes 786440 | tf_op jit(solution)/shard_map/ppermute | solution.py:558
  102.2 0.0 collective-permute-done.6.refs_1_
  102.2 0.7 collective-permute-start.2
  102.9 9.3 %collective-permute-done.7.refs_2_ = bf16[512,512]{1,0:T(8,128)(2,1)S(1)} collective-permute-done((bf16[512,512]{1,0:T(8,128)(2,1)}, bf16[512,512]{1,0:T(8,128)(2,1)S(1)}, u32[]{:S(2)}, u32[]{:S(2)}) %collective-permute-start.7) | collective-permute-done | bytes 524320 | tf_op jit(solution)/shard_map/ppermute | solution.py:634
  112.2 0.0 copy-start
  112.2 1.6 %copy-done = bf16[4,512,512]{2,1,0:T(8,128)(2,1)S(1)} copy-done((bf16[4,512,512]{2,1,0:T(8,128)(2,1)S(1)}, bf16[4,512,512]{2,1,0:T(8,128)(2,1)}, u32[]{:S(2)}) %copy-start) | copy-done | bytes 2097176
  113.8 5.1 %direct_final.1.after_ref.rest_0_ = bf16[1024,512]{1,0:T(8,128)(2,1)} custom-call(s32[1]{0:T(128)} %bitcast.where_ref, bf16[512,2048]{1,0:T(8,128)(2,1)} %get-tuple-element.47.rest_2_.after_ref.normed_ref, bf16[2048,2048]{1,0:T(8,128)(2,1)} %w_ref.5, bf16[512,512]{1,0:T(8,128)(2,1)S(1)} %collective-permute-done.5.refs_0_, ...), custom_call_target="tpu_custom_call" | custom-call | tf_op jit(solution)/shard_map/direct_final/pallas_call | solution.py:520
  118.9 0.0 collective-permute-done.3.up_ref
  118.9 0.0 collective-permute-done.4.down_ref
  118.9 0.0 copy-start.2
  118.9 1.2 copy-done.2
  120.1 1.2 onward.4
  121.3 0.7 collective-permute-start.11
  122.0 1.4 collective-permute-start.10
  123.4 0.0 collective-permute-done.1.up_ref
  123.4 0.0 collective-permute-done.2.down_ref
  123.4 1.2 onward.5
  124.7 0.7 collective-permute-start.9
  125.4 5.2 %collective-permute-start.8 = (bf16[256,512]{1,0:T(8,128)(2,1)S(1)}, bf16[256,512]{1,0:T(8,128)(2,1)S(1)}, u32[]{:S(2)}, u32[]{:S(2)}) collective-permute-start(bf16[256,512]{1,0:T(8,128)(2,1)S(1)} %get-tuple-element.58.after_ref), channel_id=1, source_target_pairs={{0,1},{1,2},{4,5},{5,6},{8,9},{9,10},{12,13},{13,14},{16,17},{17,1... | collective-permute-start | bytes 786440 | tf_op jit(solution)/shard_map/ppermute | solution.py:558
  130.5 0.0 collective-permute-done.11.down_ref
  130.5 0.0 collective-permute-done.10.up_ref
  130.5 1.2 onward.6
  131.8 1.3 collective-permute-start.15
  133.1 5.2 %collective-permute-start.14 = (bf16[256,512]{1,0:T(8,128)(2,1)S(1)}, bf16[256,512]{1,0:T(8,128)(2,1)S(1)}, u32[]{:S(2)}, u32[]{:S(2)}) collective-permute-start(bf16[256,512]{1,0:T(8,128)(2,1)S(1)} %get-tuple-element.61.after_ref), channel_id=1, source_target_pairs={{0,1},{1,2},{2,3},{4,5},{5,6},{6,7},{8,9},{9,10},{10,11},{12,13},{... | collective-permute-start | bytes 786440 | tf_op jit(solution)/shard_map/ppermute | solution.py:558
  138.3 0.0 collective-permute-done.9.down_ref
  138.3 0.0 collective-permute-done.8.up_ref
  138.3 1.2 onward.7
  139.5 3.9 %collective-permute-start.12 = (bf16[256,512]{1,0:T(8,128)(2,1)S(1)}, bf16[256,512]{1,0:T(8,128)(2,1)S(1)}, u32[]{:S(2)}, u32[]{:S(2)}) collective-permute-start(bf16[256,512]{1,0:T(8,128)(2,1)S(1)} %get-tuple-element.62), channel_id=1, source_target_pairs={{0,1},{1,2},{2,3},{4,5},{5,6},{6,7},{8,9},{9,10},{10,11},{12,13},{... | collective-permute-start | bytes 786440 | tf_op jit(solution)/shard_map/ppermute | solution.py:558
  143.4 1.3 collective-permute-start.13
  144.7 0.0 collective-permute-done.15.down_ref
  144.7 0.0 collective-permute-done.14.up_ref
  144.7 1.7 %final.2.rest_0_ = bf16[1024,512]{1,0:T(8,128)(2,1)} custom-call(s32[1]{0:T(128)} %bitcast.where_ref, bf16[4,512,512]{2,1,0:T(8,128)(2,1)} %get-tuple-element.49.refs_3_.up_own_ref.down_own_ref.own_ref, bf16[256,512]{1,0:T(8,128)(2,1)S(1)} %collective-permute-done.14.up_ref, ...), custom_call_target="tpu_custom_call", output_to_operand_aliasing={{}: (4, {})} | custom-call | tf_op jit(solution)/shard_map/final/pallas_call | solution.py:614
  146.4 1.6 %collective-permute-done.12.up_ref = bf16[256,512]{1,0:T(8,128)(2,1)S(1)} collective-permute-done((bf16[256,512]{1,0:T(8,128)(2,1)S(1)}, bf16[256,512]{1,0:T(8,128)(2,1)S(1)}, u32[]{:S(2)}, u32[]{:S(2)}) %collective-permute-start.12) | collective-permute-done | bytes 262176 | tf_op jit(solution)/shard_map/ppermute | solution.py:558
  148.0 3.7 %collective-permute-done.13.down_ref = bf16[256,512]{1,0:T(8,128)(2,1)S(1)} collective-permute-done((bf16[256,512]{1,0:T(8,128)(2,1)S(1)}, bf16[256,512]{1,0:T(8,128)(2,1)S(1)}, u32[]{:S(2)}, u32[]{:S(2)}) %collective-permute-start.13) | collective-permute-done | bytes 262176 | tf_op jit(solution)/shard_map/ppermute | solution.py:559
  151.7 1.7 %final.3 = bf16[1024,512]{1,0:T(8,128)(2,1)} custom-call(s32[1]{0:T(128)} %bitcast.where_ref, bf16[4,512,512]{2,1,0:T(8,128)(2,1)} %get-tuple-element.49.refs_3_.up_own_ref.down_own_ref.own_ref, bf16[256,512]{1,0:T(8,128)(2,1)S(1)} %collective-permute-done.12.up_ref, ...), custom_call_target="tpu_custom_call", output_to_operand_aliasing={{}: (4, {})} | custom-call | tf_op jit(solution)/shard_map/final/pallas_call | solution.py:614
  (2 shorter events, 0.0 us)
Async XLA Ops:
  1.5 5.3 %collective-permute-start = (bf16[8,2560]{1,0:T(8,128)(2,1)S(1)}, bf16[8,2560]{1,0:T(8,128)(2,1)S(1)}, u32[]{:S(2)}, u32[]{:S(2)}) collective-permute-start(bf16[8,2560]{1,0:T(8,128)(2,1)S(1)} %pad_maximum_fusion), channel_id=1, source_target_pairs={{0,4},{4,8},{8,12},{12,16},{16,20},{20,24},{24,28},{1,5},{5,9},{9,... | collective-permute-start | bytes 122888 | tf_op jit(solution)/shard_map/ppermute | solution.py:349
  6.8 0.6 copy-start.5
  21.1 12.9 %all-to-all-start = ((bf16[8,16,2176]{2,1,0:T(8,128)(2,1)}), bf16[8,16,2176]{2,1,0:T(8,128)(2,1)S(1)}, u32[]{:S(2)}, u32[]{:S(2)}) async-start(bf16[8,16,2176]{2,1,0:T(8,128)(2,1)} %bitcast.12), calls=%async_computation | async-start | bytes 1114112 | tf_op jit(solution)/shard_map/all_to_all | solution.py:399
  25.4 8.6 %copy-start.1 = (bf16[128,2048]{1,0:T(8,128)(2,1)S(1)}, bf16[128,2048]{1,0:T(8,128)(2,1)}, u32[]{:S(2)}) copy-start(bf16[128,2048]{1,0:T(8,128)(2,1)} %constant.9.clone.high_ref.e_ref) | copy-start | bytes 1572868
  34.0 1.2 copy-start.3
  36.3 13.2 %all-to-all-start.1 = ((bf16[8,16,2048]{2,1,0:T(8,128)(2,1)}), bf16[8,16,2048]{2,1,0:T(8,128)(2,1)S(1)}, u32[]{:S(2)}, u32[]{:S(2)}) async-start(bf16[8,16,2048]{2,1,0:T(8,128)(2,1)} %prefix.1.rest_2_), calls=%async_computation.1 | async-start | bytes 1048576 | tf_op jit(solution)/shard_map/all_to_all | solution.py:456
  49.4 0.8 copy-start.4
  62.5 30.9 %collective-permute-start.5 = (bf16[512,512]{1,0:T(8,128)(2,1)}, bf16[512,512]{1,0:T(8,128)(2,1)S(1)}, u32[]{:S(2)}, u32[]{:S(2)}) collective-permute-start(bf16[512,512]{1,0:T(8,128)(2,1)} %get-tuple-element.54), channel_id=1, source_target_pairs={{0,1},{1,2},{2,3},{3,0},{4,5},{5,6},{6,7},{7,4},{8,9},{9,10},{10,1... | collective-permute-start | bytes 1572872 | tf_op jit(solution)/shard_map/ppermute | solution.py:634
  64.1 38.1 %collective-permute-start.6 = (bf16[512,512]{1,0:T(8,128)(2,1)}, bf16[512,512]{1,0:T(8,128)(2,1)S(1)}, u32[]{:S(2)}, u32[]{:S(2)}) collective-permute-start(bf16[512,512]{1,0:T(8,128)(2,1)} %get-tuple-element.55), channel_id=1, source_target_pairs={{0,3},{1,0},{2,1},{3,2},{4,7},{5,4},{6,5},{7,6},{8,11},{9,8},{10,9... | collective-permute-start | bytes 1572872 | tf_op jit(solution)/shard_map/ppermute | solution.py:634
  66.3 45.8 %collective-permute-start.7 = (bf16[512,512]{1,0:T(8,128)(2,1)}, bf16[512,512]{1,0:T(8,128)(2,1)S(1)}, u32[]{:S(2)}, u32[]{:S(2)}) collective-permute-start(bf16[512,512]{1,0:T(8,128)(2,1)} %get-tuple-element.56), channel_id=1, source_target_pairs={{0,2},{1,3},{2,0},{3,1},{4,6},{5,7},{6,4},{7,5},{8,10},{9,11},{10,... | collective-permute-start | bytes 1572872 | tf_op jit(solution)/shard_map/ppermute | solution.py:634
  89.2 29.7 %collective-permute-start.3 = (bf16[256,512]{1,0:T(8,128)(2,1)}, bf16[256,512]{1,0:T(8,128)(2,1)S(1)}, u32[]{:S(2)}, u32[]{:S(2)}) collective-permute-start(bf16[256,512]{1,0:T(8,128)(2,1)} %get-tuple-element.52), channel_id=1, source_target_pairs={{0,1},{4,5},{8,9},{12,13},{16,17},{20,21},{24,25},{28,29}} | collective-permute-start | bytes 786440 | tf_op jit(solution)/shard_map/ppermute | solution.py:558
  92.7 26.2 %collective-permute-start.4 = (bf16[256,512]{1,0:T(8,128)(2,1)}, bf16[256,512]{1,0:T(8,128)(2,1)S(1)}, u32[]{:S(2)}, u32[]{:S(2)}) collective-permute-start(bf16[256,512]{1,0:T(8,128)(2,1)} %get-tuple-element.53), channel_id=1, source_target_pairs={{3,2},{7,6},{11,10},{15,14},{19,18},{23,22},{27,26},{31,30}} | collective-permute-start | bytes 786440 | tf_op jit(solution)/shard_map/ppermute | solution.py:559
  93.4 30.0 %collective-permute-start.1 = (bf16[256,512]{1,0:T(8,128)(2,1)}, bf16[256,512]{1,0:T(8,128)(2,1)S(1)}, u32[]{:S(2)}, u32[]{:S(2)}) collective-permute-start(bf16[256,512]{1,0:T(8,128)(2,1)} %get-tuple-element.50), channel_id=1, source_target_pairs={{0,1},{4,5},{8,9},{12,13},{16,17},{20,21},{24,25},{28,29}} | collective-permute-start | bytes 786440 | tf_op jit(solution)/shard_map/ppermute | solution.py:558
  102.2 21.2 %collective-permute-start.2 = (bf16[256,512]{1,0:T(8,128)(2,1)}, bf16[256,512]{1,0:T(8,128)(2,1)S(1)}, u32[]{:S(2)}, u32[]{:S(2)}) collective-permute-start(bf16[256,512]{1,0:T(8,128)(2,1)} %get-tuple-element.51), channel_id=1, source_target_pairs={{3,2},{7,6},{11,10},{15,14},{19,18},{23,22},{27,26},{31,30}} | collective-permute-start | bytes 786440 | tf_op jit(solution)/shard_map/ppermute | solution.py:559
  112.2 1.6 %copy-start = (bf16[4,512,512]{2,1,0:T(8,128)(2,1)S(1)}, bf16[4,512,512]{2,1,0:T(8,128)(2,1)}, u32[]{:S(2)}) copy-start(bf16[4,512,512]{2,1,0:T(8,128)(2,1)} %get-tuple-element.49.refs_3_.up_own_ref.down_own_ref.own_ref) | copy-start | bytes 6291460
  118.9 1.2 copy-start.2
  121.3 9.2 %collective-permute-start.11 = (bf16[256,512]{1,0:T(8,128)(2,1)S(1)}, bf16[256,512]{1,0:T(8,128)(2,1)S(1)}, u32[]{:S(2)}, u32[]{:S(2)}) collective-permute-start(bf16[256,512]{1,0:T(8,128)(2,1)S(1)} %get-tuple-element.60), channel_id=1, source_target_pairs={{2,1},{3,2},{6,5},{7,6},{10,9},{11,10},{14,13},{15,14},{18,17},{19... | collective-permute-start | bytes 786440 | tf_op jit(solution)/shard_map/ppermute | solution.py:559
  122.0 8.6 %collective-permute-start.10 = (bf16[256,512]{1,0:T(8,128)(2,1)S(1)}, bf16[256,512]{1,0:T(8,128)(2,1)S(1)}, u32[]{:S(2)}, u32[]{:S(2)}) collective-permute-start(bf16[256,512]{1,0:T(8,128)(2,1)S(1)} %get-tuple-element.57.after_ref), channel_id=1, source_target_pairs={{0,1},{1,2},{4,5},{5,6},{8,9},{9,10},{12,13},{13,14},{16,17},{17,1... | collective-permute-start | bytes 786440 | tf_op jit(solution)/shard_map/ppermute | solution.py:558
  124.7 13.6 %collective-permute-start.9 = (bf16[256,512]{1,0:T(8,128)(2,1)S(1)}, bf16[256,512]{1,0:T(8,128)(2,1)S(1)}, u32[]{:S(2)}, u32[]{:S(2)}) collective-permute-start(bf16[256,512]{1,0:T(8,128)(2,1)S(1)} %get-tuple-element.59), channel_id=1, source_target_pairs={{2,1},{3,2},{6,5},{7,6},{10,9},{11,10},{14,13},{15,14},{18,17},{19... | collective-permute-start | bytes 786440 | tf_op jit(solution)/shard_map/ppermute | solution.py:559
  125.4 12.9 %collective-permute-start.8 = (bf16[256,512]{1,0:T(8,128)(2,1)S(1)}, bf16[256,512]{1,0:T(8,128)(2,1)S(1)}, u32[]{:S(2)}, u32[]{:S(2)}) collective-permute-start(bf16[256,512]{1,0:T(8,128)(2,1)S(1)} %get-tuple-element.58.after_ref), channel_id=1, source_target_pairs={{0,1},{1,2},{4,5},{5,6},{8,9},{9,10},{12,13},{13,14},{16,17},{17,1... | collective-permute-start | bytes 786440 | tf_op jit(solution)/shard_map/ppermute | solution.py:558
  131.8 13.0 %collective-permute-start.15 = (bf16[256,512]{1,0:T(8,128)(2,1)S(1)}, bf16[256,512]{1,0:T(8,128)(2,1)S(1)}, u32[]{:S(2)}, u32[]{:S(2)}) collective-permute-start(bf16[256,512]{1,0:T(8,128)(2,1)S(1)} %get-tuple-element.64), channel_id=1, source_target_pairs={{1,0},{2,1},{3,2},{5,4},{6,5},{7,6},{9,8},{10,9},{11,10},{13,12},{... | collective-permute-start | bytes 786440 | tf_op jit(solution)/shard_map/ppermute | solution.py:559
  133.1 11.7 %collective-permute-start.14 = (bf16[256,512]{1,0:T(8,128)(2,1)S(1)}, bf16[256,512]{1,0:T(8,128)(2,1)S(1)}, u32[]{:S(2)}, u32[]{:S(2)}) collective-permute-start(bf16[256,512]{1,0:T(8,128)(2,1)S(1)} %get-tuple-element.61.after_ref), channel_id=1, source_target_pairs={{0,1},{1,2},{2,3},{4,5},{5,6},{6,7},{8,9},{9,10},{10,11},{12,13},{... | collective-permute-start | bytes 786440 | tf_op jit(solution)/shard_map/ppermute | solution.py:558
  139.5 8.5 %collective-permute-start.12 = (bf16[256,512]{1,0:T(8,128)(2,1)S(1)}, bf16[256,512]{1,0:T(8,128)(2,1)S(1)}, u32[]{:S(2)}, u32[]{:S(2)}) collective-permute-start(bf16[256,512]{1,0:T(8,128)(2,1)S(1)} %get-tuple-element.62), channel_id=1, source_target_pairs={{0,1},{1,2},{2,3},{4,5},{5,6},{6,7},{8,9},{9,10},{10,11},{12,13},{... | collective-permute-start | bytes 786440 | tf_op jit(solution)/shard_map/ppermute | solution.py:558
  143.4 8.3 %collective-permute-start.13 = (bf16[256,512]{1,0:T(8,128)(2,1)S(1)}, bf16[256,512]{1,0:T(8,128)(2,1)S(1)}, u32[]{:S(2)}, u32[]{:S(2)}) collective-permute-start(bf16[256,512]{1,0:T(8,128)(2,1)S(1)} %get-tuple-element.63), channel_id=1, source_target_pairs={{1,0},{2,1},{3,2},{5,4},{6,5},{7,6},{9,8},{10,9},{11,10},{13,12},{... | collective-permute-start | bytes 786440 | tf_op jit(solution)/shard_map/ppermute | solution.py:559

commit v7 on v6

--- a/solution.py
+++ b/solution.py
@@ -14,7 +14,7 @@
 LANES = 128
 HALO = 8
 ROWS = 16
-WIDE = 256
+WIDE = 512
 
 step_limit = 0.5
 epsilon = 1e-05
@@ -35,11 +35,11 @@
     return high, v - high
 
 
-def spread(first_row, heads, width):
+def spread(heads, width):
     result = np.zeros((LANES, width), np.float32)
     for k in range(2 * heads):
         h = k % heads
-        result[first_row + k, h * HEAD_DIM : (h + 1) * HEAD_DIM] = 1.0
+        result[k, h * HEAD_DIM : (h + 1) * HEAD_DIM] = 1.0
     return jnp.asarray(result, BF16)
 
 
@@ -76,8 +76,8 @@
 
 def states_kernel(
     x_ref, maps_ref, step_ref, tail_ref, mtail_ref, bias_ref, rate_ref, ck_ref, mk_ref, e_ref,
-    xc_ref, bc_ref, bt_ref, crow_ref, cols_ref, w_ref, g_ref, pay_ref,
-    weighted,
+    xc_ref, bc_ref, bt_ref, crow_ref, cols_ref, wrow_ref, g_ref, pay_ref,
+    weighted, w_ref,
 ):
     c = pl.program_id(0)
     heads, tokens = step_ref.shape
@@ -116,13 +116,12 @@
             at = slice(b * BLK, (b + 1) * BLK)
             cum, step_b = cums[b], step[:, at]
             total = cum[:, BLK - 1 : BLK]
-            block_weight = jnp.exp(total - cum) * step_b
+            wrow_ref[:, at] = jnp.exp(total - cum) * step_b
             slab_weight = jnp.exp(leads[blocks] - (leads[b] + cum)) * step_b
-            grown = jnp.exp(cum)
             entered = jnp.exp(cum + leads[b])
             crow_ref[:, at] = (cum - jnp.log(step_b)) * LOG2E
-            w_ref[at, :] = padded(high_low(slab_weight) + high_low(block_weight)).T.astype(BF16)
-            last = padded(high_low(grown) + high_low(entered)).T
+            w_ref[at, :] = padded(high_low(slab_weight)).T.astype(BF16)
+            last = padded(high_low(entered)).T
             g_ref[at, :] = last.astype(BF16)
             cols_ref[at, :] = padded((cum * LOG2E,)).T
         pay_ref[:, heads * HEAD_DIM :] = jnp.broadcast_to(last[BLK - 1 :], (STATE, LANES)).astype(BF16)
@@ -161,21 +160,15 @@
     pay_ref[:, at] = dot(bt_ref[group], weighted[...]).astype(BF16)
 
 
-def local_kernel(
-    xc_ref, bc_ref, bt_ref, crow_ref, cols_ref, w_ref, g_ref, skip_ref, low_ref, high_ref, *rest
-):
-    y_ref, state, gain_ref = rest[-3:]
-    heads = crow_ref.shape[0]
+def local_kernel(xc_ref, bc_ref, bt_ref, crow_ref, cols_ref, wrow_ref, skip_ref, *rest):
+    y_ref, state = rest[-2:]
     width = xc_ref.shape[1]
     groups = bt_ref.shape[0]
     gw = width // groups
 
     @pl.when(pl.program_id(0) == 0)
     def _():
-        state[...] = rest[0][...] if len(rest) > 4 else jnp.zeros_like(state)
-        skip = jnp.concatenate(high_low(skip_ref[...]), 1)
-        skip = jnp.concatenate([skip, jnp.zeros((1, LANES - 2 * heads), F32)], 1)
-        gain_ref[...] = dot(jnp.broadcast_to(skip, (HALO, LANES)).astype(BF16), low_ref[...])
+        state[...] = rest[0][...] if len(rest) > 3 else jnp.zeros_like(state)
 
     left = lax.broadcasted_iota(jnp.int32, (BLK, LANES), 1) < HEAD_DIM
     row = lax.broadcasted_iota(jnp.int32, (BLK, BLK), 0)
@@ -184,26 +177,33 @@
         b_g = bc_ref[:, g * STATE : (g + 1) * STATE]
         c_g = bc_ref[:, (groups + g) * STATE : (groups + g + 1) * STATE]
         scores = jnp.where(causal, dot_t(c_g, b_g), 0.0)
+        b_t = bt_ref[g].astype(F32)
         for wide in range(g * gw, (g + 1) * gw, 2 * LANES):
-            at_wide = slice(wide, wide + 2 * LANES)
-            grown = dot(g_ref[...], low_ref[:, at_wide])
-            before = state[:, at_wide]
-            carry = grown * dot(c_g, before.astype(BF16))
-            x_wide = xc_ref[:, at_wide].astype(F32)
-            weighted = (x_wide * dot(w_ref[...], high_ref[:, at_wide])).astype(BF16)
-            state[:, at_wide] = grown[BLK - 1 :] * before + dot(bt_ref[g], weighted)
-            carry = carry + gain_ref[0:1, at_wide] * x_wide
+            before = state[:, wide : wide + 2 * LANES]
+            carry = dot(c_g, before.astype(BF16))
             for k in range(2):
                 at = slice(wide + k * LANES, wide + (k + 1) * LANES)
-                mixing = []
-                for h in (at.start // HEAD_DIM, at.start // HEAD_DIM + 1):
-                    gap = jnp.minimum(cols_ref[:, h : h + 1] - crow_ref[h : h + 1], 0.0)
+                part = slice(k * LANES, (k + 1) * LANES)
+                first = at.start // HEAD_DIM
+                mixing, weighted, cums = [], [], []
+                for h in (first, first + 1):
+                    cum = jnp.broadcast_to(cols_ref[:, h : h + 1], (BLK, BLK))
+                    gap = jnp.minimum(cum - crow_ref[h : h + 1], 0.0)
                     mixing.append((jnp.exp2(gap) * scores).astype(BF16))
+                    weighted.append((b_t * wrow_ref[h : h + 1]).astype(BF16))
+                    cums.append(cum)
                 x = xc_ref[:, at]
                 nil = jnp.zeros_like(x)
                 stacked = jnp.concatenate([jnp.where(left, x, nil), jnp.where(left, nil, x)], 0)
-                y = dot(jnp.concatenate(mixing, 1), stacked) + carry[:, k * LANES : (k + 1) * LANES]
+                both = jnp.concatenate(
+                    [jnp.concatenate(mixing, 1), jnp.concatenate(weighted, 1)], 0
+                )
+                result = dot(both, stacked)
+                grown = jnp.exp2(jnp.where(left, cums[0], cums[1]))
+                skip = jnp.where(left, skip_ref[0, first], skip_ref[0, first + 1])
+                y = result[:BLK] + grown * carry[:, part] + skip * x.astype(F32)
                 y_ref[:, at] = y.astype(BF16)
+                state[:, at] = grown[BLK - 1 :] * before[:, part] + result[BLK:]
 
 
 def prefix_kernel(pay_ref, e_ref, after_ref, out_ref):
@@ -225,9 +225,10 @@
     for g in range(groups):
         at = slice(g * gw, (g + 1) * gw)
         carry[:, at] = dot(bc_ref[:, (groups + g) * STATE : (groups + g + 1) * STATE], enter_ref[:, at])
-    for r in range(0, BLK, ROWS):
+    size = y_ref.shape[0]
+    for r in range(0, size, ROWS):
         rows = slice(r, r + ROWS)
-        out_rows = pl.ds(pl.multiple_of(i * BLK + r, ROWS), ROWS)
+        out_rows = pl.ds(pl.multiple_of(i * size + r, ROWS), ROWS)
         for g in range(groups):
             at = slice(g * gw, (g + 1) * gw)
             y = y_ref[rows, at].astype(F32) + grown[rows, at] * carry[rows, at]
@@ -341,7 +342,7 @@
     chans = lax.axis_size("chan")
     features = out_weight.shape[1]
     map_width = parts * STATE
-    low, high = spread(0, heads, width), spread(2 * heads, heads, width)
+    low = spread(heads, width)
 
     tail = jnp.concatenate(
         [inner_input[tokens - HALO :], state_maps[tokens - HALO :].reshape(HALO, map_width)], 1
@@ -351,7 +352,7 @@
     def lanes_at(count):
         return pl.BlockSpec((count, WIDE), lambda c: (0, c))
 
-    xc, bc, bt, crow, cols, w_hl, g_hl, pay = pl.pallas_call(
+    xc, bc, bt, crow, cols, wrow, g_hl, pay = pl.pallas_call(
         states_kernel,
         grid=(width // WIDE,),
         in_specs=[
@@ -372,7 +373,7 @@
             whole((groups, STATE, tokens)),
             whole((heads, tokens)),
             whole((tokens, LANES)),
-            whole((tokens, LANES)),
+            whole((heads, tokens)),
             whole((tokens, LANES)),
             whole((STATE, width + LANES)),
         ],
@@ -382,11 +383,11 @@
             shaped((groups, STATE, tokens)),
             shaped((heads, tokens), F32),
             shaped((tokens, LANES), F32),
-            shaped((tokens, LANES)),
+            shaped((heads, tokens), F32),
             shaped((tokens, LANES)),
             shaped((STATE, width + LANES)),
         ],
-        scratch_shapes=[pltpu.VMEM((tokens, WIDE), BF16)],
+        scratch_shapes=[pltpu.VMEM((tokens, WIDE), BF16), pltpu.VMEM((tokens, LANES), BF16)],
         compiler_params=params(),
         name="states",
     )(
@@ -404,26 +405,23 @@
         def tile(width):
             return pl.BlockSpec((BLK, width), lambda b: (start + b, 0))
 
-        operands = [xc, bc, bt, crow, cols, w_hl, g_hl, skip_gain.reshape(1, heads), low, high]
+        operands = [xc, bc, bt, crow, cols, wrow, skip_gain.reshape(1, heads)]
         specs = [
             tile(width),
             tile(map_width),
             pl.BlockSpec((groups, STATE, BLK), lambda b: (0, 0, start + b)),
             pl.BlockSpec((heads, BLK), lambda b: (0, start + b)),
             tile(LANES),
-            tile(LANES),
-            tile(LANES),
-            whole((1, heads)),
-            whole((LANES, width)),
-            whole((LANES, width)),
+            pl.BlockSpec((heads, BLK), lambda b: (0, start + b)),
+            pl.BlockSpec(memory_space=pltpu.SMEM),
         ]
         aliases = {}
         if before is not None:
             y, state = before
             aliases = {len(operands) + 1: 0}
-            operands += [state, y]
+            operands += [state, in_hbm(y)]
             specs += [whole((STATE, width)), unread()]
-        operands.append(after)
+        operands.append(in_hbm(after))
         specs.append(unread())
         return pl.pallas_call(
             local_kernel,
@@ -432,13 +430,12 @@
             out_specs=[tile(width), whole((STATE, width))],
             out_shape=[shaped((tokens, width)), shaped((STATE, width), F32)],
             input_output_aliases=aliases,
-            scratch_shapes=[pltpu.VMEM((HALO, width), F32)],
             compiler_params=params(),
             cost_estimate=brief(),
             name="local_part",
         )(*operands)
 
-    some = blocks // 4
+    some = blocks // 2
     y_first = local_part(0, some, None, pay)
     entering = pl.pallas_call(
         prefix_kernel,
@@ -451,7 +448,7 @@
         out_specs=pl.BlockSpec(memory_space=pltpu.VMEM),
         compiler_params=pltpu.CompilerParams(vmem_limit_bytes=SMALL_LIMIT),
         name="prefix",
-    )(arrived, high, y_first[1])
+    )(arrived, low, in_hbm(y_first[0]))
     y_second = local_part(some, some, y_first, entering)
     entering = lax.all_to_all(entering, "seq", split_axis=0, concat_axis=0, tiled=True)
     entering = entering.reshape(STATE, width)
@@ -461,11 +458,11 @@
     mine = lax.axis_index("chan").astype(jnp.int32)
     where = mine.reshape(1)
 
-    def norm_operands(start, count, y):
+    def norm_operands(start, count, tokens_each, y):
         def tile(width):
-            return pl.BlockSpec((BLK, width), lambda i, *_: (start + jnp.minimum(i, count - 1), 0))
-
-        operands = [y, bc, g_hl, entering, gate_input, norm_row, high]
+            return pl.BlockSpec((tokens_each, width), lambda i, *_: (start + jnp.minimum(i, count - 1), 0))
+
+        operands = [y, bc, g_hl, entering, gate_input, norm_row, low]
         specs = [
             tile(width),
             tile(map_width),
@@ -477,9 +474,9 @@
         ]
         return operands, specs
 
-    def project_direct(start, count, y, after, slots):
-        operands, specs = norm_operands(start, count, y)
-        size = count * BLK
+    def project_direct(start, count, tokens_each, y, after, slots):
+        operands, specs = norm_operands(start, count, tokens_each, y)
+        size = count * tokens_each
 
         def weights(i, where):
             step = i - count
@@ -495,18 +492,18 @@
                 grid=(count + len(slots),),
                 in_specs=specs + [pl.BlockSpec((width, part_out), weights), unread()],
                 out_specs=[whole((size, part_out))] * len(slots) + [whole((size, width))],
-                scratch_shapes=[pltpu.VMEM((BLK, width), F32)] * 2,
+                scratch_shapes=[pltpu.VMEM((tokens_each, width), F32)] * 2,
             ),
             out_shape=[shaped((size, part_out))] * len(slots) + [shaped((size, width))],
             compiler_params=params(),
             name="project_direct",
-        )(where, *operands, out_weight, after)
+        )(where, *operands, out_weight, in_hbm(after))
 
     def direct_final(start, normed, pieces, out, after):
         def tile(width, start=0):
             return pl.BlockSpec((BLK, width), lambda i, where: (start + i, 0))
 
-        operands = [where, in_hbm(normed), in_hbm(out_weight)] + pieces + [after]
+        operands = [where, in_hbm(normed), in_hbm(out_weight)] + pieces + [in_hbm(after)]
         specs = [
             tile(width),
             pl.BlockSpec((width, part_out), lambda i, where: (0, where[0])),
@@ -515,7 +512,7 @@
         aliases = {}
         if out is not None:
             aliases = {len(operands): 0}
-            operands.append(out)
+            operands.append(in_hbm(out))
             specs.append(unread())
         return pl.pallas_call(
             functools.partial(direct_final_kernel, count=len(pieces)),
@@ -531,9 +528,9 @@
             name="direct_final",
         )(*operands)
 
-    def project_line(start, count, y, after):
-        operands, specs = norm_operands(start, count, y)
-        size = count * BLK
+    def project_line(start, count, tokens_each, split, y, after):
+        operands, specs = norm_operands(start, count, tokens_each, y)
+        size = count * tokens_each
 
         def dest(i):
             return jnp.maximum(i - count, 0)
@@ -546,13 +543,13 @@
             out_specs=[
                 pl.BlockSpec((1, size, part_out), lambda i: (dest(i), 0, 0)),
             ]
-            + [whole((size // 2, part_out))] * 4,
-            out_shape=[shaped((chans, size, part_out))] + [shaped((size // 2, part_out))] * 4,
-            scratch_shapes=[pltpu.VMEM((size, width), BF16)] + [pltpu.VMEM((BLK, width), F32)] * 2,
+            + [whole((k, part_out)) for k in split * 2],
+            out_shape=[shaped((chans, size, part_out))] + [shaped((k, part_out)) for k in split * 2],
+            scratch_shapes=[pltpu.VMEM((size, width), BF16)] + [pltpu.VMEM((tokens_each, width), F32)] * 2,
             compiler_params=params(),
             cost_estimate=brief(),
             name="project_line",
-        )(*operands, out_weight, after)
+        )(*operands, out_weight, in_hbm(after))
 
     def permuted(up, down, s):
         up = lax.ppermute(up, "chan", [(a, a + 1) for a in range(s + 1)])
@@ -561,6 +558,7 @@
 
     def onward(shares, half, up, down, s, after):
         count = up.shape[0] // BLK
+        skipped = (shares.shape[1] // BLK - count) * half
 
         def plain(i, where):
             return (i, 0)
@@ -574,13 +572,13 @@
                     pl.BlockSpec(
                         (1, BLK, part_out),
                         lambda i, where: (
-                            jnp.minimum(chans - 1 - s + where[0], chans - 1), half * count + i, 0
+                            jnp.minimum(chans - 1 - s + where[0], chans - 1), skipped + i, 0
                         ),
                     ),
                     pl.BlockSpec(
                         (1, BLK, part_out),
                         lambda i, where: (
-                            jnp.maximum(where[0] - (chans - 1) + s, 0), half * count + i, 0
+                            jnp.maximum(where[0] - (chans - 1) + s, 0), skipped + i, 0
                         ),
                     ),
                     pl.BlockSpec((BLK, part_out), plain),
@@ -589,27 +587,28 @@
                 ],
                 out_specs=[pl.BlockSpec((BLK, part_out), plain)] * 2,
             ),
-            out_shape=[shaped(up.shape)] * 2,
+            out_shape=[shaped((count * BLK, part_out))] * 2,
             compiler_params=params(SMALL_LIMIT),
             name="onward",
         )(where, in_hbm(shares), in_hbm(shares), up, down, after)
 
     def final(start, shares, half, up, down, out):
         count = up.shape[0] // BLK
+        skipped = (shares.shape[1] // BLK - count) * half
 
         def plain(i, where):
             return (i, 0)
 
         operands = [where, in_hbm(shares), up, down]
         in_specs = [
-            pl.BlockSpec((1, BLK, part_out), lambda i, where: (where[0], half * count + i, 0)),
+            pl.BlockSpec((1, BLK, part_out), lambda i, where: (where[0], skipped + i, 0)),
             pl.BlockSpec((BLK, part_out), plain),
             pl.BlockSpec((BLK, part_out), plain),
         ]
         aliases = {}
         if out is not None:
             aliases = {len(operands): 0}
-            operands.append(out)
+            operands.append(in_hbm(out))
             in_specs.append(unread())
         return pl.pallas_call(
             final_kernel,
@@ -617,7 +616,7 @@
                 num_scalar_prefetch=1,
                 grid=(count,),
                 in_specs=in_specs,
-                out_specs=pl.BlockSpec((BLK, part_out), lambda i, where: (start + half * count + i, 0)),
+                out_specs=pl.BlockSpec((BLK, part_out), lambda i, where: (start + skipped + i, 0)),
             ),
             out_shape=shaped((tokens, part_out)),
             input_output_aliases=aliases,
@@ -625,26 +624,29 @@
             name="final",
         )(*operands)
 
-    half = blocks // 2
+    lead = blocks * 3 // 8
     order = sorted(range(1, chans), key=lambda k: (min(k, chans - k), k))
-    *slots, normed = project_direct(0, half, y_second[0], y_second[1], order)
+    *slots, normed = project_direct(0, 2, lead * BLK // 2, y_second[0], y_second[1], order)
     pieces = []
     for k, slot in zip(order, slots):
         turn = [(a, (a + k) % chans) for a in range(chans)]
         pieces.append(lax.ppermute(slot, "chan", turn))
 
-    y_third = local_part(2 * some, blocks - 2 * some, y_second, normed)
-    shares, up_a, up_b, down_a, down_b = project_line(half, blocks - half, y_third[0], normed)
+    rest = blocks - lead
+    split = [(rest + 1) // 2 * BLK, rest // 2 * BLK]
+    shares, up_a, up_b, down_a, down_b = project_line(
+        lead, rest, BLK, split, y_second[0], normed
+    )
     moving = [permuted(up_a, down_a, 0), permuted(up_b, down_b, 0)]
     out = direct_final(0, normed, pieces, None, shares)
-    after = out
+    after = in_hbm(out)
     for s in range(1, chans - 1):
         for k in range(2):
             up, down = onward(shares, k, *moving[k], s, after)
             after = up
             moving[k] = permuted(up, down, s)
     for k in range(2):
-        out = final(half, shares, k, *moving[k], out)
+        out = final(lead, shares, k, *moving[k], out)
     return out
 
 

time: 155 us -> 143 us (0.923)
  local copies, waits for them, and re-layouts: 6.93 us -> 2.89 us
  waiting for transfers between devices: 23.1 us -> 19.3 us
  Pallas kernels: 74.1 us -> 70.3 us
    pallas_call x3 -> x2, Pallas kernels: 20.5 us -> 15.7 us  [local_part(): pl.pallas_call(local_kernel, grid=(count,), in_specs=specs, out_specs=[ti...]
    unnamed x12 -> x6, local copies, waits for them, and re-layouts: 5.45 us -> 1.41 us
    ppermute x3, waiting for transfers between devices: 9.26 us -> 6.46 us  [local(): pieces.append(lax.ppermute(slot, 'chan', turn))]
    pallas_call x1, Pallas kernels: 12.3 us -> 10 us  [project_direct(): pl.pallas_call(functools.partial(direct_kernel, tiles=count), grid_spec=p...]
    all_to_all x1, waiting for transfers between devices: 2.26 us -> 0.12 us  [local(): lax.all_to_all(entering, 'seq', split_axis=0, concat_axis=0, tiled=True)]
    pallas_call x1, Pallas kernels: 13.4 us -> 15.3 us  [project_line(): pl.pallas_call(functools.partial(line_kernel, tiles=count), grid=(count +...]
    ppermute x6, waiting for transfers between devices: 1.59 us -> 3.45 us  [permuted(): up = lax.ppermute(up, 'chan', [(a, a + 1) for a in range(s + 1)])]
    pallas_call x4, Pallas kernels: 4.82 us -> 6.67 us  [onward(): pl.pallas_call(onward_kernel, grid_spec=pltpu.PrefetchScalarGridSpec(num_...]
  transfers between devices with their start and end apart: 18 -> 18, of which waited for: 6 -> 7; matrix products, arithmetic and copies ran while one was open for 0% -> 0% of each run, Pallas kernels for 30% -> 32%
where the time goes in v7:
time: 143 us; the launch traced here: 141 us
  Pallas kernels  70.3 us (49%)
  starting transfers between devices  48.2 us (34%)
  waiting for transfers between devices  19.3 us (13%)
  local copies, waits for them, and re-layouts  2.89 us (2%)
    ppermute x6, starting transfers between devices, permuted(): up = lax.ppermute(up, 'chan', [(a, a + 1) for a in range(s + 1)])  27.1 us
    pallas_call x2, Pallas kernels, local_part(): pl.pallas_call(local_kernel, grid=(count,), in_specs=specs, out_specs=[ti...  15.7 us
    pallas_call x1, Pallas kernels, project_line(): pl.pallas_call(functools.partial(line_kernel, tiles=count), grid=(count +...  15.3 us
    pallas_call x1, Pallas kernels, local(): pl.pallas_call(states_kernel, grid=(width // WIDE,), in_specs=[lanes_at(t...  12.7 us
    pallas_call x1, Pallas kernels, project_direct(): pl.pallas_call(functools.partial(direct_kernel, tiles=count), grid_spec=p...  10 us
    pallas_call x4, Pallas kernels, onward(): pl.pallas_call(onward_kernel, grid_spec=pltpu.PrefetchScalarGridSpec(num_...  6.67 us
    ppermute x3, waiting for transfers between devices, local(): pieces.append(lax.ppermute(slot, 'chan', turn))  6.46 us
    ppermute x6, starting transfers between devices, permuted(): lax.ppermute(down, 'chan', [(a, a - 1) for a in range(chans - 1 - s, chan...  5.31 us
  transfers between devices with their start and end apart: 18, of which 7 were waited for; matrix products, arithmetic and copies ran while one was open for 0% of the time, Pallas kernels for 32%

profile of v7, /device:TPU:2, one launch (start us, length us, event | category | flops | bytes accessed | tf_op | source)
XLA Modules:
  0.0 140.9 jit_solution(13941873308365634249)
XLA Ops:
  0.0 0.8 slice.6
  0.8 0.7 slice.7
  1.5 1.9 %collective-permute-start = (bf16[8,2560]{1,0:T(8,128)(2,1)S(1)}, bf16[8,2560]{1,0:T(8,128)(2,1)S(1)}, u32[]{:S(2)}, u32[]{:S(2)}) collective-permute-start(bf16[8,2560]{1,0:T(8,128)(2,1)S(1)} %pad_maximum_fusion), channel_id=1, source_target_pairs={{0,4},{4,8},{8,12},{12,16},{16,20},{20,24},{24,28},{1,5},{5,9},{9,... | collective-permute-start | bytes 122888 | tf_op jit(solution)/shard_map/ppermute | solution.py:350
  3.4 3.4 %collective-permute-done.tail_ref.mtail_ref = bf16[8,2560]{1,0:T(8,128)(2,1)S(1)} collective-permute-done((bf16[8,2560]{1,0:T(8,128)(2,1)S(1)}, bf16[8,2560]{1,0:T(8,128)(2,1)S(1)}, u32[]{:S(2)}, u32[]{:S(2)}) %collective-permute-start) | collective-permute-done | bytes 40992 | tf_op jit(solution)/shard_map/ppermute | solution.py:350
  6.8 0.0 copy-start.2
  6.8 0.6 copy-done.2
  7.4 12.7 %states.1 = (bf16[1024,2048]{1,0:T(8,128)(2,1)}, bf16[1024,512]{1,0:T(8,128)(2,1)}, bf16[2,128,1024]{2,1,0:T(8,128)(2,1)}, f32[32,1024]{1,0:T(8,128)}, f32[1024,...) custom-call(bf16[1024,2048]{1,0:T(8,128)(2,1)} %x_ref.1, ...), custom_call_target="tpu_custom_call" | custom-call | tf_op jit(solution)/shard_map/states/pallas_call | solution.py:355
  20.1 0.0 copy-start
  20.1 4.4 %all-to-all-start = ((bf16[8,16,2176]{2,1,0:T(8,128)(2,1)}), bf16[8,16,2176]{2,1,0:T(8,128)(2,1)S(1)}, u32[]{:S(2)}, u32[]{:S(2)}) async-start(bf16[8,16,2176]{2,1,0:T(8,128)(2,1)} %bitcast.12), calls=%async_computation | async-start | bytes 1114112 | tf_op jit(solution)/shard_map/all_to_all | solution.py:400
  24.5 7.5 %local_part.2 = (bf16[1024,2048]{1,0:T(8,128)(2,1)}, f32[128,2048]{1,0:T(8,128)}) custom-call(bf16[1024,2048]{1,0:T(8,128)(2,1)} %get-tuple-element.34.xc_ref, bf16[1024,512]{1,0:T(8,128)(2,1)} %get-tuple-element.35.bc_ref, bf16[2,128,1024]{2,1,0:T(8,128)(2,1)} %get-tuple-element.36.bt_ref, f32[32,1024]{1,0:T(8,128)} %get-tuple-element.37.crow_ref, ...), custom_call_target="tpu_custom_call" | custom-call | flops 1 | bytes 1 | tf_op jit(solution)/shard_map/local_part/pallas_call | solution.py:426
  32.1 1.1 all-to-all-done.pay_ref
  33.2 0.0 copy-done
  33.2 1.1 prefix.1.rest_2_
  34.2 4.9 %all-to-all-start.1 = ((bf16[8,16,2048]{2,1,0:T(8,128)(2,1)}), bf16[8,16,2048]{2,1,0:T(8,128)(2,1)S(1)}, u32[]{:S(2)}, u32[]{:S(2)}) async-start(bf16[8,16,2048]{2,1,0:T(8,128)(2,1)} %prefix.1.rest_2_), calls=%async_computation.1 | async-start | bytes 1048576 | tf_op jit(solution)/shard_map/all_to_all | solution.py:453
  39.1 8.2 %local_part.3 = (bf16[1024,2048]{1,0:T(8,128)(2,1)}, f32[128,2048]{1,0:T(8,128)}) custom-call(bf16[1024,2048]{1,0:T(8,128)(2,1)} %get-tuple-element.34.xc_ref, bf16[1024,512]{1,0:T(8,128)(2,1)} %get-tuple-element.35.bc_ref, bf16[2,128,1024]{2,1,0:T(8,128)(2,1)} %get-tuple-element.36.bt_ref, ...), custom_call_target="tpu_custom_call", output_to_operand_aliasing={{0}: (8, {})} | custom-call | flops 1 | bytes 1 | tf_op jit(solution)/shard_map/local_part/pallas_call | solution.py:426
  47.3 0.1 all-to-all-done.1
  47.4 0.0 copy-start.1
  47.4 0.8 copy-done.1
  48.2 10.0 %project_direct.1 = (bf16[384,512]{1,0:T(8,128)(2,1)}, bf16[384,512]{1,0:T(8,128)(2,1)}, bf16[384,512]{1,0:T(8,128)(2,1)}, bf16[384,2048]{1,0:T(8,128)(2,1)}) custom-call(s32[1]{0:T(128)} %bitcast.where_ref, bf16[1024,2048]{1,0:T(8,128)(2,1)} %get-tuple-element.43.y_ref, bf16[1024,512]{1,0:T(8,128)(2,1)} %get-tuple-element.35.bc_ref, ...), custom_call_target="tpu_custom_call" | custom-call | tf_op jit(solution)/shard_map/project_direct/pallas_call | solution.py:488
  58.2 1.6 %collective-permute-start.5 = (bf16[384,512]{1,0:T(8,128)(2,1)}, bf16[384,512]{1,0:T(8,128)(2,1)S(1)}, u32[]{:S(2)}, u32[]{:S(2)}) collective-permute-start(bf16[384,512]{1,0:T(8,128)(2,1)} %get-tuple-element.52), channel_id=1, source_target_pairs={{0,1},{1,2},{2,3},{3,0},{4,5},{5,6},{6,7},{7,4},{8,9},{9,10},{10,1... | collective-permute-start | bytes 1179656 | tf_op jit(solution)/shard_map/ppermute | solution.py:633
  59.8 2.2 %collective-permute-start.6 = (bf16[384,512]{1,0:T(8,128)(2,1)}, bf16[384,512]{1,0:T(8,128)(2,1)S(1)}, u32[]{:S(2)}, u32[]{:S(2)}) collective-permute-start(bf16[384,512]{1,0:T(8,128)(2,1)} %get-tuple-element.53), channel_id=1, source_target_pairs={{0,3},{1,0},{2,1},{3,2},{4,7},{5,4},{6,5},{7,6},{8,11},{9,8},{10,9... | collective-permute-start | bytes 1179656 | tf_op jit(solution)/shard_map/ppermute | solution.py:633
  62.0 0.8 collective-permute-start.7
  62.8 15.3 %project_line.1 = (bf16[4,640,512]{2,1,0:T(8,128)(2,1)}, bf16[384,512]{1,0:T(8,128)(2,1)}, bf16[256,512]{1,0:T(8,128)(2,1)}, bf16[384,512]{1,0:T(8,128)(2,1)}, bf16[256,512]{1,0:T(8,128)(2,1)}) custom-call(bf16[1024,2048]{1,0:T(8,128)(2,1)} %get-tuple-element.43.y_ref, bf16[1024,512]{1,0:T(8,128)(2,1)} %get-tuple-element.35.bc_ref, ...), custom_call_target="tpu_custom_call" | custom-call | flops 1 | bytes 1 | tf_op jit(solution)/shard_map/project_line/pallas_call | solution.py:538
  78.2 3.5 %collective-permute-start.3 = (bf16[384,512]{1,0:T(8,128)(2,1)}, bf16[384,512]{1,0:T(8,128)(2,1)S(1)}, u32[]{:S(2)}, u32[]{:S(2)}) collective-permute-start(bf16[384,512]{1,0:T(8,128)(2,1)} %get-tuple-element.50), channel_id=1, source_target_pairs={{0,1},{4,5},{8,9},{12,13},{16,17},{20,21},{24,25},{28,29}} | collective-permute-start | bytes 1179656 | tf_op jit(solution)/shard_map/ppermute | solution.py:555
  81.7 0.7 collective-permute-start.4
  82.4 0.0 collective-permute-done.5.refs_0_
  82.4 7.1 %collective-permute-start.1 = (bf16[256,512]{1,0:T(8,128)(2,1)}, bf16[256,512]{1,0:T(8,128)(2,1)S(1)}, u32[]{:S(2)}, u32[]{:S(2)}) collective-permute-start(bf16[256,512]{1,0:T(8,128)(2,1)} %get-tuple-element.48), channel_id=1, source_target_pairs={{0,1},{4,5},{8,9},{12,13},{16,17},{20,21},{24,25},{28,29}} | collective-permute-start | bytes 786440 | tf_op jit(solution)/shard_map/ppermute | solution.py:555
  89.5 0.0 collective-permute-done.6.refs_1_
  89.5 0.7 collective-permute-start.2
  90.2 6.5 %collective-permute-done.7.refs_2_ = bf16[384,512]{1,0:T(8,128)(2,1)S(1)} collective-permute-done((bf16[384,512]{1,0:T(8,128)(2,1)}, bf16[384,512]{1,0:T(8,128)(2,1)S(1)}, u32[]{:S(2)}, u32[]{:S(2)}) %collective-permute-start.7) | collective-permute-done | bytes 393248 | tf_op jit(solution)/shard_map/ppermute | solution.py:633
  96.6 4.5 %direct_final.1.after_ref.rest_0_ = bf16[1024,512]{1,0:T(8,128)(2,1)} custom-call(s32[1]{0:T(128)} %bitcast.where_ref, bf16[384,2048]{1,0:T(8,128)(2,1)} %get-tuple-element.46.after_ref.normed_ref, bf16[2048,2048]{1,0:T(8,128)(2,1)} %w_ref.5, bf16[384,512]{1,0:T(8,128)(2,1)S(1)} %collective-permute-done.5.refs_0_, ...), custom_call_target="tpu_custom_call" | custom-call | tf_op jit(solution)/shard_map/direct_final/pallas_call | solution.py:517
  101.1 0.0 collective-permute-done.3.up_ref
  101.1 0.0 collective-permute-done.4.down_ref
  101.1 2.1 %onward.4 = (bf16[384,512]{1,0:T(8,128)(2,1)S(1)}, bf16[384,512]{1,0:T(8,128)(2,1)S(1)}) custom-call(s32[1]{0:T(128)} %bitcast.where_ref, bf16[4,640,512]{2,1,0:T(8,128)(2,1)} %get-tuple-element.47.refs_3_.up_own_ref.down_own_ref.own_ref, bf16[4,640,512]{2,1,0:T(8,128)(2,1)} %get-tuple-element.47.refs_3_.up_own_ref.down_own_ref.own_ref, ...), custom_call_target="tpu_custom_call" | custom-call | tf_op jit(solution)/shard_map/onward/pallas_call | solution.py:566
  103.2 1.3 collective-permute-start.10
  104.6 0.7 collective-permute-start.11
  105.3 0.0 collective-permute-done.1.up_ref
  105.3 0.0 collective-permute-done.2.down_ref
  105.3 1.2 onward.5
  106.5 3.3 %collective-permute-start.8 = (bf16[256,512]{1,0:T(8,128)(2,1)S(1)}, bf16[256,512]{1,0:T(8,128)(2,1)S(1)}, u32[]{:S(2)}, u32[]{:S(2)}) collective-permute-start(bf16[256,512]{1,0:T(8,128)(2,1)S(1)} %get-tuple-element.56.after_ref), channel_id=1, source_target_pairs={{0,1},{1,2},{4,5},{5,6},{8,9},{9,10},{12,13},{13,14},{16,17},{17,1... | collective-permute-start | bytes 786440 | tf_op jit(solution)/shard_map/ppermute | solution.py:555
  109.9 0.7 collective-permute-start.9
  110.5 3.4 %collective-permute-done.10.up_ref = bf16[384,512]{1,0:T(8,128)(2,1)S(1)} collective-permute-done((bf16[384,512]{1,0:T(8,128)(2,1)S(1)}, bf16[384,512]{1,0:T(8,128)(2,1)S(1)}, u32[]{:S(2)}, u32[]{:S(2)}) %collective-permute-start.10) | collective-permute-done | bytes 393248 | tf_op jit(solution)/shard_map/ppermute | solution.py:555
  114.0 0.0 collective-permute-done.11.down_ref
  114.0 2.1 %onward.6 = (bf16[384,512]{1,0:T(8,128)(2,1)S(1)}, bf16[384,512]{1,0:T(8,128)(2,1)S(1)}) custom-call(s32[1]{0:T(128)} %bitcast.where_ref, bf16[4,640,512]{2,1,0:T(8,128)(2,1)} %get-tuple-element.47.refs_3_.up_own_ref.down_own_ref.own_ref, bf16[4,640,512]{2,1,0:T(8,128)(2,1)} %get-tuple-element.47.refs_3_.up_own_ref.down_own_ref.own_ref, ...), custom_call_target="tpu_custom_call" | custom-call | tf_op jit(solution)/shard_map/onward/pallas_call | solution.py:566
  116.1 7.2 %collective-permute-start.14 = (bf16[384,512]{1,0:T(8,128)(2,1)S(1)}, bf16[384,512]{1,0:T(8,128)(2,1)S(1)}, u32[]{:S(2)}, u32[]{:S(2)}) collective-permute-start(bf16[384,512]{1,0:T(8,128)(2,1)S(1)} %get-tuple-element.59.after_ref), channel_id=1, source_target_pairs={{0,1},{1,2},{2,3},{4,5},{5,6},{6,7},{8,9},{9,10},{10,11},{12,13},{... | collective-permute-start | bytes 1179656 | tf_op jit(solution)/shard_map/ppermute | solution.py:555
  123.3 1.3 collective-permute-start.15
  124.6 0.0 collective-permute-done.8.up_ref
  124.7 0.0 collective-permute-done.9.down_ref
  124.7 1.2 onward.7
  125.9 4.6 %collective-permute-start.12 = (bf16[256,512]{1,0:T(8,128)(2,1)S(1)}, bf16[256,512]{1,0:T(8,128)(2,1)S(1)}, u32[]{:S(2)}, u32[]{:S(2)}) collective-permute-start(bf16[256,512]{1,0:T(8,128)(2,1)S(1)} %get-tuple-element.60), channel_id=1, source_target_pairs={{0,1},{1,2},{2,3},{4,5},{5,6},{6,7},{8,9},{9,10},{10,11},{12,13},{... | collective-permute-start | bytes 786440 | tf_op jit(solution)/shard_map/ppermute | solution.py:555
  130.5 1.3 collective-permute-start.13
  131.8 0.0 collective-permute-done.14.up_ref
  131.8 3.6 %collective-permute-done.15.down_ref = bf16[384,512]{1,0:T(8,128)(2,1)S(1)} collective-permute-done((bf16[384,512]{1,0:T(8,128)(2,1)S(1)}, bf16[384,512]{1,0:T(8,128)(2,1)S(1)}, u32[]{:S(2)}, u32[]{:S(2)}) %collective-permute-start.15) | collective-permute-done | bytes 393248 | tf_op jit(solution)/shard_map/ppermute | solution.py:556
  135.4 2.7 %final.2.rest_0_ = bf16[1024,512]{1,0:T(8,128)(2,1)} custom-call(s32[1]{0:T(128)} %bitcast.where_ref, bf16[4,640,512]{2,1,0:T(8,128)(2,1)} %get-tuple-element.47.refs_3_.up_own_ref.down_own_ref.own_ref, bf16[384,512]{1,0:T(8,128)(2,1)S(1)} %collective-permute-done.14.up_ref, ...), custom_call_target="tpu_custom_call", output_to_operand_aliasing={{}: (4, {})} | custom-call | tf_op jit(solution)/shard_map/final/pallas_call | solution.py:613
  138.0 0.0 collective-permute-done.12.up_ref
  138.1 1.1 collective-permute-done.13.down_ref
  139.2 1.7 %final.3 = bf16[1024,512]{1,0:T(8,128)(2,1)} custom-call(s32[1]{0:T(128)} %bitcast.where_ref, bf16[4,640,512]{2,1,0:T(8,128)(2,1)} %get-tuple-element.47.refs_3_.up_own_ref.down_own_ref.own_ref, bf16[256,512]{1,0:T(8,128)(2,1)S(1)} %collective-permute-done.12.up_ref, ...), custom_call_target="tpu_custom_call", output_to_operand_aliasing={{}: (4, {})} | custom-call | tf_op jit(solution)/shard_map/final/pallas_call | solution.py:613
  (2 shorter events, 0.0 us)
Async XLA Ops:
  1.5 5.3 %collective-permute-start = (bf16[8,2560]{1,0:T(8,128)(2,1)S(1)}, bf16[8,2560]{1,0:T(8,128)(2,1)S(1)}, u32[]{:S(2)}, u32[]{:S(2)}) collective-permute-start(bf16[8,2560]{1,0:T(8,128)(2,1)S(1)} %pad_maximum_fusion), channel_id=1, source_target_pairs={{0,4},{4,8},{8,12},{12,16},{16,20},{20,24},{24,28},{1,5},{5,9},{9,... | collective-permute-start | bytes 122888 | tf_op jit(solution)/shard_map/ppermute | solution.py:350
  6.8 0.6 copy-start.2
  20.1 13.0 %copy-start = (bf16[128,2048]{1,0:T(8,128)(2,1)S(1)}, bf16[128,2048]{1,0:T(8,128)(2,1)}, u32[]{:S(2)}) copy-start(bf16[128,2048]{1,0:T(8,128)(2,1)} %constant.6.clone.e_ref) | copy-start | bytes 1572868
  20.1 13.0 %all-to-all-start = ((bf16[8,16,2176]{2,1,0:T(8,128)(2,1)}), bf16[8,16,2176]{2,1,0:T(8,128)(2,1)S(1)}, u32[]{:S(2)}, u32[]{:S(2)}) async-start(bf16[8,16,2176]{2,1,0:T(8,128)(2,1)} %bitcast.12), calls=%async_computation | async-start | bytes 1114112 | tf_op jit(solution)/shard_map/all_to_all | solution.py:400
  34.2 13.2 %all-to-all-start.1 = ((bf16[8,16,2048]{2,1,0:T(8,128)(2,1)}), bf16[8,16,2048]{2,1,0:T(8,128)(2,1)S(1)}, u32[]{:S(2)}, u32[]{:S(2)}) async-start(bf16[8,16,2048]{2,1,0:T(8,128)(2,1)} %prefix.1.rest_2_), calls=%async_computation.1 | async-start | bytes 1048576 | tf_op jit(solution)/shard_map/all_to_all | solution.py:453
  47.4 0.8 copy-start.1
  58.2 24.2 %collective-permute-start.5 = (bf16[384,512]{1,0:T(8,128)(2,1)}, bf16[384,512]{1,0:T(8,128)(2,1)S(1)}, u32[]{:S(2)}, u32[]{:S(2)}) collective-permute-start(bf16[384,512]{1,0:T(8,128)(2,1)} %get-tuple-element.52), channel_id=1, source_target_pairs={{0,1},{1,2},{2,3},{3,0},{4,5},{5,6},{6,7},{7,4},{8,9},{9,10},{10,1... | collective-permute-start | bytes 1179656 | tf_op jit(solution)/shard_map/ppermute | solution.py:633
  59.8 29.7 %collective-permute-start.6 = (bf16[384,512]{1,0:T(8,128)(2,1)}, bf16[384,512]{1,0:T(8,128)(2,1)S(1)}, u32[]{:S(2)}, u32[]{:S(2)}) collective-permute-start(bf16[384,512]{1,0:T(8,128)(2,1)} %get-tuple-element.53), channel_id=1, source_target_pairs={{0,3},{1,0},{2,1},{3,2},{4,7},{5,4},{6,5},{7,6},{8,11},{9,8},{10,9... | collective-permute-start | bytes 1179656 | tf_op jit(solution)/shard_map/ppermute | solution.py:633
  62.0 34.6 %collective-permute-start.7 = (bf16[384,512]{1,0:T(8,128)(2,1)}, bf16[384,512]{1,0:T(8,128)(2,1)S(1)}, u32[]{:S(2)}, u32[]{:S(2)}) collective-permute-start(bf16[384,512]{1,0:T(8,128)(2,1)} %get-tuple-element.54), channel_id=1, source_target_pairs={{0,2},{1,3},{2,0},{3,1},{4,6},{5,7},{6,4},{7,5},{8,10},{9,11},{10,... | collective-permute-start | bytes 1179656 | tf_op jit(solution)/shard_map/ppermute | solution.py:633
  78.2 23.0 %collective-permute-start.3 = (bf16[384,512]{1,0:T(8,128)(2,1)}, bf16[384,512]{1,0:T(8,128)(2,1)S(1)}, u32[]{:S(2)}, u32[]{:S(2)}) collective-permute-start(bf16[384,512]{1,0:T(8,128)(2,1)} %get-tuple-element.50), channel_id=1, source_target_pairs={{0,1},{4,5},{8,9},{12,13},{16,17},{20,21},{24,25},{28,29}} | collective-permute-start | bytes 1179656 | tf_op jit(solution)/shard_map/ppermute | solution.py:555
  81.7 19.4 %collective-permute-start.4 = (bf16[384,512]{1,0:T(8,128)(2,1)}, bf16[384,512]{1,0:T(8,128)(2,1)S(1)}, u32[]{:S(2)}, u32[]{:S(2)}) collective-permute-start(bf16[384,512]{1,0:T(8,128)(2,1)} %get-tuple-element.51), channel_id=1, source_target_pairs={{3,2},{7,6},{11,10},{15,14},{19,18},{23,22},{27,26},{31,30}} | collective-permute-start | bytes 1179656 | tf_op jit(solution)/shard_map/ppermute | solution.py:556
  82.4 22.9 %collective-permute-start.1 = (bf16[256,512]{1,0:T(8,128)(2,1)}, bf16[256,512]{1,0:T(8,128)(2,1)S(1)}, u32[]{:S(2)}, u32[]{:S(2)}) collective-permute-start(bf16[256,512]{1,0:T(8,128)(2,1)} %get-tuple-element.48), channel_id=1, source_target_pairs={{0,1},{4,5},{8,9},{12,13},{16,17},{20,21},{24,25},{28,29}} | collective-permute-start | bytes 786440 | tf_op jit(solution)/shard_map/ppermute | solution.py:555
  89.5 15.8 %collective-permute-start.2 = (bf16[256,512]{1,0:T(8,128)(2,1)}, bf16[256,512]{1,0:T(8,128)(2,1)S(1)}, u32[]{:S(2)}, u32[]{:S(2)}) collective-permute-start(bf16[256,512]{1,0:T(8,128)(2,1)} %get-tuple-element.49), channel_id=1, source_target_pairs={{3,2},{7,6},{11,10},{15,14},{19,18},{23,22},{27,26},{31,30}} | collective-permute-start | bytes 786440 | tf_op jit(solution)/shard_map/ppermute | solution.py:556
  103.2 10.7 %collective-permute-start.10 = (bf16[384,512]{1,0:T(8,128)(2,1)S(1)}, bf16[384,512]{1,0:T(8,128)(2,1)S(1)}, u32[]{:S(2)}, u32[]{:S(2)}) collective-permute-start(bf16[384,512]{1,0:T(8,128)(2,1)S(1)} %get-tuple-element.55.after_ref), channel_id=1, source_target_pairs={{0,1},{1,2},{4,5},{5,6},{8,9},{9,10},{12,13},{13,14},{16,17},{17,1... | collective-permute-start | bytes 1179656 | tf_op jit(solution)/shard_map/ppermute | solution.py:555
  104.6 9.4 %collective-permute-start.11 = (bf16[384,512]{1,0:T(8,128)(2,1)S(1)}, bf16[384,512]{1,0:T(8,128)(2,1)S(1)}, u32[]{:S(2)}, u32[]{:S(2)}) collective-permute-start(bf16[384,512]{1,0:T(8,128)(2,1)S(1)} %get-tuple-element.58), channel_id=1, source_target_pairs={{2,1},{3,2},{6,5},{7,6},{10,9},{11,10},{14,13},{15,14},{18,17},{19... | collective-permute-start | bytes 1179656 | tf_op jit(solution)/shard_map/ppermute | solution.py:556
  106.5 18.1 %collective-permute-start.8 = (bf16[256,512]{1,0:T(8,128)(2,1)S(1)}, bf16[256,512]{1,0:T(8,128)(2,1)S(1)}, u32[]{:S(2)}, u32[]{:S(2)}) collective-permute-start(bf16[256,512]{1,0:T(8,128)(2,1)S(1)} %get-tuple-element.56.after_ref), channel_id=1, source_target_pairs={{0,1},{1,2},{4,5},{5,6},{8,9},{9,10},{12,13},{13,14},{16,17},{17,1... | collective-permute-start | bytes 786440 | tf_op jit(solution)/shard_map/ppermute | solution.py:555
  109.9 14.8 %collective-permute-start.9 = (bf16[256,512]{1,0:T(8,128)(2,1)S(1)}, bf16[256,512]{1,0:T(8,128)(2,1)S(1)}, u32[]{:S(2)}, u32[]{:S(2)}) collective-permute-start(bf16[256,512]{1,0:T(8,128)(2,1)S(1)} %get-tuple-element.57), channel_id=1, source_target_pairs={{2,1},{3,2},{6,5},{7,6},{10,9},{11,10},{14,13},{15,14},{18,17},{19... | collective-permute-start | bytes 786440 | tf_op jit(solution)/shard_map/ppermute | solution.py:556
  116.1 15.7 %collective-permute-start.14 = (bf16[384,512]{1,0:T(8,128)(2,1)S(1)}, bf16[384,512]{1,0:T(8,128)(2,1)S(1)}, u32[]{:S(2)}, u32[]{:S(2)}) collective-permute-start(bf16[384,512]{1,0:T(8,128)(2,1)S(1)} %get-tuple-element.59.after_ref), channel_id=1, source_target_pairs={{0,1},{1,2},{2,3},{4,5},{5,6},{6,7},{8,9},{9,10},{10,11},{12,13},{... | collective-permute-start | bytes 1179656 | tf_op jit(solution)/shard_map/ppermute | solution.py:555
  123.3 12.0 %collective-permute-start.15 = (bf16[384,512]{1,0:T(8,128)(2,1)S(1)}, bf16[384,512]{1,0:T(8,128)(2,1)S(1)}, u32[]{:S(2)}, u32[]{:S(2)}) collective-permute-start(bf16[384,512]{1,0:T(8,128)(2,1)S(1)} %get-tuple-element.62), channel_id=1, source_target_pairs={{1,0},{2,1},{3,2},{5,4},{6,5},{7,6},{9,8},{10,9},{11,10},{13,12},{... | collective-permute-start | bytes 1179656 | tf_op jit(solution)/shard_map/ppermute | solution.py:556
  125.9 12.2 %collective-permute-start.12 = (bf16[256,512]{1,0:T(8,128)(2,1)S(1)}, bf16[256,512]{1,0:T(8,128)(2,1)S(1)}, u32[]{:S(2)}, u32[]{:S(2)}) collective-permute-start(bf16[256,512]{1,0:T(8,128)(2,1)S(1)} %get-tuple-element.60), channel_id=1, source_target_pairs={{0,1},{1,2},{2,3},{4,5},{5,6},{6,7},{8,9},{9,10},{10,11},{12,13},{... | collective-permute-start | bytes 786440 | tf_op jit(solution)/shard_map/ppermute | solution.py:555
  130.5 8.7 %collective-permute-start.13 = (bf16[256,512]{1,0:T(8,128)(2,1)S(1)}, bf16[256,512]{1,0:T(8,128)(2,1)S(1)}, u32[]{:S(2)}, u32[]{:S(2)}) collective-permute-start(bf16[256,512]{1,0:T(8,128)(2,1)S(1)} %get-tuple-element.61), channel_id=1, source_target_pairs={{1,0},{2,1},{3,2},{5,4},{6,5},{7,6},{9,8},{10,9},{11,10},{13,12},{... | collective-permute-start | bytes 786440 | tf_op jit(solution)/shard_map/ppermute | solution.py:556

commit v8 on v7

--- a/solution.py
+++ b/solution.py
@@ -71,13 +71,13 @@
     late = pltpu.roll(full, 1, 0)
     early = taps[1] * full + taps[0] * late
     acc = taps[3] * cur + taps[2] * late[HALO:] + pltpu.roll(early, 2, 0)[HALO:]
-    return silu(acc).astype(BF16)
+    return silu(acc)
 
 
 def states_kernel(
     x_ref, maps_ref, step_ref, tail_ref, mtail_ref, bias_ref, rate_ref, ck_ref, mk_ref, e_ref,
     xc_ref, bc_ref, bt_ref, crow_ref, cols_ref, wrow_ref, g_ref, pay_ref,
-    weighted, w_ref,
+    weighted, w_ref, scale,
 ):
     c = pl.program_id(0)
     heads, tokens = step_ref.shape
@@ -126,22 +126,27 @@
             cols_ref[at, :] = padded((cum * LOG2E,)).T
         pay_ref[:, heads * HEAD_DIM :] = jnp.broadcast_to(last[BLK - 1 :], (STATE, LANES)).astype(BF16)
 
-        row = lax.broadcasted_iota(jnp.int32, (BLK * parts, BLK * parts), 0)
-        col = lax.broadcasted_iota(jnp.int32, (BLK * parts, BLK * parts), 1)
-        source = (row & (BLK - 1)) * parts + row // BLK
+        few = BLK // 2
+        row = lax.broadcasted_iota(jnp.int32, (few * parts, few * parts), 0)
+        col = lax.broadcasted_iota(jnp.int32, (few * parts, few * parts), 1)
+        source = (row & (few - 1)) * parts + row // few
         pick = jnp.where(col == source, 1.0, 0.0).astype(BF16)
         before = [mtail_ref[:, q * STATE : (q + 1) * STATE].astype(F32) for q in range(parts)]
         for b in range(blocks):
-            ordered = dot(pick, maps_ref[b * BLK * parts : (b + 1) * BLK * parts, :])
+            at = 2 * b * few * parts
+            mixed = [maps_ref[at + k * few * parts : at + (k + 1) * few * parts] for k in range(2)]
+            ordered = dot(pick, jnp.concatenate(mixed, 1))
             for q in range(parts):
-                cur = ordered[q * BLK : (q + 1) * BLK]
+                own = ordered[q * few : (q + 1) * few]
+                cur = jnp.concatenate([own[:, :STATE], own[:, STATE:]], 0)
                 taps = [mk_ref[k * parts + q : k * parts + q + 1] for k in range(4)]
-                result = conv(before[q], cur, taps)
+                result = conv(before[q], cur, taps).astype(BF16)
                 before[q] = cur[BLK - HALO :]
                 bc_ref[b * BLK : (b + 1) * BLK, q * STATE : (q + 1) * STATE] = result
                 if q < groups:
                     bt_ref[q, :, b * BLK : (b + 1) * BLK] = result.astype(F32).T.astype(BF16)
 
+    scale[...] = dot(w_ref[...], e_ref[...])
     for lane in range(0, x_ref.shape[1], LANES):
         at_lanes = slice(lane, lane + LANES)
         taps = [ck_ref[k : k + 1, at_lanes] for k in range(4)]
@@ -151,9 +156,8 @@
             cur = x_ref[at, at_lanes].astype(F32)
             result = conv(before, cur, taps)
             before = cur[BLK - HALO :]
-            xc_ref[at, at_lanes] = result
-            scale = dot(w_ref[at, :], e_ref[:, at_lanes])
-            weighted[at, at_lanes] = (result.astype(F32) * scale).astype(BF16)
+            xc_ref[at, at_lanes] = result.astype(BF16)
+            weighted[at, at_lanes] = (result * scale[at, at_lanes]).astype(BF16)
     step_width = x_ref.shape[1]
     group = c * step_width * groups // (heads * HEAD_DIM)
     at = pl.ds(pl.multiple_of(c * step_width, step_width), step_width)
@@ -286,7 +290,8 @@
         up_b_ref[...] = shares_ref[0, size:]
 
 
-def onward_kernel(where_ref, up_own_ref, down_own_ref, up_ref, down_ref, after_ref, up_out, down_out):
+def onward_kernel(where_ref, up_own_ref, down_own_ref, up_ref, down_ref, *rest):
+    up_out, down_out = rest[-2:]
     up_out[...] = (up_own_ref[0].astype(F32) + up_ref[...].astype(F32)).astype(BF16)
     down_out[...] = (down_own_ref[0].astype(F32) + down_ref[...].astype(F32)).astype(BF16)
 
@@ -295,6 +300,10 @@
     out_ref = rest[-1]
     total = own_ref[0].astype(F32) + up_ref[...].astype(F32) + down_ref[...].astype(F32)
     out_ref[...] = total.astype(BF16)
+
+
+def arrived_kernel(*refs):
+    refs[-1][...] = jnp.zeros_like(refs[-1])
 
 
 def direct_final_kernel(where_ref, normed_ref, w_ref, *refs, count):
@@ -387,7 +396,11 @@
             shaped((tokens, LANES)),
             shaped((STATE, width + LANES)),
         ],
-        scratch_shapes=[pltpu.VMEM((tokens, WIDE), BF16), pltpu.VMEM((tokens, LANES), BF16)],
+        scratch_shapes=[
+            pltpu.VMEM((tokens, WIDE), BF16),
+            pltpu.VMEM((tokens, LANES), BF16),
+            pltpu.VMEM((tokens, WIDE), F32),
+        ],
         compiler_params=params(),
         name="states",
     )(
@@ -435,7 +448,7 @@
             name="local_part",
         )(*operands)
 
-    some = blocks // 2
+    some = blocks * 3 // 8
     y_first = local_part(0, some, None, pay)
     entering = pl.pallas_call(
         prefix_kernel,
@@ -499,34 +512,27 @@
             name="project_direct",
         )(where, *operands, out_weight, in_hbm(after))
 
-    def direct_final(start, normed, pieces, out, after):
+    def direct_final(start, normed, pieces, after):
         def tile(width, start=0):
             return pl.BlockSpec((BLK, width), lambda i, where: (start + i, 0))
 
-        operands = [where, in_hbm(normed), in_hbm(out_weight)] + pieces + [in_hbm(after)]
-        specs = [
-            tile(width),
-            pl.BlockSpec((width, part_out), lambda i, where: (0, where[0])),
-        ]
-        specs += [tile(part_out)] * len(pieces) + [unread()]
-        aliases = {}
-        if out is not None:
-            aliases = {len(operands): 0}
-            operands.append(in_hbm(out))
-            specs.append(unread())
         return pl.pallas_call(
             functools.partial(direct_final_kernel, count=len(pieces)),
             grid_spec=pltpu.PrefetchScalarGridSpec(
                 num_scalar_prefetch=1,
                 grid=(normed.shape[0] // BLK,),
-                in_specs=specs,
+                in_specs=[
+                    tile(width),
+                    pl.BlockSpec((width, part_out), lambda i, where: (0, where[0])),
+                ]
+                + [tile(part_out)] * len(pieces)
+                + [unread()],
                 out_specs=tile(part_out, start),
             ),
             out_shape=shaped((tokens, part_out)),
-            input_output_aliases=aliases,
             compiler_params=params(SMALL_LIMIT),
             name="direct_final",
-        )(*operands)
+        )(where, in_hbm(normed), in_hbm(out_weight), *pieces, after)
 
     def project_line(start, count, tokens_each, split, y, after):
         operands, specs = norm_operands(start, count, tokens_each, y)
@@ -583,14 +589,14 @@
                     ),
                     pl.BlockSpec((BLK, part_out), plain),
                     pl.BlockSpec((BLK, part_out), plain),
-                    unread(),
-                ],
+                ]
+                + [unread()] * len(after),
                 out_specs=[pl.BlockSpec((BLK, part_out), plain)] * 2,
             ),
             out_shape=[shaped((count * BLK, part_out))] * 2,
             compiler_params=params(SMALL_LIMIT),
             name="onward",
-        )(where, in_hbm(shares), in_hbm(shares), up, down, after)
+        )(where, in_hbm(shares), in_hbm(shares), up, down, *after)
 
     def final(start, shares, half, up, down, out):
         count = up.shape[0] // BLK
@@ -632,19 +638,31 @@
         turn = [(a, (a + k) % chans) for a in range(chans)]
         pieces.append(lax.ppermute(slot, "chan", turn))
 
+    y_third = local_part(2 * some, blocks - 2 * some, y_second, normed)
     rest = blocks - lead
     split = [(rest + 1) // 2 * BLK, rest // 2 * BLK]
     shares, up_a, up_b, down_a, down_b = project_line(
-        lead, rest, BLK, split, y_second[0], normed
+        lead, rest, BLK, split, y_third[0], normed
     )
     moving = [permuted(up_a, down_a, 0), permuted(up_b, down_b, 0)]
-    out = direct_final(0, normed, pieces, None, shares)
-    after = in_hbm(out)
+    mark = pl.pallas_call(
+        arrived_kernel,
+        in_specs=[unread()] * (len(pieces) + 1),
+        out_specs=pl.BlockSpec(memory_space=pltpu.VMEM),
+        out_shape=shaped((HALO, LANES), F32),
+        compiler_params=pltpu.CompilerParams(vmem_limit_bytes=SMALL_LIMIT),
+        cost_estimate=pl.CostEstimate(flops=20000000000, transcendentals=0, bytes_accessed=1),
+        name="arrived",
+    )(*pieces, in_hbm(shares))
+    after = [mark]
     for s in range(1, chans - 1):
         for k in range(2):
             up, down = onward(shares, k, *moving[k], s, after)
-            after = up
+            after = [up]
             moving[k] = permuted(up, down, s)
+        if s == 1:
+            out = direct_final(0, normed, pieces, up)
+            after = [in_hbm(out)]
     for k in range(2):
         out = final(lead, shares, k, *moving[k], out)
     return out

time: 143 us -> 145 us (1.014)
  Pallas kernels: 70.3 us -> 73.3 us
  waiting for transfers between devices: 19.3 us -> 21.7 us
  starting transfers between devices: 48.2 us -> 46 us
    ppermute x6, waiting for transfers between devices: 3.45 us -> 6.81 us  [permuted(): up = lax.ppermute(up, 'chan', [(a, a + 1) for a in range(s + 1)])]
    ppermute x6, waiting for transfers between devices: 4.75 us -> 1.58 us  [permuted(): lax.ppermute(down, 'chan', [(a, a - 1) for a in range(chans - 1 - s, chan...]
    pallas_call x2 -> x3, Pallas kernels: 15.7 us -> 18.4 us  [local_part(): pl.pallas_call(local_kernel, grid=(count,), in_specs=specs, out_specs=[ti...]
    ppermute x6, starting transfers between devices: 27.1 us -> 24.9 us  [permuted(): up = lax.ppermute(up, 'chan', [(a, a + 1) for a in range(s + 1)])]
  transfers between devices with their start and end apart: 18 -> 18, of which waited for: 7 -> 8; matrix products, arithmetic and copies ran while one was open for 0% -> 0% of each run, Pallas kernels for 32% -> 33%
where the time goes in v8:
time: 145 us; the launch traced here: 144 us
  Pallas kernels  73.3 us (51%)
  starting transfers between devices  46 us (32%)
  waiting for transfers between devices  21.7 us (15%)
  local copies, waits for them, and re-layouts  2.88 us (2%)
    ppermute x6, starting transfers between devices, permuted(): up = lax.ppermute(up, 'chan', [(a, a + 1) for a in range(s + 1)])  24.9 us
    pallas_call x3, Pallas kernels, local_part(): pl.pallas_call(local_kernel, grid=(count,), in_specs=specs, out_specs=[ti...  18.4 us
    pallas_call x1, Pallas kernels, project_line(): pl.pallas_call(functools.partial(line_kernel, tiles=count), grid=(count +...  15.4 us
    pallas_call x1, Pallas kernels, local(): pl.pallas_call(states_kernel, grid=(width // WIDE,), in_specs=[lanes_at(t...  13 us
    pallas_call x1, Pallas kernels, project_direct(): pl.pallas_call(functools.partial(direct_kernel, tiles=count), grid_spec=p...  10 us
    ppermute x6, waiting for transfers between devices, permuted(): up = lax.ppermute(up, 'chan', [(a, a + 1) for a in range(s + 1)])  6.81 us
    pallas_call x4, Pallas kernels, onward(): pl.pallas_call(onward_kernel, grid_spec=pltpu.PrefetchScalarGridSpec(num_...  6.67 us
    ppermute x3, waiting for transfers between devices, local(): pieces.append(lax.ppermute(slot, 'chan', turn))  6 us
  transfers between devices with their start and end apart: 18, of which 8 were waited for; matrix products, arithmetic and copies ran while one was open for 0% of the time, Pallas kernels for 33%

profile of v8, /device:TPU:2, one launch (start us, length us, event | category | flops | bytes accessed | tf_op | source)
XLA Modules:
  0.0 144.1 jit_solution(16578748890734162908)
XLA Ops:
  0.0 0.7 slice.7
  0.7 0.8 slice.6
  1.5 1.9 %collective-permute-start = (bf16[8,2560]{1,0:T(8,128)(2,1)S(1)}, bf16[8,2560]{1,0:T(8,128)(2,1)S(1)}, u32[]{:S(2)}, u32[]{:S(2)}) collective-permute-start(bf16[8,2560]{1,0:T(8,128)(2,1)S(1)} %pad_maximum_fusion), channel_id=1, source_target_pairs={{0,4},{4,8},{8,12},{12,16},{16,20},{20,24},{24,28},{1,5},{5,9},{9,... | collective-permute-start | bytes 122888 | tf_op jit(solution)/shard_map/ppermute | solution.py:359
  3.4 3.4 %collective-permute-done.tail_ref.mtail_ref = bf16[8,2560]{1,0:T(8,128)(2,1)S(1)} collective-permute-done((bf16[8,2560]{1,0:T(8,128)(2,1)S(1)}, bf16[8,2560]{1,0:T(8,128)(2,1)S(1)}, u32[]{:S(2)}, u32[]{:S(2)}) %collective-permute-start) | collective-permute-done | bytes 40992 | tf_op jit(solution)/shard_map/ppermute | solution.py:359
  6.8 0.0 copy-start.2
  6.8 0.6 copy-done.2
  7.4 13.0 %states.1 = (bf16[1024,2048]{1,0:T(8,128)(2,1)}, bf16[1024,512]{1,0:T(8,128)(2,1)}, bf16[2,128,1024]{2,1,0:T(8,128)(2,1)}, f32[32,1024]{1,0:T(8,128)}, f32[1024,...) custom-call(bf16[1024,2048]{1,0:T(8,128)(2,1)} %x_ref.1, ...), custom_call_target="tpu_custom_call" | custom-call | tf_op jit(solution)/shard_map/states/pallas_call | solution.py:364
  20.4 0.0 copy-start
  20.4 4.4 %all-to-all-start = ((bf16[8,16,2176]{2,1,0:T(8,128)(2,1)}), bf16[8,16,2176]{2,1,0:T(8,128)(2,1)S(1)}, u32[]{:S(2)}, u32[]{:S(2)}) async-start(bf16[8,16,2176]{2,1,0:T(8,128)(2,1)} %bitcast.12), calls=%async_computation | async-start | bytes 1114112 | tf_op jit(solution)/shard_map/all_to_all | solution.py:413
  24.8 6.2 %local_part.3 = (bf16[1024,2048]{1,0:T(8,128)(2,1)}, f32[128,2048]{1,0:T(8,128)}) custom-call(bf16[1024,2048]{1,0:T(8,128)(2,1)} %get-tuple-element.35.xc_ref, bf16[1024,512]{1,0:T(8,128)(2,1)} %get-tuple-element.36.bc_ref, bf16[2,128,1024]{2,1,0:T(8,128)(2,1)} %get-tuple-element.37.bt_ref, f32[32,1024]{1,0:T(8,128)} %get-tuple-element.38.crow_ref, ...), custom_call_target="tpu_custom_call" | custom-call | flops 1 | bytes 1 | tf_op jit(solution)/shard_map/local_part/pallas_call | solution.py:439
  31.0 2.4 %all-to-all-done.pay_ref = bf16[8,16,2176]{2,1,0:T(8,128)(2,1)S(1)} async-done(((bf16[8,16,2176]{2,1,0:T(8,128)(2,1)}), bf16[8,16,2176]{2,1,0:T(8,128)(2,1)S(1)}, u32[]{:S(2)}, u32[]{:S(2)}) %all-to-all-start) | async-done | bytes 557088 | tf_op jit(solution)/shard_map/all_to_all | solution.py:413
  33.4 0.0 copy-done
  33.4 1.0 prefix.1.rest_2_
  34.5 4.9 %all-to-all-start.1 = ((bf16[8,16,2048]{2,1,0:T(8,128)(2,1)}), bf16[8,16,2048]{2,1,0:T(8,128)(2,1)S(1)}, u32[]{:S(2)}, u32[]{:S(2)}) async-start(bf16[8,16,2048]{2,1,0:T(8,128)(2,1)} %prefix.1.rest_2_), calls=%async_computation.1 | async-start | bytes 1048576 | tf_op jit(solution)/shard_map/all_to_all | solution.py:466
  39.3 6.8 %local_part.4 = (bf16[1024,2048]{1,0:T(8,128)(2,1)}, f32[128,2048]{1,0:T(8,128)}) custom-call(bf16[1024,2048]{1,0:T(8,128)(2,1)} %get-tuple-element.35.xc_ref, bf16[1024,512]{1,0:T(8,128)(2,1)} %get-tuple-element.36.bc_ref, bf16[2,128,1024]{2,1,0:T(8,128)(2,1)} %get-tuple-element.37.bt_ref, ...), custom_call_target="tpu_custom_call", output_to_operand_aliasing={{0}: (8, {})} | custom-call | flops 1 | bytes 1 | tf_op jit(solution)/shard_map/local_part/pallas_call | solution.py:439
  46.1 1.5 %all-to-all-done.1 = bf16[8,16,2048]{2,1,0:T(8,128)(2,1)S(1)} async-done(((bf16[8,16,2048]{2,1,0:T(8,128)(2,1)}), bf16[8,16,2048]{2,1,0:T(8,128)(2,1)S(1)}, u32[]{:S(2)}, u32[]{:S(2)}) %all-to-all-start.1) | async-done | bytes 524320 | tf_op jit(solution)/shard_map/all_to_all | solution.py:466
  47.6 0.0 copy-start.1
  47.6 0.8 copy-done.1
  48.4 10.0 %project_direct.1 = (bf16[384,512]{1,0:T(8,128)(2,1)}, bf16[384,512]{1,0:T(8,128)(2,1)}, bf16[384,512]{1,0:T(8,128)(2,1)}, bf16[384,2048]{1,0:T(8,128)(2,1)}) custom-call(s32[1]{0:T(128)} %bitcast.where_ref, bf16[1024,2048]{1,0:T(8,128)(2,1)} %get-tuple-element.45.y_ref.rest_1_, bf16[1024,512]{1,0:T(8,128)(2,1)} %get-tuple-element.36.bc_ref, ...), custom_call_target="tpu_custom_call" | custom-call | tf_op jit(solution)/shard_map/project_direct/pallas_call | solution.py:501
  58.4 1.6 %collective-permute-start.5 = (bf16[384,512]{1,0:T(8,128)(2,1)}, bf16[384,512]{1,0:T(8,128)(2,1)S(1)}, u32[]{:S(2)}, u32[]{:S(2)}) collective-permute-start(bf16[384,512]{1,0:T(8,128)(2,1)} %get-tuple-element.54), channel_id=1, source_target_pairs={{0,1},{1,2},{2,3},{3,0},{4,5},{5,6},{6,7},{7,4},{8,9},{9,10},{10,1... | collective-permute-start | bytes 1179656 | tf_op jit(solution)/shard_map/ppermute | solution.py:639
  60.0 2.3 %collective-permute-start.6 = (bf16[384,512]{1,0:T(8,128)(2,1)}, bf16[384,512]{1,0:T(8,128)(2,1)S(1)}, u32[]{:S(2)}, u32[]{:S(2)}) collective-permute-start(bf16[384,512]{1,0:T(8,128)(2,1)} %get-tuple-element.55), channel_id=1, source_target_pairs={{0,3},{1,0},{2,1},{3,2},{4,7},{5,4},{6,5},{7,6},{8,11},{9,8},{10,9... | collective-permute-start | bytes 1179656 | tf_op jit(solution)/shard_map/ppermute | solution.py:639
  62.3 0.8 collective-permute-start.7
  63.0 5.4 %local_part.5 = (bf16[1024,2048]{1,0:T(8,128)(2,1)}, f32[128,2048]{1,0:T(8,128)}) custom-call(bf16[1024,2048]{1,0:T(8,128)(2,1)} %get-tuple-element.35.xc_ref, bf16[1024,512]{1,0:T(8,128)(2,1)} %get-tuple-element.36.bc_ref, bf16[2,128,1024]{2,1,0:T(8,128)(2,1)} %get-tuple-element.37.bt_ref, ...), custom_call_target="tpu_custom_call", output_to_operand_aliasing={{0}: (8, {})} | custom-call | flops 1 | bytes 1 | tf_op jit(solution)/shard_map/local_part/pallas_call | solution.py:439
  68.4 15.4 %project_line.1 = (bf16[4,640,512]{2,1,0:T(8,128)(2,1)}, bf16[384,512]{1,0:T(8,128)(2,1)}, bf16[256,512]{1,0:T(8,128)(2,1)}, bf16[384,512]{1,0:T(8,128)(2,1)}, bf16[256,512]{1,0:T(8,128)(2,1)}) custom-call(bf16[1024,2048]{1,0:T(8,128)(2,1)} %get-tuple-element.48.y_ref, bf16[1024,512]{1,0:T(8,128)(2,1)} %get-tuple-element.36.bc_ref, ...), custom_call_target="tpu_custom_call" | custom-call | flops 1 | bytes 1 | tf_op jit(solution)/shard_map/project_line/pallas_call | solution.py:544
  83.8 3.5 %collective-permute-start.1 = (bf16[256,512]{1,0:T(8,128)(2,1)}, bf16[256,512]{1,0:T(8,128)(2,1)S(1)}, u32[]{:S(2)}, u32[]{:S(2)}) collective-permute-start(bf16[256,512]{1,0:T(8,128)(2,1)} %get-tuple-element.50), channel_id=1, source_target_pairs={{0,1},{4,5},{8,9},{12,13},{16,17},{20,21},{24,25},{28,29}} | collective-permute-start | bytes 786440 | tf_op jit(solution)/shard_map/ppermute | solution.py:561
  87.3 0.7 collective-permute-start.2
  88.0 0.0 collective-permute-done.5.refs_0_
  88.0 2.2 %collective-permute-start.3 = (bf16[384,512]{1,0:T(8,128)(2,1)}, bf16[384,512]{1,0:T(8,128)(2,1)S(1)}, u32[]{:S(2)}, u32[]{:S(2)}) collective-permute-start(bf16[384,512]{1,0:T(8,128)(2,1)} %get-tuple-element.52), channel_id=1, source_target_pairs={{0,1},{4,5},{8,9},{12,13},{16,17},{20,21},{24,25},{28,29}} | collective-permute-start | bytes 1179656 | tf_op jit(solution)/shard_map/ppermute | solution.py:561
  90.2 0.0 collective-permute-done.6.refs_1_
  90.2 0.7 collective-permute-start.4
  90.9 6.0 %collective-permute-done.7.refs_2_ = bf16[384,512]{1,0:T(8,128)(2,1)S(1)} collective-permute-done((bf16[384,512]{1,0:T(8,128)(2,1)}, bf16[384,512]{1,0:T(8,128)(2,1)S(1)}, u32[]{:S(2)}, u32[]{:S(2)}) %collective-permute-start.7) | collective-permute-done | bytes 393248 | tf_op jit(solution)/shard_map/ppermute | solution.py:639
  96.9 4.1 %collective-permute-done.3.up_ref = bf16[384,512]{1,0:T(8,128)(2,1)S(1)} collective-permute-done((bf16[384,512]{1,0:T(8,128)(2,1)}, bf16[384,512]{1,0:T(8,128)(2,1)S(1)}, u32[]{:S(2)}, u32[]{:S(2)}) %collective-permute-start.3) | collective-permute-done | bytes 393248 | tf_op jit(solution)/shard_map/ppermute | solution.py:561
  101.0 0.0 collective-permute-done.4.down_ref
  101.0 2.1 %onward.4 = (bf16[384,512]{1,0:T(8,128)(2,1)S(1)}, bf16[384,512]{1,0:T(8,128)(2,1)S(1)}) custom-call(s32[1]{0:T(128)} %bitcast.where_ref, bf16[4,640,512]{2,1,0:T(8,128)(2,1)} %get-tuple-element.49.refs_3_.up_own_ref.down_own_ref.own_ref, bf16[4,640,512]{2,1,0:T(8,128)(2,1)} %get-tuple-element.49.refs_3_.up_own_ref.down_own_ref.own_ref, ...), custom_call_target="tpu_custom_call" | custom-call | tf_op jit(solution)/shard_map/onward/pallas_call | solution.py:572
  103.1 0.7 collective-permute-start.11
  103.8 4.9 %collective-permute-start.10 = (bf16[384,512]{1,0:T(8,128)(2,1)S(1)}, bf16[384,512]{1,0:T(8,128)(2,1)S(1)}, u32[]{:S(2)}, u32[]{:S(2)}) collective-permute-start(bf16[384,512]{1,0:T(8,128)(2,1)S(1)} %get-tuple-element.57.rest_0_), channel_id=1, source_target_pairs={{0,1},{1,2},{4,5},{5,6},{8,9},{9,10},{12,13},{13,14},{16,17},{17,1... | collective-permute-start | bytes 1179656 | tf_op jit(solution)/shard_map/ppermute | solution.py:561
  108.7 0.0 collective-permute-done.1.up_ref
  108.7 0.0 collective-permute-done.2.down_ref
  108.7 1.2 onward.5
  109.9 0.7 collective-permute-start.9
  110.6 5.2 %collective-permute-start.8 = (bf16[256,512]{1,0:T(8,128)(2,1)S(1)}, bf16[256,512]{1,0:T(8,128)(2,1)S(1)}, u32[]{:S(2)}, u32[]{:S(2)}) collective-permute-start(bf16[256,512]{1,0:T(8,128)(2,1)S(1)} %get-tuple-element.58.refs_3_), channel_id=1, source_target_pairs={{0,1},{1,2},{4,5},{5,6},{8,9},{9,10},{12,13},{13,14},{16,17},{17,1... | collective-permute-start | bytes 786440 | tf_op jit(solution)/shard_map/ppermute | solution.py:561
  115.9 4.5 %direct_final.1.rest_0_ = bf16[1024,512]{1,0:T(8,128)(2,1)} custom-call(s32[1]{0:T(128)} %bitcast.where_ref, bf16[384,2048]{1,0:T(8,128)(2,1)} %get-tuple-element.47.rest_2_.after_ref.normed_ref, bf16[2048,2048]{1,0:T(8,128)(2,1)} %w_ref.5, bf16[384,512]{1,0:T(8,128)(2,1)S(1)} %collective-permute-done.5.refs_0_, ...), custom_call_target="tpu_custom_call" | custom-call | tf_op jit(solution)/shard_map/direct_final/pallas_call | solution.py:519
  120.4 0.0 collective-permute-done.11.down_ref
  120.4 0.0 collective-permute-done.10.up_ref
  120.4 2.1 %onward.6 = (bf16[384,512]{1,0:T(8,128)(2,1)S(1)}, bf16[384,512]{1,0:T(8,128)(2,1)S(1)}) custom-call(s32[1]{0:T(128)} %bitcast.where_ref, bf16[4,640,512]{2,1,0:T(8,128)(2,1)} %get-tuple-element.49.refs_3_.up_own_ref.down_own_ref.own_ref, bf16[4,640,512]{2,1,0:T(8,128)(2,1)} %get-tuple-element.49.refs_3_.up_own_ref.down_own_ref.own_ref, ...), custom_call_target="tpu_custom_call" | custom-call | tf_op jit(solution)/shard_map/onward/pallas_call | solution.py:572
  122.5 1.3 collective-permute-start.15
  123.8 5.2 %collective-permute-start.14 = (bf16[384,512]{1,0:T(8,128)(2,1)S(1)}, bf16[384,512]{1,0:T(8,128)(2,1)S(1)}, u32[]{:S(2)}, u32[]{:S(2)}) collective-permute-start(bf16[384,512]{1,0:T(8,128)(2,1)S(1)} %get-tuple-element.61.rest_0_), channel_id=1, source_target_pairs={{0,1},{1,2},{2,3},{4,5},{5,6},{6,7},{8,9},{9,10},{10,11},{12,13},{... | collective-permute-start | bytes 1179656 | tf_op jit(solution)/shard_map/ppermute | solution.py:561
  129.0 0.0 collective-permute-done.9.down_ref
  129.0 0.0 collective-permute-done.8.up_ref
  129.0 1.2 onward.7
  130.2 3.9 %collective-permute-start.12 = (bf16[256,512]{1,0:T(8,128)(2,1)S(1)}, bf16[256,512]{1,0:T(8,128)(2,1)S(1)}, u32[]{:S(2)}, u32[]{:S(2)}) collective-permute-start(bf16[256,512]{1,0:T(8,128)(2,1)S(1)} %get-tuple-element.62), channel_id=1, source_target_pairs={{0,1},{1,2},{2,3},{4,5},{5,6},{6,7},{8,9},{9,10},{10,11},{12,13},{... | collective-permute-start | bytes 786440 | tf_op jit(solution)/shard_map/ppermute | solution.py:561
  134.2 1.3 collective-permute-start.13
  135.5 0.0 collective-permute-done.15.down_ref
  135.5 2.6 %collective-permute-done.14.up_ref = bf16[384,512]{1,0:T(8,128)(2,1)S(1)} collective-permute-done((bf16[384,512]{1,0:T(8,128)(2,1)S(1)}, bf16[384,512]{1,0:T(8,128)(2,1)S(1)}, u32[]{:S(2)}, u32[]{:S(2)}) %collective-permute-start.14) | collective-permute-done | bytes 393248 | tf_op jit(solution)/shard_map/ppermute | solution.py:561
  138.1 2.7 %final.2.rest_0_ = bf16[1024,512]{1,0:T(8,128)(2,1)} custom-call(s32[1]{0:T(128)} %bitcast.where_ref, bf16[4,640,512]{2,1,0:T(8,128)(2,1)} %get-tuple-element.49.refs_3_.up_own_ref.down_own_ref.own_ref, bf16[384,512]{1,0:T(8,128)(2,1)S(1)} %collective-permute-done.14.up_ref, ...), custom_call_target="tpu_custom_call", output_to_operand_aliasing={{}: (4, {})} | custom-call | tf_op jit(solution)/shard_map/final/pallas_call | solution.py:619
  140.7 0.1 collective-permute-done.12.up_ref
  140.9 1.6 %collective-permute-done.13.down_ref = bf16[256,512]{1,0:T(8,128)(2,1)S(1)} collective-permute-done((bf16[256,512]{1,0:T(8,128)(2,1)S(1)}, bf16[256,512]{1,0:T(8,128)(2,1)S(1)}, u32[]{:S(2)}, u32[]{:S(2)}) %collective-permute-start.13) | collective-permute-done | bytes 262176 | tf_op jit(solution)/shard_map/ppermute | solution.py:562
  142.4 1.7 %final.3 = bf16[1024,512]{1,0:T(8,128)(2,1)} custom-call(s32[1]{0:T(128)} %bitcast.where_ref, bf16[4,640,512]{2,1,0:T(8,128)(2,1)} %get-tuple-element.49.refs_3_.up_own_ref.down_own_ref.own_ref, bf16[256,512]{1,0:T(8,128)(2,1)S(1)} %collective-permute-done.12.up_ref, ...), custom_call_target="tpu_custom_call", output_to_operand_aliasing={{}: (4, {})} | custom-call | tf_op jit(solution)/shard_map/final/pallas_call | solution.py:619
  (3 shorter events, 0.0 us)
Async XLA Ops:
  1.5 5.3 %collective-permute-start = (bf16[8,2560]{1,0:T(8,128)(2,1)S(1)}, bf16[8,2560]{1,0:T(8,128)(2,1)S(1)}, u32[]{:S(2)}, u32[]{:S(2)}) collective-permute-start(bf16[8,2560]{1,0:T(8,128)(2,1)S(1)} %pad_maximum_fusion), channel_id=1, source_target_pairs={{0,4},{4,8},{8,12},{12,16},{16,20},{20,24},{24,28},{1,5},{5,9},{9,... | collective-permute-start | bytes 122888 | tf_op jit(solution)/shard_map/ppermute | solution.py:359
  6.8 0.6 copy-start.2
  20.4 13.0 %copy-start = (bf16[128,2048]{1,0:T(8,128)(2,1)S(1)}, bf16[128,2048]{1,0:T(8,128)(2,1)}, u32[]{:S(2)}) copy-start(bf16[128,2048]{1,0:T(8,128)(2,1)} %constant.6.clone.e_ref) | copy-start | bytes 1572868
  20.4 13.0 %all-to-all-start = ((bf16[8,16,2176]{2,1,0:T(8,128)(2,1)}), bf16[8,16,2176]{2,1,0:T(8,128)(2,1)S(1)}, u32[]{:S(2)}, u32[]{:S(2)}) async-start(bf16[8,16,2176]{2,1,0:T(8,128)(2,1)} %bitcast.12), calls=%async_computation | async-start | bytes 1114112 | tf_op jit(solution)/shard_map/all_to_all | solution.py:413
  34.5 13.2 %all-to-all-start.1 = ((bf16[8,16,2048]{2,1,0:T(8,128)(2,1)}), bf16[8,16,2048]{2,1,0:T(8,128)(2,1)S(1)}, u32[]{:S(2)}, u32[]{:S(2)}) async-start(bf16[8,16,2048]{2,1,0:T(8,128)(2,1)} %prefix.1.rest_2_), calls=%async_computation.1 | async-start | bytes 1048576 | tf_op jit(solution)/shard_map/all_to_all | solution.py:466
  47.6 0.8 copy-start.1
  58.4 29.6 %collective-permute-start.5 = (bf16[384,512]{1,0:T(8,128)(2,1)}, bf16[384,512]{1,0:T(8,128)(2,1)S(1)}, u32[]{:S(2)}, u32[]{:S(2)}) collective-permute-start(bf16[384,512]{1,0:T(8,128)(2,1)} %get-tuple-element.54), channel_id=1, source_target_pairs={{0,1},{1,2},{2,3},{3,0},{4,5},{5,6},{6,7},{7,4},{8,9},{9,10},{10,1... | collective-permute-start | bytes 1179656 | tf_op jit(solution)/shard_map/ppermute | solution.py:639
  60.0 30.2 %collective-permute-start.6 = (bf16[384,512]{1,0:T(8,128)(2,1)}, bf16[384,512]{1,0:T(8,128)(2,1)S(1)}, u32[]{:S(2)}, u32[]{:S(2)}) collective-permute-start(bf16[384,512]{1,0:T(8,128)(2,1)} %get-tuple-element.55), channel_id=1, source_target_pairs={{0,3},{1,0},{2,1},{3,2},{4,7},{5,4},{6,5},{7,6},{8,11},{9,8},{10,9... | collective-permute-start | bytes 1179656 | tf_op jit(solution)/shard_map/ppermute | solution.py:639
  62.3 34.6 %collective-permute-start.7 = (bf16[384,512]{1,0:T(8,128)(2,1)}, bf16[384,512]{1,0:T(8,128)(2,1)S(1)}, u32[]{:S(2)}, u32[]{:S(2)}) collective-permute-start(bf16[384,512]{1,0:T(8,128)(2,1)} %get-tuple-element.56), channel_id=1, source_target_pairs={{0,2},{1,3},{2,0},{3,1},{4,6},{5,7},{6,4},{7,5},{8,10},{9,11},{10,... | collective-permute-start | bytes 1179656 | tf_op jit(solution)/shard_map/ppermute | solution.py:639
  83.8 24.9 %collective-permute-start.1 = (bf16[256,512]{1,0:T(8,128)(2,1)}, bf16[256,512]{1,0:T(8,128)(2,1)S(1)}, u32[]{:S(2)}, u32[]{:S(2)}) collective-permute-start(bf16[256,512]{1,0:T(8,128)(2,1)} %get-tuple-element.50), channel_id=1, source_target_pairs={{0,1},{4,5},{8,9},{12,13},{16,17},{20,21},{24,25},{28,29}} | collective-permute-start | bytes 786440 | tf_op jit(solution)/shard_map/ppermute | solution.py:561
  87.3 21.4 %collective-permute-start.2 = (bf16[256,512]{1,0:T(8,128)(2,1)}, bf16[256,512]{1,0:T(8,128)(2,1)S(1)}, u32[]{:S(2)}, u32[]{:S(2)}) collective-permute-start(bf16[256,512]{1,0:T(8,128)(2,1)} %get-tuple-element.51), channel_id=1, source_target_pairs={{3,2},{7,6},{11,10},{15,14},{19,18},{23,22},{27,26},{31,30}} | collective-permute-start | bytes 786440 | tf_op jit(solution)/shard_map/ppermute | solution.py:562
  88.0 13.0 %collective-permute-start.3 = (bf16[384,512]{1,0:T(8,128)(2,1)}, bf16[384,512]{1,0:T(8,128)(2,1)S(1)}, u32[]{:S(2)}, u32[]{:S(2)}) collective-permute-start(bf16[384,512]{1,0:T(8,128)(2,1)} %get-tuple-element.52), channel_id=1, source_target_pairs={{0,1},{4,5},{8,9},{12,13},{16,17},{20,21},{24,25},{28,29}} | collective-permute-start | bytes 1179656 | tf_op jit(solution)/shard_map/ppermute | solution.py:561
  90.2 10.8 %collective-permute-start.4 = (bf16[384,512]{1,0:T(8,128)(2,1)}, bf16[384,512]{1,0:T(8,128)(2,1)S(1)}, u32[]{:S(2)}, u32[]{:S(2)}) collective-permute-start(bf16[384,512]{1,0:T(8,128)(2,1)} %get-tuple-element.53), channel_id=1, source_target_pairs={{3,2},{7,6},{11,10},{15,14},{19,18},{23,22},{27,26},{31,30}} | collective-permute-start | bytes 1179656 | tf_op jit(solution)/shard_map/ppermute | solution.py:562
  103.1 17.3 %collective-permute-start.11 = (bf16[384,512]{1,0:T(8,128)(2,1)S(1)}, bf16[384,512]{1,0:T(8,128)(2,1)S(1)}, u32[]{:S(2)}, u32[]{:S(2)}) collective-permute-start(bf16[384,512]{1,0:T(8,128)(2,1)S(1)} %get-tuple-element.60), channel_id=1, source_target_pairs={{2,1},{3,2},{6,5},{7,6},{10,9},{11,10},{14,13},{15,14},{18,17},{19... | collective-permute-start | bytes 1179656 | tf_op jit(solution)/shard_map/ppermute | solution.py:562
  103.8 16.6 %collective-permute-start.10 = (bf16[384,512]{1,0:T(8,128)(2,1)S(1)}, bf16[384,512]{1,0:T(8,128)(2,1)S(1)}, u32[]{:S(2)}, u32[]{:S(2)}) collective-permute-start(bf16[384,512]{1,0:T(8,128)(2,1)S(1)} %get-tuple-element.57.rest_0_), channel_id=1, source_target_pairs={{0,1},{1,2},{4,5},{5,6},{8,9},{9,10},{12,13},{13,14},{16,17},{17,1... | collective-permute-start | bytes 1179656 | tf_op jit(solution)/shard_map/ppermute | solution.py:561
  109.9 19.1 %collective-permute-start.9 = (bf16[256,512]{1,0:T(8,128)(2,1)S(1)}, bf16[256,512]{1,0:T(8,128)(2,1)S(1)}, u32[]{:S(2)}, u32[]{:S(2)}) collective-permute-start(bf16[256,512]{1,0:T(8,128)(2,1)S(1)} %get-tuple-element.59), channel_id=1, source_target_pairs={{2,1},{3,2},{6,5},{7,6},{10,9},{11,10},{14,13},{15,14},{18,17},{19... | collective-permute-start | bytes 786440 | tf_op jit(solution)/shard_map/ppermute | solution.py:562
  110.6 18.4 %collective-permute-start.8 = (bf16[256,512]{1,0:T(8,128)(2,1)S(1)}, bf16[256,512]{1,0:T(8,128)(2,1)S(1)}, u32[]{:S(2)}, u32[]{:S(2)}) collective-permute-start(bf16[256,512]{1,0:T(8,128)(2,1)S(1)} %get-tuple-element.58.refs_3_), channel_id=1, source_target_pairs={{0,1},{1,2},{4,5},{5,6},{8,9},{9,10},{12,13},{13,14},{16,17},{17,1... | collective-permute-start | bytes 786440 | tf_op jit(solution)/shard_map/ppermute | solution.py:561
  122.5 13.0 %collective-permute-start.15 = (bf16[384,512]{1,0:T(8,128)(2,1)S(1)}, bf16[384,512]{1,0:T(8,128)(2,1)S(1)}, u32[]{:S(2)}, u32[]{:S(2)}) collective-permute-start(bf16[384,512]{1,0:T(8,128)(2,1)S(1)} %get-tuple-element.64), channel_id=1, source_target_pairs={{1,0},{2,1},{3,2},{5,4},{6,5},{7,6},{9,8},{10,9},{11,10},{13,12},{... | collective-permute-start | bytes 1179656 | tf_op jit(solution)/shard_map/ppermute | solution.py:562
  123.8 14.3 %collective-permute-start.14 = (bf16[384,512]{1,0:T(8,128)(2,1)S(1)}, bf16[384,512]{1,0:T(8,128)(2,1)S(1)}, u32[]{:S(2)}, u32[]{:S(2)}) collective-permute-start(bf16[384,512]{1,0:T(8,128)(2,1)S(1)} %get-tuple-element.61.rest_0_), channel_id=1, source_target_pairs={{0,1},{1,2},{2,3},{4,5},{5,6},{6,7},{8,9},{9,10},{10,11},{12,13},{... | collective-permute-start | bytes 1179656 | tf_op jit(solution)/shard_map/ppermute | solution.py:561
  130.2 10.6 %collective-permute-start.12 = (bf16[256,512]{1,0:T(8,128)(2,1)S(1)}, bf16[256,512]{1,0:T(8,128)(2,1)S(1)}, u32[]{:S(2)}, u32[]{:S(2)}) collective-permute-start(bf16[256,512]{1,0:T(8,128)(2,1)S(1)} %get-tuple-element.62), channel_id=1, source_target_pairs={{0,1},{1,2},{2,3},{4,5},{5,6},{6,7},{8,9},{9,10},{10,11},{12,13},{... | collective-permute-start | bytes 786440 | tf_op jit(solution)/shard_map/ppermute | solution.py:561
  134.2 8.3 %collective-permute-start.13 = (bf16[256,512]{1,0:T(8,128)(2,1)S(1)}, bf16[256,512]{1,0:T(8,128)(2,1)S(1)}, u32[]{:S(2)}, u32[]{:S(2)}) collective-permute-start(bf16[256,512]{1,0:T(8,128)(2,1)S(1)} %get-tuple-element.63), channel_id=1, source_target_pairs={{1,0},{2,1},{3,2},{5,4},{6,5},{7,6},{9,8},{10,9},{11,10},{13,12},{... | collective-permute-start | bytes 786440 | tf_op jit(solution)/shard_map/ppermute | solution.py:562

commit v9 on v8

--- a/solution.py
+++ b/solution.py
@@ -1,4 +1,5 @@
 import functools
+import math
 
 import jax
 import jax.numpy as jnp
@@ -76,9 +77,14 @@
 
 def states_kernel(
     x_ref, maps_ref, step_ref, tail_ref, mtail_ref, bias_ref, rate_ref, ck_ref, mk_ref, e_ref,
-    xc_ref, bc_ref, bt_ref, crow_ref, cols_ref, wrow_ref, g_ref, pay_ref,
-    weighted, w_ref, scale,
+    xc_ref, pay_ref, *rest,
 ):
+    outs, (bc_ref, bt_ref, crow_ref, cols_ref, wrow_ref, g_ref) = rest[:6], rest[6:12]
+    weighted, w_ref, scale, sems = rest[12:]
+    copies = [
+        pltpu.make_async_copy(kept, out, sems.at[k])
+        for k, (kept, out) in enumerate(zip(rest[6:12], outs))
+    ]
     c = pl.program_id(0)
     heads, tokens = step_ref.shape
     parts = mk_ref.shape[0] // 4
@@ -146,6 +152,9 @@
                 if q < groups:
                     bt_ref[q, :, b * BLK : (b + 1) * BLK] = result.astype(F32).T.astype(BF16)
 
+        for copy in copies:
+            copy.start()
+
     scale[...] = dot(w_ref[...], e_ref[...])
     for lane in range(0, x_ref.shape[1], LANES):
         at_lanes = slice(lane, lane + LANES)
@@ -162,6 +171,11 @@
     group = c * step_width * groups // (heads * HEAD_DIM)
     at = pl.ds(pl.multiple_of(c * step_width, step_width), step_width)
     pay_ref[:, at] = dot(bt_ref[group], weighted[...]).astype(BF16)
+
+    @pl.when(c == pl.num_programs(0) - 1)
+    def _():
+        for copy in copies:
+            copy.wait()
 
 
 def local_kernel(xc_ref, bc_ref, bt_ref, crow_ref, cols_ref, wrow_ref, skip_ref, *rest):
@@ -261,9 +275,9 @@
             out_ref[...] = dot(normed_ref[...], w_ref[...]).astype(BF16)
 
 
-def line_kernel(
+def ends_kernel(
     y_ref, bc_ref, g_ref, enter_ref, gate_ref, gain_ref, e_ref, w_ref, after_ref,
-    shares_ref, up_a_ref, up_b_ref, down_a_ref, down_b_ref, normed_ref, carry, grown, *, tiles,
+    shares_ref, up_ref, down_ref, normed_ref, carry, grown, *, tiles,
 ):
     i = pl.program_id(0)
 
@@ -277,17 +291,17 @@
     def _():
         shares_ref[0] = dot(normed_ref[...], w_ref[...]).astype(BF16)
 
-    size = up_a_ref.shape[0]
-
     @pl.when(i == tiles)
     def _():
-        down_a_ref[...] = shares_ref[0, :size]
-        down_b_ref[...] = shares_ref[0, size:]
-
-    @pl.when(i == pl.num_programs(0) - 1)
+        down_ref[...] = shares_ref[0]
+
+    @pl.when(i == tiles + 1)
     def _():
-        up_a_ref[...] = shares_ref[0, :size]
-        up_b_ref[...] = shares_ref[0, size:]
+        up_ref[...] = shares_ref[0]
+
+
+def middle_kernel(normed_ref, w_ref, ends_ref, shares_ref):
+    shares_ref[0] = dot(normed_ref[...], w_ref[...]).astype(BF16)
 
 
 def onward_kernel(where_ref, up_own_ref, down_own_ref, up_ref, down_ref, *rest):
@@ -361,7 +375,15 @@
     def lanes_at(count):
         return pl.BlockSpec((count, WIDE), lambda c: (0, c))
 
-    xc, bc, bt, crow, cols, wrow, g_hl, pay = pl.pallas_call(
+    kept = [
+        ((tokens, map_width), BF16),
+        ((groups, STATE, tokens), BF16),
+        ((heads, tokens), F32),
+        ((tokens, LANES), F32),
+        ((heads, tokens), F32),
+        ((tokens, LANES), BF16),
+    ]
+    xc, pay, bc, bt, crow, cols, wrow, g_hl = pl.pallas_call(
         states_kernel,
         grid=(width // WIDE,),
         in_specs=[
@@ -376,30 +398,15 @@
             whole((4 * parts, STATE)),
             lanes_at(LANES),
         ],
-        out_specs=[
-            lanes_at(tokens),
-            whole((tokens, map_width)),
-            whole((groups, STATE, tokens)),
-            whole((heads, tokens)),
-            whole((tokens, LANES)),
-            whole((heads, tokens)),
-            whole((tokens, LANES)),
-            whole((STATE, width + LANES)),
-        ],
-        out_shape=[
-            shaped((tokens, width)),
-            shaped((tokens, map_width)),
-            shaped((groups, STATE, tokens)),
-            shaped((heads, tokens), F32),
-            shaped((tokens, LANES), F32),
-            shaped((heads, tokens), F32),
-            shaped((tokens, LANES)),
-            shaped((STATE, width + LANES)),
-        ],
-        scratch_shapes=[
+        out_specs=[lanes_at(tokens), whole((STATE, width + LANES))] + [unread()] * 6,
+        out_shape=[shaped((tokens, width)), shaped((STATE, width + LANES))]
+        + [shaped(*k) for k in kept],
+        scratch_shapes=[pltpu.VMEM(*k) for k in kept]
+        + [
             pltpu.VMEM((tokens, WIDE), BF16),
             pltpu.VMEM((tokens, LANES), BF16),
             pltpu.VMEM((tokens, WIDE), F32),
+            pltpu.SemaphoreType.DMA((6,)),
         ],
         compiler_params=params(),
         name="states",
@@ -534,73 +541,97 @@
             name="direct_final",
         )(where, in_hbm(normed), in_hbm(out_weight), *pieces, after)
 
-    def project_line(start, count, tokens_each, split, y, after):
+    def project_ends(start, count, tokens_each, y, after):
         operands, specs = norm_operands(start, count, tokens_each, y)
         size = count * tokens_each
 
         def dest(i):
-            return jnp.maximum(i - count, 0)
+            return jnp.where(i <= count, 0, chans - 1)
 
         return pl.pallas_call(
-            functools.partial(line_kernel, tiles=count),
-            grid=(count + chans,),
+            functools.partial(ends_kernel, tiles=count),
+            grid=(count + 2,),
             in_specs=specs
             + [pl.BlockSpec((width, part_out), lambda i: (0, dest(i))), unread()],
             out_specs=[
                 pl.BlockSpec((1, size, part_out), lambda i: (dest(i), 0, 0)),
-            ]
-            + [whole((k, part_out)) for k in split * 2],
-            out_shape=[shaped((chans, size, part_out))] + [shaped((k, part_out)) for k in split * 2],
-            scratch_shapes=[pltpu.VMEM((size, width), BF16)] + [pltpu.VMEM((tokens_each, width), F32)] * 2,
+                whole((size, part_out)),
+                whole((size, part_out)),
+                whole((size, width)),
+            ],
+            out_shape=[
+                shaped((chans, size, part_out)),
+                shaped((size, part_out)),
+                shaped((size, part_out)),
+                shaped((size, width)),
+            ],
+            scratch_shapes=[pltpu.VMEM((tokens_each, width), F32)] * 2,
             compiler_params=params(),
             cost_estimate=brief(),
-            name="project_line",
+            name="project_ends",
         )(*operands, out_weight, in_hbm(after))
+
+    def project_middle(shares, normed):
+        size = normed.shape[0]
+        return pl.pallas_call(
+            middle_kernel,
+            grid=(chans - 2,),
+            in_specs=[
+                whole((size, width)),
+                pl.BlockSpec((width, part_out), lambda i: (0, i + 1)),
+                unread(),
+            ],
+            out_specs=pl.BlockSpec((1, size, part_out), lambda i: (i + 1, 0, 0)),
+            out_shape=shaped((chans, size, part_out)),
+            input_output_aliases={2: 0},
+            compiler_params=params(),
+            cost_estimate=brief(),
+            name="project_middle",
+        )(normed, out_weight, in_hbm(shares))
 
     def permuted(up, down, s):
         up = lax.ppermute(up, "chan", [(a, a + 1) for a in range(s + 1)])
         down = lax.ppermute(down, "chan", [(a, a - 1) for a in range(chans - 1 - s, chans)])
         return up, down
 
-    def onward(shares, half, up, down, s, after):
-        count = up.shape[0] // BLK
-        skipped = (shares.shape[1] // BLK - count) * half
+    def onward(shares, part, up, down, s, after):
+        first, count = part
+        tile = math.gcd(first, count) if first else count
+        skipped = first // tile
+        held = skipped if s == 1 else 0
 
         def plain(i, where):
             return (i, 0)
+
+        def arrived(i, where):
+            return (held + i, 0)
+
+        def own(index):
+            return pl.BlockSpec(
+                (1, tile, part_out), lambda i, where: (index(where[0]), skipped + i, 0)
+            )
 
         return pl.pallas_call(
             onward_kernel,
             grid_spec=pltpu.PrefetchScalarGridSpec(
                 num_scalar_prefetch=1,
-                grid=(count,),
+                grid=(count // tile,),
                 in_specs=[
-                    pl.BlockSpec(
-                        (1, BLK, part_out),
-                        lambda i, where: (
-                            jnp.minimum(chans - 1 - s + where[0], chans - 1), skipped + i, 0
-                        ),
-                    ),
-                    pl.BlockSpec(
-                        (1, BLK, part_out),
-                        lambda i, where: (
-                            jnp.maximum(where[0] - (chans - 1) + s, 0), skipped + i, 0
-                        ),
-                    ),
-                    pl.BlockSpec((BLK, part_out), plain),
-                    pl.BlockSpec((BLK, part_out), plain),
+                    own(lambda me: jnp.minimum(chans - 1 - s + me, chans - 1)),
+                    own(lambda me: jnp.maximum(me - (chans - 1) + s, 0)),
+                    pl.BlockSpec((tile, part_out), arrived),
+                    pl.BlockSpec((tile, part_out), arrived),
                 ]
                 + [unread()] * len(after),
-                out_specs=[pl.BlockSpec((BLK, part_out), plain)] * 2,
+                out_specs=[pl.BlockSpec((tile, part_out), plain)] * 2,
             ),
-            out_shape=[shaped((count * BLK, part_out))] * 2,
+            out_shape=[shaped((count, part_out))] * 2,
             compiler_params=params(SMALL_LIMIT),
             name="onward",
         )(where, in_hbm(shares), in_hbm(shares), up, down, *after)
 
-    def final(start, shares, half, up, down, out):
-        count = up.shape[0] // BLK
-        skipped = (shares.shape[1] // BLK - count) * half
+    def final(start, shares, part, up, down, out):
+        count, skipped = part[1] // BLK, part[0] // BLK
 
         def plain(i, where):
             return (i, 0)
@@ -640,11 +671,11 @@
 
     y_third = local_part(2 * some, blocks - 2 * some, y_second, normed)
     rest = blocks - lead
-    split = [(rest + 1) // 2 * BLK, rest // 2 * BLK]
-    shares, up_a, up_b, down_a, down_b = project_line(
-        lead, rest, BLK, split, y_third[0], normed
-    )
-    moving = [permuted(up_a, down_a, 0), permuted(up_b, down_b, 0)]
+    some = (rest + 1) // 2 * BLK
+    parts_of = [(0, some), (some, rest * BLK - some)]
+    shares, up, down, line_normed = project_ends(lead, rest, BLK, y_third[0], normed)
+    moving = [permuted(up, down, 0)] * 2
+    shares = project_middle(shares, line_normed)
     mark = pl.pallas_call(
         arrived_kernel,
         in_specs=[unread()] * (len(pieces) + 1),
@@ -657,14 +688,14 @@
     after = [mark]
     for s in range(1, chans - 1):
         for k in range(2):
-            up, down = onward(shares, k, *moving[k], s, after)
+            up, down = onward(shares, parts_of[k], *moving[k], s, after)
             after = [up]
             moving[k] = permuted(up, down, s)
         if s == 1:
             out = direct_final(0, normed, pieces, up)
             after = [in_hbm(out)]
     for k in range(2):
-        out = final(lead, shares, k, *moving[k], out)
+        out = final(lead, shares, parts_of[k], *moving[k], out)
     return out
 
 

time: 145 us -> 142 us (0.979)
  starting transfers between devices: 46 us -> 43.1 us
  Pallas kernels: 73.3 us -> 75.5 us
  waiting for transfers between devices: 21.7 us -> 19.6 us
    pallas_call x1 -> x2, Pallas kernels: 15.4 us -> 19.2 us  [the longest x1 12.9 us: project_ends(): pl.pallas_call(functools.partial(ends_kernel, tiles=count), grid=(count +...]
    ppermute x6 -> x5, starting transfers between devices: 24.9 us -> 22.7 us  [permuted(): up = lax.ppermute(up, 'chan', [(a, a + 1) for a in range(s + 1)])]
    pallas_call x4, Pallas kernels: 6.67 us -> 5.03 us  [onward(): pl.pallas_call(onward_kernel, grid_spec=pltpu.PrefetchScalarGridSpec(num_...]
    ppermute x6 -> x5, waiting for transfers between devices: 6.81 us -> 6.1 us  [permuted(): up = lax.ppermute(up, 'chan', [(a, a + 1) for a in range(s + 1)])]
    ppermute x6 -> x5, starting transfers between devices: 5.31 us -> 4.65 us  [permuted(): lax.ppermute(down, 'chan', [(a, a - 1) for a in range(chans - 1 - s, chan...]
  transfers between devices with their start and end apart: 18 -> 16, of which waited for: 8 -> 8; matrix products, arithmetic and copies ran while one was open for 0% -> 0% of each run, Pallas kernels for 33% -> 34%
where the time goes in v9:
time: 142 us; the launch traced here: 141 us
  Pallas kernels  75.5 us (53%)
  starting transfers between devices  43.1 us (30%)
  waiting for transfers between devices  19.6 us (14%)
  local copies, waits for them, and re-layouts  2.88 us (2%)
    ppermute x5, starting transfers between devices, permuted(): up = lax.ppermute(up, 'chan', [(a, a + 1) for a in range(s + 1)])  22.7 us
    pallas_call x3, Pallas kernels, local_part(): pl.pallas_call(local_kernel, grid=(count,), in_specs=specs, out_specs=[ti...  18.5 us
    pallas_call x1, Pallas kernels, project_ends(): pl.pallas_call(functools.partial(ends_kernel, tiles=count), grid=(count +...  12.9 us
    pallas_call x1, Pallas kernels, local(): pl.pallas_call(states_kernel, grid=(width // WIDE,), in_specs=[lanes_at(t...  12.9 us
    pallas_call x1, Pallas kernels, project_direct(): pl.pallas_call(functools.partial(direct_kernel, tiles=count), grid_spec=p...  10 us
    pallas_call x1, Pallas kernels, project_middle(): pl.pallas_call(middle_kernel, grid=(chans - 2,), in_specs=[whole((size, w...  6.31 us
    ppermute x5, waiting for transfers between devices, permuted(): up = lax.ppermute(up, 'chan', [(a, a + 1) for a in range(s + 1)])  6.1 us
    pallas_call x4, Pallas kernels, onward(): pl.pallas_call(onward_kernel, grid_spec=pltpu.PrefetchScalarGridSpec(num_...  5.03 us
  transfers between devices with their start and end apart: 16, of which 8 were waited for; matrix products, arithmetic and copies ran while one was open for 0% of the time, Pallas kernels for 34%

profile of v9, /device:TPU:2, one launch (start us, length us, event | category | flops | bytes accessed | tf_op | source)
XLA Modules:
  0.0 141.2 jit_solution(8535464832759033022)
XLA Ops:
  0.0 0.7 slice.7
  0.7 0.8 slice.6
  1.5 1.9 %collective-permute-start = (bf16[8,2560]{1,0:T(8,128)(2,1)S(1)}, bf16[8,2560]{1,0:T(8,128)(2,1)S(1)}, u32[]{:S(2)}, u32[]{:S(2)}) collective-permute-start(bf16[8,2560]{1,0:T(8,128)(2,1)S(1)} %pad_maximum_fusion), channel_id=1, source_target_pairs={{0,4},{4,8},{8,12},{12,16},{16,20},{20,24},{24,28},{1,5},{5,9},{9,... | collective-permute-start | bytes 122888 | tf_op jit(solution)/shard_map/ppermute | solution.py:373
  3.4 3.4 %collective-permute-done.tail_ref.mtail_ref = bf16[8,2560]{1,0:T(8,128)(2,1)S(1)} collective-permute-done((bf16[8,2560]{1,0:T(8,128)(2,1)S(1)}, bf16[8,2560]{1,0:T(8,128)(2,1)S(1)}, u32[]{:S(2)}, u32[]{:S(2)}) %collective-permute-start) | collective-permute-done | bytes 40992 | tf_op jit(solution)/shard_map/ppermute | solution.py:373
  6.8 0.0 copy-start.2
  6.8 0.6 copy-done.2
  7.4 12.9 %states.1 = (bf16[1024,2048]{1,0:T(8,128)(2,1)}, bf16[128,2176]{1,0:T(8,128)(2,1)}, bf16[1024,512]{1,0:T(8,128)(2,1)}, bf16[2,128,1024]{2,1,0:T(8,128)(2,1)}, f3...) custom-call(bf16[1024,2048]{1,0:T(8,128)(2,1)} %x_ref.1, ...), custom_call_target="tpu_custom_call" | custom-call | tf_op jit(solution)/shard_map/states/pallas_call | solution.py:386
  20.3 0.0 copy-start
  20.3 4.4 %all-to-all-start = ((bf16[8,16,2176]{2,1,0:T(8,128)(2,1)}), bf16[8,16,2176]{2,1,0:T(8,128)(2,1)S(1)}, u32[]{:S(2)}, u32[]{:S(2)}) async-start(bf16[8,16,2176]{2,1,0:T(8,128)(2,1)} %bitcast.12), calls=%async_computation | async-start | bytes 1114112 | tf_op jit(solution)/shard_map/all_to_all | solution.py:420
  24.7 6.3 %local_part.3 = (bf16[1024,2048]{1,0:T(8,128)(2,1)}, f32[128,2048]{1,0:T(8,128)}) custom-call(bf16[1024,2048]{1,0:T(8,128)(2,1)} %get-tuple-element.34.xc_ref, bf16[1024,512]{1,0:T(8,128)(2,1)} %get-tuple-element.35.bc_ref, bf16[2,128,1024]{2,1,0:T(8,128)(2,1)} %get-tuple-element.36.bt_ref, f32[32,1024]{1,0:T(8,128)} %get-tuple-element.37.crow_ref, ...), custom_call_target="tpu_custom_call" | custom-call | flops 1 | bytes 1 | tf_op jit(solution)/shard_map/local_part/pallas_call | solution.py:446
  30.9 2.4 %all-to-all-done.pay_ref = bf16[8,16,2176]{2,1,0:T(8,128)(2,1)S(1)} async-done(((bf16[8,16,2176]{2,1,0:T(8,128)(2,1)}), bf16[8,16,2176]{2,1,0:T(8,128)(2,1)S(1)}, u32[]{:S(2)}, u32[]{:S(2)}) %all-to-all-start) | async-done | bytes 557088 | tf_op jit(solution)/shard_map/all_to_all | solution.py:420
  33.3 0.0 copy-done
  33.3 1.1 prefix.1.rest_2_
  34.4 4.9 %all-to-all-start.1 = ((bf16[8,16,2048]{2,1,0:T(8,128)(2,1)}), bf16[8,16,2048]{2,1,0:T(8,128)(2,1)S(1)}, u32[]{:S(2)}, u32[]{:S(2)}) async-start(bf16[8,16,2048]{2,1,0:T(8,128)(2,1)} %prefix.1.rest_2_), calls=%async_computation.1 | async-start | bytes 1048576 | tf_op jit(solution)/shard_map/all_to_all | solution.py:473
  39.2 6.9 %local_part.4 = (bf16[1024,2048]{1,0:T(8,128)(2,1)}, f32[128,2048]{1,0:T(8,128)}) custom-call(bf16[1024,2048]{1,0:T(8,128)(2,1)} %get-tuple-element.34.xc_ref, bf16[1024,512]{1,0:T(8,128)(2,1)} %get-tuple-element.35.bc_ref, bf16[2,128,1024]{2,1,0:T(8,128)(2,1)} %get-tuple-element.36.bt_ref, ...), custom_call_target="tpu_custom_call", output_to_operand_aliasing={{0}: (8, {})} | custom-call | flops 1 | bytes 1 | tf_op jit(solution)/shard_map/local_part/pallas_call | solution.py:446
  46.1 1.4 %all-to-all-done.1 = bf16[8,16,2048]{2,1,0:T(8,128)(2,1)S(1)} async-done(((bf16[8,16,2048]{2,1,0:T(8,128)(2,1)}), bf16[8,16,2048]{2,1,0:T(8,128)(2,1)S(1)}, u32[]{:S(2)}, u32[]{:S(2)}) %all-to-all-start.1) | async-done | bytes 524320 | tf_op jit(solution)/shard_map/all_to_all | solution.py:473
  47.5 0.0 copy-start.1
  47.5 0.8 copy-done.1
  48.3 10.0 %project_direct.1 = (bf16[384,512]{1,0:T(8,128)(2,1)}, bf16[384,512]{1,0:T(8,128)(2,1)}, bf16[384,512]{1,0:T(8,128)(2,1)}, bf16[384,2048]{1,0:T(8,128)(2,1)}) custom-call(s32[1]{0:T(128)} %bitcast.where_ref, bf16[1024,2048]{1,0:T(8,128)(2,1)} %get-tuple-element.44.y_ref.rest_1_, bf16[1024,512]{1,0:T(8,128)(2,1)} %get-tuple-element.35.bc_ref, ...), custom_call_target="tpu_custom_call" | custom-call | tf_op jit(solution)/shard_map/project_direct/pallas_call | solution.py:508
  58.3 1.6 %collective-permute-start.3 = (bf16[384,512]{1,0:T(8,128)(2,1)}, bf16[384,512]{1,0:T(8,128)(2,1)S(1)}, u32[]{:S(2)}, u32[]{:S(2)}) collective-permute-start(bf16[384,512]{1,0:T(8,128)(2,1)} %get-tuple-element.52), channel_id=1, source_target_pairs={{0,1},{1,2},{2,3},{3,0},{4,5},{5,6},{6,7},{7,4},{8,9},{9,10},{10,1... | collective-permute-start | bytes 1179656 | tf_op jit(solution)/shard_map/ppermute | solution.py:670
  59.9 2.2 %collective-permute-start.4 = (bf16[384,512]{1,0:T(8,128)(2,1)}, bf16[384,512]{1,0:T(8,128)(2,1)S(1)}, u32[]{:S(2)}, u32[]{:S(2)}) collective-permute-start(bf16[384,512]{1,0:T(8,128)(2,1)} %get-tuple-element.53), channel_id=1, source_target_pairs={{0,3},{1,0},{2,1},{3,2},{4,7},{5,4},{6,5},{7,6},{8,11},{9,8},{10,9... | collective-permute-start | bytes 1179656 | tf_op jit(solution)/shard_map/ppermute | solution.py:670
  62.2 0.8 collective-permute-start.5
  62.9 5.4 %local_part.5 = (bf16[1024,2048]{1,0:T(8,128)(2,1)}, f32[128,2048]{1,0:T(8,128)}) custom-call(bf16[1024,2048]{1,0:T(8,128)(2,1)} %get-tuple-element.34.xc_ref, bf16[1024,512]{1,0:T(8,128)(2,1)} %get-tuple-element.35.bc_ref, bf16[2,128,1024]{2,1,0:T(8,128)(2,1)} %get-tuple-element.36.bt_ref, ...), custom_call_target="tpu_custom_call", output_to_operand_aliasing={{0}: (8, {})} | custom-call | flops 1 | bytes 1 | tf_op jit(solution)/shard_map/local_part/pallas_call | solution.py:446
  68.3 12.9 %project_ends.1 = (bf16[4,640,512]{2,1,0:T(8,128)(2,1)}, bf16[640,512]{1,0:T(8,128)(2,1)}, bf16[640,512]{1,0:T(8,128)(2,1)}, bf16[640,2048]{1,0:T(8,128)(2,1)}) custom-call(bf16[1024,2048]{1,0:T(8,128)(2,1)} %get-tuple-element.47.y_ref, bf16[1024,512]{1,0:T(8,128)(2,1)} %get-tuple-element.35.bc_ref, bf16[1024,128]{1,0:T(8,128)(2,1)} %get-tuple-element.45.g_ref, ...), custom_call_target="tpu_custom_call" | custom-call | flops 1 | bytes 1 | tf_op jit(solution)/shard_map/project_ends/pallas_call | solution.py:551
  81.2 3.5 %collective-permute-start.1 = (bf16[640,512]{1,0:T(8,128)(2,1)}, bf16[640,512]{1,0:T(8,128)(2,1)S(1)}, u32[]{:S(2)}, u32[]{:S(2)}) collective-permute-start(bf16[640,512]{1,0:T(8,128)(2,1)} %get-tuple-element.50), channel_id=1, source_target_pairs={{0,1},{4,5},{8,9},{12,13},{16,17},{20,21},{24,25},{28,29}} | collective-permute-start | bytes 1966088 | tf_op jit(solution)/shard_map/ppermute | solution.py:593
  84.7 0.7 collective-permute-start.2
  85.4 6.3 %project_middle.1.refs_3_.up_own_ref.down_own_ref.own_ref = bf16[4,640,512]{2,1,0:T(8,128)(2,1)} custom-call(bf16[640,2048]{1,0:T(8,128)(2,1)} %get-tuple-element.48.normed_ref, bf16[2048,2048]{1,0:T(8,128)(2,1)} %w_ref.7, bf16[4,640,512]{2,1,0:T(8,128)(2,1)} %get-tuple-element.49.ends_ref), custom_call_target="tpu_custom_call", output_to_operand_aliasing={{}: (2, {})} | custom-call | flops 1 | bytes 1 | tf_op jit(solution)/shard_map/project_middle/pallas_call | solution.py:576
  91.7 0.0 collective-permute-done.3.refs_0_
  91.7 0.0 collective-permute-done.4.refs_1_
  91.7 5.0 %collective-permute-done.5.refs_2_ = bf16[384,512]{1,0:T(8,128)(2,1)S(1)} collective-permute-done((bf16[384,512]{1,0:T(8,128)(2,1)}, bf16[384,512]{1,0:T(8,128)(2,1)S(1)}, u32[]{:S(2)}, u32[]{:S(2)}) %collective-permute-start.5) | collective-permute-done | bytes 393248 | tf_op jit(solution)/shard_map/ppermute | solution.py:670
  96.8 3.0 %collective-permute-done.1.up_ref = bf16[640,512]{1,0:T(8,128)(2,1)S(1)} collective-permute-done((bf16[640,512]{1,0:T(8,128)(2,1)}, bf16[640,512]{1,0:T(8,128)(2,1)S(1)}, u32[]{:S(2)}, u32[]{:S(2)}) %collective-permute-start.1) | collective-permute-done | bytes 655392 | tf_op jit(solution)/shard_map/ppermute | solution.py:593
  99.8 0.0 collective-permute-done.2.down_ref
  99.8 1.3 onward.4
  101.1 0.7 collective-permute-start.9
  101.8 4.9 %collective-permute-start.8 = (bf16[384,512]{1,0:T(8,128)(2,1)S(1)}, bf16[384,512]{1,0:T(8,128)(2,1)S(1)}, u32[]{:S(2)}, u32[]{:S(2)}) collective-permute-start(bf16[384,512]{1,0:T(8,128)(2,1)S(1)} %get-tuple-element.55.rest_0_), channel_id=1, source_target_pairs={{0,1},{1,2},{4,5},{5,6},{8,9},{9,10},{12,13},{13,14},{16,17},{17,1... | collective-permute-start | bytes 1179656 | tf_op jit(solution)/shard_map/ppermute | solution.py:593
  106.7 1.2 onward.5
  107.9 0.7 collective-permute-start.7
  108.6 5.2 %collective-permute-start.6 = (bf16[256,512]{1,0:T(8,128)(2,1)S(1)}, bf16[256,512]{1,0:T(8,128)(2,1)S(1)}, u32[]{:S(2)}, u32[]{:S(2)}) collective-permute-start(bf16[256,512]{1,0:T(8,128)(2,1)S(1)} %get-tuple-element.56.refs_3_), channel_id=1, source_target_pairs={{0,1},{1,2},{4,5},{5,6},{8,9},{9,10},{12,13},{13,14},{16,17},{17,1... | collective-permute-start | bytes 786440 | tf_op jit(solution)/shard_map/ppermute | solution.py:593
  113.8 4.5 %direct_final.1.rest_0_ = bf16[1024,512]{1,0:T(8,128)(2,1)} custom-call(s32[1]{0:T(128)} %bitcast.where_ref, bf16[384,2048]{1,0:T(8,128)(2,1)} %get-tuple-element.46.rest_2_.after_ref.normed_ref, bf16[2048,2048]{1,0:T(8,128)(2,1)} %w_ref.7, bf16[384,512]{1,0:T(8,128)(2,1)S(1)} %collective-permute-done.3.refs_0_, ...), custom_call_target="tpu_custom_call" | custom-call | tf_op jit(solution)/shard_map/direct_final/pallas_call | solution.py:526
  118.3 0.0 collective-permute-done.9.down_ref
  118.3 0.0 collective-permute-done.8.up_ref
  118.3 1.3 onward.6
  119.6 1.3 collective-permute-start.13
  120.9 5.2 %collective-permute-start.12 = (bf16[384,512]{1,0:T(8,128)(2,1)S(1)}, bf16[384,512]{1,0:T(8,128)(2,1)S(1)}, u32[]{:S(2)}, u32[]{:S(2)}) collective-permute-start(bf16[384,512]{1,0:T(8,128)(2,1)S(1)} %get-tuple-element.59.rest_0_), channel_id=1, source_target_pairs={{0,1},{1,2},{2,3},{4,5},{5,6},{6,7},{8,9},{9,10},{10,11},{12,13},{... | collective-permute-start | bytes 1179656 | tf_op jit(solution)/shard_map/ppermute | solution.py:593
  126.1 0.0 collective-permute-done.7.down_ref
  126.1 0.0 collective-permute-done.6.up_ref
  126.1 1.2 onward.7
  127.3 3.9 %collective-permute-start.10 = (bf16[256,512]{1,0:T(8,128)(2,1)S(1)}, bf16[256,512]{1,0:T(8,128)(2,1)S(1)}, u32[]{:S(2)}, u32[]{:S(2)}) collective-permute-start(bf16[256,512]{1,0:T(8,128)(2,1)S(1)} %get-tuple-element.60), channel_id=1, source_target_pairs={{0,1},{1,2},{2,3},{4,5},{5,6},{6,7},{8,9},{9,10},{10,11},{12,13},{... | collective-permute-start | bytes 786440 | tf_op jit(solution)/shard_map/ppermute | solution.py:593
  131.2 1.3 collective-permute-start.11
  132.5 0.0 collective-permute-done.13.down_ref
  132.5 2.9 %collective-permute-done.12.up_ref = bf16[384,512]{1,0:T(8,128)(2,1)S(1)} collective-permute-done((bf16[384,512]{1,0:T(8,128)(2,1)S(1)}, bf16[384,512]{1,0:T(8,128)(2,1)S(1)}, u32[]{:S(2)}, u32[]{:S(2)}) %collective-permute-start.12) | collective-permute-done | bytes 393248 | tf_op jit(solution)/shard_map/ppermute | solution.py:593
  135.5 2.7 %final.2.rest_0_ = bf16[1024,512]{1,0:T(8,128)(2,1)} custom-call(s32[1]{0:T(128)} %bitcast.where_ref, bf16[4,640,512]{2,1,0:T(8,128)(2,1)} %project_middle.1.refs_3_.up_own_ref.down_own_ref.own_ref, bf16[384,512]{1,0:T(8,128)(2,1)S(1)} %collective-permute-done.12.up_ref, ...), custom_call_target="tpu_custom_call", output_to_operand_aliasing={{}: (4, {})} | custom-call | tf_op jit(solution)/shard_map/final/pallas_call | solution.py:650
  138.2 0.1 collective-permute-done.10.up_ref
  138.3 1.2 collective-permute-done.11.down_ref
  139.5 1.7 %final.3 = bf16[1024,512]{1,0:T(8,128)(2,1)} custom-call(s32[1]{0:T(128)} %bitcast.where_ref, bf16[4,640,512]{2,1,0:T(8,128)(2,1)} %project_middle.1.refs_3_.up_own_ref.down_own_ref.own_ref, bf16[256,512]{1,0:T(8,128)(2,1)S(1)} %collective-permute-done.10.up_ref, ...), custom_call_target="tpu_custom_call", output_to_operand_aliasing={{}: (4, {})} | custom-call | tf_op jit(solution)/shard_map/final/pallas_call | solution.py:650
  (3 shorter events, 0.0 us)
Async XLA Ops:
  1.5 5.3 %collective-permute-start = (bf16[8,2560]{1,0:T(8,128)(2,1)S(1)}, bf16[8,2560]{1,0:T(8,128)(2,1)S(1)}, u32[]{:S(2)}, u32[]{:S(2)}) collective-permute-start(bf16[8,2560]{1,0:T(8,128)(2,1)S(1)} %pad_maximum_fusion), channel_id=1, source_target_pairs={{0,4},{4,8},{8,12},{12,16},{16,20},{20,24},{24,28},{1,5},{5,9},{9,... | collective-permute-start | bytes 122888 | tf_op jit(solution)/shard_map/ppermute | solution.py:373
  6.8 0.6 copy-start.2
  20.3 13.0 %copy-start = (bf16[128,2048]{1,0:T(8,128)(2,1)S(1)}, bf16[128,2048]{1,0:T(8,128)(2,1)}, u32[]{:S(2)}) copy-start(bf16[128,2048]{1,0:T(8,128)(2,1)} %constant.6.clone.e_ref) | copy-start | bytes 1572868
  20.3 13.0 %all-to-all-start = ((bf16[8,16,2176]{2,1,0:T(8,128)(2,1)}), bf16[8,16,2176]{2,1,0:T(8,128)(2,1)S(1)}, u32[]{:S(2)}, u32[]{:S(2)}) async-start(bf16[8,16,2176]{2,1,0:T(8,128)(2,1)} %bitcast.12), calls=%async_computation | async-start | bytes 1114112 | tf_op jit(solution)/shard_map/all_to_all | solution.py:420
  34.4 13.2 %all-to-all-start.1 = ((bf16[8,16,2048]{2,1,0:T(8,128)(2,1)}), bf16[8,16,2048]{2,1,0:T(8,128)(2,1)S(1)}, u32[]{:S(2)}, u32[]{:S(2)}) async-start(bf16[8,16,2048]{2,1,0:T(8,128)(2,1)} %prefix.1.rest_2_), calls=%async_computation.1 | async-start | bytes 1048576 | tf_op jit(solution)/shard_map/all_to_all | solution.py:473
  47.5 0.8 copy-start.1
  58.3 33.4 %collective-permute-start.3 = (bf16[384,512]{1,0:T(8,128)(2,1)}, bf16[384,512]{1,0:T(8,128)(2,1)S(1)}, u32[]{:S(2)}, u32[]{:S(2)}) collective-permute-start(bf16[384,512]{1,0:T(8,128)(2,1)} %get-tuple-element.52), channel_id=1, source_target_pairs={{0,1},{1,2},{2,3},{3,0},{4,5},{5,6},{6,7},{7,4},{8,9},{9,10},{10,1... | collective-permute-start | bytes 1179656 | tf_op jit(solution)/shard_map/ppermute | solution.py:670
  59.9 31.8 %collective-permute-start.4 = (bf16[384,512]{1,0:T(8,128)(2,1)}, bf16[384,512]{1,0:T(8,128)(2,1)S(1)}, u32[]{:S(2)}, u32[]{:S(2)}) collective-permute-start(bf16[384,512]{1,0:T(8,128)(2,1)} %get-tuple-element.53), channel_id=1, source_target_pairs={{0,3},{1,0},{2,1},{3,2},{4,7},{5,4},{6,5},{7,6},{8,11},{9,8},{10,9... | collective-permute-start | bytes 1179656 | tf_op jit(solution)/shard_map/ppermute | solution.py:670
  62.2 34.6 %collective-permute-start.5 = (bf16[384,512]{1,0:T(8,128)(2,1)}, bf16[384,512]{1,0:T(8,128)(2,1)S(1)}, u32[]{:S(2)}, u32[]{:S(2)}) collective-permute-start(bf16[384,512]{1,0:T(8,128)(2,1)} %get-tuple-element.54), channel_id=1, source_target_pairs={{0,2},{1,3},{2,0},{3,1},{4,6},{5,7},{6,4},{7,5},{8,10},{9,11},{10,... | collective-permute-start | bytes 1179656 | tf_op jit(solution)/shard_map/ppermute | solution.py:670
  81.2 18.6 %collective-permute-start.1 = (bf16[640,512]{1,0:T(8,128)(2,1)}, bf16[640,512]{1,0:T(8,128)(2,1)S(1)}, u32[]{:S(2)}, u32[]{:S(2)}) collective-permute-start(bf16[640,512]{1,0:T(8,128)(2,1)} %get-tuple-element.50), channel_id=1, source_target_pairs={{0,1},{4,5},{8,9},{12,13},{16,17},{20,21},{24,25},{28,29}} | collective-permute-start | bytes 1966088 | tf_op jit(solution)/shard_map/ppermute | solution.py:593
  84.7 15.1 %collective-permute-start.2 = (bf16[640,512]{1,0:T(8,128)(2,1)}, bf16[640,512]{1,0:T(8,128)(2,1)S(1)}, u32[]{:S(2)}, u32[]{:S(2)}) collective-permute-start(bf16[640,512]{1,0:T(8,128)(2,1)} %get-tuple-element.51), channel_id=1, source_target_pairs={{3,2},{7,6},{11,10},{15,14},{19,18},{23,22},{27,26},{31,30}} | collective-permute-start | bytes 1966088 | tf_op jit(solution)/shard_map/ppermute | solution.py:594
  101.1 17.2 %collective-permute-start.9 = (bf16[384,512]{1,0:T(8,128)(2,1)S(1)}, bf16[384,512]{1,0:T(8,128)(2,1)S(1)}, u32[]{:S(2)}, u32[]{:S(2)}) collective-permute-start(bf16[384,512]{1,0:T(8,128)(2,1)S(1)} %get-tuple-element.58), channel_id=1, source_target_pairs={{2,1},{3,2},{6,5},{7,6},{10,9},{11,10},{14,13},{15,14},{18,17},{19... | collective-permute-start | bytes 1179656 | tf_op jit(solution)/shard_map/ppermute | solution.py:594
  101.8 16.5 %collective-permute-start.8 = (bf16[384,512]{1,0:T(8,128)(2,1)S(1)}, bf16[384,512]{1,0:T(8,128)(2,1)S(1)}, u32[]{:S(2)}, u32[]{:S(2)}) collective-permute-start(bf16[384,512]{1,0:T(8,128)(2,1)S(1)} %get-tuple-element.55.rest_0_), channel_id=1, source_target_pairs={{0,1},{1,2},{4,5},{5,6},{8,9},{9,10},{12,13},{13,14},{16,17},{17,1... | collective-permute-start | bytes 1179656 | tf_op jit(solution)/shard_map/ppermute | solution.py:593
  107.9 18.2 %collective-permute-start.7 = (bf16[256,512]{1,0:T(8,128)(2,1)S(1)}, bf16[256,512]{1,0:T(8,128)(2,1)S(1)}, u32[]{:S(2)}, u32[]{:S(2)}) collective-permute-start(bf16[256,512]{1,0:T(8,128)(2,1)S(1)} %get-tuple-element.57), channel_id=1, source_target_pairs={{2,1},{3,2},{6,5},{7,6},{10,9},{11,10},{14,13},{15,14},{18,17},{19... | collective-permute-start | bytes 786440 | tf_op jit(solution)/shard_map/ppermute | solution.py:594
  108.6 17.5 %collective-permute-start.6 = (bf16[256,512]{1,0:T(8,128)(2,1)S(1)}, bf16[256,512]{1,0:T(8,128)(2,1)S(1)}, u32[]{:S(2)}, u32[]{:S(2)}) collective-permute-start(bf16[256,512]{1,0:T(8,128)(2,1)S(1)} %get-tuple-element.56.refs_3_), channel_id=1, source_target_pairs={{0,1},{1,2},{4,5},{5,6},{8,9},{9,10},{12,13},{13,14},{16,17},{17,1... | collective-permute-start | bytes 786440 | tf_op jit(solution)/shard_map/ppermute | solution.py:593
  119.6 13.0 %collective-permute-start.13 = (bf16[384,512]{1,0:T(8,128)(2,1)S(1)}, bf16[384,512]{1,0:T(8,128)(2,1)S(1)}, u32[]{:S(2)}, u32[]{:S(2)}) collective-permute-start(bf16[384,512]{1,0:T(8,128)(2,1)S(1)} %get-tuple-element.62), channel_id=1, source_target_pairs={{1,0},{2,1},{3,2},{5,4},{6,5},{7,6},{9,8},{10,9},{11,10},{13,12},{... | collective-permute-start | bytes 1179656 | tf_op jit(solution)/shard_map/ppermute | solution.py:594
  120.9 14.6 %collective-permute-start.12 = (bf16[384,512]{1,0:T(8,128)(2,1)S(1)}, bf16[384,512]{1,0:T(8,128)(2,1)S(1)}, u32[]{:S(2)}, u32[]{:S(2)}) collective-permute-start(bf16[384,512]{1,0:T(8,128)(2,1)S(1)} %get-tuple-element.59.rest_0_), channel_id=1, source_target_pairs={{0,1},{1,2},{2,3},{4,5},{5,6},{6,7},{8,9},{9,10},{10,11},{12,13},{... | collective-permute-start | bytes 1179656 | tf_op jit(solution)/shard_map/ppermute | solution.py:593
  127.3 11.0 %collective-permute-start.10 = (bf16[256,512]{1,0:T(8,128)(2,1)S(1)}, bf16[256,512]{1,0:T(8,128)(2,1)S(1)}, u32[]{:S(2)}, u32[]{:S(2)}) collective-permute-start(bf16[256,512]{1,0:T(8,128)(2,1)S(1)} %get-tuple-element.60), channel_id=1, source_target_pairs={{0,1},{1,2},{2,3},{4,5},{5,6},{6,7},{8,9},{9,10},{10,11},{12,13},{... | collective-permute-start | bytes 786440 | tf_op jit(solution)/shard_map/ppermute | solution.py:593
  131.2 8.3 %collective-permute-start.11 = (bf16[256,512]{1,0:T(8,128)(2,1)S(1)}, bf16[256,512]{1,0:T(8,128)(2,1)S(1)}, u32[]{:S(2)}, u32[]{:S(2)}) collective-permute-start(bf16[256,512]{1,0:T(8,128)(2,1)S(1)} %get-tuple-element.61), channel_id=1, source_target_pairs={{1,0},{2,1},{3,2},{5,4},{6,5},{7,6},{9,8},{10,9},{11,10},{13,12},{... | collective-permute-start | bytes 786440 | tf_op jit(solution)/shard_map/ppermute | solution.py:594

commit v10 on v9

--- a/solution.py
+++ b/solution.py
@@ -22,7 +22,7 @@
 LOG2E = 1.4426950408889634
 F32 = jnp.float32
 BF16 = jnp.bfloat16
-VMEM_LIMIT = 58 * 1024 * 1024
+VMEM_LIMIT = 40 * 1024 * 1024
 SMALL_LIMIT = 10 * 1024 * 1024
 
 
@@ -80,7 +80,7 @@
     xc_ref, pay_ref, *rest,
 ):
     outs, (bc_ref, bt_ref, crow_ref, cols_ref, wrow_ref, g_ref) = rest[:6], rest[6:12]
-    weighted, w_ref, scale, sems = rest[12:]
+    weighted, w_ref, scale, plain, early, sems = rest[12:]
     copies = [
         pltpu.make_async_copy(kept, out, sems.at[k])
         for k, (kept, out) in enumerate(zip(rest[6:12], outs))
@@ -159,14 +159,25 @@
     for lane in range(0, x_ref.shape[1], LANES):
         at_lanes = slice(lane, lane + LANES)
         taps = [ck_ref[k : k + 1, at_lanes] for k in range(4)]
-        before = tail_ref[:, at_lanes].astype(F32)
+        tail = tail_ref[:, at_lanes].astype(F32)
+        plain[:HALO] = tail
+        early[:HALO] = taps[1] * tail + taps[0] * pltpu.roll(tail, 1, 0)
+        plain[HALO:] = x_ref[:, at_lanes].astype(F32)
         for b in range(blocks):
-            at = slice(b * BLK, (b + 1) * BLK)
-            cur = x_ref[at, at_lanes].astype(F32)
-            result = conv(before, cur, taps)
-            before = cur[BLK - HALO :]
-            xc_ref[at, at_lanes] = result.astype(BF16)
-            weighted[at, at_lanes] = (result * scale[at, at_lanes]).astype(BF16)
+            at = b * BLK
+            late = plain[at + HALO - 1 : at + HALO - 1 + BLK]
+            early[at + HALO : at + HALO + BLK] = (
+                taps[1] * plain[at + HALO : at + HALO + BLK] + taps[0] * late
+            )
+            acc = (
+                taps[3] * plain[at + HALO : at + HALO + BLK]
+                + taps[2] * late
+                + early[at + HALO - 2 : at + HALO - 2 + BLK]
+            )
+            result = silu(acc)
+            xc_ref[at : at + BLK, at_lanes] = result.astype(BF16)
+            scaled = result * scale[at : at + BLK, at_lanes]
+            weighted[at : at + BLK, at_lanes] = scaled.astype(BF16)
     step_width = x_ref.shape[1]
     group = c * step_width * groups // (heads * HEAD_DIM)
     at = pl.ds(pl.multiple_of(c * step_width, step_width), step_width)
@@ -349,7 +360,7 @@
 
 
 def shaped(shape, dtype=BF16):
-    return jax.ShapeDtypeStruct(shape, dtype)
+    return pltpu.HBM(shape, dtype)
 
 
 def local(
@@ -406,14 +417,17 @@
             pltpu.VMEM((tokens, WIDE), BF16),
             pltpu.VMEM((tokens, LANES), BF16),
             pltpu.VMEM((tokens, WIDE), F32),
+            pltpu.VMEM((HALO + tokens, LANES), F32),
+            pltpu.VMEM((HALO + tokens, LANES), F32),
             pltpu.SemaphoreType.DMA((6,)),
         ],
         compiler_params=params(),
         name="states",
     )(
-        inner_input, state_maps.reshape(tokens * parts, STATE), step_input.T, tail, tail,
-        step_bias.reshape(1, heads), log_decay_rate.reshape(1, heads),
-        conv_kernel, map_kernel.reshape(4 * parts, STATE), low,
+        in_hbm(inner_input), in_hbm(state_maps.reshape(tokens * parts, STATE)),
+        in_hbm(step_input.T), tail, tail,
+        in_hbm(step_bias.reshape(1, heads)), in_hbm(log_decay_rate.reshape(1, heads)),
+        in_hbm(conv_kernel), in_hbm(map_kernel.reshape(4 * parts, STATE)), in_hbm(low),
     )
 
     part = STATE // slabs
@@ -425,7 +439,8 @@
         def tile(width):
             return pl.BlockSpec((BLK, width), lambda b: (start + b, 0))
 
-        operands = [xc, bc, bt, crow, cols, wrow, skip_gain.reshape(1, heads)]
+        operands = [in_hbm(k) for k in (xc, bc, bt, crow, cols, wrow)]
+        operands.append(skip_gain.reshape(1, heads))
         specs = [
             tile(width),
             tile(map_width),
@@ -439,7 +454,7 @@
         if before is not None:
             y, state = before
             aliases = {len(operands) + 1: 0}
-            operands += [state, in_hbm(y)]
+            operands += [in_hbm(state), in_hbm(y)]
             specs += [whole((STATE, width)), unread()]
         operands.append(in_hbm(after))
         specs.append(unread())
@@ -482,7 +497,8 @@
         def tile(width):
             return pl.BlockSpec((tokens_each, width), lambda i, *_: (start + jnp.minimum(i, count - 1), 0))
 
-        operands = [y, bc, g_hl, entering, gate_input, norm_row, low]
+        operands = [in_hbm(k) for k in (y, bc, g_hl)] + [entering]
+        operands += [in_hbm(k) for k in (gate_input, norm_row, low)]
         specs = [
             tile(width),
             tile(map_width),
@@ -587,7 +603,7 @@
             compiler_params=params(),
             cost_estimate=brief(),
             name="project_middle",
-        )(normed, out_weight, in_hbm(shares))
+        )(in_hbm(normed), out_weight, in_hbm(shares))
 
     def permuted(up, down, s):
         up = lax.ppermute(up, "chan", [(a, a + 1) for a in range(s + 1)])
@@ -625,7 +641,7 @@
                 + [unread()] * len(after),
                 out_specs=[pl.BlockSpec((tile, part_out), plain)] * 2,
             ),
-            out_shape=[shaped((count, part_out))] * 2,
+            out_shape=[jax.ShapeDtypeStruct((count, part_out), BF16)] * 2,
             compiler_params=params(SMALL_LIMIT),
             name="onward",
         )(where, in_hbm(shares), in_hbm(shares), up, down, *after)
@@ -680,7 +696,7 @@
         arrived_kernel,
         in_specs=[unread()] * (len(pieces) + 1),
         out_specs=pl.BlockSpec(memory_space=pltpu.VMEM),
-        out_shape=shaped((HALO, LANES), F32),
+        out_shape=jax.ShapeDtypeStruct((HALO, LANES), F32),
         compiler_params=pltpu.CompilerParams(vmem_limit_bytes=SMALL_LIMIT),
         cost_estimate=pl.CostEstimate(flops=20000000000, transcendentals=0, bytes_accessed=1),
         name="arrived",

time: 142 us -> 143 us (level)
  Pallas kernels: 75.5 us -> 72.7 us
  local copies, waits for them, and re-layouts: 2.88 us -> 4.88 us
    unnamed x6, local copies, waits for them, and re-layouts: 1.4 us -> 3.39 us
  transfers between devices with their start and end apart: 16 -> 16, of which waited for: 8 -> 8; matrix products, arithmetic and copies ran while one was open for 0% -> 0% of each run, Pallas kernels for 34% -> 33%
where the time goes in v10:
time: 143 us; the launch traced here: 142 us
  Pallas kernels  72.7 us (51%)
  starting transfers between devices  43.1 us (30%)
  waiting for transfers between devices  21 us (15%)
  local copies, waits for them, and re-layouts  4.88 us (3%)
    ppermute x5, starting transfers between devices, permuted(): up = lax.ppermute(up, 'chan', [(a, a + 1) for a in range(s + 1)])  22.7 us
    pallas_call x3, Pallas kernels, local_part(): pl.pallas_call(local_kernel, grid=(count,), in_specs=specs, out_specs=[ti...  18.3 us
    pallas_call x1, Pallas kernels, local(): pl.pallas_call(states_kernel, grid=(width // WIDE,), in_specs=[lanes_at(t...  12.7 us
    pallas_call x1, Pallas kernels, project_ends(): pl.pallas_call(functools.partial(ends_kernel, tiles=count), grid=(count +...  12.1 us
    pallas_call x1, Pallas kernels, project_direct(): pl.pallas_call(functools.partial(direct_kernel, tiles=count), grid_spec=p...  8.87 us
    ppermute x3, waiting for transfers between devices, local(): pieces.append(lax.ppermute(slot, 'chan', turn))  6.28 us
    ppermute x5, waiting for transfers between devices, permuted(): up = lax.ppermute(up, 'chan', [(a, a + 1) for a in range(s + 1)])  6.09 us
    pallas_call x1, Pallas kernels, project_middle(): pl.pallas_call(middle_kernel, grid=(chans - 2,), in_specs=[whole((size, w...  5.83 us
  transfers between devices with their start and end apart: 16, of which 8 were waited for; matrix products, arithmetic and copies ran while one was open for 0% of the time, Pallas kernels for 33%

profile of v10, /device:TPU:2, one launch (start us, length us, event | category | flops | bytes accessed | tf_op | source)
XLA Modules:
  0.0 141.9 jit_solution(4965453754306287560)
XLA Ops:
  0.0 0.0 copy-start.2
  0.0 0.7 slice.7
  0.7 0.8 slice.6
  1.5 1.9 %collective-permute-start = (bf16[8,2560]{1,0:T(8,128)(2,1)S(1)}, bf16[8,2560]{1,0:T(8,128)(2,1)S(1)}, u32[]{:S(2)}, u32[]{:S(2)}) collective-permute-start(bf16[8,2560]{1,0:T(8,128)(2,1)S(1)} %pad_maximum_fusion), channel_id=1, source_target_pairs={{0,4},{4,8},{8,12},{12,16},{16,20},{20,24},{24,28},{1,5},{5,9},{9,... | collective-permute-start | bytes 122888 | tf_op jit(solution)/shard_map/ppermute | solution.py:384
  3.4 3.4 %collective-permute-done.tail_ref.mtail_ref = bf16[8,2560]{1,0:T(8,128)(2,1)S(1)} collective-permute-done((bf16[8,2560]{1,0:T(8,128)(2,1)S(1)}, bf16[8,2560]{1,0:T(8,128)(2,1)S(1)}, u32[]{:S(2)}, u32[]{:S(2)}) %collective-permute-start) | collective-permute-done | bytes 40992 | tf_op jit(solution)/shard_map/ppermute | solution.py:384
  6.8 12.7 %states.1 = (bf16[1024,2048]{1,0:T(8,128)(2,1)}, bf16[128,2176]{1,0:T(8,128)(2,1)}, bf16[1024,512]{1,0:T(8,128)(2,1)}, bf16[2,128,1024]{2,1,0:T(8,128)(2,1)}, f3...) custom-call(bf16[1024,2048]{1,0:T(8,128)(2,1)} %x_ref.1, ...), custom_call_target="tpu_custom_call" | custom-call | tf_op jit(solution)/shard_map/states/pallas_call | solution.py:397
  19.5 0.0 copy-start.1
  19.5 4.4 %all-to-all-start = ((bf16[8,16,2176]{2,1,0:T(8,128)(2,1)}), bf16[8,16,2176]{2,1,0:T(8,128)(2,1)S(1)}, u32[]{:S(2)}, u32[]{:S(2)}) async-start(bf16[8,16,2176]{2,1,0:T(8,128)(2,1)} %bitcast.15), calls=%async_computation | async-start | bytes 1114112 | tf_op jit(solution)/shard_map/all_to_all | solution.py:434
  23.9 0.0 copy-done.2
  23.9 6.3 %local_part.3 = (bf16[1024,2048]{1,0:T(8,128)(2,1)}, f32[128,2048]{1,0:T(8,128)}) custom-call(bf16[1024,2048]{1,0:T(8,128)(2,1)} %get-tuple-element.34.xc_ref, bf16[1024,512]{1,0:T(8,128)(2,1)} %get-tuple-element.35.bc_ref, bf16[2,128,1024]{2,1,0:T(8,128)(2,1)} %get-tuple-element.36.bt_ref, f32[32,1024]{1,0:T(8,128)} %get-tuple-element.37.crow_ref, ...), custom_call_target="tpu_custom_call" | custom-call | flops 1 | bytes 1 | tf_op jit(solution)/shard_map/local_part/pallas_call | solution.py:461
  30.2 2.4 %all-to-all-done.pay_ref = bf16[8,16,2176]{2,1,0:T(8,128)(2,1)S(1)} async-done(((bf16[8,16,2176]{2,1,0:T(8,128)(2,1)}), bf16[8,16,2176]{2,1,0:T(8,128)(2,1)S(1)}, u32[]{:S(2)}, u32[]{:S(2)}) %all-to-all-start) | async-done | bytes 557088 | tf_op jit(solution)/shard_map/all_to_all | solution.py:434
  32.6 0.0 copy-done.1
  32.6 1.1 prefix.1.rest_2_
  33.6 4.9 %all-to-all-start.1 = ((bf16[8,16,2048]{2,1,0:T(8,128)(2,1)}), bf16[8,16,2048]{2,1,0:T(8,128)(2,1)S(1)}, u32[]{:S(2)}, u32[]{:S(2)}) async-start(bf16[8,16,2048]{2,1,0:T(8,128)(2,1)} %prefix.1.rest_2_), calls=%async_computation.1 | async-start | bytes 1048576 | tf_op jit(solution)/shard_map/all_to_all | solution.py:488
  38.5 6.7 %local_part.4 = (bf16[1024,2048]{1,0:T(8,128)(2,1)}, f32[128,2048]{1,0:T(8,128)}) custom-call(bf16[1024,2048]{1,0:T(8,128)(2,1)} %get-tuple-element.34.xc_ref, bf16[1024,512]{1,0:T(8,128)(2,1)} %get-tuple-element.35.bc_ref, bf16[2,128,1024]{2,1,0:T(8,128)(2,1)} %get-tuple-element.36.bt_ref, ...), custom_call_target="tpu_custom_call", output_to_operand_aliasing={{0}: (8, {})} | custom-call | flops 1 | bytes 1 | tf_op jit(solution)/shard_map/local_part/pallas_call | solution.py:461
  45.2 1.6 %all-to-all-done.1 = bf16[8,16,2048]{2,1,0:T(8,128)(2,1)S(1)} async-done(((bf16[8,16,2048]{2,1,0:T(8,128)(2,1)}), bf16[8,16,2048]{2,1,0:T(8,128)(2,1)S(1)}, u32[]{:S(2)}, u32[]{:S(2)}) %all-to-all-start.1) | async-done | bytes 524320 | tf_op jit(solution)/shard_map/all_to_all | solution.py:488
  46.8 0.0 copy-start
  46.8 3.4 %copy-done = bf16[2048,2048]{1,0:T(8,128)(2,1)S(1)} copy-done((bf16[2048,2048]{1,0:T(8,128)(2,1)S(1)}, bf16[2048,2048]{1,0:T(8,128)(2,1)}, u32[]{:S(2)}) %copy-start) | copy-done | bytes 8388632
  50.2 8.9 %project_direct.1 = (bf16[384,512]{1,0:T(8,128)(2,1)}, bf16[384,512]{1,0:T(8,128)(2,1)}, bf16[384,512]{1,0:T(8,128)(2,1)}, bf16[384,2048]{1,0:T(8,128)(2,1)}) custom-call(s32[1]{0:T(128)} %bitcast.where_ref, bf16[1024,2048]{1,0:T(8,128)(2,1)} %get-tuple-element.44.y_ref.rest_1_, bf16[1024,512]{1,0:T(8,128)(2,1)} %get-tuple-element.35.bc_ref, ...), custom_call_target="tpu_custom_call" | custom-call | tf_op jit(solution)/shard_map/project_direct/pallas_call | solution.py:524
  59.0 1.6 %collective-permute-start.3 = (bf16[384,512]{1,0:T(8,128)(2,1)}, bf16[384,512]{1,0:T(8,128)(2,1)S(1)}, u32[]{:S(2)}, u32[]{:S(2)}) collective-permute-start(bf16[384,512]{1,0:T(8,128)(2,1)} %get-tuple-element.52), channel_id=1, source_target_pairs={{0,1},{1,2},{2,3},{3,0},{4,5},{5,6},{6,7},{7,4},{8,9},{9,10},{10,1... | collective-permute-start | bytes 1179656 | tf_op jit(solution)/shard_map/ppermute | solution.py:686
  60.6 2.3 %collective-permute-start.4 = (bf16[384,512]{1,0:T(8,128)(2,1)}, bf16[384,512]{1,0:T(8,128)(2,1)S(1)}, u32[]{:S(2)}, u32[]{:S(2)}) collective-permute-start(bf16[384,512]{1,0:T(8,128)(2,1)} %get-tuple-element.53), channel_id=1, source_target_pairs={{0,3},{1,0},{2,1},{3,2},{4,7},{5,4},{6,5},{7,6},{8,11},{9,8},{10,9... | collective-permute-start | bytes 1179656 | tf_op jit(solution)/shard_map/ppermute | solution.py:686
  62.9 0.8 collective-permute-start.5
  63.6 5.4 %local_part.5 = (bf16[1024,2048]{1,0:T(8,128)(2,1)}, f32[128,2048]{1,0:T(8,128)}) custom-call(bf16[1024,2048]{1,0:T(8,128)(2,1)} %get-tuple-element.34.xc_ref, bf16[1024,512]{1,0:T(8,128)(2,1)} %get-tuple-element.35.bc_ref, bf16[2,128,1024]{2,1,0:T(8,128)(2,1)} %get-tuple-element.36.bt_ref, ...), custom_call_target="tpu_custom_call", output_to_operand_aliasing={{0}: (8, {})} | custom-call | flops 1 | bytes 1 | tf_op jit(solution)/shard_map/local_part/pallas_call | solution.py:461
  69.0 12.1 %project_ends.1 = (bf16[4,640,512]{2,1,0:T(8,128)(2,1)}, bf16[640,512]{1,0:T(8,128)(2,1)}, bf16[640,512]{1,0:T(8,128)(2,1)}, bf16[640,2048]{1,0:T(8,128)(2,1)}) custom-call(bf16[1024,2048]{1,0:T(8,128)(2,1)} %get-tuple-element.47.y_ref, bf16[1024,512]{1,0:T(8,128)(2,1)} %get-tuple-element.35.bc_ref, bf16[1024,128]{1,0:T(8,128)(2,1)} %get-tuple-element.45.g_ref, ...), custom_call_target="tpu_custom_call" | custom-call | flops 1 | bytes 1 | tf_op jit(solution)/shard_map/project_ends/pallas_call | solution.py:567
  81.1 3.5 %collective-permute-start.1 = (bf16[640,512]{1,0:T(8,128)(2,1)}, bf16[640,512]{1,0:T(8,128)(2,1)S(1)}, u32[]{:S(2)}, u32[]{:S(2)}) collective-permute-start(bf16[640,512]{1,0:T(8,128)(2,1)} %get-tuple-element.50), channel_id=1, source_target_pairs={{0,1},{4,5},{8,9},{12,13},{16,17},{20,21},{24,25},{28,29}} | collective-permute-start | bytes 1966088 | tf_op jit(solution)/shard_map/ppermute | solution.py:609
  84.6 0.7 collective-permute-start.2
  85.3 5.8 %project_middle.1.refs_3_.up_own_ref.down_own_ref.own_ref = bf16[4,640,512]{2,1,0:T(8,128)(2,1)} custom-call(bf16[640,2048]{1,0:T(8,128)(2,1)} %get-tuple-element.48.normed_ref, bf16[2048,2048]{1,0:T(8,128)(2,1)S(1)} %copy-done, bf16[4,640,512]{2,1,0:T(8,128)(2,1)} %get-tuple-element.49.ends_ref), custom_call_target="tpu_custom_call", output_to_operand_aliasing={{}: (2, {})} | custom-call | flops 1 | bytes 1 | tf_op jit(solution)/shard_map/project_middle/pallas_call | solution.py:592
  91.2 0.0 collective-permute-done.3.refs_0_
  91.2 0.0 collective-permute-done.4.refs_1_
  91.2 6.3 %collective-permute-done.5.refs_2_ = bf16[384,512]{1,0:T(8,128)(2,1)S(1)} collective-permute-done((bf16[384,512]{1,0:T(8,128)(2,1)}, bf16[384,512]{1,0:T(8,128)(2,1)S(1)}, u32[]{:S(2)}, u32[]{:S(2)}) %collective-permute-start.5) | collective-permute-done | bytes 393248 | tf_op jit(solution)/shard_map/ppermute | solution.py:686
  97.5 3.0 %collective-permute-done.1.up_ref = bf16[640,512]{1,0:T(8,128)(2,1)S(1)} collective-permute-done((bf16[640,512]{1,0:T(8,128)(2,1)}, bf16[640,512]{1,0:T(8,128)(2,1)S(1)}, u32[]{:S(2)}, u32[]{:S(2)}) %collective-permute-start.1) | collective-permute-done | bytes 655392 | tf_op jit(solution)/shard_map/ppermute | solution.py:609
  100.5 0.0 collective-permute-done.2.down_ref
  100.5 1.3 onward.4
  101.8 0.7 collective-permute-start.9
  102.5 4.9 %collective-permute-start.8 = (bf16[384,512]{1,0:T(8,128)(2,1)S(1)}, bf16[384,512]{1,0:T(8,128)(2,1)S(1)}, u32[]{:S(2)}, u32[]{:S(2)}) collective-permute-start(bf16[384,512]{1,0:T(8,128)(2,1)S(1)} %get-tuple-element.55.rest_0_), channel_id=1, source_target_pairs={{0,1},{1,2},{4,5},{5,6},{8,9},{9,10},{12,13},{13,14},{16,17},{17,1... | collective-permute-start | bytes 1179656 | tf_op jit(solution)/shard_map/ppermute | solution.py:609
  107.4 1.2 onward.5
  108.6 0.7 collective-permute-start.7
  109.3 5.2 %collective-permute-start.6 = (bf16[256,512]{1,0:T(8,128)(2,1)S(1)}, bf16[256,512]{1,0:T(8,128)(2,1)S(1)}, u32[]{:S(2)}, u32[]{:S(2)}) collective-permute-start(bf16[256,512]{1,0:T(8,128)(2,1)S(1)} %get-tuple-element.56.refs_3_), channel_id=1, source_target_pairs={{0,1},{1,2},{4,5},{5,6},{8,9},{9,10},{12,13},{13,14},{16,17},{17,1... | collective-permute-start | bytes 786440 | tf_op jit(solution)/shard_map/ppermute | solution.py:609
  114.5 4.5 %direct_final.1.rest_0_ = bf16[1024,512]{1,0:T(8,128)(2,1)} custom-call(s32[1]{0:T(128)} %bitcast.where_ref, bf16[384,2048]{1,0:T(8,128)(2,1)} %get-tuple-element.46.rest_2_.after_ref.normed_ref, bf16[2048,2048]{1,0:T(8,128)(2,1)} %w_ref.7, bf16[384,512]{1,0:T(8,128)(2,1)S(1)} %collective-permute-done.3.refs_0_, ...), custom_call_target="tpu_custom_call" | custom-call | tf_op jit(solution)/shard_map/direct_final/pallas_call | solution.py:542
  119.0 0.0 collective-permute-done.9.down_ref
  119.0 0.0 collective-permute-done.8.up_ref
  119.0 1.3 onward.6
  120.3 1.3 collective-permute-start.13
  121.6 5.2 %collective-permute-start.12 = (bf16[384,512]{1,0:T(8,128)(2,1)S(1)}, bf16[384,512]{1,0:T(8,128)(2,1)S(1)}, u32[]{:S(2)}, u32[]{:S(2)}) collective-permute-start(bf16[384,512]{1,0:T(8,128)(2,1)S(1)} %get-tuple-element.59.rest_0_), channel_id=1, source_target_pairs={{0,1},{1,2},{2,3},{4,5},{5,6},{6,7},{8,9},{9,10},{10,11},{12,13},{... | collective-permute-start | bytes 1179656 | tf_op jit(solution)/shard_map/ppermute | solution.py:609
  126.8 0.0 collective-permute-done.7.down_ref
  126.8 0.0 collective-permute-done.6.up_ref
  126.8 1.2 onward.7
  128.0 3.9 %collective-permute-start.10 = (bf16[256,512]{1,0:T(8,128)(2,1)S(1)}, bf16[256,512]{1,0:T(8,128)(2,1)S(1)}, u32[]{:S(2)}, u32[]{:S(2)}) collective-permute-start(bf16[256,512]{1,0:T(8,128)(2,1)S(1)} %get-tuple-element.60), channel_id=1, source_target_pairs={{0,1},{1,2},{2,3},{4,5},{5,6},{6,7},{8,9},{9,10},{10,11},{12,13},{... | collective-permute-start | bytes 786440 | tf_op jit(solution)/shard_map/ppermute | solution.py:609
  131.9 1.3 collective-permute-start.11
  133.2 0.0 collective-permute-done.13.down_ref
  133.2 2.9 %collective-permute-done.12.up_ref = bf16[384,512]{1,0:T(8,128)(2,1)S(1)} collective-permute-done((bf16[384,512]{1,0:T(8,128)(2,1)S(1)}, bf16[384,512]{1,0:T(8,128)(2,1)S(1)}, u32[]{:S(2)}, u32[]{:S(2)}) %collective-permute-start.12) | collective-permute-done | bytes 393248 | tf_op jit(solution)/shard_map/ppermute | solution.py:609
  136.2 2.7 %final.2.rest_0_ = bf16[1024,512]{1,0:T(8,128)(2,1)} custom-call(s32[1]{0:T(128)} %bitcast.where_ref, bf16[4,640,512]{2,1,0:T(8,128)(2,1)} %project_middle.1.refs_3_.up_own_ref.down_own_ref.own_ref, bf16[384,512]{1,0:T(8,128)(2,1)S(1)} %collective-permute-done.12.up_ref, ...), custom_call_target="tpu_custom_call", output_to_operand_aliasing={{}: (4, {})} | custom-call | tf_op jit(solution)/shard_map/final/pallas_call | solution.py:666
  138.9 0.1 collective-permute-done.10.up_ref
  139.0 1.2 collective-permute-done.11.down_ref
  140.2 1.7 %final.3 = bf16[1024,512]{1,0:T(8,128)(2,1)} custom-call(s32[1]{0:T(128)} %bitcast.where_ref, bf16[4,640,512]{2,1,0:T(8,128)(2,1)} %project_middle.1.refs_3_.up_own_ref.down_own_ref.own_ref, bf16[256,512]{1,0:T(8,128)(2,1)S(1)} %collective-permute-done.10.up_ref, ...), custom_call_target="tpu_custom_call", output_to_operand_aliasing={{}: (4, {})} | custom-call | tf_op jit(solution)/shard_map/final/pallas_call | solution.py:666
  (3 shorter events, 0.0 us)
Async XLA Ops:
  0.0 23.9 %copy-start.2 = (f32[32]{0:T(128)S(1)}, f32[32]{0:T(128)}, u32[]{:S(2)}) copy-start(f32[32]{0:T(128)} %param.18) | copy-start | bytes 388
  1.5 5.3 %collective-permute-start = (bf16[8,2560]{1,0:T(8,128)(2,1)S(1)}, bf16[8,2560]{1,0:T(8,128)(2,1)S(1)}, u32[]{:S(2)}, u32[]{:S(2)}) collective-permute-start(bf16[8,2560]{1,0:T(8,128)(2,1)S(1)} %pad_maximum_fusion), channel_id=1, source_target_pairs={{0,4},{4,8},{8,12},{12,16},{16,20},{20,24},{24,28},{1,5},{5,9},{9,... | collective-permute-start | bytes 122888 | tf_op jit(solution)/shard_map/ppermute | solution.py:384
  19.5 13.0 %copy-start.1 = (bf16[128,2048]{1,0:T(8,128)(2,1)S(1)}, bf16[128,2048]{1,0:T(8,128)(2,1)}, u32[]{:S(2)}) copy-start(bf16[128,2048]{1,0:T(8,128)(2,1)} %constant.6.clone.e_ref) | copy-start | bytes 1572868
  19.5 13.0 %all-to-all-start = ((bf16[8,16,2176]{2,1,0:T(8,128)(2,1)}), bf16[8,16,2176]{2,1,0:T(8,128)(2,1)S(1)}, u32[]{:S(2)}, u32[]{:S(2)}) async-start(bf16[8,16,2176]{2,1,0:T(8,128)(2,1)} %bitcast.15), calls=%async_computation | async-start | bytes 1114112 | tf_op jit(solution)/shard_map/all_to_all | solution.py:434
  33.6 13.2 %all-to-all-start.1 = ((bf16[8,16,2048]{2,1,0:T(8,128)(2,1)}), bf16[8,16,2048]{2,1,0:T(8,128)(2,1)S(1)}, u32[]{:S(2)}, u32[]{:S(2)}) async-start(bf16[8,16,2048]{2,1,0:T(8,128)(2,1)} %prefix.1.rest_2_), calls=%async_computation.1 | async-start | bytes 1048576 | tf_op jit(solution)/shard_map/all_to_all | solution.py:488
  46.8 3.4 %copy-start = (bf16[2048,2048]{1,0:T(8,128)(2,1)S(1)}, bf16[2048,2048]{1,0:T(8,128)(2,1)}, u32[]{:S(2)}) copy-start(bf16[2048,2048]{1,0:T(8,128)(2,1)} %w_ref.7) | copy-start | bytes 25165828
  59.0 32.2 %collective-permute-start.3 = (bf16[384,512]{1,0:T(8,128)(2,1)}, bf16[384,512]{1,0:T(8,128)(2,1)S(1)}, u32[]{:S(2)}, u32[]{:S(2)}) collective-permute-start(bf16[384,512]{1,0:T(8,128)(2,1)} %get-tuple-element.52), channel_id=1, source_target_pairs={{0,1},{1,2},{2,3},{3,0},{4,5},{5,6},{6,7},{7,4},{8,9},{9,10},{10,1... | collective-permute-start | bytes 1179656 | tf_op jit(solution)/shard_map/ppermute | solution.py:686
  60.6 30.6 %collective-permute-start.4 = (bf16[384,512]{1,0:T(8,128)(2,1)}, bf16[384,512]{1,0:T(8,128)(2,1)S(1)}, u32[]{:S(2)}, u32[]{:S(2)}) collective-permute-start(bf16[384,512]{1,0:T(8,128)(2,1)} %get-tuple-element.53), channel_id=1, source_target_pairs={{0,3},{1,0},{2,1},{3,2},{4,7},{5,4},{6,5},{7,6},{8,11},{9,8},{10,9... | collective-permute-start | bytes 1179656 | tf_op jit(solution)/shard_map/ppermute | solution.py:686
  62.9 34.6 %collective-permute-start.5 = (bf16[384,512]{1,0:T(8,128)(2,1)}, bf16[384,512]{1,0:T(8,128)(2,1)S(1)}, u32[]{:S(2)}, u32[]{:S(2)}) collective-permute-start(bf16[384,512]{1,0:T(8,128)(2,1)} %get-tuple-element.54), channel_id=1, source_target_pairs={{0,2},{1,3},{2,0},{3,1},{4,6},{5,7},{6,4},{7,5},{8,10},{9,11},{10,... | collective-permute-start | bytes 1179656 | tf_op jit(solution)/shard_map/ppermute | solution.py:686
  81.1 19.4 %collective-permute-start.1 = (bf16[640,512]{1,0:T(8,128)(2,1)}, bf16[640,512]{1,0:T(8,128)(2,1)S(1)}, u32[]{:S(2)}, u32[]{:S(2)}) collective-permute-start(bf16[640,512]{1,0:T(8,128)(2,1)} %get-tuple-element.50), channel_id=1, source_target_pairs={{0,1},{4,5},{8,9},{12,13},{16,17},{20,21},{24,25},{28,29}} | collective-permute-start | bytes 1966088 | tf_op jit(solution)/shard_map/ppermute | solution.py:609
  84.6 15.8 %collective-permute-start.2 = (bf16[640,512]{1,0:T(8,128)(2,1)}, bf16[640,512]{1,0:T(8,128)(2,1)S(1)}, u32[]{:S(2)}, u32[]{:S(2)}) collective-permute-start(bf16[640,512]{1,0:T(8,128)(2,1)} %get-tuple-element.51), channel_id=1, source_target_pairs={{3,2},{7,6},{11,10},{15,14},{19,18},{23,22},{27,26},{31,30}} | collective-permute-start | bytes 1966088 | tf_op jit(solution)/shard_map/ppermute | solution.py:610
  101.8 17.2 %collective-permute-start.9 = (bf16[384,512]{1,0:T(8,128)(2,1)S(1)}, bf16[384,512]{1,0:T(8,128)(2,1)S(1)}, u32[]{:S(2)}, u32[]{:S(2)}) collective-permute-start(bf16[384,512]{1,0:T(8,128)(2,1)S(1)} %get-tuple-element.58), channel_id=1, source_target_pairs={{2,1},{3,2},{6,5},{7,6},{10,9},{11,10},{14,13},{15,14},{18,17},{19... | collective-permute-start | bytes 1179656 | tf_op jit(solution)/shard_map/ppermute | solution.py:610
  102.5 16.5 %collective-permute-start.8 = (bf16[384,512]{1,0:T(8,128)(2,1)S(1)}, bf16[384,512]{1,0:T(8,128)(2,1)S(1)}, u32[]{:S(2)}, u32[]{:S(2)}) collective-permute-start(bf16[384,512]{1,0:T(8,128)(2,1)S(1)} %get-tuple-element.55.rest_0_), channel_id=1, source_target_pairs={{0,1},{1,2},{4,5},{5,6},{8,9},{9,10},{12,13},{13,14},{16,17},{17,1... | collective-permute-start | bytes 1179656 | tf_op jit(solution)/shard_map/ppermute | solution.py:609
  108.6 18.2 %collective-permute-start.7 = (bf16[256,512]{1,0:T(8,128)(2,1)S(1)}, bf16[256,512]{1,0:T(8,128)(2,1)S(1)}, u32[]{:S(2)}, u32[]{:S(2)}) collective-permute-start(bf16[256,512]{1,0:T(8,128)(2,1)S(1)} %get-tuple-element.57), channel_id=1, source_target_pairs={{2,1},{3,2},{6,5},{7,6},{10,9},{11,10},{14,13},{15,14},{18,17},{19... | collective-permute-start | bytes 786440 | tf_op jit(solution)/shard_map/ppermute | solution.py:610
  109.3 17.5 %collective-permute-start.6 = (bf16[256,512]{1,0:T(8,128)(2,1)S(1)}, bf16[256,512]{1,0:T(8,128)(2,1)S(1)}, u32[]{:S(2)}, u32[]{:S(2)}) collective-permute-start(bf16[256,512]{1,0:T(8,128)(2,1)S(1)} %get-tuple-element.56.refs_3_), channel_id=1, source_target_pairs={{0,1},{1,2},{4,5},{5,6},{8,9},{9,10},{12,13},{13,14},{16,17},{17,1... | collective-permute-start | bytes 786440 | tf_op jit(solution)/shard_map/ppermute | solution.py:609
  120.3 13.0 %collective-permute-start.13 = (bf16[384,512]{1,0:T(8,128)(2,1)S(1)}, bf16[384,512]{1,0:T(8,128)(2,1)S(1)}, u32[]{:S(2)}, u32[]{:S(2)}) collective-permute-start(bf16[384,512]{1,0:T(8,128)(2,1)S(1)} %get-tuple-element.62), channel_id=1, source_target_pairs={{1,0},{2,1},{3,2},{5,4},{6,5},{7,6},{9,8},{10,9},{11,10},{13,12},{... | collective-permute-start | bytes 1179656 | tf_op jit(solution)/shard_map/ppermute | solution.py:610
  121.6 14.6 %collective-permute-start.12 = (bf16[384,512]{1,0:T(8,128)(2,1)S(1)}, bf16[384,512]{1,0:T(8,128)(2,1)S(1)}, u32[]{:S(2)}, u32[]{:S(2)}) collective-permute-start(bf16[384,512]{1,0:T(8,128)(2,1)S(1)} %get-tuple-element.59.rest_0_), channel_id=1, source_target_pairs={{0,1},{1,2},{2,3},{4,5},{5,6},{6,7},{8,9},{9,10},{10,11},{12,13},{... | collective-permute-start | bytes 1179656 | tf_op jit(solution)/shard_map/ppermute | solution.py:609
  128.0 11.0 %collective-permute-start.10 = (bf16[256,512]{1,0:T(8,128)(2,1)S(1)}, bf16[256,512]{1,0:T(8,128)(2,1)S(1)}, u32[]{:S(2)}, u32[]{:S(2)}) collective-permute-start(bf16[256,512]{1,0:T(8,128)(2,1)S(1)} %get-tuple-element.60), channel_id=1, source_target_pairs={{0,1},{1,2},{2,3},{4,5},{5,6},{6,7},{8,9},{9,10},{10,11},{12,13},{... | collective-permute-start | bytes 786440 | tf_op jit(solution)/shard_map/ppermute | solution.py:609
  131.9 8.3 %collective-permute-start.11 = (bf16[256,512]{1,0:T(8,128)(2,1)S(1)}, bf16[256,512]{1,0:T(8,128)(2,1)S(1)}, u32[]{:S(2)}, u32[]{:S(2)}) collective-permute-start(bf16[256,512]{1,0:T(8,128)(2,1)S(1)} %get-tuple-element.61), channel_id=1, source_target_pairs={{1,0},{2,1},{3,2},{5,4},{6,5},{7,6},{9,8},{10,9},{11,10},{13,12},{... | collective-permute-start | bytes 786440 | tf_op jit(solution)/shard_map/ppermute | solution.py:610

commit v11 on v10

--- a/solution.py
+++ b/solution.py
@@ -27,8 +27,7 @@
 
 
 def silu(v):
-    half = 0.5 * v
-    return half + half * jnp.tanh(half)
+    return v * pl.reciprocal(1.0 + jnp.exp2(v * -LOG2E), approx=True)
 
 
 def high_low(v):
@@ -533,7 +532,7 @@
             out_shape=[shaped((size, part_out))] * len(slots) + [shaped((size, width))],
             compiler_params=params(),
             name="project_direct",
-        )(where, *operands, out_weight, in_hbm(after))
+        )(where, *operands, in_hbm(out_weight), in_hbm(after))
 
     def direct_final(start, normed, pieces, after):
         def tile(width, start=0):
@@ -585,7 +584,7 @@
             compiler_params=params(),
             cost_estimate=brief(),
             name="project_ends",
-        )(*operands, out_weight, in_hbm(after))
+        )(*operands, in_hbm(out_weight), in_hbm(after))
 
     def project_middle(shares, normed):
         size = normed.shape[0]
@@ -603,7 +602,7 @@
             compiler_params=params(),
             cost_estimate=brief(),
             name="project_middle",
-        )(in_hbm(normed), out_weight, in_hbm(shares))
+        )(in_hbm(normed), in_hbm(out_weight), in_hbm(shares))
 
     def permuted(up, down, s):
         up = lax.ppermute(up, "chan", [(a, a + 1) for a in range(s + 1)])

time: 143 us -> 141 us (0.986)
  local copies, waits for them, and re-layouts: 4.88 us -> 1.5 us
  Pallas kernels: 72.7 us -> 75.2 us
    unnamed x6 -> x4, local copies, waits for them, and re-layouts: 3.39 us -> 0.01 us
  transfers between devices with their start and end apart: 16 -> 16, of which waited for: 8 -> 8; matrix products, arithmetic and copies ran while one was open for 0% -> 0% of each run, Pallas kernels for 33% -> 35%
where the time goes in v11:
time: 141 us; the launch traced here: 140 us
  Pallas kernels  75.2 us (53%)
  starting transfers between devices  43.1 us (31%)
  waiting for transfers between devices  19.7 us (14%)
  local copies, waits for them, and re-layouts  1.5 us (1%)
    ppermute x5, starting transfers between devices, permuted(): up = lax.ppermute(up, 'chan', [(a, a + 1) for a in range(s + 1)])  22.7 us
    pallas_call x3, Pallas kernels, local_part(): pl.pallas_call(local_kernel, grid=(count,), in_specs=specs, out_specs=[ti...  18.4 us
    pallas_call x1, Pallas kernels, project_ends(): pl.pallas_call(functools.partial(ends_kernel, tiles=count), grid=(count +...  12.9 us
    pallas_call x1, Pallas kernels, local(): pl.pallas_call(states_kernel, grid=(width // WIDE,), in_specs=[lanes_at(t...  12.7 us
    pallas_call x1, Pallas kernels, project_direct(): pl.pallas_call(functools.partial(direct_kernel, tiles=count), grid_spec=p...  10 us
    pallas_call x1, Pallas kernels, project_middle(): pl.pallas_call(middle_kernel, grid=(chans - 2,), in_specs=[whole((size, w...  6.32 us
    ppermute x5, waiting for transfers between devices, permuted(): up = lax.ppermute(up, 'chan', [(a, a + 1) for a in range(s + 1)])  6.11 us
    pallas_call x4, Pallas kernels, onward(): pl.pallas_call(onward_kernel, grid_spec=pltpu.PrefetchScalarGridSpec(num_...  5.03 us
  transfers between devices with their start and end apart: 16, of which 8 were waited for; matrix products, arithmetic and copies ran while one was open for 0% of the time, Pallas kernels for 35%

profile of v11, /device:TPU:2, one launch (start us, length us, event | category | flops | bytes accessed | tf_op | source)
XLA Modules:
  0.0 139.6 jit_solution(17331645179563554930)
XLA Ops:
  0.0 0.0 copy-start.1
  0.0 0.7 slice.7
  0.7 0.8 slice.6
  1.5 1.9 %collective-permute-start = (bf16[8,2560]{1,0:T(8,128)(2,1)S(1)}, bf16[8,2560]{1,0:T(8,128)(2,1)S(1)}, u32[]{:S(2)}, u32[]{:S(2)}) collective-permute-start(bf16[8,2560]{1,0:T(8,128)(2,1)S(1)} %pad_maximum_fusion), channel_id=1, source_target_pairs={{0,4},{4,8},{8,12},{12,16},{16,20},{20,24},{24,28},{1,5},{5,9},{9,... | collective-permute-start | bytes 122888 | tf_op jit(solution)/shard_map/ppermute | solution.py:383
  3.4 3.4 %collective-permute-done.tail_ref.mtail_ref = bf16[8,2560]{1,0:T(8,128)(2,1)S(1)} collective-permute-done((bf16[8,2560]{1,0:T(8,128)(2,1)S(1)}, bf16[8,2560]{1,0:T(8,128)(2,1)S(1)}, u32[]{:S(2)}, u32[]{:S(2)}) %collective-permute-start) | collective-permute-done | bytes 40992 | tf_op jit(solution)/shard_map/ppermute | solution.py:383
  6.8 12.7 %states.1 = (bf16[1024,2048]{1,0:T(8,128)(2,1)}, bf16[128,2176]{1,0:T(8,128)(2,1)}, bf16[1024,512]{1,0:T(8,128)(2,1)}, bf16[2,128,1024]{2,1,0:T(8,128)(2,1)}, f3...) custom-call(bf16[1024,2048]{1,0:T(8,128)(2,1)} %x_ref.1, ...), custom_call_target="tpu_custom_call" | custom-call | tf_op jit(solution)/shard_map/states/pallas_call | solution.py:396
  19.5 0.0 copy-start
  19.5 4.4 %all-to-all-start = ((bf16[8,16,2176]{2,1,0:T(8,128)(2,1)}), bf16[8,16,2176]{2,1,0:T(8,128)(2,1)S(1)}, u32[]{:S(2)}, u32[]{:S(2)}) async-start(bf16[8,16,2176]{2,1,0:T(8,128)(2,1)} %bitcast.15), calls=%async_computation | async-start | bytes 1114112 | tf_op jit(solution)/shard_map/all_to_all | solution.py:433
  23.9 0.0 copy-done.1
  23.9 6.3 %local_part.3 = (bf16[1024,2048]{1,0:T(8,128)(2,1)}, f32[128,2048]{1,0:T(8,128)}) custom-call(bf16[1024,2048]{1,0:T(8,128)(2,1)} %get-tuple-element.34.xc_ref, bf16[1024,512]{1,0:T(8,128)(2,1)} %get-tuple-element.35.bc_ref, bf16[2,128,1024]{2,1,0:T(8,128)(2,1)} %get-tuple-element.36.bt_ref, f32[32,1024]{1,0:T(8,128)} %get-tuple-element.37.crow_ref, ...), custom_call_target="tpu_custom_call" | custom-call | flops 1 | bytes 1 | tf_op jit(solution)/shard_map/local_part/pallas_call | solution.py:460
  30.2 2.4 %all-to-all-done.pay_ref = bf16[8,16,2176]{2,1,0:T(8,128)(2,1)S(1)} async-done(((bf16[8,16,2176]{2,1,0:T(8,128)(2,1)}), bf16[8,16,2176]{2,1,0:T(8,128)(2,1)S(1)}, u32[]{:S(2)}, u32[]{:S(2)}) %all-to-all-start) | async-done | bytes 557088 | tf_op jit(solution)/shard_map/all_to_all | solution.py:433
  32.5 0.0 copy-done
  32.5 1.0 prefix.1.rest_2_
  33.6 4.9 %all-to-all-start.1 = ((bf16[8,16,2048]{2,1,0:T(8,128)(2,1)}), bf16[8,16,2048]{2,1,0:T(8,128)(2,1)S(1)}, u32[]{:S(2)}, u32[]{:S(2)}) async-start(bf16[8,16,2048]{2,1,0:T(8,128)(2,1)} %prefix.1.rest_2_), calls=%async_computation.1 | async-start | bytes 1048576 | tf_op jit(solution)/shard_map/all_to_all | solution.py:487
  38.4 6.7 %local_part.4 = (bf16[1024,2048]{1,0:T(8,128)(2,1)}, f32[128,2048]{1,0:T(8,128)}) custom-call(bf16[1024,2048]{1,0:T(8,128)(2,1)} %get-tuple-element.34.xc_ref, bf16[1024,512]{1,0:T(8,128)(2,1)} %get-tuple-element.35.bc_ref, bf16[2,128,1024]{2,1,0:T(8,128)(2,1)} %get-tuple-element.36.bt_ref, ...), custom_call_target="tpu_custom_call", output_to_operand_aliasing={{0}: (8, {})} | custom-call | flops 1 | bytes 1 | tf_op jit(solution)/shard_map/local_part/pallas_call | solution.py:460
  45.2 1.6 %all-to-all-done.1 = bf16[8,16,2048]{2,1,0:T(8,128)(2,1)S(1)} async-done(((bf16[8,16,2048]{2,1,0:T(8,128)(2,1)}), bf16[8,16,2048]{2,1,0:T(8,128)(2,1)S(1)}, u32[]{:S(2)}, u32[]{:S(2)}) %all-to-all-start.1) | async-done | bytes 524320 | tf_op jit(solution)/shard_map/all_to_all | solution.py:487
  46.7 10.0 %project_direct.1 = (bf16[384,512]{1,0:T(8,128)(2,1)}, bf16[384,512]{1,0:T(8,128)(2,1)}, bf16[384,512]{1,0:T(8,128)(2,1)}, bf16[384,2048]{1,0:T(8,128)(2,1)}) custom-call(s32[1]{0:T(128)} %bitcast.where_ref, bf16[1024,2048]{1,0:T(8,128)(2,1)} %get-tuple-element.44.y_ref.rest_1_, bf16[1024,512]{1,0:T(8,128)(2,1)} %get-tuple-element.35.bc_ref, ...), custom_call_target="tpu_custom_call" | custom-call | tf_op jit(solution)/shard_map/project_direct/pallas_call | solution.py:523
  56.7 1.6 %collective-permute-start.3 = (bf16[384,512]{1,0:T(8,128)(2,1)}, bf16[384,512]{1,0:T(8,128)(2,1)S(1)}, u32[]{:S(2)}, u32[]{:S(2)}) collective-permute-start(bf16[384,512]{1,0:T(8,128)(2,1)} %get-tuple-element.52), channel_id=1, source_target_pairs={{0,1},{1,2},{2,3},{3,0},{4,5},{5,6},{6,7},{7,4},{8,9},{9,10},{10,1... | collective-permute-start | bytes 1179656 | tf_op jit(solution)/shard_map/ppermute | solution.py:685
  58.3 2.2 %collective-permute-start.4 = (bf16[384,512]{1,0:T(8,128)(2,1)}, bf16[384,512]{1,0:T(8,128)(2,1)S(1)}, u32[]{:S(2)}, u32[]{:S(2)}) collective-permute-start(bf16[384,512]{1,0:T(8,128)(2,1)} %get-tuple-element.53), channel_id=1, source_target_pairs={{0,3},{1,0},{2,1},{3,2},{4,7},{5,4},{6,5},{7,6},{8,11},{9,8},{10,9... | collective-permute-start | bytes 1179656 | tf_op jit(solution)/shard_map/ppermute | solution.py:685
  60.6 0.8 collective-permute-start.5
  61.4 5.4 %local_part.5 = (bf16[1024,2048]{1,0:T(8,128)(2,1)}, f32[128,2048]{1,0:T(8,128)}) custom-call(bf16[1024,2048]{1,0:T(8,128)(2,1)} %get-tuple-element.34.xc_ref, bf16[1024,512]{1,0:T(8,128)(2,1)} %get-tuple-element.35.bc_ref, bf16[2,128,1024]{2,1,0:T(8,128)(2,1)} %get-tuple-element.36.bt_ref, ...), custom_call_target="tpu_custom_call", output_to_operand_aliasing={{0}: (8, {})} | custom-call | flops 1 | bytes 1 | tf_op jit(solution)/shard_map/local_part/pallas_call | solution.py:460
  66.8 12.9 %project_ends.1 = (bf16[4,640,512]{2,1,0:T(8,128)(2,1)}, bf16[640,512]{1,0:T(8,128)(2,1)}, bf16[640,512]{1,0:T(8,128)(2,1)}, bf16[640,2048]{1,0:T(8,128)(2,1)}) custom-call(bf16[1024,2048]{1,0:T(8,128)(2,1)} %get-tuple-element.47.y_ref, bf16[1024,512]{1,0:T(8,128)(2,1)} %get-tuple-element.35.bc_ref, bf16[1024,128]{1,0:T(8,128)(2,1)} %get-tuple-element.45.g_ref, ...), custom_call_target="tpu_custom_call" | custom-call | flops 1 | bytes 1 | tf_op jit(solution)/shard_map/project_ends/pallas_call | solution.py:566
  79.7 3.5 %collective-permute-start.1 = (bf16[640,512]{1,0:T(8,128)(2,1)}, bf16[640,512]{1,0:T(8,128)(2,1)S(1)}, u32[]{:S(2)}, u32[]{:S(2)}) collective-permute-start(bf16[640,512]{1,0:T(8,128)(2,1)} %get-tuple-element.50), channel_id=1, source_target_pairs={{0,1},{4,5},{8,9},{12,13},{16,17},{20,21},{24,25},{28,29}} | collective-permute-start | bytes 1966088 | tf_op jit(solution)/shard_map/ppermute | solution.py:608
  83.2 0.7 collective-permute-start.2
  83.9 6.3 %project_middle.1.refs_3_.up_own_ref.down_own_ref.own_ref = bf16[4,640,512]{2,1,0:T(8,128)(2,1)} custom-call(bf16[640,2048]{1,0:T(8,128)(2,1)} %get-tuple-element.48.normed_ref, bf16[2048,2048]{1,0:T(8,128)(2,1)} %w_ref.7, bf16[4,640,512]{2,1,0:T(8,128)(2,1)} %get-tuple-element.49.ends_ref), custom_call_target="tpu_custom_call", output_to_operand_aliasing={{}: (2, {})} | custom-call | flops 1 | bytes 1 | tf_op jit(solution)/shard_map/project_middle/pallas_call | solution.py:591
  90.2 0.0 collective-permute-done.3.refs_0_
  90.2 0.0 collective-permute-done.4.refs_1_
  90.2 5.0 %collective-permute-done.5.refs_2_ = bf16[384,512]{1,0:T(8,128)(2,1)S(1)} collective-permute-done((bf16[384,512]{1,0:T(8,128)(2,1)}, bf16[384,512]{1,0:T(8,128)(2,1)S(1)}, u32[]{:S(2)}, u32[]{:S(2)}) %collective-permute-start.5) | collective-permute-done | bytes 393248 | tf_op jit(solution)/shard_map/ppermute | solution.py:685
  95.2 3.0 %collective-permute-done.1.up_ref = bf16[640,512]{1,0:T(8,128)(2,1)S(1)} collective-permute-done((bf16[640,512]{1,0:T(8,128)(2,1)}, bf16[640,512]{1,0:T(8,128)(2,1)S(1)}, u32[]{:S(2)}, u32[]{:S(2)}) %collective-permute-start.1) | collective-permute-done | bytes 655392 | tf_op jit(solution)/shard_map/ppermute | solution.py:608
  98.2 0.0 collective-permute-done.2.down_ref
  98.2 1.3 onward.4
  99.5 0.7 collective-permute-start.9
  100.2 4.9 %collective-permute-start.8 = (bf16[384,512]{1,0:T(8,128)(2,1)S(1)}, bf16[384,512]{1,0:T(8,128)(2,1)S(1)}, u32[]{:S(2)}, u32[]{:S(2)}) collective-permute-start(bf16[384,512]{1,0:T(8,128)(2,1)S(1)} %get-tuple-element.55.rest_0_), channel_id=1, source_target_pairs={{0,1},{1,2},{4,5},{5,6},{8,9},{9,10},{12,13},{13,14},{16,17},{17,1... | collective-permute-start | bytes 1179656 | tf_op jit(solution)/shard_map/ppermute | solution.py:608
  105.1 1.2 onward.5
  106.3 0.7 collective-permute-start.7
  107.0 5.2 %collective-permute-start.6 = (bf16[256,512]{1,0:T(8,128)(2,1)S(1)}, bf16[256,512]{1,0:T(8,128)(2,1)S(1)}, u32[]{:S(2)}, u32[]{:S(2)}) collective-permute-start(bf16[256,512]{1,0:T(8,128)(2,1)S(1)} %get-tuple-element.56.refs_3_), channel_id=1, source_target_pairs={{0,1},{1,2},{4,5},{5,6},{8,9},{9,10},{12,13},{13,14},{16,17},{17,1... | collective-permute-start | bytes 786440 | tf_op jit(solution)/shard_map/ppermute | solution.py:608
  112.2 4.5 %direct_final.1.rest_0_ = bf16[1024,512]{1,0:T(8,128)(2,1)} custom-call(s32[1]{0:T(128)} %bitcast.where_ref, bf16[384,2048]{1,0:T(8,128)(2,1)} %get-tuple-element.46.rest_2_.after_ref.normed_ref, bf16[2048,2048]{1,0:T(8,128)(2,1)} %w_ref.7, bf16[384,512]{1,0:T(8,128)(2,1)S(1)} %collective-permute-done.3.refs_0_, ...), custom_call_target="tpu_custom_call" | custom-call | tf_op jit(solution)/shard_map/direct_final/pallas_call | solution.py:541
  116.7 0.0 collective-permute-done.9.down_ref
  116.7 0.0 collective-permute-done.8.up_ref
  116.7 1.3 onward.6
  118.0 1.3 collective-permute-start.13
  119.3 5.2 %collective-permute-start.12 = (bf16[384,512]{1,0:T(8,128)(2,1)S(1)}, bf16[384,512]{1,0:T(8,128)(2,1)S(1)}, u32[]{:S(2)}, u32[]{:S(2)}) collective-permute-start(bf16[384,512]{1,0:T(8,128)(2,1)S(1)} %get-tuple-element.59.rest_0_), channel_id=1, source_target_pairs={{0,1},{1,2},{2,3},{4,5},{5,6},{6,7},{8,9},{9,10},{10,11},{12,13},{... | collective-permute-start | bytes 1179656 | tf_op jit(solution)/shard_map/ppermute | solution.py:608
  124.5 0.0 collective-permute-done.7.down_ref
  124.5 0.0 collective-permute-done.6.up_ref
  124.5 1.2 onward.7
  125.7 3.9 %collective-permute-start.10 = (bf16[256,512]{1,0:T(8,128)(2,1)S(1)}, bf16[256,512]{1,0:T(8,128)(2,1)S(1)}, u32[]{:S(2)}, u32[]{:S(2)}) collective-permute-start(bf16[256,512]{1,0:T(8,128)(2,1)S(1)} %get-tuple-element.60), channel_id=1, source_target_pairs={{0,1},{1,2},{2,3},{4,5},{5,6},{6,7},{8,9},{9,10},{10,11},{12,13},{... | collective-permute-start | bytes 786440 | tf_op jit(solution)/shard_map/ppermute | solution.py:608
  129.7 1.3 collective-permute-start.11
  131.0 0.0 collective-permute-done.13.down_ref
  131.0 2.9 %collective-permute-done.12.up_ref = bf16[384,512]{1,0:T(8,128)(2,1)S(1)} collective-permute-done((bf16[384,512]{1,0:T(8,128)(2,1)S(1)}, bf16[384,512]{1,0:T(8,128)(2,1)S(1)}, u32[]{:S(2)}, u32[]{:S(2)}) %collective-permute-start.12) | collective-permute-done | bytes 393248 | tf_op jit(solution)/shard_map/ppermute | solution.py:608
  133.9 2.7 %final.2.rest_0_ = bf16[1024,512]{1,0:T(8,128)(2,1)} custom-call(s32[1]{0:T(128)} %bitcast.where_ref, bf16[4,640,512]{2,1,0:T(8,128)(2,1)} %project_middle.1.refs_3_.up_own_ref.down_own_ref.own_ref, bf16[384,512]{1,0:T(8,128)(2,1)S(1)} %collective-permute-done.12.up_ref, ...), custom_call_target="tpu_custom_call", output_to_operand_aliasing={{}: (4, {})} | custom-call | tf_op jit(solution)/shard_map/final/pallas_call | solution.py:665
  136.6 0.1 collective-permute-done.10.up_ref
  136.7 1.2 collective-permute-done.11.down_ref
  137.9 1.7 %final.3 = bf16[1024,512]{1,0:T(8,128)(2,1)} custom-call(s32[1]{0:T(128)} %bitcast.where_ref, bf16[4,640,512]{2,1,0:T(8,128)(2,1)} %project_middle.1.refs_3_.up_own_ref.down_own_ref.own_ref, bf16[256,512]{1,0:T(8,128)(2,1)S(1)} %collective-permute-done.10.up_ref, ...), custom_call_target="tpu_custom_call", output_to_operand_aliasing={{}: (4, {})} | custom-call | tf_op jit(solution)/shard_map/final/pallas_call | solution.py:665
  (3 shorter events, 0.0 us)
Async XLA Ops:
  0.0 23.9 %copy-start.1 = (f32[32]{0:T(128)S(1)}, f32[32]{0:T(128)}, u32[]{:S(2)}) copy-start(f32[32]{0:T(128)} %param.18) | copy-start | bytes 388
  1.5 5.3 %collective-permute-start = (bf16[8,2560]{1,0:T(8,128)(2,1)S(1)}, bf16[8,2560]{1,0:T(8,128)(2,1)S(1)}, u32[]{:S(2)}, u32[]{:S(2)}) collective-permute-start(bf16[8,2560]{1,0:T(8,128)(2,1)S(1)} %pad_maximum_fusion), channel_id=1, source_target_pairs={{0,4},{4,8},{8,12},{12,16},{16,20},{20,24},{24,28},{1,5},{5,9},{9,... | collective-permute-start | bytes 122888 | tf_op jit(solution)/shard_map/ppermute | solution.py:383
  19.5 13.0 %copy-start = (bf16[128,2048]{1,0:T(8,128)(2,1)S(1)}, bf16[128,2048]{1,0:T(8,128)(2,1)}, u32[]{:S(2)}) copy-start(bf16[128,2048]{1,0:T(8,128)(2,1)} %constant.6.clone.e_ref) | copy-start | bytes 1572868
  19.5 13.0 %all-to-all-start = ((bf16[8,16,2176]{2,1,0:T(8,128)(2,1)}), bf16[8,16,2176]{2,1,0:T(8,128)(2,1)S(1)}, u32[]{:S(2)}, u32[]{:S(2)}) async-start(bf16[8,16,2176]{2,1,0:T(8,128)(2,1)} %bitcast.15), calls=%async_computation | async-start | bytes 1114112 | tf_op jit(solution)/shard_map/all_to_all | solution.py:433
  33.6 13.2 %all-to-all-start.1 = ((bf16[8,16,2048]{2,1,0:T(8,128)(2,1)}), bf16[8,16,2048]{2,1,0:T(8,128)(2,1)S(1)}, u32[]{:S(2)}, u32[]{:S(2)}) async-start(bf16[8,16,2048]{2,1,0:T(8,128)(2,1)} %prefix.1.rest_2_), calls=%async_computation.1 | async-start | bytes 1048576 | tf_op jit(solution)/shard_map/all_to_all | solution.py:487
  56.7 33.4 %collective-permute-start.3 = (bf16[384,512]{1,0:T(8,128)(2,1)}, bf16[384,512]{1,0:T(8,128)(2,1)S(1)}, u32[]{:S(2)}, u32[]{:S(2)}) collective-permute-start(bf16[384,512]{1,0:T(8,128)(2,1)} %get-tuple-element.52), channel_id=1, source_target_pairs={{0,1},{1,2},{2,3},{3,0},{4,5},{5,6},{6,7},{7,4},{8,9},{9,10},{10,1... | collective-permute-start | bytes 1179656 | tf_op jit(solution)/shard_map/ppermute | solution.py:685
  58.3 31.9 %collective-permute-start.4 = (bf16[384,512]{1,0:T(8,128)(2,1)}, bf16[384,512]{1,0:T(8,128)(2,1)S(1)}, u32[]{:S(2)}, u32[]{:S(2)}) collective-permute-start(bf16[384,512]{1,0:T(8,128)(2,1)} %get-tuple-element.53), channel_id=1, source_target_pairs={{0,3},{1,0},{2,1},{3,2},{4,7},{5,4},{6,5},{7,6},{8,11},{9,8},{10,9... | collective-permute-start | bytes 1179656 | tf_op jit(solution)/shard_map/ppermute | solution.py:685
  60.6 34.6 %collective-permute-start.5 = (bf16[384,512]{1,0:T(8,128)(2,1)}, bf16[384,512]{1,0:T(8,128)(2,1)S(1)}, u32[]{:S(2)}, u32[]{:S(2)}) collective-permute-start(bf16[384,512]{1,0:T(8,128)(2,1)} %get-tuple-element.54), channel_id=1, source_target_pairs={{0,2},{1,3},{2,0},{3,1},{4,6},{5,7},{6,4},{7,5},{8,10},{9,11},{10,... | collective-permute-start | bytes 1179656 | tf_op jit(solution)/shard_map/ppermute | solution.py:685
  79.7 18.5 %collective-permute-start.1 = (bf16[640,512]{1,0:T(8,128)(2,1)}, bf16[640,512]{1,0:T(8,128)(2,1)S(1)}, u32[]{:S(2)}, u32[]{:S(2)}) collective-permute-start(bf16[640,512]{1,0:T(8,128)(2,1)} %get-tuple-element.50), channel_id=1, source_target_pairs={{0,1},{4,5},{8,9},{12,13},{16,17},{20,21},{24,25},{28,29}} | collective-permute-start | bytes 1966088 | tf_op jit(solution)/shard_map/ppermute | solution.py:608
  83.2 15.0 %collective-permute-start.2 = (bf16[640,512]{1,0:T(8,128)(2,1)}, bf16[640,512]{1,0:T(8,128)(2,1)S(1)}, u32[]{:S(2)}, u32[]{:S(2)}) collective-permute-start(bf16[640,512]{1,0:T(8,128)(2,1)} %get-tuple-element.51), channel_id=1, source_target_pairs={{3,2},{7,6},{11,10},{15,14},{19,18},{23,22},{27,26},{31,30}} | collective-permute-start | bytes 1966088 | tf_op jit(solution)/shard_map/ppermute | solution.py:609
  99.5 17.2 %collective-permute-start.9 = (bf16[384,512]{1,0:T(8,128)(2,1)S(1)}, bf16[384,512]{1,0:T(8,128)(2,1)S(1)}, u32[]{:S(2)}, u32[]{:S(2)}) collective-permute-start(bf16[384,512]{1,0:T(8,128)(2,1)S(1)} %get-tuple-element.58), channel_id=1, source_target_pairs={{2,1},{3,2},{6,5},{7,6},{10,9},{11,10},{14,13},{15,14},{18,17},{19... | collective-permute-start | bytes 1179656 | tf_op jit(solution)/shard_map/ppermute | solution.py:609
  100.2 16.5 %collective-permute-start.8 = (bf16[384,512]{1,0:T(8,128)(2,1)S(1)}, bf16[384,512]{1,0:T(8,128)(2,1)S(1)}, u32[]{:S(2)}, u32[]{:S(2)}) collective-permute-start(bf16[384,512]{1,0:T(8,128)(2,1)S(1)} %get-tuple-element.55.rest_0_), channel_id=1, source_target_pairs={{0,1},{1,2},{4,5},{5,6},{8,9},{9,10},{12,13},{13,14},{16,17},{17,1... | collective-permute-start | bytes 1179656 | tf_op jit(solution)/shard_map/ppermute | solution.py:608
  106.3 18.2 %collective-permute-start.7 = (bf16[256,512]{1,0:T(8,128)(2,1)S(1)}, bf16[256,512]{1,0:T(8,128)(2,1)S(1)}, u32[]{:S(2)}, u32[]{:S(2)}) collective-permute-start(bf16[256,512]{1,0:T(8,128)(2,1)S(1)} %get-tuple-element.57), channel_id=1, source_target_pairs={{2,1},{3,2},{6,5},{7,6},{10,9},{11,10},{14,13},{15,14},{18,17},{19... | collective-permute-start | bytes 786440 | tf_op jit(solution)/shard_map/ppermute | solution.py:609
  107.0 17.5 %collective-permute-start.6 = (bf16[256,512]{1,0:T(8,128)(2,1)S(1)}, bf16[256,512]{1,0:T(8,128)(2,1)S(1)}, u32[]{:S(2)}, u32[]{:S(2)}) collective-permute-start(bf16[256,512]{1,0:T(8,128)(2,1)S(1)} %get-tuple-element.56.refs_3_), channel_id=1, source_target_pairs={{0,1},{1,2},{4,5},{5,6},{8,9},{9,10},{12,13},{13,14},{16,17},{17,1... | collective-permute-start | bytes 786440 | tf_op jit(solution)/shard_map/ppermute | solution.py:608
  118.0 13.0 %collective-permute-start.13 = (bf16[384,512]{1,0:T(8,128)(2,1)S(1)}, bf16[384,512]{1,0:T(8,128)(2,1)S(1)}, u32[]{:S(2)}, u32[]{:S(2)}) collective-permute-start(bf16[384,512]{1,0:T(8,128)(2,1)S(1)} %get-tuple-element.62), channel_id=1, source_target_pairs={{1,0},{2,1},{3,2},{5,4},{6,5},{7,6},{9,8},{10,9},{11,10},{13,12},{... | collective-permute-start | bytes 1179656 | tf_op jit(solution)/shard_map/ppermute | solution.py:609
  119.3 14.6 %collective-permute-start.12 = (bf16[384,512]{1,0:T(8,128)(2,1)S(1)}, bf16[384,512]{1,0:T(8,128)(2,1)S(1)}, u32[]{:S(2)}, u32[]{:S(2)}) collective-permute-start(bf16[384,512]{1,0:T(8,128)(2,1)S(1)} %get-tuple-element.59.rest_0_), channel_id=1, source_target_pairs={{0,1},{1,2},{2,3},{4,5},{5,6},{6,7},{8,9},{9,10},{10,11},{12,13},{... | collective-permute-start | bytes 1179656 | tf_op jit(solution)/shard_map/ppermute | solution.py:608
  125.7 11.0 %collective-permute-start.10 = (bf16[256,512]{1,0:T(8,128)(2,1)S(1)}, bf16[256,512]{1,0:T(8,128)(2,1)S(1)}, u32[]{:S(2)}, u32[]{:S(2)}) collective-permute-start(bf16[256,512]{1,0:T(8,128)(2,1)S(1)} %get-tuple-element.60), channel_id=1, source_target_pairs={{0,1},{1,2},{2,3},{4,5},{5,6},{6,7},{8,9},{9,10},{10,11},{12,13},{... | collective-permute-start | bytes 786440 | tf_op jit(solution)/shard_map/ppermute | solution.py:608
  129.7 8.3 %collective-permute-start.11 = (bf16[256,512]{1,0:T(8,128)(2,1)S(1)}, bf16[256,512]{1,0:T(8,128)(2,1)S(1)}, u32[]{:S(2)}, u32[]{:S(2)}) collective-permute-start(bf16[256,512]{1,0:T(8,128)(2,1)S(1)} %get-tuple-element.61), channel_id=1, source_target_pairs={{1,0},{2,1},{3,2},{5,4},{6,5},{7,6},{9,8},{10,9},{11,10},{13,12},{... | collective-permute-start | bytes 786440 | tf_op jit(solution)/shard_map/ppermute | solution.py:609

commit v12 on v11

--- a/solution.py
+++ b/solution.py
@@ -268,10 +268,21 @@
 
 def direct_kernel(
     where_ref, y_ref, bc_ref, g_ref, enter_ref, gate_ref, gain_ref, e_ref, w_ref, after_ref,
-    *rest, tiles,
+    *rest, tiles, slots, chans,
 ):
-    *out_refs, normed_ref, carry, grown = rest
+    out_refs, (normed_ref, carry, grown, kept, sems) = rest[:-5], rest[-5:]
     i = pl.program_id(0)
+    part = kept.shape[2]
+
+    def fetch(k):
+        dest = lax.rem(where_ref[0] + slots[k], chans)
+        columns = pl.ds(pl.multiple_of(dest * part, part), part)
+        return pltpu.make_async_copy(w_ref.at[:, columns], kept.at[k], sems.at[k])
+
+    @pl.when(i == 0)
+    def _():
+        for k in range(len(slots)):
+            fetch(k).start()
 
     @pl.when(i < tiles)
     def _():
@@ -281,8 +292,9 @@
 
     for k, out_ref in enumerate(out_refs):
         @pl.when(i == tiles + k)
-        def _(out_ref=out_ref):
-            out_ref[...] = dot(normed_ref[...], w_ref[...]).astype(BF16)
+        def _(k=k, out_ref=out_ref):
+            fetch(k).wait()
+            out_ref[...] = dot(normed_ref[...], kept[k]).astype(BF16)
 
 
 def ends_kernel(
@@ -513,21 +525,18 @@
         operands, specs = norm_operands(start, count, tokens_each, y)
         size = count * tokens_each
 
-        def weights(i, where):
-            step = i - count
-            slot = slots[-1]
-            for k in range(len(slots) - 1, -1, -1):
-                slot = jnp.where(step <= k, slots[k], slot)
-            return (0, lax.rem(where[0] + slot, chans))
-
         return pl.pallas_call(
-            functools.partial(direct_kernel, tiles=count),
+            functools.partial(direct_kernel, tiles=count, slots=slots, chans=chans),
             grid_spec=pltpu.PrefetchScalarGridSpec(
                 num_scalar_prefetch=1,
                 grid=(count + len(slots),),
-                in_specs=specs + [pl.BlockSpec((width, part_out), weights), unread()],
+                in_specs=specs + [unread(), unread()],
                 out_specs=[whole((size, part_out))] * len(slots) + [whole((size, width))],
-                scratch_shapes=[pltpu.VMEM((tokens_each, width), F32)] * 2,
+                scratch_shapes=[pltpu.VMEM((tokens_each, width), F32)] * 2
+                + [
+                    pltpu.VMEM((len(slots), width, part_out), BF16),
+                    pltpu.SemaphoreType.DMA((len(slots),)),
+                ],
             ),
             out_shape=[shaped((size, part_out))] * len(slots) + [shaped((size, width))],
             compiler_params=params(),

time: 141 us -> 139 us (0.986)
  no operation moved by 1% of the time
where the time goes in v12:
time: 139 us; the launch traced here: 138 us
  Pallas kernels  73.9 us (53%)
  starting transfers between devices  43.2 us (31%)
  waiting for transfers between devices  19.6 us (14%)
  local copies, waits for them, and re-layouts  1.5 us (1%)
    ppermute x5, starting transfers between devices, permuted(): up = lax.ppermute(up, 'chan', [(a, a + 1) for a in range(s + 1)])  22.7 us
    pallas_call x3, Pallas kernels, local_part(): pl.pallas_call(local_kernel, grid=(count,), in_specs=specs, out_specs=[ti...  18.4 us
    pallas_call x1, Pallas kernels, project_ends(): pl.pallas_call(functools.partial(ends_kernel, tiles=count), grid=(count +...  12.9 us
    pallas_call x1, Pallas kernels, local(): pl.pallas_call(states_kernel, grid=(width // WIDE,), in_specs=[lanes_at(t...  12.7 us
    pallas_call x1, Pallas kernels, project_direct(): pl.pallas_call(functools.partial(direct_kernel, tiles=count, slots=slots,...  8.71 us
    pallas_call x1, Pallas kernels, project_middle(): pl.pallas_call(middle_kernel, grid=(chans - 2,), in_specs=[whole((size, w...  6.31 us
    ppermute x5, waiting for transfers between devices, permuted(): up = lax.ppermute(up, 'chan', [(a, a + 1) for a in range(s + 1)])  6.08 us
    pallas_call x4, Pallas kernels, onward(): pl.pallas_call(onward_kernel, grid_spec=pltpu.PrefetchScalarGridSpec(num_...  5.03 us
  transfers between devices with their start and end apart: 16, of which 8 were waited for; matrix products, arithmetic and copies ran while one was open for 0% of the time, Pallas kernels for 35%

profile of v12, /device:TPU:2, one launch (start us, length us, event | category | flops | bytes accessed | tf_op | source)
XLA Modules:
  0.0 138.4 jit_solution(17769355599780462919)
XLA Ops:
  0.0 0.0 copy-start.1
  0.0 0.7 slice.7
  0.7 0.8 slice.6
  1.5 1.9 %collective-permute-start = (bf16[8,2560]{1,0:T(8,128)(2,1)S(1)}, bf16[8,2560]{1,0:T(8,128)(2,1)S(1)}, u32[]{:S(2)}, u32[]{:S(2)}) collective-permute-start(bf16[8,2560]{1,0:T(8,128)(2,1)S(1)} %pad_maximum_fusion), channel_id=1, source_target_pairs={{0,4},{4,8},{8,12},{12,16},{16,20},{20,24},{24,28},{1,5},{5,9},{9,... | collective-permute-start | bytes 122888 | tf_op jit(solution)/shard_map/ppermute | solution.py:395
  3.4 3.4 %collective-permute-done.tail_ref.mtail_ref = bf16[8,2560]{1,0:T(8,128)(2,1)S(1)} collective-permute-done((bf16[8,2560]{1,0:T(8,128)(2,1)S(1)}, bf16[8,2560]{1,0:T(8,128)(2,1)S(1)}, u32[]{:S(2)}, u32[]{:S(2)}) %collective-permute-start) | collective-permute-done | bytes 40992 | tf_op jit(solution)/shard_map/ppermute | solution.py:395
  6.8 12.7 %states.1 = (bf16[1024,2048]{1,0:T(8,128)(2,1)}, bf16[128,2176]{1,0:T(8,128)(2,1)}, bf16[1024,512]{1,0:T(8,128)(2,1)}, bf16[2,128,1024]{2,1,0:T(8,128)(2,1)}, f3...) custom-call(bf16[1024,2048]{1,0:T(8,128)(2,1)} %x_ref.1, ...), custom_call_target="tpu_custom_call" | custom-call | tf_op jit(solution)/shard_map/states/pallas_call | solution.py:408
  19.5 0.0 copy-start
  19.5 4.4 %all-to-all-start = ((bf16[8,16,2176]{2,1,0:T(8,128)(2,1)}), bf16[8,16,2176]{2,1,0:T(8,128)(2,1)S(1)}, u32[]{:S(2)}, u32[]{:S(2)}) async-start(bf16[8,16,2176]{2,1,0:T(8,128)(2,1)} %bitcast.15), calls=%async_computation | async-start | bytes 1114112 | tf_op jit(solution)/shard_map/all_to_all | solution.py:445
  23.9 0.0 copy-done.1
  23.9 6.3 %local_part.3 = (bf16[1024,2048]{1,0:T(8,128)(2,1)}, f32[128,2048]{1,0:T(8,128)}) custom-call(bf16[1024,2048]{1,0:T(8,128)(2,1)} %get-tuple-element.34.xc_ref, bf16[1024,512]{1,0:T(8,128)(2,1)} %get-tuple-element.35.bc_ref, bf16[2,128,1024]{2,1,0:T(8,128)(2,1)} %get-tuple-element.36.bt_ref, f32[32,1024]{1,0:T(8,128)} %get-tuple-element.37.crow_ref, ...), custom_call_target="tpu_custom_call" | custom-call | flops 1 | bytes 1 | tf_op jit(solution)/shard_map/local_part/pallas_call | solution.py:472
  30.2 2.4 %all-to-all-done.pay_ref = bf16[8,16,2176]{2,1,0:T(8,128)(2,1)S(1)} async-done(((bf16[8,16,2176]{2,1,0:T(8,128)(2,1)}), bf16[8,16,2176]{2,1,0:T(8,128)(2,1)S(1)}, u32[]{:S(2)}, u32[]{:S(2)}) %all-to-all-start) | async-done | bytes 557088 | tf_op jit(solution)/shard_map/all_to_all | solution.py:445
  32.5 0.0 copy-done
  32.5 1.0 prefix.1.rest_2_
  33.6 4.9 %all-to-all-start.1 = ((bf16[8,16,2048]{2,1,0:T(8,128)(2,1)}), bf16[8,16,2048]{2,1,0:T(8,128)(2,1)S(1)}, u32[]{:S(2)}, u32[]{:S(2)}) async-start(bf16[8,16,2048]{2,1,0:T(8,128)(2,1)} %prefix.1.rest_2_), calls=%async_computation.1 | async-start | bytes 1048576 | tf_op jit(solution)/shard_map/all_to_all | solution.py:499
  38.4 6.7 %local_part.4 = (bf16[1024,2048]{1,0:T(8,128)(2,1)}, f32[128,2048]{1,0:T(8,128)}) custom-call(bf16[1024,2048]{1,0:T(8,128)(2,1)} %get-tuple-element.34.xc_ref, bf16[1024,512]{1,0:T(8,128)(2,1)} %get-tuple-element.35.bc_ref, bf16[2,128,1024]{2,1,0:T(8,128)(2,1)} %get-tuple-element.36.bt_ref, ...), custom_call_target="tpu_custom_call", output_to_operand_aliasing={{0}: (8, {})} | custom-call | flops 1 | bytes 1 | tf_op jit(solution)/shard_map/local_part/pallas_call | solution.py:472
  45.2 1.6 %all-to-all-done.1 = bf16[8,16,2048]{2,1,0:T(8,128)(2,1)S(1)} async-done(((bf16[8,16,2048]{2,1,0:T(8,128)(2,1)}), bf16[8,16,2048]{2,1,0:T(8,128)(2,1)S(1)}, u32[]{:S(2)}, u32[]{:S(2)}) %all-to-all-start.1) | async-done | bytes 524320 | tf_op jit(solution)/shard_map/all_to_all | solution.py:499
  46.7 8.7 %project_direct.1 = (bf16[384,512]{1,0:T(8,128)(2,1)}, bf16[384,512]{1,0:T(8,128)(2,1)}, bf16[384,512]{1,0:T(8,128)(2,1)}, bf16[384,2048]{1,0:T(8,128)(2,1)}) custom-call(s32[1]{0:T(128)} %bitcast.where_ref, bf16[1024,2048]{1,0:T(8,128)(2,1)} %get-tuple-element.44.y_ref.rest_1_, bf16[1024,512]{1,0:T(8,128)(2,1)} %get-tuple-element.35.bc_ref, ...), custom_call_target="tpu_custom_call" | custom-call | tf_op jit(solution)/shard_map/project_direct/pallas_call | solution.py:528
  55.5 1.6 %collective-permute-start.3 = (bf16[384,512]{1,0:T(8,128)(2,1)}, bf16[384,512]{1,0:T(8,128)(2,1)S(1)}, u32[]{:S(2)}, u32[]{:S(2)}) collective-permute-start(bf16[384,512]{1,0:T(8,128)(2,1)} %get-tuple-element.52), channel_id=1, source_target_pairs={{0,1},{1,2},{2,3},{3,0},{4,5},{5,6},{6,7},{7,4},{8,9},{9,10},{10,1... | collective-permute-start | bytes 1179656 | tf_op jit(solution)/shard_map/ppermute | solution.py:694
  57.1 2.3 %collective-permute-start.4 = (bf16[384,512]{1,0:T(8,128)(2,1)}, bf16[384,512]{1,0:T(8,128)(2,1)S(1)}, u32[]{:S(2)}, u32[]{:S(2)}) collective-permute-start(bf16[384,512]{1,0:T(8,128)(2,1)} %get-tuple-element.53), channel_id=1, source_target_pairs={{0,3},{1,0},{2,1},{3,2},{4,7},{5,4},{6,5},{7,6},{8,11},{9,8},{10,9... | collective-permute-start | bytes 1179656 | tf_op jit(solution)/shard_map/ppermute | solution.py:694
  59.4 0.8 collective-permute-start.5
  60.1 5.4 %local_part.5 = (bf16[1024,2048]{1,0:T(8,128)(2,1)}, f32[128,2048]{1,0:T(8,128)}) custom-call(bf16[1024,2048]{1,0:T(8,128)(2,1)} %get-tuple-element.34.xc_ref, bf16[1024,512]{1,0:T(8,128)(2,1)} %get-tuple-element.35.bc_ref, bf16[2,128,1024]{2,1,0:T(8,128)(2,1)} %get-tuple-element.36.bt_ref, ...), custom_call_target="tpu_custom_call", output_to_operand_aliasing={{0}: (8, {})} | custom-call | flops 1 | bytes 1 | tf_op jit(solution)/shard_map/local_part/pallas_call | solution.py:472
  65.5 12.9 %project_ends.1 = (bf16[4,640,512]{2,1,0:T(8,128)(2,1)}, bf16[640,512]{1,0:T(8,128)(2,1)}, bf16[640,512]{1,0:T(8,128)(2,1)}, bf16[640,2048]{1,0:T(8,128)(2,1)}) custom-call(bf16[1024,2048]{1,0:T(8,128)(2,1)} %get-tuple-element.47.y_ref, bf16[1024,512]{1,0:T(8,128)(2,1)} %get-tuple-element.35.bc_ref, bf16[1024,128]{1,0:T(8,128)(2,1)} %get-tuple-element.45.g_ref, ...), custom_call_target="tpu_custom_call" | custom-call | flops 1 | bytes 1 | tf_op jit(solution)/shard_map/project_ends/pallas_call | solution.py:575
  78.4 3.5 %collective-permute-start.1 = (bf16[640,512]{1,0:T(8,128)(2,1)}, bf16[640,512]{1,0:T(8,128)(2,1)S(1)}, u32[]{:S(2)}, u32[]{:S(2)}) collective-permute-start(bf16[640,512]{1,0:T(8,128)(2,1)} %get-tuple-element.50), channel_id=1, source_target_pairs={{0,1},{4,5},{8,9},{12,13},{16,17},{20,21},{24,25},{28,29}} | collective-permute-start | bytes 1966088 | tf_op jit(solution)/shard_map/ppermute | solution.py:617
  81.9 0.7 collective-permute-start.2
  82.6 6.3 %project_middle.1.refs_3_.up_own_ref.down_own_ref.own_ref = bf16[4,640,512]{2,1,0:T(8,128)(2,1)} custom-call(bf16[640,2048]{1,0:T(8,128)(2,1)} %get-tuple-element.48.normed_ref, bf16[2048,2048]{1,0:T(8,128)(2,1)} %w_ref.7, bf16[4,640,512]{2,1,0:T(8,128)(2,1)} %get-tuple-element.49.ends_ref), custom_call_target="tpu_custom_call", output_to_operand_aliasing={{}: (2, {})} | custom-call | flops 1 | bytes 1 | tf_op jit(solution)/shard_map/project_middle/pallas_call | solution.py:600
  89.0 0.0 collective-permute-done.3.refs_0_
  89.0 0.0 collective-permute-done.4.refs_1_
  89.0 5.0 %collective-permute-done.5.refs_2_ = bf16[384,512]{1,0:T(8,128)(2,1)S(1)} collective-permute-done((bf16[384,512]{1,0:T(8,128)(2,1)}, bf16[384,512]{1,0:T(8,128)(2,1)S(1)}, u32[]{:S(2)}, u32[]{:S(2)}) %collective-permute-start.5) | collective-permute-done | bytes 393248 | tf_op jit(solution)/shard_map/ppermute | solution.py:694
  93.9 3.0 %collective-permute-done.1.up_ref = bf16[640,512]{1,0:T(8,128)(2,1)S(1)} collective-permute-done((bf16[640,512]{1,0:T(8,128)(2,1)}, bf16[640,512]{1,0:T(8,128)(2,1)S(1)}, u32[]{:S(2)}, u32[]{:S(2)}) %collective-permute-start.1) | collective-permute-done | bytes 655392 | tf_op jit(solution)/shard_map/ppermute | solution.py:617
  97.0 0.0 collective-permute-done.2.down_ref
  97.0 1.3 onward.4
  98.3 0.7 collective-permute-start.9
  98.9 4.9 %collective-permute-start.8 = (bf16[384,512]{1,0:T(8,128)(2,1)S(1)}, bf16[384,512]{1,0:T(8,128)(2,1)S(1)}, u32[]{:S(2)}, u32[]{:S(2)}) collective-permute-start(bf16[384,512]{1,0:T(8,128)(2,1)S(1)} %get-tuple-element.55.rest_0_), channel_id=1, source_target_pairs={{0,1},{1,2},{4,5},{5,6},{8,9},{9,10},{12,13},{13,14},{16,17},{17,1... | collective-permute-start | bytes 1179656 | tf_op jit(solution)/shard_map/ppermute | solution.py:617
  103.9 1.2 onward.5
  105.1 0.7 collective-permute-start.7
  105.8 5.2 %collective-permute-start.6 = (bf16[256,512]{1,0:T(8,128)(2,1)S(1)}, bf16[256,512]{1,0:T(8,128)(2,1)S(1)}, u32[]{:S(2)}, u32[]{:S(2)}) collective-permute-start(bf16[256,512]{1,0:T(8,128)(2,1)S(1)} %get-tuple-element.56.refs_3_), channel_id=1, source_target_pairs={{0,1},{1,2},{4,5},{5,6},{8,9},{9,10},{12,13},{13,14},{16,17},{17,1... | collective-permute-start | bytes 786440 | tf_op jit(solution)/shard_map/ppermute | solution.py:617
  110.9 4.5 %direct_final.1.rest_0_ = bf16[1024,512]{1,0:T(8,128)(2,1)} custom-call(s32[1]{0:T(128)} %bitcast.where_ref, bf16[384,2048]{1,0:T(8,128)(2,1)} %get-tuple-element.46.rest_2_.after_ref.normed_ref, bf16[2048,2048]{1,0:T(8,128)(2,1)} %w_ref.7, bf16[384,512]{1,0:T(8,128)(2,1)S(1)} %collective-permute-done.3.refs_0_, ...), custom_call_target="tpu_custom_call" | custom-call | tf_op jit(solution)/shard_map/direct_final/pallas_call | solution.py:550
  115.4 0.0 collective-permute-done.9.down_ref
  115.4 0.0 collective-permute-done.8.up_ref
  115.4 1.3 onward.6
  116.7 1.3 collective-permute-start.13
  118.0 5.2 %collective-permute-start.12 = (bf16[384,512]{1,0:T(8,128)(2,1)S(1)}, bf16[384,512]{1,0:T(8,128)(2,1)S(1)}, u32[]{:S(2)}, u32[]{:S(2)}) collective-permute-start(bf16[384,512]{1,0:T(8,128)(2,1)S(1)} %get-tuple-element.59.rest_0_), channel_id=1, source_target_pairs={{0,1},{1,2},{2,3},{4,5},{5,6},{6,7},{8,9},{9,10},{10,11},{12,13},{... | collective-permute-start | bytes 1179656 | tf_op jit(solution)/shard_map/ppermute | solution.py:617
  123.2 0.0 collective-permute-done.7.down_ref
  123.3 0.0 collective-permute-done.6.up_ref
  123.3 1.2 onward.7
  124.5 3.9 %collective-permute-start.10 = (bf16[256,512]{1,0:T(8,128)(2,1)S(1)}, bf16[256,512]{1,0:T(8,128)(2,1)S(1)}, u32[]{:S(2)}, u32[]{:S(2)}) collective-permute-start(bf16[256,512]{1,0:T(8,128)(2,1)S(1)} %get-tuple-element.60), channel_id=1, source_target_pairs={{0,1},{1,2},{2,3},{4,5},{5,6},{6,7},{8,9},{9,10},{10,11},{12,13},{... | collective-permute-start | bytes 786440 | tf_op jit(solution)/shard_map/ppermute | solution.py:617
  128.4 1.3 collective-permute-start.11
  129.7 0.0 collective-permute-done.13.down_ref
  129.7 2.9 %collective-permute-done.12.up_ref = bf16[384,512]{1,0:T(8,128)(2,1)S(1)} collective-permute-done((bf16[384,512]{1,0:T(8,128)(2,1)S(1)}, bf16[384,512]{1,0:T(8,128)(2,1)S(1)}, u32[]{:S(2)}, u32[]{:S(2)}) %collective-permute-start.12) | collective-permute-done | bytes 393248 | tf_op jit(solution)/shard_map/ppermute | solution.py:617
  132.7 2.7 %final.2.rest_0_ = bf16[1024,512]{1,0:T(8,128)(2,1)} custom-call(s32[1]{0:T(128)} %bitcast.where_ref, bf16[4,640,512]{2,1,0:T(8,128)(2,1)} %project_middle.1.refs_3_.up_own_ref.down_own_ref.own_ref, bf16[384,512]{1,0:T(8,128)(2,1)S(1)} %collective-permute-done.12.up_ref, ...), custom_call_target="tpu_custom_call", output_to_operand_aliasing={{}: (4, {})} | custom-call | tf_op jit(solution)/shard_map/final/pallas_call | solution.py:674
  135.3 0.1 collective-permute-done.10.up_ref
  135.5 1.2 collective-permute-done.11.down_ref
  136.7 1.7 %final.3 = bf16[1024,512]{1,0:T(8,128)(2,1)} custom-call(s32[1]{0:T(128)} %bitcast.where_ref, bf16[4,640,512]{2,1,0:T(8,128)(2,1)} %project_middle.1.refs_3_.up_own_ref.down_own_ref.own_ref, bf16[256,512]{1,0:T(8,128)(2,1)S(1)} %collective-permute-done.10.up_ref, ...), custom_call_target="tpu_custom_call", output_to_operand_aliasing={{}: (4, {})} | custom-call | tf_op jit(solution)/shard_map/final/pallas_call | solution.py:674
  (3 shorter events, 0.0 us)
Async XLA Ops:
  0.0 23.9 %copy-start.1 = (f32[32]{0:T(128)S(1)}, f32[32]{0:T(128)}, u32[]{:S(2)}) copy-start(f32[32]{0:T(128)} %param.18) | copy-start | bytes 388
  1.5 5.3 %collective-permute-start = (bf16[8,2560]{1,0:T(8,128)(2,1)S(1)}, bf16[8,2560]{1,0:T(8,128)(2,1)S(1)}, u32[]{:S(2)}, u32[]{:S(2)}) collective-permute-start(bf16[8,2560]{1,0:T(8,128)(2,1)S(1)} %pad_maximum_fusion), channel_id=1, source_target_pairs={{0,4},{4,8},{8,12},{12,16},{16,20},{20,24},{24,28},{1,5},{5,9},{9,... | collective-permute-start | bytes 122888 | tf_op jit(solution)/shard_map/ppermute | solution.py:395
  19.5 13.0 %copy-start = (bf16[128,2048]{1,0:T(8,128)(2,1)S(1)}, bf16[128,2048]{1,0:T(8,128)(2,1)}, u32[]{:S(2)}) copy-start(bf16[128,2048]{1,0:T(8,128)(2,1)} %constant.6.clone.e_ref) | copy-start | bytes 1572868
  19.5 13.0 %all-to-all-start = ((bf16[8,16,2176]{2,1,0:T(8,128)(2,1)}), bf16[8,16,2176]{2,1,0:T(8,128)(2,1)S(1)}, u32[]{:S(2)}, u32[]{:S(2)}) async-start(bf16[8,16,2176]{2,1,0:T(8,128)(2,1)} %bitcast.15), calls=%async_computation | async-start | bytes 1114112 | tf_op jit(solution)/shard_map/all_to_all | solution.py:445
  33.6 13.2 %all-to-all-start.1 = ((bf16[8,16,2048]{2,1,0:T(8,128)(2,1)}), bf16[8,16,2048]{2,1,0:T(8,128)(2,1)S(1)}, u32[]{:S(2)}, u32[]{:S(2)}) async-start(bf16[8,16,2048]{2,1,0:T(8,128)(2,1)} %prefix.1.rest_2_), calls=%async_computation.1 | async-start | bytes 1048576 | tf_op jit(solution)/shard_map/all_to_all | solution.py:499
  55.5 33.5 %collective-permute-start.3 = (bf16[384,512]{1,0:T(8,128)(2,1)}, bf16[384,512]{1,0:T(8,128)(2,1)S(1)}, u32[]{:S(2)}, u32[]{:S(2)}) collective-permute-start(bf16[384,512]{1,0:T(8,128)(2,1)} %get-tuple-element.52), channel_id=1, source_target_pairs={{0,1},{1,2},{2,3},{3,0},{4,5},{5,6},{6,7},{7,4},{8,9},{9,10},{10,1... | collective-permute-start | bytes 1179656 | tf_op jit(solution)/shard_map/ppermute | solution.py:694
  57.1 31.9 %collective-permute-start.4 = (bf16[384,512]{1,0:T(8,128)(2,1)}, bf16[384,512]{1,0:T(8,128)(2,1)S(1)}, u32[]{:S(2)}, u32[]{:S(2)}) collective-permute-start(bf16[384,512]{1,0:T(8,128)(2,1)} %get-tuple-element.53), channel_id=1, source_target_pairs={{0,3},{1,0},{2,1},{3,2},{4,7},{5,4},{6,5},{7,6},{8,11},{9,8},{10,9... | collective-permute-start | bytes 1179656 | tf_op jit(solution)/shard_map/ppermute | solution.py:694
  59.4 34.6 %collective-permute-start.5 = (bf16[384,512]{1,0:T(8,128)(2,1)}, bf16[384,512]{1,0:T(8,128)(2,1)S(1)}, u32[]{:S(2)}, u32[]{:S(2)}) collective-permute-start(bf16[384,512]{1,0:T(8,128)(2,1)} %get-tuple-element.54), channel_id=1, source_target_pairs={{0,2},{1,3},{2,0},{3,1},{4,6},{5,7},{6,4},{7,5},{8,10},{9,11},{10,... | collective-permute-start | bytes 1179656 | tf_op jit(solution)/shard_map/ppermute | solution.py:694
  78.4 18.5 %collective-permute-start.1 = (bf16[640,512]{1,0:T(8,128)(2,1)}, bf16[640,512]{1,0:T(8,128)(2,1)S(1)}, u32[]{:S(2)}, u32[]{:S(2)}) collective-permute-start(bf16[640,512]{1,0:T(8,128)(2,1)} %get-tuple-element.50), channel_id=1, source_target_pairs={{0,1},{4,5},{8,9},{12,13},{16,17},{20,21},{24,25},{28,29}} | collective-permute-start | bytes 1966088 | tf_op jit(solution)/shard_map/ppermute | solution.py:617
  81.9 15.0 %collective-permute-start.2 = (bf16[640,512]{1,0:T(8,128)(2,1)}, bf16[640,512]{1,0:T(8,128)(2,1)S(1)}, u32[]{:S(2)}, u32[]{:S(2)}) collective-permute-start(bf16[640,512]{1,0:T(8,128)(2,1)} %get-tuple-element.51), channel_id=1, source_target_pairs={{3,2},{7,6},{11,10},{15,14},{19,18},{23,22},{27,26},{31,30}} | collective-permute-start | bytes 1966088 | tf_op jit(solution)/shard_map/ppermute | solution.py:618
  98.3 17.2 %collective-permute-start.9 = (bf16[384,512]{1,0:T(8,128)(2,1)S(1)}, bf16[384,512]{1,0:T(8,128)(2,1)S(1)}, u32[]{:S(2)}, u32[]{:S(2)}) collective-permute-start(bf16[384,512]{1,0:T(8,128)(2,1)S(1)} %get-tuple-element.58), channel_id=1, source_target_pairs={{2,1},{3,2},{6,5},{7,6},{10,9},{11,10},{14,13},{15,14},{18,17},{19... | collective-permute-start | bytes 1179656 | tf_op jit(solution)/shard_map/ppermute | solution.py:618
  98.9 16.5 %collective-permute-start.8 = (bf16[384,512]{1,0:T(8,128)(2,1)S(1)}, bf16[384,512]{1,0:T(8,128)(2,1)S(1)}, u32[]{:S(2)}, u32[]{:S(2)}) collective-permute-start(bf16[384,512]{1,0:T(8,128)(2,1)S(1)} %get-tuple-element.55.rest_0_), channel_id=1, source_target_pairs={{0,1},{1,2},{4,5},{5,6},{8,9},{9,10},{12,13},{13,14},{16,17},{17,1... | collective-permute-start | bytes 1179656 | tf_op jit(solution)/shard_map/ppermute | solution.py:617
  105.1 18.2 %collective-permute-start.7 = (bf16[256,512]{1,0:T(8,128)(2,1)S(1)}, bf16[256,512]{1,0:T(8,128)(2,1)S(1)}, u32[]{:S(2)}, u32[]{:S(2)}) collective-permute-start(bf16[256,512]{1,0:T(8,128)(2,1)S(1)} %get-tuple-element.57), channel_id=1, source_target_pairs={{2,1},{3,2},{6,5},{7,6},{10,9},{11,10},{14,13},{15,14},{18,17},{19... | collective-permute-start | bytes 786440 | tf_op jit(solution)/shard_map/ppermute | solution.py:618
  105.8 17.5 %collective-permute-start.6 = (bf16[256,512]{1,0:T(8,128)(2,1)S(1)}, bf16[256,512]{1,0:T(8,128)(2,1)S(1)}, u32[]{:S(2)}, u32[]{:S(2)}) collective-permute-start(bf16[256,512]{1,0:T(8,128)(2,1)S(1)} %get-tuple-element.56.refs_3_), channel_id=1, source_target_pairs={{0,1},{1,2},{4,5},{5,6},{8,9},{9,10},{12,13},{13,14},{16,17},{17,1... | collective-permute-start | bytes 786440 | tf_op jit(solution)/shard_map/ppermute | solution.py:617
  116.7 13.0 %collective-permute-start.13 = (bf16[384,512]{1,0:T(8,128)(2,1)S(1)}, bf16[384,512]{1,0:T(8,128)(2,1)S(1)}, u32[]{:S(2)}, u32[]{:S(2)}) collective-permute-start(bf16[384,512]{1,0:T(8,128)(2,1)S(1)} %get-tuple-element.62), channel_id=1, source_target_pairs={{1,0},{2,1},{3,2},{5,4},{6,5},{7,6},{9,8},{10,9},{11,10},{13,12},{... | collective-permute-start | bytes 1179656 | tf_op jit(solution)/shard_map/ppermute | solution.py:618
  118.0 14.6 %collective-permute-start.12 = (bf16[384,512]{1,0:T(8,128)(2,1)S(1)}, bf16[384,512]{1,0:T(8,128)(2,1)S(1)}, u32[]{:S(2)}, u32[]{:S(2)}) collective-permute-start(bf16[384,512]{1,0:T(8,128)(2,1)S(1)} %get-tuple-element.59.rest_0_), channel_id=1, source_target_pairs={{0,1},{1,2},{2,3},{4,5},{5,6},{6,7},{8,9},{9,10},{10,11},{12,13},{... | collective-permute-start | bytes 1179656 | tf_op jit(solution)/shard_map/ppermute | solution.py:617
  124.5 11.0 %collective-permute-start.10 = (bf16[256,512]{1,0:T(8,128)(2,1)S(1)}, bf16[256,512]{1,0:T(8,128)(2,1)S(1)}, u32[]{:S(2)}, u32[]{:S(2)}) collective-permute-start(bf16[256,512]{1,0:T(8,128)(2,1)S(1)} %get-tuple-element.60), channel_id=1, source_target_pairs={{0,1},{1,2},{2,3},{4,5},{5,6},{6,7},{8,9},{9,10},{10,11},{12,13},{... | collective-permute-start | bytes 786440 | tf_op jit(solution)/shard_map/ppermute | solution.py:617
  128.4 8.3 %collective-permute-start.11 = (bf16[256,512]{1,0:T(8,128)(2,1)S(1)}, bf16[256,512]{1,0:T(8,128)(2,1)S(1)}, u32[]{:S(2)}, u32[]{:S(2)}) collective-permute-start(bf16[256,512]{1,0:T(8,128)(2,1)S(1)} %get-tuple-element.61), channel_id=1, source_target_pairs={{1,0},{2,1},{3,2},{5,4},{6,5},{7,6},{9,8},{10,9},{11,10},{13,12},{... | collective-permute-start | bytes 786440 | tf_op jit(solution)/shard_map/ppermute | solution.py:618

commit v13 on v12

--- a/solution.py
+++ b/solution.py
@@ -75,7 +75,7 @@
 
 
 def states_kernel(
-    x_ref, maps_ref, step_ref, tail_ref, mtail_ref, bias_ref, rate_ref, ck_ref, mk_ref, e_ref,
+    xa_ref, xb_ref, xc_in_ref, xd_ref, maps_ref, step_ref, tail_ref, mtail_ref, bias_ref, rate_ref, ck_ref, mk_ref, e_ref,
     xc_ref, pay_ref, *rest,
 ):
     outs, (bc_ref, bt_ref, crow_ref, cols_ref, wrow_ref, g_ref) = rest[:6], rest[6:12]
@@ -155,13 +155,16 @@
             copy.start()
 
     scale[...] = dot(w_ref[...], e_ref[...])
-    for lane in range(0, x_ref.shape[1], LANES):
+    for lane in range(0, xa_ref.shape[1], LANES):
         at_lanes = slice(lane, lane + LANES)
         taps = [ck_ref[k : k + 1, at_lanes] for k in range(4)]
         tail = tail_ref[:, at_lanes].astype(F32)
         plain[:HALO] = tail
         early[:HALO] = taps[1] * tail + taps[0] * pltpu.roll(tail, 1, 0)
-        plain[HALO:] = x_ref[:, at_lanes].astype(F32)
+        quarter = tokens // 4
+        for k, x_ref in enumerate((xa_ref, xb_ref, xc_in_ref, xd_ref)):
+            first = HALO + k * quarter
+            plain[first : first + quarter] = x_ref[:, at_lanes].astype(F32)
         for b in range(blocks):
             at = b * BLK
             late = plain[at + HALO - 1 : at + HALO - 1 + BLK]
@@ -177,7 +180,7 @@
             xc_ref[at : at + BLK, at_lanes] = result.astype(BF16)
             scaled = result * scale[at : at + BLK, at_lanes]
             weighted[at : at + BLK, at_lanes] = scaled.astype(BF16)
-    step_width = x_ref.shape[1]
+    step_width = xa_ref.shape[1]
     group = c * step_width * groups // (heads * HEAD_DIM)
     at = pl.ds(pl.multiple_of(c * step_width, step_width), step_width)
     pay_ref[:, at] = dot(bt_ref[group], weighted[...]).astype(BF16)
@@ -408,8 +411,8 @@
     xc, pay, bc, bt, crow, cols, wrow, g_hl = pl.pallas_call(
         states_kernel,
         grid=(width // WIDE,),
-        in_specs=[
-            lanes_at(tokens),
+        in_specs=[pl.BlockSpec((tokens // 4, WIDE), lambda c, k=k: (k, c)) for k in range(4)]
+        + [
             whole((tokens * parts, STATE)),
             whole((heads, tokens)),
             lanes_at(HALO),
@@ -435,7 +438,7 @@
         compiler_params=params(),
         name="states",
     )(
-        in_hbm(inner_input), in_hbm(state_maps.reshape(tokens * parts, STATE)),
+        *[in_hbm(inner_input)] * 4, in_hbm(state_maps.reshape(tokens * parts, STATE)),
         in_hbm(step_input.T), tail, tail,
         in_hbm(step_bias.reshape(1, heads)), in_hbm(log_decay_rate.reshape(1, heads)),
         in_hbm(conv_kernel), in_hbm(map_kernel.reshape(4 * parts, STATE)), in_hbm(low),

time: 139 us -> 140 us (level)
  no operation moved by 1% of the time
where the time goes in v13:
time: 140 us; the launch traced here: 139 us
  Pallas kernels  74.1 us (53%)
  starting transfers between devices  43.2 us (31%)
  waiting for transfers between devices  19.7 us (14%)
  local copies, waits for them, and re-layouts  1.49 us (1%)
    ppermute x5, starting transfers between devices, permuted(): up = lax.ppermute(up, 'chan', [(a, a + 1) for a in range(s + 1)])  22.7 us
    pallas_call x3, Pallas kernels, local_part(): pl.pallas_call(local_kernel, grid=(count,), in_specs=specs, out_specs=[ti...  18.4 us
    pallas_call x1, Pallas kernels, project_ends(): pl.pallas_call(functools.partial(ends_kernel, tiles=count), grid=(count +...  12.9 us
    pallas_call x1, Pallas kernels, local(): pl.pallas_call(states_kernel, grid=(width // WIDE,), in_specs=[pl.BlockSp...  12.9 us
    pallas_call x1, Pallas kernels, project_direct(): pl.pallas_call(functools.partial(direct_kernel, tiles=count, slots=slots,...  8.71 us
    pallas_call x1, Pallas kernels, project_middle(): pl.pallas_call(middle_kernel, grid=(chans - 2,), in_specs=[whole((size, w...  6.32 us
    ppermute x5, waiting for transfers between devices, permuted(): up = lax.ppermute(up, 'chan', [(a, a + 1) for a in range(s + 1)])  6.09 us
    pallas_call x4, Pallas kernels, onward(): pl.pallas_call(onward_kernel, grid_spec=pltpu.PrefetchScalarGridSpec(num_...  5.03 us
  transfers between devices with their start and end apart: 16, of which 8 were waited for; matrix products, arithmetic and copies ran while one was open for 0% of the time, Pallas kernels for 35%

profile of v13, /device:TPU:2, one launch (start us, length us, event | category | flops | bytes accessed | tf_op | source)
XLA Modules:
  0.0 138.6 jit_solution(2304229459453317738)
XLA Ops:
  0.0 0.7 slice.7
  0.7 0.8 slice.6
  1.5 1.9 %collective-permute-start = (bf16[8,2560]{1,0:T(8,128)(2,1)S(1)}, bf16[8,2560]{1,0:T(8,128)(2,1)S(1)}, u32[]{:S(2)}, u32[]{:S(2)}) collective-permute-start(bf16[8,2560]{1,0:T(8,128)(2,1)S(1)} %pad_maximum_fusion), channel_id=1, source_target_pairs={{0,4},{4,8},{8,12},{12,16},{16,20},{20,24},{24,28},{1,5},{5,9},{9,... | collective-permute-start | bytes 122888 | tf_op jit(solution)/shard_map/ppermute | solution.py:398
  3.4 3.4 %collective-permute-done.tail_ref.mtail_ref = bf16[8,2560]{1,0:T(8,128)(2,1)S(1)} collective-permute-done((bf16[8,2560]{1,0:T(8,128)(2,1)S(1)}, bf16[8,2560]{1,0:T(8,128)(2,1)S(1)}, u32[]{:S(2)}, u32[]{:S(2)}) %collective-permute-start) | collective-permute-done | bytes 40992 | tf_op jit(solution)/shard_map/ppermute | solution.py:398
  6.8 0.0 copy-start.1
  6.8 12.9 %states.1 = (bf16[1024,2048]{1,0:T(8,128)(2,1)}, bf16[128,2176]{1,0:T(8,128)(2,1)}, bf16[1024,512]{1,0:T(8,128)(2,1)}, bf16[2,128,1024]{2,1,0:T(8,128)(2,1)}, f3...) custom-call(bf16[1024,2048]{1,0:T(8,128)(2,1)} %xd_ref.1, ...), custom_call_target="tpu_custom_call" | custom-call | tf_op jit(solution)/shard_map/states/pallas_call | solution.py:411
  19.7 0.0 copy-start
  19.7 4.4 %all-to-all-start = ((bf16[8,16,2176]{2,1,0:T(8,128)(2,1)}), bf16[8,16,2176]{2,1,0:T(8,128)(2,1)S(1)}, u32[]{:S(2)}, u32[]{:S(2)}) async-start(bf16[8,16,2176]{2,1,0:T(8,128)(2,1)} %bitcast.15), calls=%async_computation | async-start | bytes 1114112 | tf_op jit(solution)/shard_map/all_to_all | solution.py:448
  24.1 0.0 copy-done.1
  24.1 6.3 %local_part.3 = (bf16[1024,2048]{1,0:T(8,128)(2,1)}, f32[128,2048]{1,0:T(8,128)}) custom-call(bf16[1024,2048]{1,0:T(8,128)(2,1)} %get-tuple-element.34.xc_ref, bf16[1024,512]{1,0:T(8,128)(2,1)} %get-tuple-element.35.bc_ref, bf16[2,128,1024]{2,1,0:T(8,128)(2,1)} %get-tuple-element.36.bt_ref, f32[32,1024]{1,0:T(8,128)} %get-tuple-element.37.crow_ref, ...), custom_call_target="tpu_custom_call" | custom-call | flops 1 | bytes 1 | tf_op jit(solution)/shard_map/local_part/pallas_call | solution.py:475
  30.4 2.4 %all-to-all-done.pay_ref = bf16[8,16,2176]{2,1,0:T(8,128)(2,1)S(1)} async-done(((bf16[8,16,2176]{2,1,0:T(8,128)(2,1)}), bf16[8,16,2176]{2,1,0:T(8,128)(2,1)S(1)}, u32[]{:S(2)}, u32[]{:S(2)}) %all-to-all-start) | async-done | bytes 557088 | tf_op jit(solution)/shard_map/all_to_all | solution.py:448
  32.7 0.0 copy-done
  32.7 1.0 prefix.1.rest_2_
  33.8 4.9 %all-to-all-start.1 = ((bf16[8,16,2048]{2,1,0:T(8,128)(2,1)}), bf16[8,16,2048]{2,1,0:T(8,128)(2,1)S(1)}, u32[]{:S(2)}, u32[]{:S(2)}) async-start(bf16[8,16,2048]{2,1,0:T(8,128)(2,1)} %prefix.1.rest_2_), calls=%async_computation.1 | async-start | bytes 1048576 | tf_op jit(solution)/shard_map/all_to_all | solution.py:502
  38.6 6.7 %local_part.4 = (bf16[1024,2048]{1,0:T(8,128)(2,1)}, f32[128,2048]{1,0:T(8,128)}) custom-call(bf16[1024,2048]{1,0:T(8,128)(2,1)} %get-tuple-element.34.xc_ref, bf16[1024,512]{1,0:T(8,128)(2,1)} %get-tuple-element.35.bc_ref, bf16[2,128,1024]{2,1,0:T(8,128)(2,1)} %get-tuple-element.36.bt_ref, ...), custom_call_target="tpu_custom_call", output_to_operand_aliasing={{0}: (8, {})} | custom-call | flops 1 | bytes 1 | tf_op jit(solution)/shard_map/local_part/pallas_call | solution.py:475
  45.3 1.6 %all-to-all-done.1 = bf16[8,16,2048]{2,1,0:T(8,128)(2,1)S(1)} async-done(((bf16[8,16,2048]{2,1,0:T(8,128)(2,1)}), bf16[8,16,2048]{2,1,0:T(8,128)(2,1)S(1)}, u32[]{:S(2)}, u32[]{:S(2)}) %all-to-all-start.1) | async-done | bytes 524320 | tf_op jit(solution)/shard_map/all_to_all | solution.py:502
  46.9 8.7 %project_direct.1 = (bf16[384,512]{1,0:T(8,128)(2,1)}, bf16[384,512]{1,0:T(8,128)(2,1)}, bf16[384,512]{1,0:T(8,128)(2,1)}, bf16[384,2048]{1,0:T(8,128)(2,1)}) custom-call(s32[1]{0:T(128)} %bitcast.where_ref, bf16[1024,2048]{1,0:T(8,128)(2,1)} %get-tuple-element.44.y_ref.rest_1_, bf16[1024,512]{1,0:T(8,128)(2,1)} %get-tuple-element.35.bc_ref, ...), custom_call_target="tpu_custom_call" | custom-call | tf_op jit(solution)/shard_map/project_direct/pallas_call | solution.py:531
  55.6 1.6 %collective-permute-start.3 = (bf16[384,512]{1,0:T(8,128)(2,1)}, bf16[384,512]{1,0:T(8,128)(2,1)S(1)}, u32[]{:S(2)}, u32[]{:S(2)}) collective-permute-start(bf16[384,512]{1,0:T(8,128)(2,1)} %get-tuple-element.52), channel_id=1, source_target_pairs={{0,1},{1,2},{2,3},{3,0},{4,5},{5,6},{6,7},{7,4},{8,9},{9,10},{10,1... | collective-permute-start | bytes 1179656 | tf_op jit(solution)/shard_map/ppermute | solution.py:697
  57.3 2.2 %collective-permute-start.4 = (bf16[384,512]{1,0:T(8,128)(2,1)}, bf16[384,512]{1,0:T(8,128)(2,1)S(1)}, u32[]{:S(2)}, u32[]{:S(2)}) collective-permute-start(bf16[384,512]{1,0:T(8,128)(2,1)} %get-tuple-element.53), channel_id=1, source_target_pairs={{0,3},{1,0},{2,1},{3,2},{4,7},{5,4},{6,5},{7,6},{8,11},{9,8},{10,9... | collective-permute-start | bytes 1179656 | tf_op jit(solution)/shard_map/ppermute | solution.py:697
  59.5 0.8 collective-permute-start.5
  60.3 5.4 %local_part.5 = (bf16[1024,2048]{1,0:T(8,128)(2,1)}, f32[128,2048]{1,0:T(8,128)}) custom-call(bf16[1024,2048]{1,0:T(8,128)(2,1)} %get-tuple-element.34.xc_ref, bf16[1024,512]{1,0:T(8,128)(2,1)} %get-tuple-element.35.bc_ref, bf16[2,128,1024]{2,1,0:T(8,128)(2,1)} %get-tuple-element.36.bt_ref, ...), custom_call_target="tpu_custom_call", output_to_operand_aliasing={{0}: (8, {})} | custom-call | flops 1 | bytes 1 | tf_op jit(solution)/shard_map/local_part/pallas_call | solution.py:475
  65.7 12.9 %project_ends.1 = (bf16[4,640,512]{2,1,0:T(8,128)(2,1)}, bf16[640,512]{1,0:T(8,128)(2,1)}, bf16[640,512]{1,0:T(8,128)(2,1)}, bf16[640,2048]{1,0:T(8,128)(2,1)}) custom-call(bf16[1024,2048]{1,0:T(8,128)(2,1)} %get-tuple-element.47.y_ref, bf16[1024,512]{1,0:T(8,128)(2,1)} %get-tuple-element.35.bc_ref, bf16[1024,128]{1,0:T(8,128)(2,1)} %get-tuple-element.45.g_ref, ...), custom_call_target="tpu_custom_call" | custom-call | flops 1 | bytes 1 | tf_op jit(solution)/shard_map/project_ends/pallas_call | solution.py:578
  78.6 3.5 %collective-permute-start.1 = (bf16[640,512]{1,0:T(8,128)(2,1)}, bf16[640,512]{1,0:T(8,128)(2,1)S(1)}, u32[]{:S(2)}, u32[]{:S(2)}) collective-permute-start(bf16[640,512]{1,0:T(8,128)(2,1)} %get-tuple-element.50), channel_id=1, source_target_pairs={{0,1},{4,5},{8,9},{12,13},{16,17},{20,21},{24,25},{28,29}} | collective-permute-start | bytes 1966088 | tf_op jit(solution)/shard_map/ppermute | solution.py:620
  82.1 0.7 collective-permute-start.2
  82.8 6.3 %project_middle.1.refs_3_.up_own_ref.down_own_ref.own_ref = bf16[4,640,512]{2,1,0:T(8,128)(2,1)} custom-call(bf16[640,2048]{1,0:T(8,128)(2,1)} %get-tuple-element.48.normed_ref, bf16[2048,2048]{1,0:T(8,128)(2,1)} %w_ref.7, bf16[4,640,512]{2,1,0:T(8,128)(2,1)} %get-tuple-element.49.ends_ref), custom_call_target="tpu_custom_call", output_to_operand_aliasing={{}: (2, {})} | custom-call | flops 1 | bytes 1 | tf_op jit(solution)/shard_map/project_middle/pallas_call | solution.py:603
  89.1 0.0 collective-permute-done.3.refs_0_
  89.2 0.0 collective-permute-done.4.refs_1_
  89.2 5.0 %collective-permute-done.5.refs_2_ = bf16[384,512]{1,0:T(8,128)(2,1)S(1)} collective-permute-done((bf16[384,512]{1,0:T(8,128)(2,1)}, bf16[384,512]{1,0:T(8,128)(2,1)S(1)}, u32[]{:S(2)}, u32[]{:S(2)}) %collective-permute-start.5) | collective-permute-done | bytes 393248 | tf_op jit(solution)/shard_map/ppermute | solution.py:697
  94.1 3.0 %collective-permute-done.1.up_ref = bf16[640,512]{1,0:T(8,128)(2,1)S(1)} collective-permute-done((bf16[640,512]{1,0:T(8,128)(2,1)}, bf16[640,512]{1,0:T(8,128)(2,1)S(1)}, u32[]{:S(2)}, u32[]{:S(2)}) %collective-permute-start.1) | collective-permute-done | bytes 655392 | tf_op jit(solution)/shard_map/ppermute | solution.py:620
  97.2 0.0 collective-permute-done.2.down_ref
  97.2 1.3 onward.4
  98.5 0.7 collective-permute-start.9
  99.1 4.9 %collective-permute-start.8 = (bf16[384,512]{1,0:T(8,128)(2,1)S(1)}, bf16[384,512]{1,0:T(8,128)(2,1)S(1)}, u32[]{:S(2)}, u32[]{:S(2)}) collective-permute-start(bf16[384,512]{1,0:T(8,128)(2,1)S(1)} %get-tuple-element.55.rest_0_), channel_id=1, source_target_pairs={{0,1},{1,2},{4,5},{5,6},{8,9},{9,10},{12,13},{13,14},{16,17},{17,1... | collective-permute-start | bytes 1179656 | tf_op jit(solution)/shard_map/ppermute | solution.py:620
  104.1 1.2 onward.5
  105.3 0.7 collective-permute-start.7
  106.0 5.2 %collective-permute-start.6 = (bf16[256,512]{1,0:T(8,128)(2,1)S(1)}, bf16[256,512]{1,0:T(8,128)(2,1)S(1)}, u32[]{:S(2)}, u32[]{:S(2)}) collective-permute-start(bf16[256,512]{1,0:T(8,128)(2,1)S(1)} %get-tuple-element.56.refs_3_), channel_id=1, source_target_pairs={{0,1},{1,2},{4,5},{5,6},{8,9},{9,10},{12,13},{13,14},{16,17},{17,1... | collective-permute-start | bytes 786440 | tf_op jit(solution)/shard_map/ppermute | solution.py:620
  111.1 4.5 %direct_final.1.rest_0_ = bf16[1024,512]{1,0:T(8,128)(2,1)} custom-call(s32[1]{0:T(128)} %bitcast.where_ref, bf16[384,2048]{1,0:T(8,128)(2,1)} %get-tuple-element.46.rest_2_.after_ref.normed_ref, bf16[2048,2048]{1,0:T(8,128)(2,1)} %w_ref.7, bf16[384,512]{1,0:T(8,128)(2,1)S(1)} %collective-permute-done.3.refs_0_, ...), custom_call_target="tpu_custom_call" | custom-call | tf_op jit(solution)/shard_map/direct_final/pallas_call | solution.py:553
  115.6 0.0 collective-permute-done.9.down_ref
  115.6 0.0 collective-permute-done.8.up_ref
  115.6 1.3 onward.6
  116.9 1.3 collective-permute-start.13
  118.2 5.2 %collective-permute-start.12 = (bf16[384,512]{1,0:T(8,128)(2,1)S(1)}, bf16[384,512]{1,0:T(8,128)(2,1)S(1)}, u32[]{:S(2)}, u32[]{:S(2)}) collective-permute-start(bf16[384,512]{1,0:T(8,128)(2,1)S(1)} %get-tuple-element.59.rest_0_), channel_id=1, source_target_pairs={{0,1},{1,2},{2,3},{4,5},{5,6},{6,7},{8,9},{9,10},{10,11},{12,13},{... | collective-permute-start | bytes 1179656 | tf_op jit(solution)/shard_map/ppermute | solution.py:620
  123.4 0.0 collective-permute-done.7.down_ref
  123.5 0.0 collective-permute-done.6.up_ref
  123.5 1.2 onward.7
  124.7 3.9 %collective-permute-start.10 = (bf16[256,512]{1,0:T(8,128)(2,1)S(1)}, bf16[256,512]{1,0:T(8,128)(2,1)S(1)}, u32[]{:S(2)}, u32[]{:S(2)}) collective-permute-start(bf16[256,512]{1,0:T(8,128)(2,1)S(1)} %get-tuple-element.60), channel_id=1, source_target_pairs={{0,1},{1,2},{2,3},{4,5},{5,6},{6,7},{8,9},{9,10},{10,11},{12,13},{... | collective-permute-start | bytes 786440 | tf_op jit(solution)/shard_map/ppermute | solution.py:620
  128.6 1.3 collective-permute-start.11
  129.9 0.0 collective-permute-done.13.down_ref
  129.9 2.9 %collective-permute-done.12.up_ref = bf16[384,512]{1,0:T(8,128)(2,1)S(1)} collective-permute-done((bf16[384,512]{1,0:T(8,128)(2,1)S(1)}, bf16[384,512]{1,0:T(8,128)(2,1)S(1)}, u32[]{:S(2)}, u32[]{:S(2)}) %collective-permute-start.12) | collective-permute-done | bytes 393248 | tf_op jit(solution)/shard_map/ppermute | solution.py:620
  132.8 2.7 %final.2.rest_0_ = bf16[1024,512]{1,0:T(8,128)(2,1)} custom-call(s32[1]{0:T(128)} %bitcast.where_ref, bf16[4,640,512]{2,1,0:T(8,128)(2,1)} %project_middle.1.refs_3_.up_own_ref.down_own_ref.own_ref, bf16[384,512]{1,0:T(8,128)(2,1)S(1)} %collective-permute-done.12.up_ref, ...), custom_call_target="tpu_custom_call", output_to_operand_aliasing={{}: (4, {})} | custom-call | tf_op jit(solution)/shard_map/final/pallas_call | solution.py:677
  135.5 0.1 collective-permute-done.10.up_ref
  135.7 1.2 collective-permute-done.11.down_ref
  136.9 1.7 %final.3 = bf16[1024,512]{1,0:T(8,128)(2,1)} custom-call(s32[1]{0:T(128)} %bitcast.where_ref, bf16[4,640,512]{2,1,0:T(8,128)(2,1)} %project_middle.1.refs_3_.up_own_ref.down_own_ref.own_ref, bf16[256,512]{1,0:T(8,128)(2,1)S(1)} %collective-permute-done.10.up_ref, ...), custom_call_target="tpu_custom_call", output_to_operand_aliasing={{}: (4, {})} | custom-call | tf_op jit(solution)/shard_map/final/pallas_call | solution.py:677
  (3 shorter events, 0.0 us)
Async XLA Ops:
  1.5 5.3 %collective-permute-start = (bf16[8,2560]{1,0:T(8,128)(2,1)S(1)}, bf16[8,2560]{1,0:T(8,128)(2,1)S(1)}, u32[]{:S(2)}, u32[]{:S(2)}) collective-permute-start(bf16[8,2560]{1,0:T(8,128)(2,1)S(1)} %pad_maximum_fusion), channel_id=1, source_target_pairs={{0,4},{4,8},{8,12},{12,16},{16,20},{20,24},{24,28},{1,5},{5,9},{9,... | collective-permute-start | bytes 122888 | tf_op jit(solution)/shard_map/ppermute | solution.py:398
  6.8 17.3 %copy-start.1 = (f32[32]{0:T(128)S(1)}, f32[32]{0:T(128)}, u32[]{:S(2)}) copy-start(f32[32]{0:T(128)} %param.18) | copy-start | bytes 388
  19.7 13.0 %copy-start = (bf16[128,2048]{1,0:T(8,128)(2,1)S(1)}, bf16[128,2048]{1,0:T(8,128)(2,1)}, u32[]{:S(2)}) copy-start(bf16[128,2048]{1,0:T(8,128)(2,1)} %constant.6.clone.e_ref) | copy-start | bytes 1572868
  19.7 13.0 %all-to-all-start = ((bf16[8,16,2176]{2,1,0:T(8,128)(2,1)}), bf16[8,16,2176]{2,1,0:T(8,128)(2,1)S(1)}, u32[]{:S(2)}, u32[]{:S(2)}) async-start(bf16[8,16,2176]{2,1,0:T(8,128)(2,1)} %bitcast.15), calls=%async_computation | async-start | bytes 1114112 | tf_op jit(solution)/shard_map/all_to_all | solution.py:448
  33.8 13.2 %all-to-all-start.1 = ((bf16[8,16,2048]{2,1,0:T(8,128)(2,1)}), bf16[8,16,2048]{2,1,0:T(8,128)(2,1)S(1)}, u32[]{:S(2)}, u32[]{:S(2)}) async-start(bf16[8,16,2048]{2,1,0:T(8,128)(2,1)} %prefix.1.rest_2_), calls=%async_computation.1 | async-start | bytes 1048576 | tf_op jit(solution)/shard_map/all_to_all | solution.py:502
  55.6 33.5 %collective-permute-start.3 = (bf16[384,512]{1,0:T(8,128)(2,1)}, bf16[384,512]{1,0:T(8,128)(2,1)S(1)}, u32[]{:S(2)}, u32[]{:S(2)}) collective-permute-start(bf16[384,512]{1,0:T(8,128)(2,1)} %get-tuple-element.52), channel_id=1, source_target_pairs={{0,1},{1,2},{2,3},{3,0},{4,5},{5,6},{6,7},{7,4},{8,9},{9,10},{10,1... | collective-permute-start | bytes 1179656 | tf_op jit(solution)/shard_map/ppermute | solution.py:697
  57.3 31.9 %collective-permute-start.4 = (bf16[384,512]{1,0:T(8,128)(2,1)}, bf16[384,512]{1,0:T(8,128)(2,1)S(1)}, u32[]{:S(2)}, u32[]{:S(2)}) collective-permute-start(bf16[384,512]{1,0:T(8,128)(2,1)} %get-tuple-element.53), channel_id=1, source_target_pairs={{0,3},{1,0},{2,1},{3,2},{4,7},{5,4},{6,5},{7,6},{8,11},{9,8},{10,9... | collective-permute-start | bytes 1179656 | tf_op jit(solution)/shard_map/ppermute | solution.py:697
  59.5 34.6 %collective-permute-start.5 = (bf16[384,512]{1,0:T(8,128)(2,1)}, bf16[384,512]{1,0:T(8,128)(2,1)S(1)}, u32[]{:S(2)}, u32[]{:S(2)}) collective-permute-start(bf16[384,512]{1,0:T(8,128)(2,1)} %get-tuple-element.54), channel_id=1, source_target_pairs={{0,2},{1,3},{2,0},{3,1},{4,6},{5,7},{6,4},{7,5},{8,10},{9,11},{10,... | collective-permute-start | bytes 1179656 | tf_op jit(solution)/shard_map/ppermute | solution.py:697
  78.6 18.5 %collective-permute-start.1 = (bf16[640,512]{1,0:T(8,128)(2,1)}, bf16[640,512]{1,0:T(8,128)(2,1)S(1)}, u32[]{:S(2)}, u32[]{:S(2)}) collective-permute-start(bf16[640,512]{1,0:T(8,128)(2,1)} %get-tuple-element.50), channel_id=1, source_target_pairs={{0,1},{4,5},{8,9},{12,13},{16,17},{20,21},{24,25},{28,29}} | collective-permute-start | bytes 1966088 | tf_op jit(solution)/shard_map/ppermute | solution.py:620
  82.1 15.0 %collective-permute-start.2 = (bf16[640,512]{1,0:T(8,128)(2,1)}, bf16[640,512]{1,0:T(8,128)(2,1)S(1)}, u32[]{:S(2)}, u32[]{:S(2)}) collective-permute-start(bf16[640,512]{1,0:T(8,128)(2,1)} %get-tuple-element.51), channel_id=1, source_target_pairs={{3,2},{7,6},{11,10},{15,14},{19,18},{23,22},{27,26},{31,30}} | collective-permute-start | bytes 1966088 | tf_op jit(solution)/shard_map/ppermute | solution.py:621
  98.5 17.2 %collective-permute-start.9 = (bf16[384,512]{1,0:T(8,128)(2,1)S(1)}, bf16[384,512]{1,0:T(8,128)(2,1)S(1)}, u32[]{:S(2)}, u32[]{:S(2)}) collective-permute-start(bf16[384,512]{1,0:T(8,128)(2,1)S(1)} %get-tuple-element.58), channel_id=1, source_target_pairs={{2,1},{3,2},{6,5},{7,6},{10,9},{11,10},{14,13},{15,14},{18,17},{19... | collective-permute-start | bytes 1179656 | tf_op jit(solution)/shard_map/ppermute | solution.py:621
  99.1 16.5 %collective-permute-start.8 = (bf16[384,512]{1,0:T(8,128)(2,1)S(1)}, bf16[384,512]{1,0:T(8,128)(2,1)S(1)}, u32[]{:S(2)}, u32[]{:S(2)}) collective-permute-start(bf16[384,512]{1,0:T(8,128)(2,1)S(1)} %get-tuple-element.55.rest_0_), channel_id=1, source_target_pairs={{0,1},{1,2},{4,5},{5,6},{8,9},{9,10},{12,13},{13,14},{16,17},{17,1... | collective-permute-start | bytes 1179656 | tf_op jit(solution)/shard_map/ppermute | solution.py:620
  105.3 18.2 %collective-permute-start.7 = (bf16[256,512]{1,0:T(8,128)(2,1)S(1)}, bf16[256,512]{1,0:T(8,128)(2,1)S(1)}, u32[]{:S(2)}, u32[]{:S(2)}) collective-permute-start(bf16[256,512]{1,0:T(8,128)(2,1)S(1)} %get-tuple-element.57), channel_id=1, source_target_pairs={{2,1},{3,2},{6,5},{7,6},{10,9},{11,10},{14,13},{15,14},{18,17},{19... | collective-permute-start | bytes 786440 | tf_op jit(solution)/shard_map/ppermute | solution.py:621
  106.0 17.5 %collective-permute-start.6 = (bf16[256,512]{1,0:T(8,128)(2,1)S(1)}, bf16[256,512]{1,0:T(8,128)(2,1)S(1)}, u32[]{:S(2)}, u32[]{:S(2)}) collective-permute-start(bf16[256,512]{1,0:T(8,128)(2,1)S(1)} %get-tuple-element.56.refs_3_), channel_id=1, source_target_pairs={{0,1},{1,2},{4,5},{5,6},{8,9},{9,10},{12,13},{13,14},{16,17},{17,1... | collective-permute-start | bytes 786440 | tf_op jit(solution)/shard_map/ppermute | solution.py:620
  116.9 13.0 %collective-permute-start.13 = (bf16[384,512]{1,0:T(8,128)(2,1)S(1)}, bf16[384,512]{1,0:T(8,128)(2,1)S(1)}, u32[]{:S(2)}, u32[]{:S(2)}) collective-permute-start(bf16[384,512]{1,0:T(8,128)(2,1)S(1)} %get-tuple-element.62), channel_id=1, source_target_pairs={{1,0},{2,1},{3,2},{5,4},{6,5},{7,6},{9,8},{10,9},{11,10},{13,12},{... | collective-permute-start | bytes 1179656 | tf_op jit(solution)/shard_map/ppermute | solution.py:621
  118.2 14.6 %collective-permute-start.12 = (bf16[384,512]{1,0:T(8,128)(2,1)S(1)}, bf16[384,512]{1,0:T(8,128)(2,1)S(1)}, u32[]{:S(2)}, u32[]{:S(2)}) collective-permute-start(bf16[384,512]{1,0:T(8,128)(2,1)S(1)} %get-tuple-element.59.rest_0_), channel_id=1, source_target_pairs={{0,1},{1,2},{2,3},{4,5},{5,6},{6,7},{8,9},{9,10},{10,11},{12,13},{... | collective-permute-start | bytes 1179656 | tf_op jit(solution)/shard_map/ppermute | solution.py:620
  124.7 11.0 %collective-permute-start.10 = (bf16[256,512]{1,0:T(8,128)(2,1)S(1)}, bf16[256,512]{1,0:T(8,128)(2,1)S(1)}, u32[]{:S(2)}, u32[]{:S(2)}) collective-permute-start(bf16[256,512]{1,0:T(8,128)(2,1)S(1)} %get-tuple-element.60), channel_id=1, source_target_pairs={{0,1},{1,2},{2,3},{4,5},{5,6},{6,7},{8,9},{9,10},{10,11},{12,13},{... | collective-permute-start | bytes 786440 | tf_op jit(solution)/shard_map/ppermute | solution.py:620
  128.6 8.3 %collective-permute-start.11 = (bf16[256,512]{1,0:T(8,128)(2,1)S(1)}, bf16[256,512]{1,0:T(8,128)(2,1)S(1)}, u32[]{:S(2)}, u32[]{:S(2)}) collective-permute-start(bf16[256,512]{1,0:T(8,128)(2,1)S(1)} %get-tuple-element.61), channel_id=1, source_target_pairs={{1,0},{2,1},{3,2},{5,4},{6,5},{7,6},{9,8},{10,9},{11,10},{13,12},{... | collective-permute-start | bytes 786440 | tf_op jit(solution)/shard_map/ppermute | solution.py:621
